TPU v7x, 32 devices: a whole 2x2x4 slice. The times are simulated.
32 devices in a mesh: dp: 4 (over y, x), expert: 8 (over z, core).
Axes of the slice: x: 2, y: 2, z: 4, core: 2. Of those that a mesh axis runs over, the one named last changes fastest.
Arguments:
- tokens: bfloat16 [2048, 2048], P(('dp', 'expert')), may hold values from -6 to 6
- expert_ids: int32 [2048, 6], P(('dp', 'expert')), may hold values from 0 to 7, as said below
- gate_probs: float32 [2048, 6], P(('dp', 'expert')), may hold values from 0.1 to 0.5
- cotangent: bfloat16 [2048, 2048], P(('dp', 'expert')), may hold values from -6 to 6
- gate_proj: bfloat16 [8, 2048, 768], P('expert', 'dp'), may hold values from -0.125 to 0.125
- up_proj: bfloat16 [8, 2048, 768], P('expert', 'dp'), may hold values from -0.125 to 0.125
- down_proj: bfloat16 [8, 2048, 768], P('expert', 'dp'), may hold values from -0.21875 to 0.21875
Outputs:
- mixed: bfloat16 [2048, 2048], P(('dp', 'expert'))
- token_grads: bfloat16 [2048, 2048], P(('dp', 'expert'))
- prob_grads: float32 [2048, 6], P(('dp', 'expert'))
- grad_gate_proj: float32 [8, 2048, 768], P('expert', 'dp')
- grad_up_proj: float32 [8, 2048, 768], P('expert', 'dp')
- grad_down_proj: float32 [8, 2048, 768], P('expert', 'dp')
Inputs may be any that keep to these rules, and one draw needn't show every extreme that they name: `expert_ids`: each row names 6 different experts. Among the 64 rows of one device no expert is named by more than 64 rows, and in every data group some expert is named by exactly 64 rows of every device of that group.
All inputs are finite; a program needn't handle non-finite values.
Results may differ from a plain program's by a relative error of at most 0.0065.
Values may be sent and summed in bfloat16 or wider, within the bound.
No kernel may reach another device: no remote copies, remote signals or barrier semaphores. Data moves between devices by JAX's collectives and lax.ppermute only.
A program may use at most 128 MiB of HBM per device.

v0:
```python
import jax
import jax.numpy as jnp
from jax import lax
from jax.sharding import PartitionSpec as P


def routing_slots(expert_ids, experts):
    onehot = (expert_ids[:, :, None] == jnp.arange(experts, dtype=jnp.int32)[None, None, :]).astype(
        jnp.int32
    )
    per_token = jnp.sum(onehot, axis=1)
    earlier = jnp.cumsum(per_token, axis=0) - per_token
    return jnp.sum(onehot * earlier[:, None, :], axis=2)


def forward_rows(rows, gate_proj, up_proj, down_proj):
    gate_pre = jnp.dot(rows, gate_proj, preferred_element_type=jnp.float32)
    up_pre = jnp.dot(rows, up_proj, preferred_element_type=jnp.float32)
    hidden = (jax.nn.silu(gate_pre) * up_pre).astype(jnp.bfloat16)
    expert_out = lax.dot_general(
        hidden, down_proj, (((1,), (1,)), ((), ())), preferred_element_type=jnp.float32
    ).astype(jnp.bfloat16)
    return (expert_out, gate_pre, up_pre, hidden)


def backward_rows(grad_rows, gate_pre, up_pre, gate_proj, up_proj, down_proj):
    d_hidden = jnp.dot(grad_rows, down_proj, preferred_element_type=jnp.float32)
    sigmoid_gate = jax.nn.sigmoid(gate_pre)
    silu_gate = gate_pre * sigmoid_gate
    d_gate = (d_hidden * up_pre * sigmoid_gate * (1.0 + gate_pre * (1.0 - sigmoid_gate))).astype(
        jnp.bfloat16
    )
    d_up = (d_hidden * silu_gate).astype(jnp.bfloat16)
    across = (((1,), (1,)), ((), ()))
    d_rows = lax.dot_general(d_gate, gate_proj, across, preferred_element_type=jnp.float32)
    d_rows = d_rows + lax.dot_general(d_up, up_proj, across, preferred_element_type=jnp.float32)
    return (d_rows.astype(jnp.bfloat16), d_gate, d_up)


def pick_rows(source_rows, position, top_count):
    chosen = jnp.take(source_rows, position.reshape(-1), axis=0)
    return chosen.reshape(position.shape[0], top_count, source_rows.shape[1])


def on_device(tokens, expert_ids, gate_probs, cotangent, gate_proj, up_proj, down_proj):
    experts = lax.axis_size("expert")
    tok_dev, top_count = expert_ids.shape
    model_width = tokens.shape[1]
    capacity = min(tok_dev, (tok_dev * top_count * 4 + 3 * experts - 1) // (3 * experts))
    slot_index = routing_slots(expert_ids, experts)
    position = expert_ids * capacity + slot_index
    placing = (
        position[None, :, :] == jnp.arange(experts * capacity, dtype=jnp.int32)[:, None, None]
    ).astype(jnp.float32)
    placer = jnp.sum(placing, axis=2)
    weighted = jnp.sum(placing * gate_probs[None, :, :], axis=2)
    row_send = (
        jnp.dot(placer.astype(jnp.bfloat16), tokens, preferred_element_type=jnp.float32)
        .astype(jnp.bfloat16)
        .reshape(experts, capacity, model_width)
    )
    grad_send = (
        jnp.dot(weighted, cotangent.astype(jnp.float32), precision=lax.Precision.HIGHEST)
        .astype(jnp.bfloat16)
        .reshape(experts, capacity, model_width)
    )
    full_gate, full_up, full_down = (
        lax.all_gather(gate_proj[0], "dp", axis=0, tiled=True),
        lax.all_gather(up_proj[0], "dp", axis=0, tiled=True),
        lax.all_gather(down_proj[0], "dp", axis=0, tiled=True),
    )
    rows_in = lax.all_to_all(row_send, "expert", split_axis=0, concat_axis=0, tiled=True)
    rows_flat = rows_in.reshape(-1, model_width)
    expert_out, gate_pre, up_pre, hidden = forward_rows(rows_flat, full_gate, full_up, full_down)
    returned = lax.all_to_all(
        expert_out.reshape(experts, capacity, model_width),
        "expert",
        split_axis=0,
        concat_axis=0,
        tiled=True,
    )
    grads_in = lax.all_to_all(grad_send, "expert", split_axis=0, concat_axis=0, tiled=True)
    grads_flat = grads_in.reshape(-1, model_width)
    d_rows, d_gate, d_up = backward_rows(
        grads_flat, gate_pre, up_pre, full_gate, full_up, full_down
    )
    grad_back = lax.all_to_all(
        d_rows.reshape(experts, capacity, model_width),
        "expert",
        split_axis=0,
        concat_axis=0,
        tiled=True,
    )
    picked = pick_rows(returned.reshape(-1, model_width), position, top_count).astype(jnp.float32)
    mixed = jnp.sum(gate_probs[:, :, None] * picked, axis=1).astype(jnp.bfloat16)
    prob_grads = jnp.sum(cotangent.astype(jnp.float32)[:, None, :] * picked, axis=2)
    picked_grads = pick_rows(grad_back.reshape(-1, model_width), position, top_count).astype(
        jnp.float32
    )
    token_grads = jnp.sum(picked_grads, axis=1).astype(jnp.bfloat16)
    contract_rows = (((0,), (0,)), ((), ()))
    hidden_units = hidden.shape[1]
    gate_term = lax.dot_general(
        rows_flat, d_gate, contract_rows, preferred_element_type=jnp.float32
    )
    up_term = lax.dot_general(rows_flat, d_up, contract_rows, preferred_element_type=jnp.float32)
    down_term = lax.dot_general(
        grads_flat, hidden, contract_rows, preferred_element_type=jnp.float32
    )
    shares = lax.psum_scatter(
        jnp.concatenate([gate_term, up_term, down_term], axis=1),
        "dp",
        scatter_dimension=0,
        tiled=True,
    )
    grad_gate = shares[:, :hidden_units]
    grad_up = shares[:, hidden_units : 2 * hidden_units]
    grad_down = shares[:, 2 * hidden_units :]
    return (mixed, token_grads, prob_grads, grad_gate[None], grad_up[None], grad_down[None])


def solution(mesh):
    in_specs = (
        P(("dp", "expert"), None),
        P(("dp", "expert"), None),
        P(("dp", "expert"), None),
        P(("dp", "expert"), None),
        P("expert", "dp", None),
        P("expert", "dp", None),
        P("expert", "dp", None),
    )
    out_specs = (
        P(("dp", "expert"), None),
        P(("dp", "expert"), None),
        P(("dp", "expert"), None),
        P("expert", "dp", None),
        P("expert", "dp", None),
        P("expert", "dp", None),
    )
    return jax.shard_map(
        on_device, mesh=mesh, in_specs=in_specs, out_specs=out_specs, check_vma=False
    )
```

profile of v0, /device:TPU:0, one launch (start us, length us, event | category | flops | bytes accessed | tf_op | source)
XLA Modules:
  0.0 354.2 jit_solution(13552222249019314881)
XLA Ops:
  7.2 0.7 all-gather.11.cloned.1.call-update
  8.0 0.7 all-gather.9.cloned.1.call-update
  8.7 0.7 convert_reduce_fusion.1
  9.6 0.7 select_reduce_fusion.1
  10.3 0.7 multiply_add_fusion
  11.0 0.9 select_reduce_fusion
  12.0 3.2 convolution_convert_fusion
  15.1 6.3 %all-to-all-start.2 = ((bf16[8,64,2048]{2,1,0:T(8,128)(2,1)}), bf16[8,64,2048]{2,1,0:T(8,128)(2,1)S(1)}, u32[]{:S(2)}, u32[]{:S(2)}) async-start(bf16[8,64,2048]{2,1,0:T(8,128)(2,1)} %bitcast.58), calls=%async_computation.2 | async-start | bytes 4194304 | tf_op jit(solution)/shard_map/all_to_all | solution.py:82
  21.5 0.7 all-gather.7.cloned.1.call-update
  22.2 2.0 convolution_convert_fusion.1
  24.3 46.3 %all-to-all-done.2 = bf16[8,64,2048]{2,1,0:T(8,128)(2,1)S(1)} async-done(((bf16[8,64,2048]{2,1,0:T(8,128)(2,1)}), bf16[8,64,2048]{2,1,0:T(8,128)(2,1)S(1)}, u32[]{:S(2)}, u32[]{:S(2)}) %all-to-all-start.2) | async-done | bytes 2097184 | tf_op jit(solution)/shard_map/all_to_all | solution.py:82
  70.5 1.3 copy-done.3
  71.9 3.6 %all-to-all-start = ((bf16[8,64,2048]{2,1,0:T(8,128)(2,1)}), bf16[8,64,2048]{2,1,0:T(8,128)(2,1)S(1)}, u32[]{:S(2)}, u32[]{:S(2)}) async-start(bf16[8,64,2048]{2,1,0:T(8,128)(2,1)} %bitcast.59), calls=%async_computation | async-start | bytes 4194304 | tf_op jit(solution)/shard_map/all_to_all | solution.py:72
  75.5 0.2 reduce-scatter.2.cloned.1.call-start
  75.8 5.5 %fusion = f32[512,768]{1,0:T(8,128)} fusion(bf16[512,2048]{1,0:T(8,128)(2,1)} %bitcast.56, bf16[1,2048,768]{2,1,0:T(8,128)(2,1)} %all-gather.11.cloned.1.call-done), kind=kOutput, calls=%fused_computation.5 | convolution fusion | flops 1610612736 | bytes 6815744 | tf_op jit(solution)/shard_map/dot_general | solution.py:27
  81.2 43.3 %all-to-all-done = bf16[8,64,2048]{2,1,0:T(8,128)(2,1)S(1)} async-done(((bf16[8,64,2048]{2,1,0:T(8,128)(2,1)}), bf16[8,64,2048]{2,1,0:T(8,128)(2,1)S(1)}, u32[]{:S(2)}, u32[]{:S(2)}) %all-to-all-start) | async-done | bytes 2097184 | tf_op jit(solution)/shard_map/all_to_all | solution.py:72
  124.5 4.8 %fusion.6 = f32[512,768]{1,0:T(8,128)} fusion(bf16[512,2048]{1,0:T(8,128)(2,1)S(1)} %bitcast.52, bf16[1,2048,768]{2,1,0:T(8,128)(2,1)} %all-gather.9.cloned.1.call-done), kind=kOutput, calls=%fused_computation.11 | convolution fusion | flops 1610612736 | bytes 6815744 | tf_op jit(solution)/shard_map/dot_general | solution.py:18
  129.3 19.0 %all-gather.7.cloned.1.call-done = bf16[1,2048,768]{2,1,0:T(8,128)(2,1)} async-done(((bf16[1,512,768]{2,1,0:T(8,128)(2,1)}), bf16[1,2048,768]{2,1,0:T(8,128)(2,1)}) %all-gather.7.cloned.1.call-update) | async-done | bytes 3145744 | tf_op jit(solution)/shard_map/all_gather | solution.py:68
  148.3 5.3 %multiply_convert_fusion.1 = (bf16[512,768]{1,0:T(8,128)(2,1)S(1)}, bf16[512,768]{1,0:T(8,128)(2,1)S(1)}, bf16[512,768]{1,0:T(8,128)(2,1)S(1)}) fusion(f32[512,768]{1,0:T(8,128)} %fusion, f32[512,768]{1,0:T(8,128)} %fusion.6, bf16[512,2048]{1,0:T(8,128)(2,1)S(1)} %bitcast.53, bf16[1,2048,768]{2,1,0:T(8,128)(2,1)} %all-gather.7.cloned.1.call-done), kind=kOutput, calls=%fused_computation.26 | convolution fusion | flops 1616510976 | bytes 10747904 | tf_op jit(solution)/shard_map/dot_general | solution.py:17
  153.6 1.9 fusion.21
  155.5 1.9 fusion.19
  157.5 1.9 fusion.20
  159.4 7.0 %pad_maximum_fusion = f32[2048,2304]{0,1:T(8,128)} fusion(f32[2048,768]{0,1:T(8,128)S(1)} %fusion.21, f32[2048,768]{0,1:T(8,128)S(1)} %fusion.20, f32[2048,768]{0,1:T(8,128)S(1)} %fusion.19), kind=kLoop, calls=%fused_computation.2 | loop fusion | flops 9437184 | bytes 37748736 | tf_op jit(solution)/shard_map/concatenate | solution.py:111
  166.4 1.1 copy-done.8
  167.5 5.0 %fusion.12 = bf16[512,2048]{1,0:T(8,128)(2,1)} fusion(bf16[512,768]{1,0:T(8,128)(2,1)S(1)} %copy-done.8, bf16[1,2048,768]{2,1,0:T(8,128)(2,1)} %all-gather.11.cloned.1.call-done), kind=kOutput, calls=%fused_computation.18 | convolution fusion | flops 1611661312 | bytes 6029312 | tf_op jit(solution)/shard_map/dot_general | solution.py:20
  172.5 4.6 %all-to-all-start.1 = ((bf16[8,64,2048]{2,1,0:T(8,128)(2,1)}), bf16[8,64,2048]{2,1,0:T(8,128)(2,1)S(1)}, u32[]{:S(2)}, u32[]{:S(2)}) async-start(bf16[8,64,2048]{2,1,0:T(8,128)(2,1)} %bitcast.61), calls=%async_computation.1 | async-start | bytes 4194304 | tf_op jit(solution)/shard_map/all_to_all | solution.py:75
  177.1 4.1 %fusion.4 = f32[512,2048]{1,0:T(8,128)S(1)} fusion(bf16[512,768]{1,0:T(8,128)(2,1)} %copy-done.6, bf16[1,2048,768]{2,1,0:T(8,128)(2,1)} %all-gather.9.cloned.1.call-done), kind=kOutput, calls=%fused_computation.9 | convolution fusion | flops 1610612736 | bytes 8126464 | tf_op jit(solution)/shard_map/dot_general | solution.py:36
  181.2 3.2 add_convert_fusion
  184.4 41.8 %all-to-all-done.1 = bf16[8,64,2048]{2,1,0:T(8,128)(2,1)S(1)} async-done(((bf16[8,64,2048]{2,1,0:T(8,128)(2,1)}), bf16[8,64,2048]{2,1,0:T(8,128)(2,1)S(1)}, u32[]{:S(2)}, u32[]{:S(2)}) %all-to-all-start.1) | async-done | bytes 2097184 | tf_op jit(solution)/shard_map/all_to_all | solution.py:75
  226.2 4.5 %all-to-all-start.3 = ((bf16[8,64,2048]{2,1,0:T(8,128)(2,1)}), bf16[8,64,2048]{2,1,0:T(8,128)(2,1)}, u32[]{:S(2)}, u32[]{:S(2)}) async-start(bf16[8,64,2048]{2,1,0:T(8,128)(2,1)} %bitcast.60), calls=%async_computation.3 | async-start | bytes 4194304 | tf_op jit(solution)/shard_map/all_to_all | solution.py:87
  231.0 2.6 mul.79
  233.6 4.8 %mul.80 = f32[384,2048]{1,0:T(8,128)} reshape(f32[64,6,2048]{2,1,0:T(8,128)} %mul.79) | data formatting | bytes 6291456 | tf_op jit(solution)/shard_map/mul | solution.py:96
  238.5 3.1 gather_fusion
  241.6 38.2 %all-to-all-done.3 = bf16[8,64,2048]{2,1,0:T(8,128)(2,1)} async-done(((bf16[8,64,2048]{2,1,0:T(8,128)(2,1)}), bf16[8,64,2048]{2,1,0:T(8,128)(2,1)}, u32[]{:S(2)}, u32[]{:S(2)}) %all-to-all-start.3) | async-done | bytes 2097184 | tf_op jit(solution)/shard_map/all_to_all | solution.py:87
  279.7 7.0 %gather_fusion.1 = bf16[384,2048]{1,0:T(8,128)(2,1)} fusion(bf16[512,2048]{1,0:T(8,128)(2,1)} %bitcast.10, s32[1024]{0:T(1024)S(1)} %pad_clamp_fusion), kind=kCustom, calls=%fused_computation.1.clone | custom fusion | bytes 3147264 | tf_op jit(solution)/shard_map/jit(_take)/gather | solution.py:41
  286.8 3.4 broadcast_select_fusion
  290.2 1.6 reshape.76
  291.8 4.6 %reshape.77 = f32[64,6,2048]{2,1,0:T(8,128)} reshape(f32[384,2048]{1,0:T(8,128)} %get-tuple-element.34) | data formatting | bytes 6291456 | tf_op jit(solution)/shard_map/convert_element_type | solution.py:94
  296.4 2.5 multiply_reduce_fusion.1
  298.9 0.1 reduce_sum.75
  299.0 0.7 copy.34
  299.7 3.6 %reduce_sum.73 = bf16[64,2048]{1,0:T(8,128)(2,1)} reduce(bf16[64,6,2048]{2,1,0:T(8,128)(2,1)} %reshape.76, bf16[]{:T(256)} %constant.26.clone.1), dimensions={1}, to_apply=%region_6.8 | reduce | flops 655360 | bytes 1835010 | tf_op jit(solution)/shard_map/reduce_sum | solution.py:100
  303.3 4.5 %multiply_reduce_fusion = bf16[64,2048]{1,0:T(8,128)(2,1)} fusion(f32[64,6,2048]{2,1,0:T(8,128)} %reshape.77, f32[64,6]{1,0:T(8,128)S(1)} %copy.29), kind=kLoop, calls=%fused_computation.4 | loop fusion | flops 1441792 | bytes 3409408 | tf_op jit(solution)/shard_map/reduce_sum | solution.py:95
  307.8 29.6 %reduce-scatter.2.cloned.1.call-done = f32[512,2304]{0,1:T(8,128)} async-done(((f32[2048,2304]{0,1:T(8,128)}), f32[512,2304]{0,1:T(8,128)}) %reduce-scatter.2.cloned.1.call-update) | async-done | bytes 4718608 | tf_op jit(solution)/shard_map/reduce_scatter | solution.py:110
  337.4 4.0 %slice_bitcast_fusion = (f32[1,512,768]{1,2,0:T(8,128)}, f32[1,512,768]{1,2,0:T(8,128)S(1)}, f32[1,512,768]{1,2,0:T(8,128)S(1)}) fusion(f32[512,2304]{0,1:T(8,128)} %reduce-scatter.2.cloned.1.call-done), kind=kLoop, calls=%fused_computation.21 | loop fusion | bytes 9437184 | tf_op jit(solution)/shard_map/broadcast_in_dim | solution.py:119
  341.4 3.0 copy.37
  344.4 1.6 copy.36
  346.0 1.6 copy.35
  (36 shorter events, 0.8 us)
Async XLA Ops:
  7.2 15.0 %copy-start = (bf16[64,2048]{1,0:T(8,128)(2,1)S(1)}, bf16[64,2048]{1,0:T(8,128)(2,1)}, u32[]{:S(2)}) copy-start(bf16[64,2048]{1,0:T(8,128)(2,1)} %param.9) | copy-start | bytes 786436
  7.2 4.8 %copy-start.5 = (bf16[64,2048]{1,0:T(8,128)(2,1)S(1)}, bf16[64,2048]{1,0:T(8,128)(2,1)}, u32[]{:S(2)}) copy-start(bf16[64,2048]{1,0:T(8,128)(2,1)} %param.12) | copy-start | bytes 786436
  7.2 68.6 %all-gather.11.cloned.1.call-start = ((), (), s32[]{:S(2)}) async-start(), calls=%async_computation.8 | async-start | bytes 3932160 | tf_op jit(solution)/shard_map/all_gather | solution.py:70
  7.9 116.6 %all-gather.9.cloned.1.call-start = ((), (), s32[]{:S(2)}) async-start(), calls=%async_computation.7 | async-start | bytes 3932160 | tf_op jit(solution)/shard_map/all_gather | solution.py:69
  15.1 55.4 %all-to-all-start.2 = ((bf16[8,64,2048]{2,1,0:T(8,128)(2,1)}), bf16[8,64,2048]{2,1,0:T(8,128)(2,1)S(1)}, u32[]{:S(2)}, u32[]{:S(2)}) async-start(bf16[8,64,2048]{2,1,0:T(8,128)(2,1)} %bitcast.58), calls=%async_computation.2 | async-start | bytes 4194304 | tf_op jit(solution)/shard_map/all_to_all | solution.py:82
  21.5 126.8 %all-gather.7.cloned.1.call-start = ((), (), s32[]{:S(2)}) async-start(), calls=%async_computation.6 | async-start | bytes 3932160 | tf_op jit(solution)/shard_map/all_gather | solution.py:68
  70.5 1.3 copy-start.3
  71.9 52.6 %all-to-all-start = ((bf16[8,64,2048]{2,1,0:T(8,128)(2,1)}), bf16[8,64,2048]{2,1,0:T(8,128)(2,1)S(1)}, u32[]{:S(2)}, u32[]{:S(2)}) async-start(bf16[8,64,2048]{2,1,0:T(8,128)(2,1)} %bitcast.59), calls=%async_computation | async-start | bytes 4194304 | tf_op jit(solution)/shard_map/all_to_all | solution.py:72
  75.5 261.9 %reduce-scatter.2.cloned.1.call-start = ((), (), s32[]{:S(2)}) async-start(), calls=%async_computation.5 | async-start | bytes 23592960 | tf_op jit(solution)/shard_map/reduce_scatter | solution.py:110
  148.3 5.3 %copy-start.4 = (bf16[8,64,2048]{2,1,0:T(8,128)(2,1)S(1)}, bf16[8,64,2048]{2,1,0:T(8,128)(2,1)}, u32[]{:S(2)}) copy-start(bf16[8,64,2048]{2,1,0:T(8,128)(2,1)} %copy-done.3) | copy-start | bytes 6291460
  153.6 2.0 copy-start.7
  153.6 3.9 %copy-start.6 = (bf16[512,768]{1,0:T(8,128)(2,1)}, bf16[512,768]{1,0:T(8,128)(2,1)S(1)}, u32[]{:S(2)}) copy-start(bf16[512,768]{1,0:T(8,128)(2,1)S(1)} %get-tuple-element.31) | copy-start | bytes 2359300
  166.4 1.1 copy-start.8
  172.5 53.7 %all-to-all-start.1 = ((bf16[8,64,2048]{2,1,0:T(8,128)(2,1)}), bf16[8,64,2048]{2,1,0:T(8,128)(2,1)S(1)}, u32[]{:S(2)}, u32[]{:S(2)}) async-start(bf16[8,64,2048]{2,1,0:T(8,128)(2,1)} %bitcast.61), calls=%async_computation.1 | async-start | bytes 4194304 | tf_op jit(solution)/shard_map/all_to_all | solution.py:75
  177.1 4.1 %copy-start.10 = (bf16[1,2048,768]{2,1,0:T(8,128)(2,1)S(1)}, bf16[1,2048,768]{2,1,0:T(8,128)(2,1)}, u32[]{:S(2)}) copy-start(bf16[1,2048,768]{2,1,0:T(8,128)(2,1)} %all-gather.7.cloned.1.call-done) | copy-start | bytes 9437188
  226.2 4.6 %copy-start.9 = (f32[64,6]{0,1:T(8,128)S(1)}, f32[64,6]{0,1:T(8,128)}, u32[]{:S(2)}) copy-start(f32[64,6]{0,1:T(8,128)} %param.11) | copy-start | bytes 4612
  226.2 53.5 %all-to-all-start.3 = ((bf16[8,64,2048]{2,1,0:T(8,128)(2,1)}), bf16[8,64,2048]{2,1,0:T(8,128)(2,1)}, u32[]{:S(2)}, u32[]{:S(2)}) async-start(bf16[8,64,2048]{2,1,0:T(8,128)(2,1)} %bitcast.60), calls=%async_computation.3 | async-start | bytes 4194304 | tf_op jit(solution)/shard_map/all_to_all | solution.py:87
  279.7 7.0 %copy-start.2 = (bf16[384,2048]{1,0:T(8,128)(2,1)S(1)}, bf16[384,2048]{1,0:T(8,128)(2,1)}, u32[]{:S(2)}) copy-start(bf16[384,2048]{1,0:T(8,128)(2,1)} %gather_fusion) | copy-start | bytes 4718596
  344.4 3.2 copy-start.1
Sparse Core Ops, SparseCore 0:
  9.9 46.6 all-gather.10
  58.4 43.9 all-gather.8
  104.3 43.9 all-gather.6
  166.5 170.8 reduce-scatter.1
where the time goes:
time: 355 us; the launch traced here: 354 us
  waiting for transfers between devices  220 us (62%)
  matrix products  38.8 us (11%)
  local copies, waits for them, and re-layouts  37.8 us (11%)
  other arithmetic  24.1 us (7%)
  starting transfers between devices  19.3 us (5%)
  between operations  13.9 us (4%)
    all_to_all x1, waiting for transfers between devices, on_device(): lax.all_to_all(grad_send, 'expert', split_axis=0, concat_axis=0, tiled=True)  46.3 us
    all_to_all x1, waiting for transfers between devices, on_device(): lax.all_to_all(row_send, 'expert', split_axis=0, concat_axis=0, tiled=True)  43.3 us
    all_to_all x1, waiting for transfers between devices, on_device(): lax.all_to_all(expert_out.reshape(experts, capacity, model_width), 'exper...  41.8 us
    all_to_all x1, waiting for transfers between devices, on_device(): lax.all_to_all(d_rows.reshape(experts, capacity, model_width), 'expert',...  38.2 us
    reduce_scatter x1, waiting for transfers between devices, on_device(): lax.psum_scatter(jnp.concatenate([gate_term, up_term, down_term], axis=1)...  29.6 us
    all_gather x1, waiting for transfers between devices, on_device(): lax.all_gather(gate_proj[0], 'dp', axis=0, tiled=True)  19 us
    gather x2, local copies, waits for them, and re-layouts, pick_rows(): chosen = jnp.take(source_rows, position.reshape(-1), axis=0)  10.1 us
    unnamed x27, local copies, waits for them, and re-layouts  9.52 us
  transfers between devices with their start and end apart: 8, of which 6 were waited for; matrix products, arithmetic and copies ran while one was open for 20% of the time, Pallas kernels for 0%

commit v1 on v0

v1 whole, which is shorter than its diff:
```python
import jax
import jax.numpy as jnp
from jax import lax
from jax.sharding import PartitionSpec as P

AXES = ("dp", "expert")
ACROSS = (((1,), (1,)), ((), ()))
OVER_ROWS = (((0,), (0,)), ((), ()))


def routing_slots(expert_ids, experts):
    onehot = (expert_ids[:, :, None] == jnp.arange(experts, dtype=jnp.int32)[None, None, :]).astype(
        jnp.int32
    )
    per_token = jnp.sum(onehot, axis=1)
    earlier = jnp.cumsum(per_token, axis=0) - per_token
    return jnp.sum(onehot * earlier[:, None, :], axis=2)


def forward_rows(rows, gate_proj, up_proj, down_proj):
    gate_pre = jnp.dot(rows, gate_proj, preferred_element_type=jnp.float32)
    up_pre = jnp.dot(rows, up_proj, preferred_element_type=jnp.float32)
    hidden = (jax.nn.silu(gate_pre) * up_pre).astype(jnp.bfloat16)
    expert_out = lax.dot_general(
        hidden, down_proj, ACROSS, preferred_element_type=jnp.float32
    ).astype(jnp.bfloat16)
    return (expert_out, gate_pre, up_pre, hidden)


def backward_rows(grad_rows, gate_pre, up_pre, gate_proj, up_proj, down_proj):
    d_hidden = jnp.dot(grad_rows, down_proj, preferred_element_type=jnp.float32)
    sigmoid_gate = jax.nn.sigmoid(gate_pre)
    silu_gate = gate_pre * sigmoid_gate
    d_gate = (d_hidden * up_pre * sigmoid_gate * (1.0 + gate_pre * (1.0 - sigmoid_gate))).astype(
        jnp.bfloat16
    )
    d_up = (d_hidden * silu_gate).astype(jnp.bfloat16)
    d_rows = lax.dot_general(d_gate, gate_proj, ACROSS, preferred_element_type=jnp.float32)
    d_rows = d_rows + lax.dot_general(d_up, up_proj, ACROSS, preferred_element_type=jnp.float32)
    return (d_rows.astype(jnp.bfloat16), d_gate, d_up)


def pick_rows(source_rows, position, top_count):
    chosen = jnp.take(source_rows, position.reshape(-1), axis=0)
    return chosen.reshape(position.shape[0], top_count, source_rows.shape[1])


def capacity_of(tok_dev, top_count, experts):
    return min(tok_dev, (tok_dev * top_count * 4 + 3 * experts - 1) // (3 * experts))


def slot_plan(tokens, expert_ids, gate_probs, cotangent, gate_proj, up_proj, down_proj):
    experts = lax.axis_size("expert")
    tok_dev, top_count = expert_ids.shape
    model_width = tokens.shape[1]
    capacity = capacity_of(tok_dev, top_count, experts)
    slot_index = routing_slots(expert_ids, experts)
    position = expert_ids * capacity + slot_index
    placing = (
        position[None, :, :] == jnp.arange(experts * capacity, dtype=jnp.int32)[:, None, None]
    ).astype(jnp.float32)
    placer = jnp.sum(placing, axis=2)
    weighted = jnp.sum(placing * gate_probs[None, :, :], axis=2)
    row_send = (
        jnp.dot(placer.astype(jnp.bfloat16), tokens, preferred_element_type=jnp.float32)
        .astype(jnp.bfloat16)
        .reshape(experts, capacity, model_width)
    )
    grad_send = (
        jnp.dot(weighted, cotangent.astype(jnp.float32), precision=lax.Precision.HIGHEST)
        .astype(jnp.bfloat16)
        .reshape(experts, capacity, model_width)
    )
    full_gate, full_up, full_down = (
        lax.all_gather(gate_proj[0], "dp", axis=0, tiled=True),
        lax.all_gather(up_proj[0], "dp", axis=0, tiled=True),
        lax.all_gather(down_proj[0], "dp", axis=0, tiled=True),
    )

    def exchange(rows):
        return lax.all_to_all(
            rows.reshape(experts, capacity, model_width),
            "expert",
            split_axis=0,
            concat_axis=0,
            tiled=True,
        ).reshape(-1, model_width)

    rows_flat = exchange(row_send)
    expert_out, gate_pre, up_pre, hidden = forward_rows(rows_flat, full_gate, full_up, full_down)
    returned = exchange(expert_out)
    grads_flat = exchange(grad_send)
    d_rows, d_gate, d_up = backward_rows(
        grads_flat, gate_pre, up_pre, full_gate, full_up, full_down
    )
    grad_back = exchange(d_rows)
    picked = pick_rows(returned, position, top_count).astype(jnp.float32)
    mixed = jnp.sum(gate_probs[:, :, None] * picked, axis=1).astype(jnp.bfloat16)
    prob_grads = jnp.sum(cotangent.astype(jnp.float32)[:, None, :] * picked, axis=2)
    picked_grads = pick_rows(grad_back, position, top_count).astype(jnp.float32)
    token_grads = jnp.sum(picked_grads, axis=1).astype(jnp.bfloat16)
    hidden_units = hidden.shape[1]
    gate_term = lax.dot_general(rows_flat, d_gate, OVER_ROWS, preferred_element_type=jnp.float32)
    up_term = lax.dot_general(rows_flat, d_up, OVER_ROWS, preferred_element_type=jnp.float32)
    down_term = lax.dot_general(grads_flat, hidden, OVER_ROWS, preferred_element_type=jnp.float32)
    shares = lax.psum_scatter(
        jnp.concatenate([gate_term, up_term, down_term], axis=1),
        "dp",
        scatter_dimension=0,
        tiled=True,
    )
    grad_gate = shares[:, :hidden_units]
    grad_up = shares[:, hidden_units : 2 * hidden_units]
    grad_down = shares[:, 2 * hidden_units :]
    return (mixed, token_grads, prob_grads, grad_gate[None], grad_up[None], grad_down[None])


def flat_index(y, x, z, core):
    return ((y * 2 + x) * 4 + z) * 2 + core


def pairs(target):
    found = []
    for y in range(2):
        for x in range(2):
            for z in range(4):
                for core in range(2):
                    there = target(y, x, z, core)
                    if there is not None:
                        found.append((flat_index(y, x, z, core), flat_index(*there)))
    return found


TO_X = pairs(lambda y, x, z, core: (y, 1 - x, z, core))
TO_Y = pairs(lambda y, x, z, core: (1 - y, x, z, core))
TO_CORE = pairs(lambda y, x, z, core: (y, x, z, 1 - core))


def z_up(first, last):
    return pairs(lambda y, x, z, core: (y, x, z + 1, core) if first <= z <= last else None)


def z_down(first, last):
    return pairs(lambda y, x, z, core: (y, x, z - 1, core) if first <= z <= last else None)


def send(array, where):
    return lax.ppermute(array, AXES, where)


def gather_weight(shard):
    half = shard.shape[0] // 2
    from_x = send(shard, TO_X)
    from_y = send(shard, TO_Y)
    corner_first = send(from_x[:half], TO_Y)
    corner_last = send(from_y[half:], TO_X)
    return jnp.concatenate([shard, from_x, from_y, corner_first, corner_last], axis=0)


def reduce_grad(grad):
    block = grad.shape[0] // 4
    half = block // 2
    narrow = jnp.bfloat16
    first = send(grad[3 * block : 3 * block + half].astype(narrow), TO_Y)
    last = send(grad[3 * block + half :].astype(narrow), TO_X)
    for_x = jnp.concatenate(
        [grad[block : block + half] + first.astype(jnp.float32), grad[block + half : 2 * block]]
    ).astype(narrow)
    for_y = jnp.concatenate(
        [grad[2 * block : 2 * block + half], grad[2 * block + half : 3 * block] + last.astype(jnp.float32)]
    ).astype(narrow)
    from_x = send(for_x, TO_X)
    from_y = send(for_y, TO_Y)
    return grad[:block] + from_x.astype(jnp.float32) + from_y.astype(jnp.float32)


def gather_line(own, z):
    ups, downs = [own], [own]
    for step in range(3):
        ups.append(send(ups[-1], z_up(step, 2)))
        downs.append(send(downs[-1], z_down(1, 3 - step)))
    slots = [own] + [jnp.where(z >= s, ups[s], downs[4 - s]) for s in range(1, 4)]
    own_core = jnp.stack(slots)
    other_core = send(own_core, TO_CORE)
    return jnp.concatenate([own_core, other_core])


def reduce_line(partial):
    rest = send(partial[4:].astype(jnp.bfloat16), TO_CORE)
    mine = partial[:4] + rest.astype(jnp.float32)
    going_up = mine[1].astype(jnp.bfloat16)
    going_down = mine[3].astype(jnp.bfloat16)
    for step in range(3):
        arrived_up = send(going_up, z_up(0, step))
        arrived_down = send(going_down, z_down(3 - step, 3))
        if step < 2:
            going_up = (mine[2 + step] + arrived_up.astype(jnp.float32)).astype(jnp.bfloat16)
            going_down = (mine[2 - step] + arrived_down.astype(jnp.float32)).astype(jnp.bfloat16)
    total = mine[0] + arrived_up.astype(jnp.float32) + arrived_down.astype(jnp.float32)
    return total.astype(jnp.bfloat16)


def relative_columns(rows, dp):
    blocks = rows.reshape(rows.shape[0], 4, -1)
    swapped = jnp.where(dp % 2 == 1, blocks[:, jnp.array([1, 0, 3, 2])], blocks)
    swapped = jnp.where(dp >= 2, swapped[:, jnp.array([2, 3, 0, 1])], swapped)
    return swapped.reshape(rows.shape)


def dense_plan(tokens, expert_ids, gate_probs, cotangent, gate_proj, up_proj, down_proj):
    f32 = jnp.float32
    experts = lax.axis_size("expert")
    tok_dev = tokens.shape[0]
    width = tokens.shape[1]
    dp = lax.axis_index("dp")
    me = lax.axis_index("expert")
    z, core = me // 2, me % 2
    chosen = expert_ids[:, :, None] == jnp.arange(experts, dtype=jnp.int32)[None, None, :]
    prob_of = jnp.sum(jnp.where(chosen, gate_probs[:, :, None], 0.0), axis=1)
    prob_all = lax.all_gather(prob_of, "expert", axis=0)
    prob_mine = jnp.sum(
        jnp.where(jnp.arange(experts)[None, None, :] == me, prob_all, 0.0), axis=2
    )
    slot = jnp.arange(8, dtype=jnp.int32)
    origin = ((z - slot % 4) % 4) * 2 + (core + slot // 4) % 2
    origin_hot = origin[:, None] == slot[None, :]
    prob = jnp.sum(jnp.where(origin_hot[:, :, None], prob_mine[None], 0.0), axis=1).reshape(-1, 1)

    full_gate = gather_weight(gate_proj[0])
    full_up = gather_weight(up_proj[0])
    full_down = gather_weight(down_proj[0])

    rows = gather_line(relative_columns(tokens, dp), z).reshape(-1, width)
    grads = gather_line(relative_columns(cotangent, dp), z).reshape(-1, width)

    gate_pre = jnp.dot(rows, full_gate, preferred_element_type=f32)
    up_pre = jnp.dot(rows, full_up, preferred_element_type=f32)
    sigmoid_gate = jax.nn.sigmoid(gate_pre)
    silu_gate = gate_pre * sigmoid_gate
    hidden = silu_gate * up_pre
    hidden_scaled = (hidden * prob).astype(jnp.bfloat16)
    grad_down = reduce_grad(
        lax.dot_general(grads, hidden_scaled, OVER_ROWS, preferred_element_type=f32)
    )
    mixed = reduce_line(
        lax.dot_general(hidden_scaled, full_down, ACROSS, preferred_element_type=f32).reshape(
            8, tok_dev, width
        )
    )
    raw = jnp.dot(grads, full_down, preferred_element_type=f32)
    prob_dots = jnp.sum(raw * hidden, axis=1).reshape(8, tok_dev)
    d_hidden = raw * prob
    d_gate = (d_hidden * up_pre * sigmoid_gate * (1.0 + gate_pre * (1.0 - sigmoid_gate))).astype(
        jnp.bfloat16
    )
    d_up = (d_hidden * silu_gate).astype(jnp.bfloat16)
    grad_gate = reduce_grad(lax.dot_general(rows, d_gate, OVER_ROWS, preferred_element_type=f32))
    grad_up = reduce_grad(lax.dot_general(rows, d_up, OVER_ROWS, preferred_element_type=f32))
    d_rows = lax.dot_general(d_gate, full_gate, ACROSS, preferred_element_type=f32)
    d_rows = d_rows + lax.dot_general(d_up, full_up, ACROSS, preferred_element_type=f32)
    token_grads = reduce_line(d_rows.reshape(8, tok_dev, width))

    by_origin = jnp.sum(jnp.where(origin_hot[:, :, None], prob_dots[:, None, :], 0.0), axis=0)
    dots_all = lax.all_gather(by_origin, "expert", axis=0)
    dots_here = jnp.sum(
        jnp.where(jnp.arange(experts)[None, :, None] == me, dots_all, 0.0), axis=1
    )
    prob_grads = jnp.sum(jnp.where(chosen, dots_here.T[:, None, :], 0.0), axis=2)
    return (
        relative_columns(mixed, dp),
        relative_columns(token_grads, dp),
        prob_grads,
        grad_gate[None],
        grad_up[None],
        grad_down[None],
    )


def on_device(tokens, expert_ids, *rest):
    tok_dev, top_count = expert_ids.shape
    experts = lax.axis_size("expert")
    square_and_line = lax.axis_size("dp") == 4 and experts == 8
    if square_and_line and capacity_of(tok_dev, top_count, experts) == tok_dev:
        return dense_plan(tokens, expert_ids, *rest)
    return slot_plan(tokens, expert_ids, *rest)


def solution(mesh):
    by_token = P(AXES, None)
    by_expert = P("expert", "dp", None)
    return jax.shard_map(
        on_device,
        mesh=mesh,
        in_specs=(by_token,) * 4 + (by_expert,) * 3,
        out_specs=(by_token,) * 3 + (by_expert,) * 3,
        check_vma=False,
    )
```

time: 355 us -> 301 us (0.85)
  waiting for transfers between devices: 220 us -> 118 us
  starting transfers between devices: 19.3 us -> 77.6 us
  blocking collectives: 0 us -> 43.3 us
  matrix products: 38.8 us -> 17.9 us
  local copies, waits for them, and re-layouts: 37.8 us -> 20.6 us
  between operations: 13.9 us -> 1.89 us
    all_to_all x4 -> x0, waiting for transfers between devices: 169 us -> none  [the longest x1 46.3 us: on_device(): lax.all_to_all(grad_send, 'expert', split_axis=0, concat_axis=0, tiled=True)]
    ppermute x0 -> x52, waiting for transfers between devices: none -> 118 us  [send(): return lax.ppermute(array, AXES, where)]
    ppermute x0 -> x52, starting transfers between devices: none -> 77.6 us  [send(): return lax.ppermute(array, AXES, where)]
    all_gather x0 -> x2, blocking collectives: none -> 43.3 us  [the longest x1 29 us: dense_plan(): dots_all = lax.all_gather(by_origin, 'expert', axis=0)]
    reduce_scatter x1 -> x0, waiting for transfers between devices: 29.6 us -> none  [on_device(): lax.psum_scatter(jnp.concatenate([gate_term, up_term, down_term], axis=1)...]
    dot_general x11 -> x9, matrix products: 38.8 us -> 17.9 us  [the longest x1 3.11 us: dense_plan(): raw = jnp.dot(grads, full_down, preferred_element_type=f32)]
    all_to_all x4 -> x0, starting transfers between devices: 19 us -> none  [the longest x1 6.33 us: on_device(): lax.all_to_all(grad_send, 'expert', split_axis=0, concat_axis=0, tiled=True)]
    all_gather x3 -> x0, waiting for transfers between devices: 19 us -> none  [the longest x1 19 us: on_device(): lax.all_gather(gate_proj[0], 'dp', axis=0, tiled=True)]
  transfers between devices with their start and end apart: 8 -> 52, of which waited for: 6 -> 22; matrix products, arithmetic and copies ran while one was open for 20% -> 9% of each run, Pallas kernels for 0% -> 0%
where the time goes in v1:
time: 301 us; the launch traced here: 300 us
  waiting for transfers between devices  118 us (39%)
  starting transfers between devices  77.6 us (26%)
  blocking collectives  43.3 us (14%)
  other arithmetic  21 us (7%)
  local copies, waits for them, and re-layouts  20.6 us (7%)
  matrix products  17.9 us (6%)
    ppermute x52, waiting for transfers between devices, send(): return lax.ppermute(array, AXES, where)  118 us
    ppermute x52, starting transfers between devices, send(): return lax.ppermute(array, AXES, where)  77.6 us
    all_gather x1, blocking collectives, dense_plan(): dots_all = lax.all_gather(by_origin, 'expert', axis=0)  29 us
    all_gather x1, blocking collectives, dense_plan(): prob_all = lax.all_gather(prob_of, 'expert', axis=0)  14.4 us
    unnamed x54, local copies, waits for them, and re-layouts  8.33 us
  transfers between devices with their start and end apart: 52, of which 22 were waited for; matrix products, arithmetic and copies ran while one was open for 9% of the time, Pallas kernels for 0%

profile of v1, /device:TPU:0, one launch (start us, length us, event | category | flops | bytes accessed | tf_op | source)
XLA Modules:
  0.0 300.0 jit_solution(6222752974074059084)
XLA Ops:
  5.4 5.6 %collective-permute-start = (bf16[64,2048]{1,0:T(8,128)(2,1)}, bf16[64,2048]{1,0:T(8,128)(2,1)}, u32[]{:S(2)}, u32[]{:S(2)}) collective-permute-start(bf16[64,2048]{1,0:T(8,128)(2,1)} %get-tuple-element.15), channel_id=1, source_target_pairs={{0,2},{1,3},{2,4},{3,5},{4,6},{5,7},{8,10},{9,11},{10,12},{11,13},... | collective-permute-start | bytes 786440 | tf_op jit(solution)/shard_map/ppermute | solution.py:148
  12.3 1.6 collective-permute-start.7
  18.3 2.2 gather_fusion.5
  26.6 7.3 %collective-permute-done.27 = bf16[64,2048]{1,0:T(8,128)(2,1)S(1)} collective-permute-done((bf16[64,2048]{1,0:T(8,128)(2,1)S(1)}, bf16[64,2048]{1,0:T(8,128)(2,1)S(1)}, u32[]{:S(2)}, u32[]{:S(2)}) %collective-permute-start.27) | collective-permute-done | bytes 262176 | tf_op jit(solution)/shard_map/ppermute | solution.py:148
  35.2 4.3 %collective-permute-done.2 = bf16[64,2048]{1,0:T(8,128)(2,1)S(1)} collective-permute-done((bf16[64,2048]{1,0:T(8,128)(2,1)}, bf16[64,2048]{1,0:T(8,128)(2,1)S(1)}, u32[]{:S(2)}, u32[]{:S(2)}) %collective-permute-start.2) | collective-permute-done | bytes 262176 | tf_op jit(solution)/shard_map/ppermute | solution.py:148
  40.9 4.6 %collective-permute-start.26 = (bf16[64,2048]{1,0:T(8,128)(2,1)S(1)}, bf16[64,2048]{1,0:T(8,128)(2,1)S(1)}, u32[]{:S(2)}, u32[]{:S(2)}) collective-permute-start(bf16[64,2048]{1,0:T(8,128)(2,1)S(1)} %get-tuple-element.23), channel_id=1, source_target_pairs={{0,2},{1,3},{2,4},{3,5},{4,6},{5,7},{8,10},{9,11},{10,12},{11,13},... | collective-permute-start | bytes 786440 | tf_op jit(solution)/shard_map/ppermute | solution.py:148
  46.1 2.9 collective-permute-done.3
  50.9 6.4 %collective-permute-done.29 = bf16[64,2048]{1,0:T(8,128)(2,1)S(1)} collective-permute-done((bf16[64,2048]{1,0:T(8,128)(2,1)S(1)}, bf16[64,2048]{1,0:T(8,128)(2,1)S(1)}, u32[]{:S(2)}, u32[]{:S(2)}) %collective-permute-start.29) | collective-permute-done | bytes 262176 | tf_op jit(solution)/shard_map/ppermute | solution.py:148
  66.3 1.6 collective-permute-start.9
  67.9 3.0 collective-permute-done.12
  71.5 10.4 %collective-permute-done.15 = bf16[512,768]{1,0:T(8,128)(2,1)S(1)} collective-permute-done((bf16[512,768]{1,0:T(8,128)(2,1)S(1)}, bf16[512,768]{1,0:T(8,128)(2,1)S(1)}, u32[]{:S(2)}, u32[]{:S(2)}) %collective-permute-start.15) | collective-permute-done | bytes 786464 | tf_op jit(solution)/shard_map/ppermute | solution.py:148
  82.5 5.2 %collective-permute-done.16 = bf16[512,768]{1,0:T(8,128)(2,1)S(1)} collective-permute-done((bf16[512,768]{1,0:T(8,128)(2,1)S(1)}, bf16[512,768]{1,0:T(8,128)(2,1)S(1)}, u32[]{:S(2)}, u32[]{:S(2)}) %collective-permute-start.16) | collective-permute-done | bytes 786464 | tf_op jit(solution)/shard_map/ppermute | solution.py:148
  88.4 7.8 %collective-permute-done.9 = bf16[256,768]{1,0:T(8,128)(2,1)S(1)} collective-permute-done((bf16[256,768]{1,0:T(8,128)(2,1)S(1)}, bf16[256,768]{1,0:T(8,128)(2,1)S(1)}, u32[]{:S(2)}, u32[]{:S(2)}) %collective-permute-start.9) | collective-permute-done | bytes 393248 | tf_op jit(solution)/shard_map/ppermute | solution.py:148
  97.4 7.2 %collective-permute-done.13 = bf16[256,768]{1,0:T(8,128)(2,1)S(1)} collective-permute-done((bf16[256,768]{1,0:T(8,128)(2,1)S(1)}, bf16[256,768]{1,0:T(8,128)(2,1)S(1)}, u32[]{:S(2)}, u32[]{:S(2)}) %collective-permute-start.13) | collective-permute-done | bytes 393248 | tf_op jit(solution)/shard_map/ppermute | solution.py:148
  104.7 5.6 %collective-permute-done.17 = bf16[256,768]{1,0:T(8,128)(2,1)S(1)} collective-permute-done((bf16[256,768]{1,0:T(8,128)(2,1)S(1)}, bf16[256,768]{1,0:T(8,128)(2,1)S(1)}, u32[]{:S(2)}, u32[]{:S(2)}) %collective-permute-start.17) | collective-permute-done | bytes 393248 | tf_op jit(solution)/shard_map/ppermute | solution.py:148
  110.5 1.8 fusion.36
  112.4 1.8 fusion.37
  114.4 3.1 %multiply_reduce_fusion = (f32[512]{0:T(512)S(1)}, f32[512,768]{1,0:T(8,128)}) fusion(f32[512,768]{1,0:T(8,128)S(1)} %fusion.37, f32[512,768]{1,0:T(8,128)S(1)} %fusion.36, bf16[512,2048]{1,0:T(8,128)(2,1)S(1)} %bitcast.174, bf16[2048,768]{1,0:T(8,128)(2,1)S(1)} %constant_dynamic-update-slice_fusion.15), kind=kOutput, calls=%fused_computation.22 | convolution fusion | flops 1613364736 | bytes 9963520 | tf_op jit(solution)/shard_map/dot_general | solution.py:250
  117.7 29.0 %all-gather.1 = f32[64,64]{1,0:T(8,128)S(1)} all-gather(f32[8,64]{1,0:T(8,128)S(1)} %select_reduce_fusion), channel_id=3, replica_groups=mesh['dp'=4,'expert'=8] {'expert'}, dimensions={0}, use_global_device_ids=true | all-gather | bytes 18432 | tf_op jit(solution)/shard_map/all_gather | solution.py:264
  147.4 14.4 %all-gather.2 = f32[8,64,8]{1,2,0:T(8,128)S(1)} all-gather(f32[1,64,8]{1,2,0:T(8,128)S(1)} %bitcast.214), channel_id=2, replica_groups=mesh['dp'=4,'expert'=8] {'expert'}, dimensions={0}, use_global_device_ids=true | all-gather | bytes 18432 | tf_op jit(solution)/shard_map/all_gather | solution.py:220
  162.0 3.5 %multiply_convert_fusion.1 = (bf16[512,768]{1,0:T(8,128)(2,1)S(1)}, bf16[512,768]{1,0:T(8,128)(2,1)S(1)}, bf16[512,768]{1,0:T(8,128)(2,1)S(1)}) fusion(f32[512,768]{1,0:T(8,128)} %copy-done.7, f32[512,768]{1,0:T(8,128)} %copy-done.8, f32[512,768]{1,0:T(8,128)} %get-tuple-element.58, f32[512]{0:T(512)S(1)} %mul.50), kind=kLoop, calls=%fused_computation.24 | loop fusion | flops 6684672 | bytes 7079936 | tf_op jit(solution)/shard_map/convert_element_type | solution.py:253
  165.5 1.8 fusion.38
  167.3 2.1 copy-done.1
  170.7 1.8 fusion.39
  172.6 1.8 convolution_add_fusion
  174.5 2.0 copy-done
  176.6 1.9 fusion.33
  178.6 1.9 fusion.34
  180.5 1.9 fusion.35
  185.2 1.6 collective-permute-start.44
  186.9 8.1 %collective-permute-done.40 = bf16[256,768]{1,0:T(8,128)(2,1)S(1)} collective-permute-done((bf16[256,768]{1,0:T(8,128)(2,1)S(1)}, bf16[256,768]{1,0:T(8,128)(2,1)S(1)}, u32[]{:S(2)}, u32[]{:S(2)}) %collective-permute-start.40) | collective-permute-done | bytes 393248 | tf_op jit(solution)/shard_map/ppermute | solution.py:148
  197.6 5.9 %collective-permute-done.44 = bf16[256,768]{1,0:T(8,128)(2,1)S(1)} collective-permute-done((bf16[256,768]{1,0:T(8,128)(2,1)S(1)}, bf16[256,768]{1,0:T(8,128)(2,1)S(1)}, u32[]{:S(2)}, u32[]{:S(2)}) %collective-permute-start.44) | collective-permute-done | bytes 393248 | tf_op jit(solution)/shard_map/ppermute | solution.py:148
  205.8 6.2 %collective-permute-done.48 = bf16[256,768]{1,0:T(8,128)(2,1)S(1)} collective-permute-done((bf16[256,768]{1,0:T(8,128)(2,1)S(1)}, bf16[256,768]{1,0:T(8,128)(2,1)S(1)}, u32[]{:S(2)}, u32[]{:S(2)}) %collective-permute-start.48) | collective-permute-done | bytes 393248 | tf_op jit(solution)/shard_map/ppermute | solution.py:148
  214.3 1.5 collective-permute-start.45
  216.1 1.6 collective-permute-start.51
  218.1 10.6 %collective-permute-done.43 = bf16[512,768]{1,0:T(8,128)(2,1)S(1)} collective-permute-done((bf16[512,768]{1,0:T(8,128)(2,1)S(1)}, bf16[512,768]{1,0:T(8,128)(2,1)S(1)}, u32[]{:S(2)}, u32[]{:S(2)}) %collective-permute-start.43) | collective-permute-done | bytes 786464 | tf_op jit(solution)/shard_map/ppermute | solution.py:148
  230.3 2.1 collective-permute-done.41
  232.4 3.6 %collective-permute-start.20 = (bf16[64,2048]{1,0:T(8,128)(2,1)S(1)}, bf16[64,2048]{1,0:T(8,128)(2,1)S(1)}, u32[]{:S(2)}, u32[]{:S(2)}) collective-permute-start(bf16[64,2048]{1,0:T(8,128)(2,1)S(1)} %get-tuple-element.55), channel_id=1, source_target_pairs={{0,2},{1,3},{8,10},{9,11},{16,18},{17,19},{24,26},{25,27}} | collective-permute-start | bytes 786440 | tf_op jit(solution)/shard_map/ppermute | solution.py:148
  237.3 8.3 %collective-permute-done.47 = bf16[512,768]{1,0:T(8,128)(2,1)S(1)} collective-permute-done((bf16[512,768]{1,0:T(8,128)(2,1)S(1)}, bf16[512,768]{1,0:T(8,128)(2,1)S(1)}, u32[]{:S(2)}, u32[]{:S(2)}) %collective-permute-start.47) | collective-permute-done | bytes 786464 | tf_op jit(solution)/shard_map/ppermute | solution.py:148
  246.3 3.0 collective-permute-done.45
  249.2 3.6 %collective-permute-start.34 = (bf16[64,2048]{1,0:T(8,128)(2,1)S(1)}, bf16[64,2048]{1,0:T(8,128)(2,1)S(1)}, u32[]{:S(2)}, u32[]{:S(2)}) collective-permute-start(bf16[64,2048]{1,0:T(8,128)(2,1)S(1)} %get-tuple-element.49), channel_id=1, source_target_pairs={{0,2},{1,3},{8,10},{9,11},{16,18},{17,19},{24,26},{25,27}} | collective-permute-start | bytes 786440 | tf_op jit(solution)/shard_map/ppermute | solution.py:148
  254.2 7.6 %collective-permute-done.51 = bf16[512,768]{1,0:T(8,128)(2,1)S(1)} collective-permute-done((bf16[512,768]{1,0:T(8,128)(2,1)S(1)}, bf16[512,768]{1,0:T(8,128)(2,1)S(1)}, u32[]{:S(2)}, u32[]{:S(2)}) %collective-permute-start.51) | collective-permute-done | bytes 786464 | tf_op jit(solution)/shard_map/ppermute | solution.py:148
  265.5 3.6 %collective-permute-start.21 = (bf16[64,2048]{1,0:T(8,128)(2,1)S(1)}, bf16[64,2048]{1,0:T(8,128)(2,1)S(1)}, u32[]{:S(2)}, u32[]{:S(2)}) collective-permute-start(bf16[64,2048]{1,0:T(8,128)(2,1)S(1)} %get-tuple-element.53), channel_id=1, source_target_pairs={{0,2},{1,3},{2,4},{3,5},{8,10},{9,11},{10,12},{11,13},{16,18},{17,... | collective-permute-start | bytes 786440 | tf_op jit(solution)/shard_map/ppermute | solution.py:148
  269.9 2.5 collective-permute-start.35
  273.1 2.2 collective-permute-done.21
  276.8 5.5 %collective-permute-start.22 = (bf16[64,2048]{1,0:T(8,128)(2,1)S(1)}, bf16[64,2048]{1,0:T(8,128)(2,1)S(1)}, u32[]{:S(2)}, u32[]{:S(2)}) collective-permute-start(bf16[64,2048]{1,0:T(8,128)(2,1)S(1)} %get-tuple-element.51), channel_id=1, source_target_pairs={{0,2},{1,3},{2,4},{3,5},{4,6},{5,7},{8,10},{9,11},{10,12},{11,13},... | collective-permute-start | bytes 786440 | tf_op jit(solution)/shard_map/ppermute | solution.py:148
  284.5 8.2 %collective-permute-start.36 = (bf16[64,2048]{1,0:T(8,128)(2,1)}, bf16[64,2048]{1,0:T(8,128)(2,1)}, u32[]{:S(2)}, u32[]{:S(2)}) collective-permute-start(bf16[64,2048]{1,0:T(8,128)(2,1)} %get-tuple-element.45), channel_id=1, source_target_pairs={{0,2},{1,3},{2,4},{3,5},{4,6},{5,7},{8,10},{9,11},{10,12},{11,13},... | collective-permute-start | bytes 786440 | tf_op jit(solution)/shard_map/ppermute | solution.py:148
  294.6 1.6 collective-permute-done.36
  (211 shorter events, 66.3 us)
Async XLA Ops:
  5.4 35.5 %collective-permute-start = (bf16[64,2048]{1,0:T(8,128)(2,1)}, bf16[64,2048]{1,0:T(8,128)(2,1)}, u32[]{:S(2)}, u32[]{:S(2)}) collective-permute-start(bf16[64,2048]{1,0:T(8,128)(2,1)} %get-tuple-element.15), channel_id=1, source_target_pairs={{0,2},{1,3},{2,4},{3,5},{4,6},{5,7},{8,10},{9,11},{10,12},{11,13},... | collective-permute-start | bytes 786440 | tf_op jit(solution)/shard_map/ppermute | solution.py:148
  11.0 14.1 %collective-permute-start.1 = (bf16[64,2048]{1,0:T(8,128)(2,1)}, bf16[64,2048]{1,0:T(8,128)(2,1)}, u32[]{:S(2)}, u32[]{:S(2)}) collective-permute-start(bf16[64,2048]{1,0:T(8,128)(2,1)} %get-tuple-element.15), channel_id=1, source_target_pairs={{2,0},{3,1},{4,2},{5,3},{6,4},{7,5},{10,8},{11,9},{12,10},{13,11},... | collective-permute-start | bytes 786440 | tf_op jit(solution)/shard_map/ppermute | solution.py:148
  12.3 50.9 %collective-permute-start.7 = (bf16[512,768]{1,0:T(8,128)(2,1)}, bf16[512,768]{1,0:T(8,128)(2,1)S(1)}, u32[]{:S(2)}, u32[]{:S(2)}) collective-permute-start(bf16[512,768]{1,0:T(8,128)(2,1)} %bitcast.207), channel_id=1, source_target_pairs={{0,8},{1,9},{2,10},{3,11},{4,12},{5,13},{6,14},{7,15},{8,0},{9,1},... | collective-permute-start | bytes 2359304 | tf_op jit(solution)/shard_map/ppermute | solution.py:148
  13.8 50.1 %collective-permute-start.8 = (bf16[512,768]{1,0:T(8,128)(2,1)}, bf16[512,768]{1,0:T(8,128)(2,1)}, u32[]{:S(2)}, u32[]{:S(2)}) collective-permute-start(bf16[512,768]{1,0:T(8,128)(2,1)} %bitcast.208), channel_id=1, source_target_pairs={{0,16},{1,17},{2,18},{3,19},{4,20},{5,21},{6,22},{7,23},{8,24},{9,... | collective-permute-start | bytes 2359304 | tf_op jit(solution)/shard_map/ppermute | solution.py:148
  22.4 11.5 %collective-permute-start.27 = (bf16[64,2048]{1,0:T(8,128)(2,1)S(1)}, bf16[64,2048]{1,0:T(8,128)(2,1)S(1)}, u32[]{:S(2)}, u32[]{:S(2)}) collective-permute-start(bf16[64,2048]{1,0:T(8,128)(2,1)S(1)} %get-tuple-element.23), channel_id=1, source_target_pairs={{2,0},{3,1},{4,2},{5,3},{6,4},{7,5},{10,8},{11,9},{12,10},{13,11},... | collective-permute-start | bytes 786440 | tf_op jit(solution)/shard_map/ppermute | solution.py:148
  25.1 14.4 %collective-permute-start.2 = (bf16[64,2048]{1,0:T(8,128)(2,1)}, bf16[64,2048]{1,0:T(8,128)(2,1)S(1)}, u32[]{:S(2)}, u32[]{:S(2)}) collective-permute-start(bf16[64,2048]{1,0:T(8,128)(2,1)} %collective-permute-done.1), channel_id=1, source_target_pairs={{2,0},{3,1},{4,2},{5,3},{10,8},{11,9},{12,10},{13,11},{18,16},{19,... | collective-permute-start | bytes 786440 | tf_op jit(solution)/shard_map/ppermute | solution.py:148
  33.9 11.6 %collective-permute-start.28 = (bf16[64,2048]{1,0:T(8,128)(2,1)S(1)}, bf16[64,2048]{1,0:T(8,128)(2,1)S(1)}, u32[]{:S(2)}, u32[]{:S(2)}) collective-permute-start(bf16[64,2048]{1,0:T(8,128)(2,1)S(1)} %collective-permute-done.27), channel_id=1, source_target_pairs={{2,0},{3,1},{4,2},{5,3},{10,8},{11,9},{12,10},{13,11},{18,16},{19,... | collective-permute-start | bytes 786440 | tf_op jit(solution)/shard_map/ppermute | solution.py:148
  39.5 9.4 %collective-permute-start.3 = (bf16[64,2048]{1,0:T(8,128)(2,1)S(1)}, bf16[64,2048]{1,0:T(8,128)(2,1)S(1)}, u32[]{:S(2)}, u32[]{:S(2)}) collective-permute-start(bf16[64,2048]{1,0:T(8,128)(2,1)S(1)} %collective-permute-done.2), channel_id=1, source_target_pairs={{2,0},{3,1},{10,8},{11,9},{18,16},{19,17},{26,24},{27,25}} | collective-permute-start | bytes 786440 | tf_op jit(solution)/shard_map/ppermute | solution.py:148
  40.9 9.4 %collective-permute-start.26 = (bf16[64,2048]{1,0:T(8,128)(2,1)S(1)}, bf16[64,2048]{1,0:T(8,128)(2,1)S(1)}, u32[]{:S(2)}, u32[]{:S(2)}) collective-permute-start(bf16[64,2048]{1,0:T(8,128)(2,1)S(1)} %get-tuple-element.23), channel_id=1, source_target_pairs={{0,2},{1,3},{2,4},{3,5},{4,6},{5,7},{8,10},{9,11},{10,12},{11,13},... | collective-permute-start | bytes 786440 | tf_op jit(solution)/shard_map/ppermute | solution.py:148
  45.5 20.8 %collective-permute-start.11 = (bf16[512,768]{1,0:T(8,128)(2,1)S(1)}, bf16[512,768]{1,0:T(8,128)(2,1)S(1)}, u32[]{:S(2)}, u32[]{:S(2)}) collective-permute-start(bf16[512,768]{1,0:T(8,128)(2,1)S(1)} %bitcast.209), channel_id=1, source_target_pairs={{0,8},{1,9},{2,10},{3,11},{4,12},{5,13},{6,14},{7,15},{8,0},{9,1},... | collective-permute-start | bytes 2359304 | tf_op jit(solution)/shard_map/ppermute | solution.py:148
  49.0 8.4 %collective-permute-start.29 = (bf16[64,2048]{1,0:T(8,128)(2,1)S(1)}, bf16[64,2048]{1,0:T(8,128)(2,1)S(1)}, u32[]{:S(2)}, u32[]{:S(2)}) collective-permute-start(bf16[64,2048]{1,0:T(8,128)(2,1)S(1)} %collective-permute-done.28), channel_id=1, source_target_pairs={{2,0},{3,1},{10,8},{11,9},{18,16},{19,17},{26,24},{27,25}} | collective-permute-start | bytes 786440 | tf_op jit(solution)/shard_map/ppermute | solution.py:148
  50.4 20.5 %collective-permute-start.12 = (bf16[512,768]{1,0:T(8,128)(2,1)S(1)}, bf16[512,768]{1,0:T(8,128)(2,1)S(1)}, u32[]{:S(2)}, u32[]{:S(2)}) collective-permute-start(bf16[512,768]{1,0:T(8,128)(2,1)S(1)} %bitcast.210), channel_id=1, source_target_pairs={{0,16},{1,17},{2,18},{3,19},{4,20},{5,21},{6,22},{7,23},{8,24},{9,... | collective-permute-start | bytes 2359304 | tf_op jit(solution)/shard_map/ppermute | solution.py:148
  61.4 20.5 %collective-permute-start.15 = (bf16[512,768]{1,0:T(8,128)(2,1)S(1)}, bf16[512,768]{1,0:T(8,128)(2,1)S(1)}, u32[]{:S(2)}, u32[]{:S(2)}) collective-permute-start(bf16[512,768]{1,0:T(8,128)(2,1)S(1)} %bitcast.211), channel_id=1, source_target_pairs={{0,8},{1,9},{2,10},{3,11},{4,12},{5,13},{6,14},{7,15},{8,0},{9,1},... | collective-permute-start | bytes 2359304 | tf_op jit(solution)/shard_map/ppermute | solution.py:148
  63.2 24.6 %collective-permute-start.16 = (bf16[512,768]{1,0:T(8,128)(2,1)S(1)}, bf16[512,768]{1,0:T(8,128)(2,1)S(1)}, u32[]{:S(2)}, u32[]{:S(2)}) collective-permute-start(bf16[512,768]{1,0:T(8,128)(2,1)S(1)} %bitcast.212), channel_id=1, source_target_pairs={{0,16},{1,17},{2,18},{3,19},{4,20},{5,21},{6,22},{7,23},{8,24},{9,... | collective-permute-start | bytes 2359304 | tf_op jit(solution)/shard_map/ppermute | solution.py:148
  63.9 46.5 %collective-permute-start.6 = (bf16[4,64,2048]{2,1,0:T(8,128)(2,1)S(1)}, bf16[4,64,2048]{2,1,0:T(8,128)(2,1)S(1)}, u32[]{:S(2)}, u32[]{:S(2)}) collective-permute-start(bf16[4,64,2048]{2,1,0:T(8,128)(2,1)S(1)} %pad_maximum_fusion), channel_id=1, source_target_pairs={{0,1},{1,0},{2,3},{3,2},{4,5},{5,4},{6,7},{7,6},{8,9},{9,8},{10,11... | collective-permute-start | bytes 3145736 | tf_op jit(solution)/shard_map/ppermute | solution.py:148
  66.3 29.9 %collective-permute-start.9 = (bf16[256,768]{1,0:T(8,128)(2,1)S(1)}, bf16[256,768]{1,0:T(8,128)(2,1)S(1)}, u32[]{:S(2)}, u32[]{:S(2)}) collective-permute-start(bf16[256,768]{1,0:T(8,128)(2,1)S(1)} %slice.202), channel_id=1, source_target_pairs={{0,16},{1,17},{2,18},{3,19},{4,20},{5,21},{6,22},{7,23},{8,24},{9,... | collective-permute-start | bytes 1179656 | tf_op jit(solution)/shard_map/ppermute | solution.py:148
  70.9 25.8 %collective-permute-start.10 = (bf16[256,768]{1,0:T(8,128)(2,1)S(1)}, bf16[256,768]{1,0:T(8,128)(2,1)S(1)}, u32[]{:S(2)}, u32[]{:S(2)}) collective-permute-start(bf16[256,768]{1,0:T(8,128)(2,1)S(1)} %slice.203), channel_id=1, source_target_pairs={{0,8},{1,9},{2,10},{3,11},{4,12},{5,13},{6,14},{7,15},{8,0},{9,1},... | collective-permute-start | bytes 1179656 | tf_op jit(solution)/shard_map/ppermute | solution.py:148
  81.9 22.7 %collective-permute-start.13 = (bf16[256,768]{1,0:T(8,128)(2,1)S(1)}, bf16[256,768]{1,0:T(8,128)(2,1)S(1)}, u32[]{:S(2)}, u32[]{:S(2)}) collective-permute-start(bf16[256,768]{1,0:T(8,128)(2,1)S(1)} %slice.204), channel_id=1, source_target_pairs={{0,16},{1,17},{2,18},{3,19},{4,20},{5,21},{6,22},{7,23},{8,24},{9,... | collective-permute-start | bytes 1179656 | tf_op jit(solution)/shard_map/ppermute | solution.py:148
  87.8 16.9 %collective-permute-start.14 = (bf16[256,768]{1,0:T(8,128)(2,1)S(1)}, bf16[256,768]{1,0:T(8,128)(2,1)S(1)}, u32[]{:S(2)}, u32[]{:S(2)}) collective-permute-start(bf16[256,768]{1,0:T(8,128)(2,1)S(1)} %slice.205), channel_id=1, source_target_pairs={{0,8},{1,9},{2,10},{3,11},{4,12},{5,13},{6,14},{7,15},{8,0},{9,1},... | collective-permute-start | bytes 1179656 | tf_op jit(solution)/shard_map/ppermute | solution.py:148
  96.2 14.1 %collective-permute-start.17 = (bf16[256,768]{1,0:T(8,128)(2,1)S(1)}, bf16[256,768]{1,0:T(8,128)(2,1)S(1)}, u32[]{:S(2)}, u32[]{:S(2)}) collective-permute-start(bf16[256,768]{1,0:T(8,128)(2,1)S(1)} %slice.206), channel_id=1, source_target_pairs={{0,16},{1,17},{2,18},{3,19},{4,20},{5,21},{6,22},{7,23},{8,24},{9,... | collective-permute-start | bytes 1179656 | tf_op jit(solution)/shard_map/ppermute | solution.py:148
  96.7 13.6 %collective-permute-start.18 = (bf16[256,768]{1,0:T(8,128)(2,1)S(1)}, bf16[256,768]{1,0:T(8,128)(2,1)S(1)}, u32[]{:S(2)}, u32[]{:S(2)}) collective-permute-start(bf16[256,768]{1,0:T(8,128)(2,1)S(1)} %slice.207), channel_id=1, source_target_pairs={{0,8},{1,9},{2,10},{3,11},{4,12},{5,13},{6,14},{7,15},{8,0},{9,1},... | collective-permute-start | bytes 1179656 | tf_op jit(solution)/shard_map/ppermute | solution.py:148
  104.6 9.6 %collective-permute-start.32 = (bf16[4,64,2048]{2,1,0:T(8,128)(2,1)S(1)}, bf16[4,64,2048]{2,1,0:T(8,128)(2,1)S(1)}, u32[]{:S(2)}, u32[]{:S(2)}) collective-permute-start(bf16[4,64,2048]{2,1,0:T(8,128)(2,1)S(1)} %pad_maximum_fusion.1), channel_id=1, source_target_pairs={{0,1},{1,0},{2,3},{3,2},{4,5},{5,4},{6,7},{7,6},{8,9},{9,8},{10,11... | collective-permute-start | bytes 3145736 | tf_op jit(solution)/shard_map/ppermute | solution.py:148
  182.4 31.9 %collective-permute-start.19 = (bf16[4,64,2048]{2,1,0:T(8,128)(2,1)S(1)}, bf16[4,64,2048]{2,1,0:T(8,128)(2,1)S(1)}, u32[]{:S(2)}, u32[]{:S(2)}) collective-permute-start(bf16[4,64,2048]{2,1,0:T(8,128)(2,1)S(1)} %bitcast.201), channel_id=1, source_target_pairs={{0,1},{1,0},{2,3},{3,2},{4,5},{5,4},{6,7},{7,6},{8,9},{9,8},{10,11... | collective-permute-start | bytes 3145736 | tf_op jit(solution)/shard_map/ppermute | solution.py:148
  182.7 33.4 %collective-permute-start.33 = (bf16[4,64,2048]{2,1,0:T(8,128)(2,1)S(1)}, bf16[4,64,2048]{2,1,0:T(8,128)(2,1)S(1)}, u32[]{:S(2)}, u32[]{:S(2)}) collective-permute-start(bf16[4,64,2048]{2,1,0:T(8,128)(2,1)S(1)} %bitcast.200), channel_id=1, source_target_pairs={{0,1},{1,0},{2,3},{3,2},{4,5},{5,4},{6,7},{7,6},{8,9},{9,8},{10,11... | collective-permute-start | bytes 3145736 | tf_op jit(solution)/shard_map/ppermute | solution.py:148
  183.0 12.0 %collective-permute-start.40 = (bf16[256,768]{1,0:T(8,128)(2,1)S(1)}, bf16[256,768]{1,0:T(8,128)(2,1)S(1)}, u32[]{:S(2)}, u32[]{:S(2)}) collective-permute-start(bf16[256,768]{1,0:T(8,128)(2,1)S(1)} %get-tuple-element.41), channel_id=1, source_target_pairs={{0,16},{1,17},{2,18},{3,19},{4,20},{5,21},{6,22},{7,23},{8,24},{9,... | collective-permute-start | bytes 1179656 | tf_op jit(solution)/shard_map/ppermute | solution.py:148
  183.6 12.9 %collective-permute-start.42 = (bf16[256,768]{1,0:T(8,128)(2,1)S(1)}, bf16[256,768]{1,0:T(8,128)(2,1)S(1)}, u32[]{:S(2)}, u32[]{:S(2)}) collective-permute-start(bf16[256,768]{1,0:T(8,128)(2,1)S(1)} %get-tuple-element.42), channel_id=1, source_target_pairs={{0,8},{1,9},{2,10},{3,11},{4,12},{5,13},{6,14},{7,15},{8,0},{9,1},... | collective-permute-start | bytes 1179656 | tf_op jit(solution)/shard_map/ppermute | solution.py:148
  185.2 18.3 %collective-permute-start.44 = (bf16[256,768]{1,0:T(8,128)(2,1)S(1)}, bf16[256,768]{1,0:T(8,128)(2,1)S(1)}, u32[]{:S(2)}, u32[]{:S(2)}) collective-permute-start(bf16[256,768]{1,0:T(8,128)(2,1)S(1)} %get-tuple-element.37), channel_id=1, source_target_pairs={{0,16},{1,17},{2,18},{3,19},{4,20},{5,21},{6,22},{7,23},{8,24},{9,... | collective-permute-start | bytes 1179656 | tf_op jit(solution)/shard_map/ppermute | solution.py:148
  195.1 9.9 %collective-permute-start.46 = (bf16[256,768]{1,0:T(8,128)(2,1)S(1)}, bf16[256,768]{1,0:T(8,128)(2,1)S(1)}, u32[]{:S(2)}, u32[]{:S(2)}) collective-permute-start(bf16[256,768]{1,0:T(8,128)(2,1)S(1)} %get-tuple-element.38), channel_id=1, source_target_pairs={{0,8},{1,9},{2,10},{3,11},{4,12},{5,13},{6,14},{7,15},{8,0},{9,1},... | collective-permute-start | bytes 1179656 | tf_op jit(solution)/shard_map/ppermute | solution.py:148
  196.5 15.4 %collective-permute-start.48 = (bf16[256,768]{1,0:T(8,128)(2,1)S(1)}, bf16[256,768]{1,0:T(8,128)(2,1)S(1)}, u32[]{:S(2)}, u32[]{:S(2)}) collective-permute-start(bf16[256,768]{1,0:T(8,128)(2,1)S(1)} %get-tuple-element.33), channel_id=1, source_target_pairs={{0,16},{1,17},{2,18},{3,19},{4,20},{5,21},{6,22},{7,23},{8,24},{9,... | collective-permute-start | bytes 1179656 | tf_op jit(solution)/shard_map/ppermute | solution.py:148
  203.5 9.9 %collective-permute-start.50 = (bf16[256,768]{1,0:T(8,128)(2,1)S(1)}, bf16[256,768]{1,0:T(8,128)(2,1)S(1)}, u32[]{:S(2)}, u32[]{:S(2)}) collective-permute-start(bf16[256,768]{1,0:T(8,128)(2,1)S(1)} %get-tuple-element.34), channel_id=1, source_target_pairs={{0,8},{1,9},{2,10},{3,11},{4,12},{5,13},{6,14},{7,15},{8,0},{9,1},... | collective-permute-start | bytes 1179656 | tf_op jit(solution)/shard_map/ppermute | solution.py:148
  205.0 23.8 %collective-permute-start.43 = (bf16[512,768]{1,0:T(8,128)(2,1)S(1)}, bf16[512,768]{1,0:T(8,128)(2,1)S(1)}, u32[]{:S(2)}, u32[]{:S(2)}) collective-permute-start(bf16[512,768]{1,0:T(8,128)(2,1)S(1)} %pad_maximum_fusion.3), channel_id=1, source_target_pairs={{0,16},{1,17},{2,18},{3,19},{4,20},{5,21},{6,22},{7,23},{8,24},{9,... | collective-permute-start | bytes 2359304 | tf_op jit(solution)/shard_map/ppermute | solution.py:148
  211.9 20.5 %collective-permute-start.41 = (bf16[512,768]{1,0:T(8,128)(2,1)S(1)}, bf16[512,768]{1,0:T(8,128)(2,1)S(1)}, u32[]{:S(2)}, u32[]{:S(2)}) collective-permute-start(bf16[512,768]{1,0:T(8,128)(2,1)S(1)} %pad_maximum_fusion.2), channel_id=1, source_target_pairs={{0,8},{1,9},{2,10},{3,11},{4,12},{5,13},{6,14},{7,15},{8,0},{9,1},... | collective-permute-start | bytes 2359304 | tf_op jit(solution)/shard_map/ppermute | solution.py:148
  213.4 32.2 %collective-permute-start.47 = (bf16[512,768]{1,0:T(8,128)(2,1)S(1)}, bf16[512,768]{1,0:T(8,128)(2,1)S(1)}, u32[]{:S(2)}, u32[]{:S(2)}) collective-permute-start(bf16[512,768]{1,0:T(8,128)(2,1)S(1)} %pad_maximum_fusion.5), channel_id=1, source_target_pairs={{0,16},{1,17},{2,18},{3,19},{4,20},{5,21},{6,22},{7,23},{8,24},{9,... | collective-permute-start | bytes 2359304 | tf_op jit(solution)/shard_map/ppermute | solution.py:148
  214.3 35.0 %collective-permute-start.45 = (bf16[512,768]{1,0:T(8,128)(2,1)S(1)}, bf16[512,768]{1,0:T(8,128)(2,1)S(1)}, u32[]{:S(2)}, u32[]{:S(2)}) collective-permute-start(bf16[512,768]{1,0:T(8,128)(2,1)S(1)} %pad_maximum_fusion.4), channel_id=1, source_target_pairs={{0,8},{1,9},{2,10},{3,11},{4,12},{5,13},{6,14},{7,15},{8,0},{9,1},... | collective-permute-start | bytes 2359304 | tf_op jit(solution)/shard_map/ppermute | solution.py:148
  216.1 45.7 %collective-permute-start.51 = (bf16[512,768]{1,0:T(8,128)(2,1)S(1)}, bf16[512,768]{1,0:T(8,128)(2,1)S(1)}, u32[]{:S(2)}, u32[]{:S(2)}) collective-permute-start(bf16[512,768]{1,0:T(8,128)(2,1)S(1)} %pad_maximum_fusion.7), channel_id=1, source_target_pairs={{0,16},{1,17},{2,18},{3,19},{4,20},{5,21},{6,22},{7,23},{8,24},{9,... | collective-permute-start | bytes 2359304 | tf_op jit(solution)/shard_map/ppermute | solution.py:148
  228.8 35.2 %collective-permute-start.49 = (bf16[512,768]{1,0:T(8,128)(2,1)S(1)}, bf16[512,768]{1,0:T(8,128)(2,1)S(1)}, u32[]{:S(2)}, u32[]{:S(2)}) collective-permute-start(bf16[512,768]{1,0:T(8,128)(2,1)S(1)} %pad_maximum_fusion.6), channel_id=1, source_target_pairs={{0,8},{1,9},{2,10},{3,11},{4,12},{5,13},{6,14},{7,15},{8,0},{9,1},... | collective-permute-start | bytes 2359304 | tf_op jit(solution)/shard_map/ppermute | solution.py:148
  232.4 32.9 %collective-permute-start.20 = (bf16[64,2048]{1,0:T(8,128)(2,1)S(1)}, bf16[64,2048]{1,0:T(8,128)(2,1)S(1)}, u32[]{:S(2)}, u32[]{:S(2)}) collective-permute-start(bf16[64,2048]{1,0:T(8,128)(2,1)S(1)} %get-tuple-element.55), channel_id=1, source_target_pairs={{0,2},{1,3},{8,10},{9,11},{16,18},{17,19},{24,26},{25,27}} | collective-permute-start | bytes 786440 | tf_op jit(solution)/shard_map/ppermute | solution.py:148
  245.6 19.7 %collective-permute-start.23 = (bf16[64,2048]{1,0:T(8,128)(2,1)S(1)}, bf16[64,2048]{1,0:T(8,128)(2,1)S(1)}, u32[]{:S(2)}, u32[]{:S(2)}) collective-permute-start(bf16[64,2048]{1,0:T(8,128)(2,1)S(1)} %get-tuple-element.56), channel_id=1, source_target_pairs={{6,4},{7,5},{14,12},{15,13},{22,20},{23,21},{30,28},{31,29}} | collective-permute-start | bytes 786440 | tf_op jit(solution)/shard_map/ppermute | solution.py:148
  249.2 20.5 %collective-permute-start.34 = (bf16[64,2048]{1,0:T(8,128)(2,1)S(1)}, bf16[64,2048]{1,0:T(8,128)(2,1)S(1)}, u32[]{:S(2)}, u32[]{:S(2)}) collective-permute-start(bf16[64,2048]{1,0:T(8,128)(2,1)S(1)} %get-tuple-element.49), channel_id=1, source_target_pairs={{0,2},{1,3},{8,10},{9,11},{16,18},{17,19},{24,26},{25,27}} | collective-permute-start | bytes 786440 | tf_op jit(solution)/shard_map/ppermute | solution.py:148
  261.8 7.9 %collective-permute-start.37 = (bf16[64,2048]{1,0:T(8,128)(2,1)S(1)}, bf16[64,2048]{1,0:T(8,128)(2,1)S(1)}, u32[]{:S(2)}, u32[]{:S(2)}) collective-permute-start(bf16[64,2048]{1,0:T(8,128)(2,1)S(1)} %get-tuple-element.50), channel_id=1, source_target_pairs={{6,4},{7,5},{14,12},{15,13},{22,20},{23,21},{30,28},{31,29}} | collective-permute-start | bytes 786440 | tf_op jit(solution)/shard_map/ppermute | solution.py:148
  265.5 9.9 %collective-permute-start.21 = (bf16[64,2048]{1,0:T(8,128)(2,1)S(1)}, bf16[64,2048]{1,0:T(8,128)(2,1)S(1)}, u32[]{:S(2)}, u32[]{:S(2)}) collective-permute-start(bf16[64,2048]{1,0:T(8,128)(2,1)S(1)} %get-tuple-element.53), channel_id=1, source_target_pairs={{0,2},{1,3},{2,4},{3,5},{8,10},{9,11},{10,12},{11,13},{16,18},{17,... | collective-permute-start | bytes 786440 | tf_op jit(solution)/shard_map/ppermute | solution.py:148
  269.1 6.3 %collective-permute-start.24 = (bf16[64,2048]{1,0:T(8,128)(2,1)S(1)}, bf16[64,2048]{1,0:T(8,128)(2,1)S(1)}, u32[]{:S(2)}, u32[]{:S(2)}) collective-permute-start(bf16[64,2048]{1,0:T(8,128)(2,1)S(1)} %get-tuple-element.54), channel_id=1, source_target_pairs={{4,2},{5,3},{6,4},{7,5},{12,10},{13,11},{14,12},{15,13},{20,18},{2... | collective-permute-start | bytes 786440 | tf_op jit(solution)/shard_map/ppermute | solution.py:148
  269.9 12.4 %collective-permute-start.35 = (bf16[64,2048]{1,0:T(8,128)(2,1)S(1)}, bf16[64,2048]{1,0:T(8,128)(2,1)S(1)}, u32[]{:S(2)}, u32[]{:S(2)}) collective-permute-start(bf16[64,2048]{1,0:T(8,128)(2,1)S(1)} %get-tuple-element.47), channel_id=1, source_target_pairs={{0,2},{1,3},{2,4},{3,5},{8,10},{9,11},{10,12},{11,13},{16,18},{17,... | collective-permute-start | bytes 786440 | tf_op jit(solution)/shard_map/ppermute | solution.py:148
  272.4 9.8 %collective-permute-start.38 = (bf16[64,2048]{1,0:T(8,128)(2,1)S(1)}, bf16[64,2048]{1,0:T(8,128)(2,1)S(1)}, u32[]{:S(2)}, u32[]{:S(2)}) collective-permute-start(bf16[64,2048]{1,0:T(8,128)(2,1)S(1)} %get-tuple-element.48), channel_id=1, source_target_pairs={{4,2},{5,3},{6,4},{7,5},{12,10},{13,11},{14,12},{15,13},{20,18},{2... | collective-permute-start | bytes 786440 | tf_op jit(solution)/shard_map/ppermute | solution.py:148
  275.5 17.3 %collective-permute-start.25 = (bf16[64,2048]{1,0:T(8,128)(2,1)S(1)}, bf16[64,2048]{1,0:T(8,128)(2,1)S(1)}, u32[]{:S(2)}, u32[]{:S(2)}) collective-permute-start(bf16[64,2048]{1,0:T(8,128)(2,1)S(1)} %get-tuple-element.52), channel_id=1, source_target_pairs={{2,0},{3,1},{4,2},{5,3},{6,4},{7,5},{10,8},{11,9},{12,10},{13,11},... | collective-permute-start | bytes 786440 | tf_op jit(solution)/shard_map/ppermute | solution.py:148
  276.8 16.0 %collective-permute-start.22 = (bf16[64,2048]{1,0:T(8,128)(2,1)S(1)}, bf16[64,2048]{1,0:T(8,128)(2,1)S(1)}, u32[]{:S(2)}, u32[]{:S(2)}) collective-permute-start(bf16[64,2048]{1,0:T(8,128)(2,1)S(1)} %get-tuple-element.51), channel_id=1, source_target_pairs={{0,2},{1,3},{2,4},{3,5},{4,6},{5,7},{8,10},{9,11},{10,12},{11,13},... | collective-permute-start | bytes 786440 | tf_op jit(solution)/shard_map/ppermute | solution.py:148
  283.2 11.4 %collective-permute-start.39 = (bf16[64,2048]{1,0:T(8,128)(2,1)}, bf16[64,2048]{1,0:T(8,128)(2,1)S(1)}, u32[]{:S(2)}, u32[]{:S(2)}) collective-permute-start(bf16[64,2048]{1,0:T(8,128)(2,1)} %get-tuple-element.46), channel_id=1, source_target_pairs={{2,0},{3,1},{4,2},{5,3},{6,4},{7,5},{10,8},{11,9},{12,10},{13,11},... | collective-permute-start | bytes 786440 | tf_op jit(solution)/shard_map/ppermute | solution.py:148
  284.5 11.7 %collective-permute-start.36 = (bf16[64,2048]{1,0:T(8,128)(2,1)}, bf16[64,2048]{1,0:T(8,128)(2,1)}, u32[]{:S(2)}, u32[]{:S(2)}) collective-permute-start(bf16[64,2048]{1,0:T(8,128)(2,1)} %get-tuple-element.45), channel_id=1, source_target_pairs={{0,2},{1,3},{2,4},{3,5},{4,6},{5,7},{8,10},{9,11},{10,12},{11,13},... | collective-permute-start | bytes 786440 | tf_op jit(solution)/shard_map/ppermute | solution.py:148
  (27 other events, 210.6 us)

commit v2 on v0

v2 whole, which is shorter than its diff:
```python
import jax
import jax.numpy as jnp
from jax import lax
from jax.experimental import pallas as pl
from jax.experimental.pallas import tpu as pltpu
from jax.sharding import PartitionSpec as P

AXES = ("dp", "expert")
ACROSS = (((1,), (1,)), ((), ()))
OVER_ROWS = (((0,), (0,)), ((), ()))


def routing_slots(expert_ids, experts):
    onehot = (expert_ids[:, :, None] == jnp.arange(experts, dtype=jnp.int32)[None, None, :]).astype(
        jnp.int32
    )
    per_token = jnp.sum(onehot, axis=1)
    earlier = jnp.cumsum(per_token, axis=0) - per_token
    return jnp.sum(onehot * earlier[:, None, :], axis=2)


def forward_rows(rows, gate_proj, up_proj, down_proj):
    gate_pre = jnp.dot(rows, gate_proj, preferred_element_type=jnp.float32)
    up_pre = jnp.dot(rows, up_proj, preferred_element_type=jnp.float32)
    hidden = (jax.nn.silu(gate_pre) * up_pre).astype(jnp.bfloat16)
    expert_out = lax.dot_general(
        hidden, down_proj, ACROSS, preferred_element_type=jnp.float32
    ).astype(jnp.bfloat16)
    return (expert_out, gate_pre, up_pre, hidden)


def backward_rows(grad_rows, gate_pre, up_pre, gate_proj, up_proj, down_proj):
    d_hidden = jnp.dot(grad_rows, down_proj, preferred_element_type=jnp.float32)
    sigmoid_gate = jax.nn.sigmoid(gate_pre)
    silu_gate = gate_pre * sigmoid_gate
    d_gate = (d_hidden * up_pre * sigmoid_gate * (1.0 + gate_pre * (1.0 - sigmoid_gate))).astype(
        jnp.bfloat16
    )
    d_up = (d_hidden * silu_gate).astype(jnp.bfloat16)
    d_rows = lax.dot_general(d_gate, gate_proj, ACROSS, preferred_element_type=jnp.float32)
    d_rows = d_rows + lax.dot_general(d_up, up_proj, ACROSS, preferred_element_type=jnp.float32)
    return (d_rows.astype(jnp.bfloat16), d_gate, d_up)


def pick_rows(source_rows, position, top_count):
    chosen = jnp.take(source_rows, position.reshape(-1), axis=0)
    return chosen.reshape(position.shape[0], top_count, source_rows.shape[1])


def capacity_of(tok_dev, top_count, experts):
    return min(tok_dev, (tok_dev * top_count * 4 + 3 * experts - 1) // (3 * experts))


def slot_plan(tokens, expert_ids, gate_probs, cotangent, gate_proj, up_proj, down_proj):
    experts = lax.axis_size("expert")
    tok_dev, top_count = expert_ids.shape
    model_width = tokens.shape[1]
    capacity = capacity_of(tok_dev, top_count, experts)
    slot_index = routing_slots(expert_ids, experts)
    position = expert_ids * capacity + slot_index
    placing = (
        position[None, :, :] == jnp.arange(experts * capacity, dtype=jnp.int32)[:, None, None]
    ).astype(jnp.float32)
    placer = jnp.sum(placing, axis=2)
    weighted = jnp.sum(placing * gate_probs[None, :, :], axis=2)
    row_send = (
        jnp.dot(placer.astype(jnp.bfloat16), tokens, preferred_element_type=jnp.float32)
        .astype(jnp.bfloat16)
        .reshape(experts, capacity, model_width)
    )
    grad_send = (
        jnp.dot(weighted, cotangent.astype(jnp.float32), precision=lax.Precision.HIGHEST)
        .astype(jnp.bfloat16)
        .reshape(experts, capacity, model_width)
    )
    full_gate, full_up, full_down = (
        lax.all_gather(gate_proj[0], "dp", axis=0, tiled=True),
        lax.all_gather(up_proj[0], "dp", axis=0, tiled=True),
        lax.all_gather(down_proj[0], "dp", axis=0, tiled=True),
    )

    def exchange(rows):
        return lax.all_to_all(
            rows.reshape(experts, capacity, model_width),
            "expert",
            split_axis=0,
            concat_axis=0,
            tiled=True,
        ).reshape(-1, model_width)

    rows_flat = exchange(row_send)
    expert_out, gate_pre, up_pre, hidden = forward_rows(rows_flat, full_gate, full_up, full_down)
    returned = exchange(expert_out)
    grads_flat = exchange(grad_send)
    d_rows, d_gate, d_up = backward_rows(
        grads_flat, gate_pre, up_pre, full_gate, full_up, full_down
    )
    grad_back = exchange(d_rows)
    picked = pick_rows(returned, position, top_count).astype(jnp.float32)
    mixed = jnp.sum(gate_probs[:, :, None] * picked, axis=1).astype(jnp.bfloat16)
    prob_grads = jnp.sum(cotangent.astype(jnp.float32)[:, None, :] * picked, axis=2)
    picked_grads = pick_rows(grad_back, position, top_count).astype(jnp.float32)
    token_grads = jnp.sum(picked_grads, axis=1).astype(jnp.bfloat16)
    hidden_units = hidden.shape[1]
    gate_term = lax.dot_general(rows_flat, d_gate, OVER_ROWS, preferred_element_type=jnp.float32)
    up_term = lax.dot_general(rows_flat, d_up, OVER_ROWS, preferred_element_type=jnp.float32)
    down_term = lax.dot_general(grads_flat, hidden, OVER_ROWS, preferred_element_type=jnp.float32)
    shares = lax.psum_scatter(
        jnp.concatenate([gate_term, up_term, down_term], axis=1),
        "dp",
        scatter_dimension=0,
        tiled=True,
    )
    grad_gate = shares[:, :hidden_units]
    grad_up = shares[:, hidden_units : 2 * hidden_units]
    grad_down = shares[:, 2 * hidden_units :]
    return (mixed, token_grads, prob_grads, grad_gate[None], grad_up[None], grad_down[None])


TILE = 256
SIDE = 128
F32 = jnp.float32
BF16 = jnp.bfloat16
VMEM = pl.BlockSpec(memory_space=pltpu.VMEM)


RING = (0, 2, 3, 1)


def flat_index(y, x, z, core):
    return ((y * 2 + x) * 4 + z) * 2 + core


def pairs(target):
    return [
        (flat_index(y, x, z, core), flat_index(*target(y, x, z, core)))
        for y in range(2)
        for x in range(2)
        for z in range(4)
        for core in range(2)
    ]


TO_X = pairs(lambda y, x, z, core: (y, 1 - x, z, core))
TO_Y = pairs(lambda y, x, z, core: (1 - y, x, z, core))
TO_CORE = pairs(lambda y, x, z, core: (y, x, z, 1 - core))
ALONG_Z = pairs(lambda y, x, z, core: (y, x, RING[(RING.index(z) + 1) % 4], core))


def send(array, where):
    return lax.ppermute(array, AXES, where)


def kernel_call(body, out_shape, **spec):
    return pl.pallas_call(
        body,
        out_shape=out_shape,
        compiler_params=pltpu.CompilerParams(vmem_limit_bytes=24 * 1024 * 1024),
        cost_estimate=pl.CostEstimate(flops=0, bytes_accessed=0, transcendentals=0),
        **spec,
    )


def shape(rows, columns, dtype):
    return jax.ShapeDtypeStruct((rows, columns), dtype)


def iota(rows, columns, axis):
    return lax.broadcasted_iota(jnp.int32, (rows, columns), axis)


def exact_parts(values, place):
    first = values.astype(BF16).astype(F32)
    rest = values - first
    second = rest.astype(BF16).astype(F32)
    third = rest - second
    parts = jnp.where(place < 8, first, jnp.where(place < 16, second, third))
    return jnp.where(place < 24, parts, 0.0).astype(BF16)


def block_at(relative, block):
    return pl.ds(pl.multiple_of((lax.axis_index("dp") ^ relative) * block, block), block)


def pack_kernel(tokens_ref, cot_ref, ids_ref, probs_ref, out_ref):
    rows, width = tokens_ref.shape
    block = width // 4
    for r in range(4):
        there = block_at(r, block)
        out_ref[:, r * block : (r + 1) * block] = tokens_ref[:, there]
        out_ref[:, width + r * block : width + (r + 1) * block] = cot_ref[:, there]
    place = iota(SIDE, rows, 0)
    prob = jnp.zeros((SIDE, rows), F32)
    for k in range(ids_ref.shape[0]):
        prob += jnp.where(place % 8 == ids_ref[k : k + 1, :], probs_ref[k : k + 1, :], 0.0)
    same = (iota(rows, rows, 0) == iota(rows, rows, 1)).astype(BF16)
    turned = lax.dot_general(same, exact_parts(prob, place), ACROSS, preferred_element_type=F32)
    out_ref[:, 2 * width :] = turned.astype(BF16)


def pack(tokens, cotangent, expert_ids, gate_probs):
    rows, width = tokens.shape
    return kernel_call(
        pack_kernel,
        shape(rows, 2 * width + SIDE, BF16),
        in_specs=[VMEM] * 4,
        out_specs=VMEM,
    )(tokens, cotangent, expert_ids.T, gate_probs.T)


def unpack_kernel(mixed_ref, back_ref, ids_ref, mixed_out, back_out, prob_out):
    rows, width = mixed_ref.shape
    block = width // 4
    for r in range(4):
        there = block_at(r, block)
        mixed_out[:, there] = mixed_ref[:, r * block : (r + 1) * block]
        back_out[:, there] = back_ref[:, r * block : (r + 1) * block]
    lane = iota(8, SIDE, 1)
    adder = ((lane < 24) & (lane % 8 == iota(8, SIDE, 0))).astype(BF16)
    by_expert = lax.dot_general(adder, back_ref[:, width:], ACROSS, preferred_element_type=F32)
    for k in range(ids_ref.shape[0]):
        hit = iota(8, rows, 0) == ids_ref[k : k + 1, :]
        prob_out[k : k + 1, :] = jnp.sum(jnp.where(hit, by_expert, 0.0), axis=0, keepdims=True)


def unpack(mixed, back, expert_ids):
    mixed, back, prob = kernel_call(
        unpack_kernel,
        (shape(*mixed.shape, BF16), shape(*mixed.shape, BF16), shape(*expert_ids.T.shape, F32)),
        in_specs=[VMEM] * 3,
        out_specs=(VMEM,) * 3,
    )(mixed, back, expert_ids.T)
    return mixed, back, prob.T


def turn_kernel(own_ref, other_ref, out_ref):
    rows = own_ref.shape[0]
    out_ref[:, :rows] = own_ref[...].T
    out_ref[:, rows:] = other_ref[...].T


def turn(whole, width):
    rows = whole[0].shape[0]
    return kernel_call(
        turn_kernel,
        shape(width, 2 * rows, BF16),
        grid=(width // TILE,),
        in_specs=[pl.BlockSpec((rows, TILE), lambda i: (0, i))] * 2,
        out_specs=pl.BlockSpec((TILE, 2 * rows), lambda i: (i, 0)),
    )(*whole)


def times_pieces(rows_ref, pieces):
    total, start = None, 0
    for piece in pieces:
        depth = piece.shape[0]
        term = jnp.dot(rows_ref[:, start : start + depth], piece[...], preferred_element_type=F32)
        total = term if total is None else total + term
        start += depth
    return total


def early_kernel(own_rows, other_rows, own_ref, x_ref, y_ref, out_ref):
    half = own_rows.shape[0]
    out_ref[:half] = times_pieces(own_rows, (own_ref, x_ref, y_ref))
    out_ref[half:] = times_pieces(other_rows, (own_ref, x_ref, y_ref))


def early_products(whole, direct, width):
    half = whole[0].shape[0]
    depth, columns = direct[0].shape
    steps = columns // TILE
    piece = pl.BlockSpec((depth, TILE), lambda j: (0, j))
    return kernel_call(
        early_kernel,
        shape(2 * half, columns, F32),
        grid=(steps,),
        in_specs=[pl.BlockSpec((half, width), lambda j: (0, j // (steps * 2 // 3)))] * 2
        + [piece] * 3,
        out_specs=pl.BlockSpec((2 * half, TILE), lambda j: (0, j)),
    )(*whole, *direct)


def forward_kernel(*refs):
    both_rows, both_parts, earlies, gates, ups = (refs[i : i + 2] for i in range(0, 10, 2))
    scaled_ref, for_gate_ref, for_up_ref, hidden_ref = refs[10:]
    half = both_rows[0].shape[0]
    for index in range(2):
        at = slice(index * half, (index + 1) * half)
        gate_pre = earlies[0][at] + times_pieces(both_rows[index], gates)
        up_pre = earlies[1][at] + times_pieces(both_rows[index], ups)
        lane = iota(half, SIDE, 1)
        mine = (lane < 24) & (lane % 8 == lax.axis_index("expert"))
        parts = both_parts[index][...].astype(F32)
        prob = jnp.sum(jnp.where(mine, parts, 0.0), axis=1, keepdims=True)
        sigmoid_gate = 1.0 / (1.0 + jnp.exp(-gate_pre))
        silu_gate = gate_pre * sigmoid_gate
        hidden = silu_gate * up_pre
        hidden_ref[at] = hidden
        scaled_ref[at] = (hidden * prob).astype(BF16)
        slope = sigmoid_gate * (1.0 + gate_pre * (1.0 - sigmoid_gate))
        for_gate_ref[at] = prob * (up_pre * slope)
        for_up_ref[at] = prob * silu_gate


def forward(whole, early, corner, width, units):
    half = whole[0].shape[0]
    rows = 2 * half
    steps = units // TILE
    block = width // 4
    tile = pl.BlockSpec((rows, TILE), lambda j: (0, j))
    next_tile = pl.BlockSpec((rows, TILE), lambda j: (0, steps + j))
    return kernel_call(
        forward_kernel,
        (shape(rows, units, BF16),) + (shape(rows, units, F32),) * 3,
        grid=(steps,),
        in_specs=[pl.BlockSpec((half, block), lambda j: (0, 3))] * 2
        + [pl.BlockSpec((half, SIDE), lambda j: (0, 2 * width // SIDE))] * 2
        + [tile, next_tile]
        + [pl.BlockSpec((block // 2, TILE), lambda j: (0, j))] * 2
        + [pl.BlockSpec((block // 2, TILE), lambda j: (0, steps + j))] * 2,
        out_specs=(tile,) * 4,
    )(*whole, *whole, early, early, *corner, *corner)


def backward_kernel(own_ref, other_ref, early_ref, first_ref, last_ref, *refs):
    for_gate_ref, for_up_ref, hidden_ref, d_gate_ref, d_up_ref, dots_ref, sum_ref = refs
    step = pl.program_id(0)
    half = own_ref.shape[0]

    @pl.when(step == 0)
    def _():
        sum_ref[...] = jnp.zeros_like(sum_ref)

    for index, grads_ref in enumerate((own_ref, other_ref)):
        at = slice(index * half, (index + 1) * half)
        raw = early_ref[at] + times_pieces(grads_ref, (first_ref, last_ref))
        d_gate_ref[at] = (raw * for_gate_ref[at]).astype(BF16)
        d_up_ref[at] = (raw * for_up_ref[at]).astype(BF16)
        sum_ref[at] += jnp.sum(raw * hidden_ref[at], axis=1, keepdims=True)

    @pl.when(step == pl.num_programs(0) - 1)
    def _():
        lane = iota(2 * half, SIDE, 1)
        mine = lane % 8 == lax.axis_index("expert")
        dots_ref[...] = exact_parts(jnp.where(mine, sum_ref[...], 0.0), lane)


def backward(whole, early, corner, for_gate, for_up, hidden, width):
    rows, units = hidden.shape
    steps = units // TILE
    block = width // 4
    tile = pl.BlockSpec((rows, TILE), lambda j: (0, j))
    return kernel_call(
        backward_kernel,
        (shape(rows, units, BF16),) * 2 + (shape(rows, SIDE, BF16),),
        grid=(steps,),
        in_specs=[pl.BlockSpec((rows // 2, block), lambda j: (0, 7))] * 2
        + [pl.BlockSpec((rows, TILE), lambda j: (0, 2 * steps + j))]
        + [pl.BlockSpec((block // 2, TILE), lambda j: (0, j))] * 2
        + [tile] * 3,
        out_specs=(tile, tile, pl.BlockSpec((rows, SIDE), lambda j: (0, 0))),
        scratch_shapes=[pltpu.VMEM((rows, 1), F32)],
    )(*whole, early, *corner, for_gate, for_up, hidden)


def first_half_blocks(i):
    return jnp.where(i == 3, 4, 7 - 4 * (i % 2) - i // 2)


def later_half_blocks(i):
    return jnp.where(i < 2, 2 + 3 * i, i - 2)


def first_grad_kernel(turned_ref, term_ref, to_x, to_y):
    step = pl.program_id(0)
    part = jnp.dot(turned_ref[...], term_ref[...], preferred_element_type=F32).astype(BF16)

    @pl.when(step < 2)
    def _():
        to_x[...] = part

    @pl.when(step >= 2)
    def _():
        to_y[...] = part


def later_grad_kernel(turned_ref, term_ref, for_x, for_y, own):
    step = pl.program_id(0)
    part = jnp.dot(turned_ref[...], term_ref[...], preferred_element_type=F32)

    @pl.when(step == 0)
    def _():
        for_x[...] = part

    @pl.when(step == 1)
    def _():
        for_y[...] = part

    @pl.when(step >= 2)
    def _():
        own[...] = part


def first_grads(turned, first, width, term):
    rows, units = term.shape
    half = width // 8

    def at(start):
        return pl.BlockSpec((half, units), lambda i: (jnp.clip(i - start, 0, 1), 0))

    return kernel_call(
        first_grad_kernel,
        (shape(2 * half, units, BF16),) * 2,
        grid=(4,),
        in_specs=[
            pl.BlockSpec((half, rows), lambda i: (first + first_half_blocks(i), 0)),
            pl.BlockSpec((rows, units), lambda i: (0, 0)),
        ],
        out_specs=(at(0), at(2)),
    )(turned, term)


def later_grads(turned, first, width, term):
    rows, units = term.shape
    half = width // 8
    once = pl.BlockSpec((half, units), lambda i: (0, 0))
    return kernel_call(
        later_grad_kernel,
        (shape(half, units, F32),) * 2 + (shape(2 * half, units, F32),),
        grid=(4,),
        in_specs=[
            pl.BlockSpec((half, rows), lambda i: (first + later_half_blocks(i), 0)),
            pl.BlockSpec((rows, units), lambda i: (0, 0)),
        ],
        out_specs=(
            once,
            once,
            pl.BlockSpec((half, units), lambda i: (jnp.clip(i - 2, 0, 1), 0)),
        ),
    )(turned, term)


def back_kernel(count, *refs):
    terms, weights, rest = refs[:count], refs[count : count + 5], refs[count + 5 :]
    out_ref = rest[-1]
    units = terms[0].shape[1]
    start = 0
    for weight in weights:
        depth = weight.shape[0]
        total = None
        for index, term in enumerate(terms):
            part = lax.dot_general(
                term[...],
                weight[:, index * units : (index + 1) * units],
                ACROSS,
                preferred_element_type=F32,
            )
            total = part if total is None else total + part
        out_ref[:, start : start + depth] = total.astype(BF16)
        start += depth
    if len(rest) == 2:
        out_ref[:, start:] = rest[0][...]


def whole_rows(piece, start, across):
    return pl.BlockSpec((piece.shape[0], across), lambda i: (0, start // across))


def back_to_rows(terms, direct, start, corner, extra):
    rows, units = terms[0].shape
    across = units * len(terms)
    pieces = [(piece, start) for piece in direct] + [(piece, 0) for piece in corner]
    width = sum(piece.shape[0] for piece, _ in pieces) + sum(e.shape[1] for e in extra)

    def body(*refs):
        back_kernel(len(terms), *refs)

    return kernel_call(
        body,
        shape(rows, width, BF16),
        grid=(rows // TILE,),
        in_specs=[pl.BlockSpec((TILE, units), lambda i: (i, 0)) for _ in terms]
        + [whole_rows(piece, first, across) for piece, first in pieces]
        + [pl.BlockSpec((TILE, e.shape[1]), lambda i: (i, 0)) for e in extra],
        out_specs=pl.BlockSpec((TILE, width), lambda i: (i, 0)),
    )(*terms, *[piece for piece, _ in pieces], *extra)


def total_kernel(own_ref, from_x, from_y, late_x, late_y, out_ref):
    out_ref[0] = own_ref[0] + (from_y[0].astype(F32) + late_x[...].astype(F32))
    out_ref[1] = own_ref[1] + (from_x[0].astype(F32) + late_y[...].astype(F32))


def total(own, from_x, from_y, late_x, late_y):
    block, units = own.shape
    half = block // 2
    step = half // 4
    both = pl.BlockSpec((2, step, units), lambda i: (0, i, 0))
    low = pl.BlockSpec((1, step, units), lambda i: (1, i, 0))
    late = pl.BlockSpec((step, units), lambda i: (i, 0))
    halves = (2, half, units)
    return kernel_call(
        total_kernel,
        jax.ShapeDtypeStruct(halves, F32),
        grid=(half // step,),
        in_specs=[both, low, low, late, late],
        out_specs=both,
    )(own.reshape(halves), from_x.reshape(halves), from_y.reshape(halves), late_x, late_y).reshape(
        1, block, units
    )


def gather_weights(shard, split):
    half = shard.shape[0] // 2
    from_x = send(shard, TO_X)
    from_y = send(shard, TO_Y)
    gate_up = [send(from_x[:half, :split], TO_Y), send(from_y[half:, :split], TO_X)]
    down = [send(from_x[:half, split:], TO_Y), send(from_y[half:, split:], TO_X)]
    return [shard, from_x, from_y], gate_up, down


def send_first(to_x, to_y):
    return send(to_x, TO_X), send(to_y, TO_Y)


def send_later(for_x, for_y, from_x, from_y):
    half = for_x.shape[0]
    late_x = send((for_x + from_y[:half].astype(F32)).astype(BF16), TO_X)
    late_y = send((for_y + from_x[:half].astype(F32)).astype(BF16), TO_Y)
    return late_x, late_y


def gather_rows(own):
    slots = [own]
    for _ in range(3):
        slots.append(send(slots[-1], ALONG_Z))
    return jnp.concatenate(slots)


def sum_over_experts(rows):
    half = rows.shape[0] // 2
    block = half // 4
    arrived = send(rows[half:], TO_CORE)

    def both_cores(slot):
        at = slice(slot * block, (slot + 1) * block)
        return rows[at].astype(F32) + arrived[at].astype(F32)

    moving = send(both_cores(1).astype(BF16), ALONG_Z)
    for slot in (2, 3):
        moving = send((both_cores(slot) + moving.astype(F32)).astype(BF16), ALONG_Z)
    return (both_cores(0) + moving.astype(F32)).astype(BF16)


def after(arrays, *others):
    return lax.optimization_barrier((arrays, others))[0]


def dense_plan(tokens, expert_ids, gate_probs, cotangent, gate_proj, up_proj, down_proj):
    width = tokens.shape[1]
    units = gate_proj.shape[2]
    halves = width // TILE
    shard = jnp.concatenate([gate_proj[0], up_proj[0], down_proj[0]], axis=1)
    direct, gate_up, down = gather_weights(shard, 2 * units)
    packed = pack(tokens, cotangent, expert_ids, gate_probs)
    own_core = gather_rows(packed)
    own_core = after(own_core, direct)
    whole = (own_core, send(own_core, TO_CORE))
    early = early_products(whole, direct, width)
    turned = turn(whole, 2 * width)
    early, turned, gate_up = lax.optimization_barrier((early, turned, gate_up))

    scaled, for_gate, for_up, hidden = forward(whole, early, gate_up, width, units)
    down_first = send_first(*(sent := first_grads(turned, halves, width, scaled)))
    scaled, down = after((scaled, down), sent)
    mixed = sum_over_experts(back_to_rows([scaled], direct, 2 * units, down, []))
    for_x, for_y, down_own = later_grads(turned, halves, width, scaled)
    hidden = after(hidden, for_x)
    d_gate, d_up, dots = backward(whole, early, down, for_gate, for_up, hidden, width)
    down_late = send_later(for_x, for_y, *down_first)
    d_gate, d_up = after((d_gate, d_up), down_first)
    gate_sent = first_grads(turned, 0, width, d_gate)
    up_sent = first_grads(turned, 0, width, d_up)
    gate_first, up_first = send_first(*gate_sent), send_first(*up_sent)
    d_gate, d_up = after((d_gate, d_up), gate_sent, up_sent)
    back = sum_over_experts(back_to_rows([d_gate, d_up], direct, 0, gate_up, [dots]))
    grad_down = total(down_own, *down_first, *down_late)
    d_gate, d_up = after((d_gate, d_up), grad_down)
    *gate_later, gate_own = later_grads(turned, 0, width, d_gate)
    *up_later, up_own = later_grads(turned, 0, width, d_up)
    gate_late = send_later(*gate_later, *gate_first)
    up_late = send_later(*up_later, *up_first)
    outs = unpack(mixed, back, expert_ids)
    gate_late = after(gate_late, outs)
    grad_gate = total(gate_own, *gate_first, *gate_late)
    up_late = after(up_late, grad_gate)
    grad_up = total(up_own, *up_first, *up_late)
    return (*outs, grad_gate, grad_up, grad_down)


def on_device(tokens, expert_ids, *rest):
    tok_dev, top_count = expert_ids.shape
    experts = lax.axis_size("expert")
    square_and_line = lax.axis_size("dp") == 4 and experts == 8
    if square_and_line and capacity_of(tok_dev, top_count, experts) == tok_dev:
        return dense_plan(tokens, expert_ids, *rest)
    return slot_plan(tokens, expert_ids, *rest)


def solution(mesh):
    by_token = P(AXES, None)
    by_expert = P("expert", "dp", None)
    return jax.shard_map(
        on_device,
        mesh=mesh,
        in_specs=(by_token,) * 4 + (by_expert,) * 3,
        out_specs=(by_token,) * 3 + (by_expert,) * 3,
        check_vma=False,
    )
```

time: 355 us -> 190 us (0.54)
  waiting for transfers between devices: 220 us -> 101 us
  matrix products: 38.8 us -> 0 us
  local copies, waits for them, and re-layouts: 37.8 us -> 0.35 us
  Pallas kernels: 0 us -> 37.4 us
  starting transfers between devices: 19.3 us -> 46.2 us
  other arithmetic: 24.1 us -> 3.11 us
  between operations: 13.9 us -> 0.92 us
    all_to_all x4 -> x0, waiting for transfers between devices: 169 us -> none  [the longest x1 46.3 us: on_device(): lax.all_to_all(grad_send, 'expert', split_axis=0, concat_axis=0, tiled=True)]
    ppermute x0 -> x30, waiting for transfers between devices: none -> 101 us  [send(): return lax.ppermute(array, AXES, where)]
    ppermute x0 -> x30, starting transfers between devices: none -> 46.2 us  [send(): return lax.ppermute(array, AXES, where)]
    dot_general x11 -> x0, matrix products: 38.8 us -> none  [the longest x1 5.45 us: backward_rows(): d_hidden = jnp.dot(grad_rows, down_proj, preferred_element_type=jnp.float32)]
    pallas_call x0 -> x17, Pallas kernels: none -> 37.4 us  [the longest x1 6.62 us: early_products(): kernel_call(early_kernel, shape(2 * half, columns, F32), grid=(steps,), i...]
    reduce_scatter x1 -> x0, waiting for transfers between devices: 29.6 us -> none  [on_device(): lax.psum_scatter(jnp.concatenate([gate_term, up_term, down_term], axis=1)...]
    all_to_all x4 -> x0, starting transfers between devices: 19 us -> none  [the longest x1 6.33 us: on_device(): lax.all_to_all(grad_send, 'expert', split_axis=0, concat_axis=0, tiled=True)]
    all_gather x3 -> x0, waiting for transfers between devices: 19 us -> none  [the longest x1 19 us: on_device(): lax.all_gather(gate_proj[0], 'dp', axis=0, tiled=True)]
  transfers between devices with their start and end apart: 8 -> 30, of which waited for: 6 -> 19; matrix products, arithmetic and copies ran while one was open for 20% -> 1% of each run, Pallas kernels for 0% -> 19%
where the time goes in v2:
time: 190 us; the launch traced here: 189 us
  waiting for transfers between devices  101 us (53%)
  starting transfers between devices  46.2 us (24%)
  Pallas kernels  37.4 us (20%)
  other arithmetic  3.11 us (2%)
    ppermute x30, waiting for transfers between devices, send(): return lax.ppermute(array, AXES, where)  101 us
    ppermute x30, starting transfers between devices, send(): return lax.ppermute(array, AXES, where)  46.2 us
    pallas_call x1, Pallas kernels, early_products(): kernel_call(early_kernel, shape(2 * half, columns, F32), grid=(steps,), i...  6.62 us
    pallas_call x2, Pallas kernels, back_to_rows(): kernel_call(body, shape(rows, width, BF16), grid=(rows // TILE,), in_spec...  6.21 us
    pallas_call x3, Pallas kernels, total(): kernel_call(total_kernel, jax.ShapeDtypeStruct(halves, F32), grid=(half /...  5.54 us
    pallas_call x3, Pallas kernels, later_grads(): kernel_call(later_grad_kernel, (shape(half, units, F32),) * 2 + (shape(2...  5.12 us
    pallas_call x3, Pallas kernels, first_grads(): kernel_call(first_grad_kernel, (shape(2 * half, units, BF16),) * 2, grid=...  4.98 us
  transfers between devices with their start and end apart: 30, of which 19 were waited for; matrix products, arithmetic and copies ran while one was open for 1% of the time, Pallas kernels for 19%

profile of v2, /device:TPU:0, one launch (start us, length us, event | category | flops | bytes accessed | tf_op | source)
XLA Modules:
  0.0 189.3 jit_solution(13306399840588778330)
XLA Ops:
  0.7 1.8 pad_maximum_fusion.own_ref.refs_1_.refs_2_
  2.5 3.0 %collective-permute-start.4 = (bf16[512,2304]{1,0:T(8,128)(2,1)S(1)}, bf16[512,2304]{1,0:T(8,128)(2,1)S(1)}, u32[]{:S(2)}, u32[]{:S(2)}) collective-permute-start(bf16[512,2304]{1,0:T(8,128)(2,1)S(1)} %pad_maximum_fusion.own_ref.refs_1_.refs_2_), channel_id=1, source_target_pairs={{0,16},{1,17},{2,18},{3,19},{4,20},{5,21},{6,22},{7,23},{8,24},{9,... | collective-permute-start | bytes 7077896 | tf_op jit(solution)/shard_map/ppermute | solution.py:151
  7.2 2.6 %collective-permute-start = (bf16[64,4224]{1,0:T(8,128)(2,1)S(1)}, bf16[64,4224]{1,0:T(8,128)(2,1)S(1)}, u32[]{:S(2)}, u32[]{:S(2)}) collective-permute-start(bf16[64,4224]{1,0:T(8,128)(2,1)S(1)} %shard_map.118), channel_id=1, source_target_pairs={{0,4},{1,5},{2,0},{3,1},{4,6},{5,7},{6,2},{7,3},{8,12},{9,13},{10,... | collective-permute-start | bytes 1622024 | tf_op jit(solution)/shard_map/ppermute | solution.py:151
  9.8 11.0 %collective-permute-done = bf16[64,4224]{1,0:T(8,128)(2,1)S(1)} collective-permute-done((bf16[64,4224]{1,0:T(8,128)(2,1)S(1)}, bf16[64,4224]{1,0:T(8,128)(2,1)S(1)}, u32[]{:S(2)}, u32[]{:S(2)}) %collective-permute-start) | collective-permute-done | bytes 540704 | tf_op jit(solution)/shard_map/ppermute | solution.py:151
  20.7 3.4 %collective-permute-start.1 = (bf16[64,4224]{1,0:T(8,128)(2,1)S(1)}, bf16[64,4224]{1,0:T(8,128)(2,1)S(1)}, u32[]{:S(2)}, u32[]{:S(2)}) collective-permute-start(bf16[64,4224]{1,0:T(8,128)(2,1)S(1)} %collective-permute-done), channel_id=1, source_target_pairs={{0,4},{1,5},{2,0},{3,1},{4,6},{5,7},{6,2},{7,3},{8,12},{9,13},{10,... | collective-permute-start | bytes 1622024 | tf_op jit(solution)/shard_map/ppermute | solution.py:151
  24.1 10.0 %collective-permute-done.1 = bf16[64,4224]{1,0:T(8,128)(2,1)S(1)} collective-permute-done((bf16[64,4224]{1,0:T(8,128)(2,1)S(1)}, bf16[64,4224]{1,0:T(8,128)(2,1)S(1)}, u32[]{:S(2)}, u32[]{:S(2)}) %collective-permute-start.1) | collective-permute-done | bytes 540704 | tf_op jit(solution)/shard_map/ppermute | solution.py:151
  34.2 3.4 %collective-permute-start.2 = (bf16[64,4224]{1,0:T(8,128)(2,1)S(1)}, bf16[64,4224]{1,0:T(8,128)(2,1)S(1)}, u32[]{:S(2)}, u32[]{:S(2)}) collective-permute-start(bf16[64,4224]{1,0:T(8,128)(2,1)S(1)} %collective-permute-done.1), channel_id=1, source_target_pairs={{0,4},{1,5},{2,0},{3,1},{4,6},{5,7},{6,2},{7,3},{8,12},{9,13},{10,... | collective-permute-start | bytes 1622024 | tf_op jit(solution)/shard_map/ppermute | solution.py:151
  37.5 9.1 %collective-permute-done.2 = bf16[64,4224]{1,0:T(8,128)(2,1)S(1)} collective-permute-done((bf16[64,4224]{1,0:T(8,128)(2,1)S(1)}, bf16[64,4224]{1,0:T(8,128)(2,1)S(1)}, u32[]{:S(2)}, u32[]{:S(2)}) %collective-permute-start.2) | collective-permute-done | bytes 540704 | tf_op jit(solution)/shard_map/ppermute | solution.py:151
  46.8 9.9 %collective-permute-done.4.y_ref.refs_3_.refs_4_ = bf16[512,2304]{1,0:T(8,128)(2,1)S(1)} collective-permute-done((bf16[512,2304]{1,0:T(8,128)(2,1)S(1)}, bf16[512,2304]{1,0:T(8,128)(2,1)S(1)}, u32[]{:S(2)}, u32[]{:S(2)}) %collective-permute-start.4) | collective-permute-done | bytes 2359328 | tf_op jit(solution)/shard_map/ppermute | solution.py:151
  58.3 1.6 collective-permute-start.7
  61.0 1.7 collective-permute-start.8
  62.7 3.2 %shard_map.120.turned_ref = bf16[4096,512]{1,0:T(8,128)(2,1)S(1)} custom-call(bf16[256,4224]{1,0:T(8,128)(2,1)S(1)} %pad_maximum_fusion.1.own_rows.own_ref.refs_0_.refs_2_, bf16[256,4224]{1,0:T(8,128)(2,1)S(1)} %collective-permute-done.5.other_rows.other_ref.refs_1_.refs_3_), custom_call_target="tpu_custom_call" | custom-call | tf_op jit(solution)/shard_map/pallas_call | solution.py:244
  65.9 6.6 %shard_map.119.refs_4_.refs_5_.early_ref = f32[512,2304]{1,0:T(8,128)S(1)} custom-call(bf16[256,4224]{1,0:T(8,128)(2,1)S(1)} %pad_maximum_fusion.1.own_rows.own_ref.refs_0_.refs_2_, bf16[256,4224]{1,0:T(8,128)(2,1)S(1)} %collective-permute-done.5.other_rows.other_ref.refs_1_.refs_3_, bf16[512,2304]{1,0:T(8,128)(2,1)S(1)} %pad_maximum_fusion.own_ref.refs_1_.refs_2_, ...), custom_call_target="tpu_custom_call" | custom-call | tf_op jit(solution)/shard_map/pallas_call | solution.py:274
  72.5 6.2 %collective-permute-done.7.refs_7_.refs_9_.refs_6_ = bf16[256,1536]{1,0:T(8,128)(2,1)S(1)} collective-permute-done((bf16[256,1536]{1,0:T(8,128)(2,1)S(1)}, bf16[256,1536]{1,0:T(8,128)(2,1)S(1)}, u32[]{:S(2)}, u32[]{:S(2)}) %collective-permute-start.7) | collective-permute-done | bytes 786464 | tf_op jit(solution)/shard_map/ppermute | solution.py:151
  78.7 1.7 collective-permute-done.6.refs_6_.refs_8_.refs_5_
  80.3 2.6 %shard_map.121 = (bf16[512,768]{1,0:T(8,128)(2,1)S(1)}, f32[512,768]{1,0:T(8,128)S(1)}, f32[512,768]{1,0:T(8,128)S(1)}, f32[512,768]{1,0:T(8,128)S(1)}) custom-call(bf16[256,4224]{1,0:T(8,128)(2,1)S(1)} %pad_maximum_fusion.1.own_rows.own_ref.refs_0_.refs_2_, bf16[256,4224]{1,0:T(8,128)(2,1)S(1)} %collective-permute-done.5.other_rows.other_ref.refs_1_.refs_3_, ...), custom_call_target="tpu_custom_call" | custom-call | tf_op jit(solution)/shard_map/pallas_call | solution.py:313
  83.0 1.7 shard_map.122
  85.6 1.5 collective-permute-done.9.refs_5_.last_ref
  87.1 1.7 collective-permute-done.8.refs_4_.first_ref
  88.8 2.2 %shard_map.123 = bf16[512,2048]{1,0:T(8,128)(2,1)S(1)} custom-call(bf16[512,768]{1,0:T(8,128)(2,1)S(1)} %get-tuple-element.58.term_ref.refs_0_, bf16[512,2304]{1,0:T(8,128)(2,1)S(1)} %pad_maximum_fusion.own_ref.refs_1_.refs_2_, bf16[512,2304]{1,0:T(8,128)(2,1)S(1)} %collective-permute-done.3.x_ref.refs_2_.refs_3_, ...), custom_call_target="tpu_custom_call" | custom-call | tf_op jit(solution)/shard_map/pallas_call | solution.py:479
  91.2 1.7 shard_map.124
  92.9 2.2 %shard_map.125 = (bf16[512,768]{1,0:T(8,128)(2,1)S(1)}, bf16[512,768]{1,0:T(8,128)(2,1)S(1)}, bf16[512,128]{1,0:T(8,128)(2,1)S(1)}) custom-call(bf16[256,4224]{1,0:T(8,128)(2,1)S(1)} %pad_maximum_fusion.1.own_rows.own_ref.refs_0_.refs_2_, bf16[256,4224]{1,0:T(8,128)(2,1)S(1)} %collective-permute-done.5.other_rows.other_ref.refs_1_.refs_3_, ...), custom_call_target="tpu_custom_call" | custom-call | tf_op jit(solution)/shard_map/pallas_call | solution.py:354
  95.1 8.5 %collective-permute-done.14 = bf16[512,768]{1,0:T(8,128)(2,1)S(1)} collective-permute-done((bf16[512,768]{1,0:T(8,128)(2,1)S(1)}, bf16[512,768]{1,0:T(8,128)(2,1)S(1)}, u32[]{:S(2)}, u32[]{:S(2)}) %collective-permute-start.14) | collective-permute-done | bytes 786464 | tf_op jit(solution)/shard_map/ppermute | solution.py:151
  106.1 1.7 shard_map.127
  107.8 1.7 collective-permute-start.26
  109.5 2.6 %collective-permute-start.11 = (bf16[64,2048]{1,0:T(8,128)(2,1)S(1)}, bf16[64,2048]{1,0:T(8,128)(2,1)S(1)}, u32[]{:S(2)}, u32[]{:S(2)}) collective-permute-start(bf16[64,2048]{1,0:T(8,128)(2,1)S(1)} %add_convert_fusion.13), channel_id=1, source_target_pairs={{0,4},{1,5},{2,0},{3,1},{4,6},{5,7},{6,2},{7,3},{8,12},{9,13},{10,... | collective-permute-start | bytes 786440 | tf_op jit(solution)/shard_map/ppermute | solution.py:151
  112.2 1.7 shard_map.126
  113.8 4.0 %shard_map.128 = bf16[512,2176]{1,0:T(8,128)(2,1)S(1)} custom-call(bf16[512,768]{1,0:T(8,128)(2,1)S(1)} %get-tuple-element.82.term_ref.refs_0_, bf16[512,768]{1,0:T(8,128)(2,1)S(1)} %get-tuple-element.88.term_ref.refs_1_, bf16[512,2304]{1,0:T(8,128)(2,1)S(1)} %pad_maximum_fusion.own_ref.refs_1_.refs_2_, ...), custom_call_target="tpu_custom_call" | custom-call | tf_op jit(solution)/shard_map/pallas_call | solution.py:479
  118.0 1.6 collective-permute-start.27
  120.1 1.8 shard_map.130
  122.0 1.7 shard_map.131
  123.7 1.7 shard_map.133
  126.1 7.9 %collective-permute-done.26 = bf16[512,768]{1,0:T(8,128)(2,1)S(1)} collective-permute-done((bf16[512,768]{1,0:T(8,128)(2,1)S(1)}, bf16[512,768]{1,0:T(8,128)(2,1)S(1)}, u32[]{:S(2)}, u32[]{:S(2)}) %collective-permute-start.26) | collective-permute-done | bytes 786464 | tf_op jit(solution)/shard_map/ppermute | solution.py:151
  134.0 2.6 %collective-permute-start.12 = (bf16[64,2048]{1,0:T(8,128)(2,1)S(1)}, bf16[64,2048]{1,0:T(8,128)(2,1)S(1)}, u32[]{:S(2)}, u32[]{:S(2)}) collective-permute-start(bf16[64,2048]{1,0:T(8,128)(2,1)S(1)} %add_convert_fusion.12), channel_id=1, source_target_pairs={{0,4},{1,5},{2,0},{3,1},{4,6},{5,7},{6,2},{7,3},{8,12},{9,13},{10,... | collective-permute-start | bytes 786440 | tf_op jit(solution)/shard_map/ppermute | solution.py:151
  136.6 1.8 collective-permute-done.27
  138.4 1.5 collective-permute-start.29
  140.7 10.1 %collective-permute-done.22 = bf16[512,768]{1,0:T(8,128)(2,1)S(1)} collective-permute-done((bf16[512,768]{1,0:T(8,128)(2,1)S(1)}, bf16[512,768]{1,0:T(8,128)(2,1)S(1)}, u32[]{:S(2)}, u32[]{:S(2)}) %collective-permute-start.22) | collective-permute-done | bytes 786464 | tf_op jit(solution)/shard_map/ppermute | solution.py:151
  150.8 2.6 %collective-permute-start.17 = (bf16[64,2176]{1,0:T(8,128)(2,1)S(1)}, bf16[64,2176]{1,0:T(8,128)(2,1)S(1)}, u32[]{:S(2)}, u32[]{:S(2)}) collective-permute-start(bf16[64,2176]{1,0:T(8,128)(2,1)S(1)} %add_convert_fusion.9), channel_id=1, source_target_pairs={{0,4},{1,5},{2,0},{3,1},{4,6},{5,7},{6,2},{7,3},{8,12},{9,13},{10,... | collective-permute-start | bytes 835592 | tf_op jit(solution)/shard_map/ppermute | solution.py:151
  153.5 1.8 collective-permute-done.23
  155.3 1.5 collective-permute-start.25
  158.1 3.4 %collective-permute-start.18 = (bf16[64,2176]{1,0:T(8,128)(2,1)S(1)}, bf16[64,2176]{1,0:T(8,128)(2,1)S(1)}, u32[]{:S(2)}, u32[]{:S(2)}) collective-permute-start(bf16[64,2176]{1,0:T(8,128)(2,1)S(1)} %add_convert_fusion.8), channel_id=1, source_target_pairs={{0,4},{1,5},{2,0},{3,1},{4,6},{5,7},{6,2},{7,3},{8,12},{9,13},{10,... | collective-permute-start | bytes 835592 | tf_op jit(solution)/shard_map/ppermute | solution.py:151
  161.7 5.2 %collective-permute-done.18 = bf16[64,2176]{1,0:T(8,128)(2,1)S(1)} collective-permute-done((bf16[64,2176]{1,0:T(8,128)(2,1)S(1)}, bf16[64,2176]{1,0:T(8,128)(2,1)S(1)}, u32[]{:S(2)}, u32[]{:S(2)}) %collective-permute-start.18) | collective-permute-done | bytes 278560 | tf_op jit(solution)/shard_map/ppermute | solution.py:151
  166.9 3.4 %collective-permute-start.13 = (bf16[64,2048]{1,0:T(8,128)(2,1)S(1)}, bf16[64,2048]{1,0:T(8,128)(2,1)S(1)}, u32[]{:S(2)}, u32[]{:S(2)}) collective-permute-start(bf16[64,2048]{1,0:T(8,128)(2,1)S(1)} %add_convert_fusion.11), channel_id=1, source_target_pairs={{0,4},{1,5},{2,0},{3,1},{4,6},{5,7},{6,2},{7,3},{8,12},{9,13},{10,... | collective-permute-start | bytes 786440 | tf_op jit(solution)/shard_map/ppermute | solution.py:151
  170.4 7.0 %collective-permute-done.13 = bf16[64,2048]{1,0:T(8,128)(2,1)S(1)} collective-permute-done((bf16[64,2048]{1,0:T(8,128)(2,1)S(1)}, bf16[64,2048]{1,0:T(8,128)(2,1)S(1)}, u32[]{:S(2)}, u32[]{:S(2)}) %collective-permute-start.13) | collective-permute-done | bytes 262176 | tf_op jit(solution)/shard_map/ppermute | solution.py:151
  177.4 2.7 %collective-permute-start.19 = (bf16[64,2176]{1,0:T(8,128)(2,1)S(1)}, bf16[64,2176]{1,0:T(8,128)(2,1)S(1)}, u32[]{:S(2)}, u32[]{:S(2)}) collective-permute-start(bf16[64,2176]{1,0:T(8,128)(2,1)S(1)} %add_convert_fusion.7), channel_id=1, source_target_pairs={{0,4},{1,5},{2,0},{3,1},{4,6},{5,7},{6,2},{7,3},{8,12},{9,13},{10,... | collective-permute-start | bytes 835592 | tf_op jit(solution)/shard_map/ppermute | solution.py:151
  180.2 4.4 %collective-permute-done.19 = bf16[64,2176]{1,0:T(8,128)(2,1)S(1)} collective-permute-done((bf16[64,2176]{1,0:T(8,128)(2,1)S(1)}, bf16[64,2176]{1,0:T(8,128)(2,1)S(1)}, u32[]{:S(2)}, u32[]{:S(2)}) %collective-permute-start.19) | collective-permute-done | bytes 278560 | tf_op jit(solution)/shard_map/ppermute | solution.py:151
  185.6 1.8 shard_map.132
  187.4 1.8 shard_map.134
  (59 shorter events, 12.9 us)
Async XLA Ops:
  0.6 6.4 %copy-start = (bf16[64,2048]{1,0:T(8,128)(2,1)S(1)}, bf16[64,2048]{1,0:T(8,128)(2,1)}, u32[]{:S(2)}) copy-start(bf16[64,2048]{1,0:T(8,128)(2,1)} %tokens_ref.1) | copy-start | bytes 786436
  0.6 6.4 %copy-start.1 = (bf16[64,2048]{1,0:T(8,128)(2,1)S(1)}, bf16[64,2048]{1,0:T(8,128)(2,1)}, u32[]{:S(2)}) copy-start(bf16[64,2048]{1,0:T(8,128)(2,1)} %cot_ref.1) | copy-start | bytes 786436
  0.7 6.4 %copy-start.2 = (s32[64,6]{0,1:T(8,128)S(1)}, s32[64,6]{0,1:T(8,128)}, u32[]{:S(2)}) copy-start(s32[64,6]{0,1:T(8,128)} %param.8) | copy-start | bytes 4612
  0.7 6.4 %copy-start.3 = (f32[64,6]{0,1:T(8,128)S(1)}, f32[64,6]{0,1:T(8,128)}, u32[]{:S(2)}) copy-start(f32[64,6]{0,1:T(8,128)} %param.9) | copy-start | bytes 4612
  2.5 54.3 %collective-permute-start.4 = (bf16[512,2304]{1,0:T(8,128)(2,1)S(1)}, bf16[512,2304]{1,0:T(8,128)(2,1)S(1)}, u32[]{:S(2)}, u32[]{:S(2)}) collective-permute-start(bf16[512,2304]{1,0:T(8,128)(2,1)S(1)} %pad_maximum_fusion.own_ref.refs_1_.refs_2_), channel_id=1, source_target_pairs={{0,16},{1,17},{2,18},{3,19},{4,20},{5,21},{6,22},{7,23},{8,24},{9,... | collective-permute-start | bytes 7077896 | tf_op jit(solution)/shard_map/ppermute | solution.py:151
  5.5 52.7 %collective-permute-start.3 = (bf16[512,2304]{1,0:T(8,128)(2,1)S(1)}, bf16[512,2304]{1,0:T(8,128)(2,1)S(1)}, u32[]{:S(2)}, u32[]{:S(2)}) collective-permute-start(bf16[512,2304]{1,0:T(8,128)(2,1)S(1)} %pad_maximum_fusion.own_ref.refs_1_.refs_2_), channel_id=1, source_target_pairs={{0,8},{1,9},{2,10},{3,11},{4,12},{5,13},{6,14},{7,15},{8,0},{9,1},... | collective-permute-start | bytes 7077896 | tf_op jit(solution)/shard_map/ppermute | solution.py:151
  7.2 13.6 %collective-permute-start = (bf16[64,4224]{1,0:T(8,128)(2,1)S(1)}, bf16[64,4224]{1,0:T(8,128)(2,1)S(1)}, u32[]{:S(2)}, u32[]{:S(2)}) collective-permute-start(bf16[64,4224]{1,0:T(8,128)(2,1)S(1)} %shard_map.118), channel_id=1, source_target_pairs={{0,4},{1,5},{2,0},{3,1},{4,6},{5,7},{6,2},{7,3},{8,12},{9,13},{10,... | collective-permute-start | bytes 1622024 | tf_op jit(solution)/shard_map/ppermute | solution.py:151
  20.7 13.4 %collective-permute-start.1 = (bf16[64,4224]{1,0:T(8,128)(2,1)S(1)}, bf16[64,4224]{1,0:T(8,128)(2,1)S(1)}, u32[]{:S(2)}, u32[]{:S(2)}) collective-permute-start(bf16[64,4224]{1,0:T(8,128)(2,1)S(1)} %collective-permute-done), channel_id=1, source_target_pairs={{0,4},{1,5},{2,0},{3,1},{4,6},{5,7},{6,2},{7,3},{8,12},{9,13},{10,... | collective-permute-start | bytes 1622024 | tf_op jit(solution)/shard_map/ppermute | solution.py:151
  34.2 12.5 %collective-permute-start.2 = (bf16[64,4224]{1,0:T(8,128)(2,1)S(1)}, bf16[64,4224]{1,0:T(8,128)(2,1)S(1)}, u32[]{:S(2)}, u32[]{:S(2)}) collective-permute-start(bf16[64,4224]{1,0:T(8,128)(2,1)S(1)} %collective-permute-done.1), channel_id=1, source_target_pairs={{0,4},{1,5},{2,0},{3,1},{4,6},{5,7},{6,2},{7,3},{8,12},{9,13},{10,... | collective-permute-start | bytes 1622024 | tf_op jit(solution)/shard_map/ppermute | solution.py:151
  58.2 4.5 %collective-permute-start.5 = (bf16[256,4224]{1,0:T(8,128)(2,1)S(1)}, bf16[256,4224]{1,0:T(8,128)(2,1)S(1)}, u32[]{:S(2)}, u32[]{:S(2)}) collective-permute-start(bf16[256,4224]{1,0:T(8,128)(2,1)S(1)} %pad_maximum_fusion.1.own_rows.own_ref.refs_0_.refs_2_), channel_id=1, source_target_pairs={{0,1},{1,0},{2,3},{3,2},{4,5},{5,4},{6,7},{7,6},{8,9},{9,8},{10,11... | collective-permute-start | bytes 6488072 | tf_op jit(solution)/shard_map/ppermute | solution.py:151
  58.3 20.4 %collective-permute-start.7 = (bf16[256,1536]{1,0:T(8,128)(2,1)S(1)}, bf16[256,1536]{1,0:T(8,128)(2,1)S(1)}, u32[]{:S(2)}, u32[]{:S(2)}) collective-permute-start(bf16[256,1536]{1,0:T(8,128)(2,1)S(1)} %slice.113), channel_id=1, source_target_pairs={{0,8},{1,9},{2,10},{3,11},{4,12},{5,13},{6,14},{7,15},{8,0},{9,1},... | collective-permute-start | bytes 2359304 | tf_op jit(solution)/shard_map/ppermute | solution.py:151
  59.9 20.4 %collective-permute-start.6 = (bf16[256,1536]{1,0:T(8,128)(2,1)S(1)}, bf16[256,1536]{1,0:T(8,128)(2,1)S(1)}, u32[]{:S(2)}, u32[]{:S(2)}) collective-permute-start(bf16[256,1536]{1,0:T(8,128)(2,1)S(1)} %slice.112), channel_id=1, source_target_pairs={{0,16},{1,17},{2,18},{3,19},{4,20},{5,21},{6,22},{7,23},{8,24},{9,... | collective-permute-start | bytes 2359304 | tf_op jit(solution)/shard_map/ppermute | solution.py:151
  60.5 26.6 %collective-permute-start.9 = (bf16[256,768]{1,0:T(8,128)(2,1)S(1)}, bf16[256,768]{1,0:T(8,128)(2,1)S(1)}, u32[]{:S(2)}, u32[]{:S(2)}) collective-permute-start(bf16[256,768]{1,0:T(8,128)(2,1)S(1)} %slice.115), channel_id=1, source_target_pairs={{0,8},{1,9},{2,10},{3,11},{4,12},{5,13},{6,14},{7,15},{8,0},{9,1},... | collective-permute-start | bytes 1179656 | tf_op jit(solution)/shard_map/ppermute | solution.py:151
  61.0 27.8 %collective-permute-start.8 = (bf16[256,768]{1,0:T(8,128)(2,1)S(1)}, bf16[256,768]{1,0:T(8,128)(2,1)S(1)}, u32[]{:S(2)}, u32[]{:S(2)}) collective-permute-start(bf16[256,768]{1,0:T(8,128)(2,1)S(1)} %slice.114), channel_id=1, source_target_pairs={{0,16},{1,17},{2,18},{3,19},{4,20},{5,21},{6,22},{7,23},{8,24},{9,... | collective-permute-start | bytes 1179656 | tf_op jit(solution)/shard_map/ppermute | solution.py:151
  84.6 19.0 %collective-permute-start.14 = (bf16[512,768]{1,0:T(8,128)(2,1)S(1)}, bf16[512,768]{1,0:T(8,128)(2,1)S(1)}, u32[]{:S(2)}, u32[]{:S(2)}) collective-permute-start(bf16[512,768]{1,0:T(8,128)(2,1)S(1)} %get-tuple-element.56), channel_id=1, source_target_pairs={{0,8},{1,9},{2,10},{3,11},{4,12},{5,13},{6,14},{7,15},{8,0},{9,1},... | collective-permute-start | bytes 2359304 | tf_op jit(solution)/shard_map/ppermute | solution.py:151
  85.2 19.7 %collective-permute-start.15 = (bf16[512,768]{1,0:T(8,128)(2,1)S(1)}, bf16[512,768]{1,0:T(8,128)(2,1)S(1)}, u32[]{:S(2)}, u32[]{:S(2)}) collective-permute-start(bf16[512,768]{1,0:T(8,128)(2,1)S(1)} %get-tuple-element.57), channel_id=1, source_target_pairs={{0,16},{1,17},{2,18},{3,19},{4,20},{5,21},{6,22},{7,23},{8,24},{9,... | collective-permute-start | bytes 2359304 | tf_op jit(solution)/shard_map/ppermute | solution.py:151
  91.1 18.4 %collective-permute-start.10 = (bf16[256,2048]{1,0:T(8,128)(2,1)S(1)}, bf16[256,2048]{1,0:T(8,128)(2,1)S(1)}, u32[]{:S(2)}, u32[]{:S(2)}) collective-permute-start(bf16[256,2048]{1,0:T(8,128)(2,1)S(1)} %slice.117), channel_id=1, source_target_pairs={{0,1},{1,0},{2,3},{3,2},{4,5},{5,4},{6,7},{7,6},{8,9},{9,8},{10,11... | collective-permute-start | bytes 3145736 | tf_op jit(solution)/shard_map/ppermute | solution.py:151
  105.0 13.0 %collective-permute-start.20 = (bf16[256,768]{1,0:T(8,128)(2,1)S(1)}, bf16[256,768]{1,0:T(8,128)(2,1)S(1)}, u32[]{:S(2)}, u32[]{:S(2)}) collective-permute-start(bf16[256,768]{1,0:T(8,128)(2,1)S(1)} %add_convert_fusion.5), channel_id=1, source_target_pairs={{0,8},{1,9},{2,10},{3,11},{4,12},{5,13},{6,14},{7,15},{8,0},{9,1},... | collective-permute-start | bytes 1179656 | tf_op jit(solution)/shard_map/ppermute | solution.py:151
  105.7 13.9 %collective-permute-start.21 = (bf16[256,768]{1,0:T(8,128)(2,1)S(1)}, bf16[256,768]{1,0:T(8,128)(2,1)S(1)}, u32[]{:S(2)}, u32[]{:S(2)}) collective-permute-start(bf16[256,768]{1,0:T(8,128)(2,1)S(1)} %add_convert_fusion.4), channel_id=1, source_target_pairs={{0,16},{1,17},{2,18},{3,19},{4,20},{5,21},{6,22},{7,23},{8,24},{9,... | collective-permute-start | bytes 1179656 | tf_op jit(solution)/shard_map/ppermute | solution.py:151
  107.8 26.2 %collective-permute-start.26 = (bf16[512,768]{1,0:T(8,128)(2,1)S(1)}, bf16[512,768]{1,0:T(8,128)(2,1)S(1)}, u32[]{:S(2)}, u32[]{:S(2)}) collective-permute-start(bf16[512,768]{1,0:T(8,128)(2,1)S(1)} %get-tuple-element.72), channel_id=1, source_target_pairs={{0,8},{1,9},{2,10},{3,11},{4,12},{5,13},{6,14},{7,15},{8,0},{9,1},... | collective-permute-start | bytes 2359304 | tf_op jit(solution)/shard_map/ppermute | solution.py:151
  109.5 15.9 %collective-permute-start.11 = (bf16[64,2048]{1,0:T(8,128)(2,1)S(1)}, bf16[64,2048]{1,0:T(8,128)(2,1)S(1)}, u32[]{:S(2)}, u32[]{:S(2)}) collective-permute-start(bf16[64,2048]{1,0:T(8,128)(2,1)S(1)} %add_convert_fusion.13), channel_id=1, source_target_pairs={{0,4},{1,5},{2,0},{3,1},{4,6},{5,7},{6,2},{7,3},{8,12},{9,13},{10,... | collective-permute-start | bytes 786440 | tf_op jit(solution)/shard_map/ppermute | solution.py:151
  117.9 22.1 %collective-permute-start.16 = (bf16[256,2176]{1,0:T(8,128)(2,1)S(1)}, bf16[256,2176]{1,0:T(8,128)(2,1)S(1)}, u32[]{:S(2)}, u32[]{:S(2)}) collective-permute-start(bf16[256,2176]{1,0:T(8,128)(2,1)S(1)} %slice.126), channel_id=1, source_target_pairs={{0,1},{1,0},{2,3},{3,2},{4,5},{5,4},{6,7},{7,6},{8,9},{9,8},{10,11... | collective-permute-start | bytes 3342344 | tf_op jit(solution)/shard_map/ppermute | solution.py:151
  118.0 20.4 %collective-permute-start.27 = (bf16[512,768]{1,0:T(8,128)(2,1)S(1)}, bf16[512,768]{1,0:T(8,128)(2,1)S(1)}, u32[]{:S(2)}, u32[]{:S(2)}) collective-permute-start(bf16[512,768]{1,0:T(8,128)(2,1)S(1)} %get-tuple-element.73), channel_id=1, source_target_pairs={{0,16},{1,17},{2,18},{3,19},{4,20},{5,21},{6,22},{7,23},{8,24},{9,... | collective-permute-start | bytes 2359304 | tf_op jit(solution)/shard_map/ppermute | solution.py:151
  119.6 31.2 %collective-permute-start.22 = (bf16[512,768]{1,0:T(8,128)(2,1)S(1)}, bf16[512,768]{1,0:T(8,128)(2,1)S(1)}, u32[]{:S(2)}, u32[]{:S(2)}) collective-permute-start(bf16[512,768]{1,0:T(8,128)(2,1)S(1)} %get-tuple-element.70), channel_id=1, source_target_pairs={{0,8},{1,9},{2,10},{3,11},{4,12},{5,13},{6,14},{7,15},{8,0},{9,1},... | collective-permute-start | bytes 2359304 | tf_op jit(solution)/shard_map/ppermute | solution.py:151
  125.4 29.9 %collective-permute-start.23 = (bf16[512,768]{1,0:T(8,128)(2,1)S(1)}, bf16[512,768]{1,0:T(8,128)(2,1)S(1)}, u32[]{:S(2)}, u32[]{:S(2)}) collective-permute-start(bf16[512,768]{1,0:T(8,128)(2,1)S(1)} %get-tuple-element.71), channel_id=1, source_target_pairs={{0,16},{1,17},{2,18},{3,19},{4,20},{5,21},{6,22},{7,23},{8,24},{9,... | collective-permute-start | bytes 2359304 | tf_op jit(solution)/shard_map/ppermute | solution.py:151
  134.0 24.2 %collective-permute-start.12 = (bf16[64,2048]{1,0:T(8,128)(2,1)S(1)}, bf16[64,2048]{1,0:T(8,128)(2,1)S(1)}, u32[]{:S(2)}, u32[]{:S(2)}) collective-permute-start(bf16[64,2048]{1,0:T(8,128)(2,1)S(1)} %add_convert_fusion.12), channel_id=1, source_target_pairs={{0,4},{1,5},{2,0},{3,1},{4,6},{5,7},{6,2},{7,3},{8,12},{9,13},{10,... | collective-permute-start | bytes 786440 | tf_op jit(solution)/shard_map/ppermute | solution.py:151
  138.4 49.0 %collective-permute-start.29 = (bf16[256,768]{1,0:T(8,128)(2,1)S(1)}, bf16[256,768]{1,0:T(8,128)(2,1)S(1)}, u32[]{:S(2)}, u32[]{:S(2)}) collective-permute-start(bf16[256,768]{1,0:T(8,128)(2,1)S(1)} %add_convert_fusion), channel_id=1, source_target_pairs={{0,16},{1,17},{2,18},{3,19},{4,20},{5,21},{6,22},{7,23},{8,24},{9,... | collective-permute-start | bytes 1179656 | tf_op jit(solution)/shard_map/ppermute | solution.py:151
  140.0 47.4 %collective-permute-start.28 = (bf16[256,768]{1,0:T(8,128)(2,1)S(1)}, bf16[256,768]{1,0:T(8,128)(2,1)S(1)}, u32[]{:S(2)}, u32[]{:S(2)}) collective-permute-start(bf16[256,768]{1,0:T(8,128)(2,1)S(1)} %add_convert_fusion.1), channel_id=1, source_target_pairs={{0,8},{1,9},{2,10},{3,11},{4,12},{5,13},{6,14},{7,15},{8,0},{9,1},... | collective-permute-start | bytes 1179656 | tf_op jit(solution)/shard_map/ppermute | solution.py:151
  150.8 6.7 %collective-permute-start.17 = (bf16[64,2176]{1,0:T(8,128)(2,1)S(1)}, bf16[64,2176]{1,0:T(8,128)(2,1)S(1)}, u32[]{:S(2)}, u32[]{:S(2)}) collective-permute-start(bf16[64,2176]{1,0:T(8,128)(2,1)S(1)} %add_convert_fusion.9), channel_id=1, source_target_pairs={{0,4},{1,5},{2,0},{3,1},{4,6},{5,7},{6,2},{7,3},{8,12},{9,13},{10,... | collective-permute-start | bytes 835592 | tf_op jit(solution)/shard_map/ppermute | solution.py:151
  155.3 30.3 %collective-permute-start.25 = (bf16[256,768]{1,0:T(8,128)(2,1)S(1)}, bf16[256,768]{1,0:T(8,128)(2,1)S(1)}, u32[]{:S(2)}, u32[]{:S(2)}) collective-permute-start(bf16[256,768]{1,0:T(8,128)(2,1)S(1)} %add_convert_fusion.2), channel_id=1, source_target_pairs={{0,16},{1,17},{2,18},{3,19},{4,20},{5,21},{6,22},{7,23},{8,24},{9,... | collective-permute-start | bytes 1179656 | tf_op jit(solution)/shard_map/ppermute | solution.py:151
  157.5 28.1 %collective-permute-start.24 = (bf16[256,768]{1,0:T(8,128)(2,1)S(1)}, bf16[256,768]{1,0:T(8,128)(2,1)S(1)}, u32[]{:S(2)}, u32[]{:S(2)}) collective-permute-start(bf16[256,768]{1,0:T(8,128)(2,1)S(1)} %add_convert_fusion.3), channel_id=1, source_target_pairs={{0,8},{1,9},{2,10},{3,11},{4,12},{5,13},{6,14},{7,15},{8,0},{9,1},... | collective-permute-start | bytes 1179656 | tf_op jit(solution)/shard_map/ppermute | solution.py:151
  158.1 8.8 %collective-permute-start.18 = (bf16[64,2176]{1,0:T(8,128)(2,1)S(1)}, bf16[64,2176]{1,0:T(8,128)(2,1)S(1)}, u32[]{:S(2)}, u32[]{:S(2)}) collective-permute-start(bf16[64,2176]{1,0:T(8,128)(2,1)S(1)} %add_convert_fusion.8), channel_id=1, source_target_pairs={{0,4},{1,5},{2,0},{3,1},{4,6},{5,7},{6,2},{7,3},{8,12},{9,13},{10,... | collective-permute-start | bytes 835592 | tf_op jit(solution)/shard_map/ppermute | solution.py:151
  166.9 10.5 %collective-permute-start.13 = (bf16[64,2048]{1,0:T(8,128)(2,1)S(1)}, bf16[64,2048]{1,0:T(8,128)(2,1)S(1)}, u32[]{:S(2)}, u32[]{:S(2)}) collective-permute-start(bf16[64,2048]{1,0:T(8,128)(2,1)S(1)} %add_convert_fusion.11), channel_id=1, source_target_pairs={{0,4},{1,5},{2,0},{3,1},{4,6},{5,7},{6,2},{7,3},{8,12},{9,13},{10,... | collective-permute-start | bytes 786440 | tf_op jit(solution)/shard_map/ppermute | solution.py:151
  177.4 7.2 %collective-permute-start.19 = (bf16[64,2176]{1,0:T(8,128)(2,1)S(1)}, bf16[64,2176]{1,0:T(8,128)(2,1)S(1)}, u32[]{:S(2)}, u32[]{:S(2)}) collective-permute-start(bf16[64,2176]{1,0:T(8,128)(2,1)S(1)} %add_convert_fusion.7), channel_id=1, source_target_pairs={{0,4},{1,5},{2,0},{3,1},{4,6},{5,7},{6,2},{7,3},{8,12},{9,13},{10,... | collective-permute-start | bytes 835592 | tf_op jit(solution)/shard_map/ppermute | solution.py:151

commit v3 on v2

--- a/solution.py
+++ b/solution.py
@@ -208,28 +208,29 @@
     )(tokens, cotangent, expert_ids.T, gate_probs.T)
 
 
-def unpack_kernel(mixed_ref, back_ref, ids_ref, mixed_out, back_out, prob_out):
-    rows, width = mixed_ref.shape
+def unpack_kernel(sums_ref, ids_ref, mixed_out, back_out, prob_out):
+    rows, width = mixed_out.shape
     block = width // 4
     for r in range(4):
         there = block_at(r, block)
-        mixed_out[:, there] = mixed_ref[:, r * block : (r + 1) * block]
-        back_out[:, there] = back_ref[:, r * block : (r + 1) * block]
+        mixed_out[:, there] = sums_ref[:, r * block : (r + 1) * block]
+        back_out[:, there] = sums_ref[:, width + r * block : width + (r + 1) * block]
     lane = iota(8, SIDE, 1)
     adder = ((lane < 24) & (lane % 8 == iota(8, SIDE, 0))).astype(BF16)
-    by_expert = lax.dot_general(adder, back_ref[:, width:], ACROSS, preferred_element_type=F32)
+    by_expert = lax.dot_general(adder, sums_ref[:, 2 * width :], ACROSS, preferred_element_type=F32)
     for k in range(ids_ref.shape[0]):
         hit = iota(8, rows, 0) == ids_ref[k : k + 1, :]
         prob_out[k : k + 1, :] = jnp.sum(jnp.where(hit, by_expert, 0.0), axis=0, keepdims=True)
 
 
-def unpack(mixed, back, expert_ids):
+def unpack(sums, expert_ids, width):
+    own = shape(sums.shape[0], width, BF16)
     mixed, back, prob = kernel_call(
         unpack_kernel,
-        (shape(*mixed.shape, BF16), shape(*mixed.shape, BF16), shape(*expert_ids.T.shape, F32)),
-        in_specs=[VMEM] * 3,
+        (own, own, shape(*expert_ids.T.shape, F32)),
+        in_specs=[VMEM] * 2,
         out_specs=(VMEM,) * 3,
-    )(mixed, back, expert_ids.T)
+    )(sums, expert_ids.T)
     return mixed, back, prob.T
 
 
@@ -266,17 +267,14 @@
     out_ref[half:] = times_pieces(other_rows, (own_ref, x_ref, y_ref))
 
 
-def early_products(whole, direct, width):
+def early_products(whole, direct, width, which, start, columns):
     half = whole[0].shape[0]
-    depth, columns = direct[0].shape
-    steps = columns // TILE
-    piece = pl.BlockSpec((depth, TILE), lambda j: (0, j))
+    piece = pl.BlockSpec((direct[0].shape[0], TILE), lambda j: (0, start // TILE + j))
     return kernel_call(
         early_kernel,
         shape(2 * half, columns, F32),
-        grid=(steps,),
-        in_specs=[pl.BlockSpec((half, width), lambda j: (0, j // (steps * 2 // 3)))] * 2
-        + [piece] * 3,
+        grid=(columns // TILE,),
+        in_specs=[pl.BlockSpec((half, width), lambda j: (0, which))] * 2 + [piece] * 3,
         out_specs=pl.BlockSpec((2 * half, TILE), lambda j: (0, j)),
     )(*whole, *direct)
 
@@ -356,7 +354,7 @@
         (shape(rows, units, BF16),) * 2 + (shape(rows, SIDE, BF16),),
         grid=(steps,),
         in_specs=[pl.BlockSpec((rows // 2, block), lambda j: (0, 7))] * 2
-        + [pl.BlockSpec((rows, TILE), lambda j: (0, 2 * steps + j))]
+        + [tile]
         + [pl.BlockSpec((block // 2, TILE), lambda j: (0, j))] * 2
         + [tile] * 3,
         out_specs=(tile, tile, pl.BlockSpec((rows, SIDE), lambda j: (0, 0))),
@@ -441,50 +439,41 @@
     )(turned, term)
 
 
-def back_kernel(count, *refs):
-    terms, weights, rest = refs[:count], refs[count : count + 5], refs[count + 5 :]
-    out_ref = rest[-1]
-    units = terms[0].shape[1]
+def back_kernel(scaled_ref, d_gate_ref, d_up_ref, dots_ref, *refs):
+    downs, gate_ups, out_ref = refs[:5], refs[5:10], refs[10]
+    units = scaled_ref.shape[1]
+    width = (out_ref.shape[1] - SIDE) // 2
+
+    def product(term, weight):
+        return lax.dot_general(term[...], weight, ACROSS, preferred_element_type=F32)
+
     start = 0
-    for weight in weights:
-        depth = weight.shape[0]
-        total = None
-        for index, term in enumerate(terms):
-            part = lax.dot_general(
-                term[...],
-                weight[:, index * units : (index + 1) * units],
-                ACROSS,
-                preferred_element_type=F32,
-            )
-            total = part if total is None else total + part
-        out_ref[:, start : start + depth] = total.astype(BF16)
+    for down, gate_up in zip(downs, gate_ups):
+        depth = down.shape[0]
+        out_ref[:, start : start + depth] = product(scaled_ref, down[...]).astype(BF16)
+        total = product(d_gate_ref, gate_up[:, :units]) + product(d_up_ref, gate_up[:, units:])
+        out_ref[:, width + start : width + start + depth] = total.astype(BF16)
         start += depth
-    if len(rest) == 2:
-        out_ref[:, start:] = rest[0][...]
-
-
-def whole_rows(piece, start, across):
-    return pl.BlockSpec((piece.shape[0], across), lambda i: (0, start // across))
-
-
-def back_to_rows(terms, direct, start, corner, extra):
-    rows, units = terms[0].shape
-    across = units * len(terms)
-    pieces = [(piece, start) for piece in direct] + [(piece, 0) for piece in corner]
-    width = sum(piece.shape[0] for piece, _ in pieces) + sum(e.shape[1] for e in extra)
-
-    def body(*refs):
-        back_kernel(len(terms), *refs)
-
-    return kernel_call(
-        body,
-        shape(rows, width, BF16),
+    out_ref[:, 2 * width :] = dots_ref[...]
+
+
+def back_to_rows(scaled, d_gate, d_up, dots, direct, down, gate_up, width):
+    rows, units = scaled.shape
+    depth = direct[0].shape[0]
+    term = pl.BlockSpec((TILE, units), lambda i: (i, 0))
+    corner = [pl.BlockSpec((depth // 2, n * units), lambda i: (0, 0)) for n in (1, 1, 2, 2)]
+    return kernel_call(
+        back_kernel,
+        shape(rows, 2 * width + SIDE, BF16),
         grid=(rows // TILE,),
-        in_specs=[pl.BlockSpec((TILE, units), lambda i: (i, 0)) for _ in terms]
-        + [whole_rows(piece, first, across) for piece, first in pieces]
-        + [pl.BlockSpec((TILE, e.shape[1]), lambda i: (i, 0)) for e in extra],
-        out_specs=pl.BlockSpec((TILE, width), lambda i: (i, 0)),
-    )(*terms, *[piece for piece, _ in pieces], *extra)
+        in_specs=[term] * 3
+        + [pl.BlockSpec((TILE, SIDE), lambda i: (i, 0))]
+        + [pl.BlockSpec((depth, units), lambda i: (0, 2))] * 3
+        + corner[:2]
+        + [pl.BlockSpec((depth, 2 * units), lambda i: (0, 0))] * 3
+        + corner[2:],
+        out_specs=pl.BlockSpec((TILE, 2 * width + SIDE), lambda i: (i, 0)),
+    )(scaled, d_gate, d_up, dots, *direct, *down, *direct, *gate_up)
 
 
 def total_kernel(own_ref, from_x, from_y, late_x, late_y, out_ref):
@@ -511,13 +500,9 @@
     )
 
 
-def gather_weights(shard, split):
-    half = shard.shape[0] // 2
-    from_x = send(shard, TO_X)
-    from_y = send(shard, TO_Y)
-    gate_up = [send(from_x[:half, :split], TO_Y), send(from_y[half:, :split], TO_X)]
-    down = [send(from_x[:half, split:], TO_Y), send(from_y[half:, split:], TO_X)]
-    return [shard, from_x, from_y], gate_up, down
+def send_corner(from_x, from_y, columns):
+    half = from_x.shape[0] // 2
+    return [send(from_x[:half, columns], TO_Y), send(from_y[half:, columns], TO_X)]
 
 
 def send_first(to_x, to_y):
@@ -531,26 +516,28 @@
     return late_x, late_y
 
 
-def gather_rows(own):
+def gather_rows(own, before):
     slots = [own]
     for _ in range(3):
         slots.append(send(slots[-1], ALONG_Z))
-    return jnp.concatenate(slots)
-
-
-def sum_over_experts(rows):
+    own_core = after(jnp.concatenate(slots), before)
+    return own_core, send(own_core, TO_CORE)
+
+
+def sum_over_experts(rows, before):
     half = rows.shape[0] // 2
     block = half // 4
-    arrived = send(rows[half:], TO_CORE)
+    arrived = send(after(rows[half:], before), TO_CORE)
 
     def both_cores(slot):
         at = slice(slot * block, (slot + 1) * block)
         return rows[at].astype(F32) + arrived[at].astype(F32)
 
-    moving = send(both_cores(1).astype(BF16), ALONG_Z)
-    for slot in (2, 3):
-        moving = send((both_cores(slot) + moving.astype(F32)).astype(BF16), ALONG_Z)
-    return (both_cores(0) + moving.astype(F32)).astype(BF16)
+    steps = [both_cores(1).astype(BF16)]
+    for slot in (2, 3, 0):
+        moving = send(steps[-1], ALONG_Z)
+        steps.append((both_cores(slot) + moving.astype(F32)).astype(BF16))
+    return steps
 
 
 def after(arrays, *others):
@@ -561,40 +548,49 @@
     width = tokens.shape[1]
     units = gate_proj.shape[2]
     halves = width // TILE
+
     shard = jnp.concatenate([gate_proj[0], up_proj[0], down_proj[0]], axis=1)
-    direct, gate_up, down = gather_weights(shard, 2 * units)
-    packed = pack(tokens, cotangent, expert_ids, gate_probs)
-    own_core = gather_rows(packed)
-    own_core = after(own_core, direct)
-    whole = (own_core, send(own_core, TO_CORE))
-    early = early_products(whole, direct, width)
+    direct = [shard, send(shard, TO_X), send(shard, TO_Y)]
+    whole = gather_rows(pack(tokens, cotangent, expert_ids, gate_probs), direct)
+    gate_up_corner = send_corner(*direct[1:], slice(0, 2 * units))
+    down_corner = send_corner(*direct[1:], slice(2 * units, 3 * units))
+    early_gate_up = early_products(whole, direct, width, 0, 0, 2 * units)
     turned = turn(whole, 2 * width)
-    early, turned, gate_up = lax.optimization_barrier((early, turned, gate_up))
-
-    scaled, for_gate, for_up, hidden = forward(whole, early, gate_up, width, units)
-    down_first = send_first(*(sent := first_grads(turned, halves, width, scaled)))
-    scaled, down = after((scaled, down), sent)
-    mixed = sum_over_experts(back_to_rows([scaled], direct, 2 * units, down, []))
-    for_x, for_y, down_own = later_grads(turned, halves, width, scaled)
-    hidden = after(hidden, for_x)
-    d_gate, d_up, dots = backward(whole, early, down, for_gate, for_up, hidden, width)
-    down_late = send_later(for_x, for_y, *down_first)
-    d_gate, d_up = after((d_gate, d_up), down_first)
+    early_down = early_products(whole, direct, width, 1, 2 * units, units)
+    early_gate_up, early_down, turned, gate_up_corner = lax.optimization_barrier(
+        (early_gate_up, early_down, turned, gate_up_corner)
+    )
+
+    scaled, for_gate, for_up, hidden = forward(whole, early_gate_up, gate_up_corner, width, units)
+    down_sent = first_grads(turned, halves, width, scaled)
+    down_first = send_first(*after(down_sent, down_corner))
+    scaled, whole, hidden = after((scaled, whole, hidden), down_sent)
+    *down_later, down_own = later_grads(turned, halves, width, scaled)
+    hidden = after(hidden, down_own)
+    d_gate, d_up, dots = backward(
+        whole, early_down, down_corner, for_gate, for_up, hidden, width
+    )
     gate_sent = first_grads(turned, 0, width, d_gate)
+    gate_first = send_first(*gate_sent)
+    d_gate, d_up = after((d_gate, d_up), gate_sent)
     up_sent = first_grads(turned, 0, width, d_up)
-    gate_first, up_first = send_first(*gate_sent), send_first(*up_sent)
-    d_gate, d_up = after((d_gate, d_up), gate_sent, up_sent)
-    back = sum_over_experts(back_to_rows([d_gate, d_up], direct, 0, gate_up, [dots]))
-    grad_down = total(down_own, *down_first, *down_late)
-    d_gate, d_up = after((d_gate, d_up), grad_down)
+    shares = back_to_rows(scaled, d_gate, d_up, dots, direct, down_corner, gate_up_corner, width)
+    steps = sum_over_experts(shares, down_first)
+    d_gate, d_up = after((d_gate, d_up), shares)
     *gate_later, gate_own = later_grads(turned, 0, width, d_gate)
     *up_later, up_own = later_grads(turned, 0, width, d_up)
+
+    up_first = send_first(*after(up_sent, down_first))
+    down_later = after(down_later, gate_first, steps[0])
+    down_late = send_later(*down_later, *down_first)
+    gate_later = after(gate_later, up_first, steps[1])
     gate_late = send_later(*gate_later, *gate_first)
+    grad_down = total(down_own, *down_first, *down_late)
+    up_later = after(up_later, grad_down, steps[2])
     up_late = send_later(*up_later, *up_first)
-    outs = unpack(mixed, back, expert_ids)
-    gate_late = after(gate_late, outs)
+    outs = unpack(steps[3], expert_ids, width)
     grad_gate = total(gate_own, *gate_first, *gate_late)
-    up_late = after(up_late, grad_gate)
+    up_late = after(up_late, grad_gate, outs)
     grad_up = total(up_own, *up_first, *up_late)
     return (*outs, grad_gate, grad_up, grad_down)
 

time: 190 us -> 177 us (0.932)
  starting transfers between devices: 46.2 us -> 34.5 us
    ppermute x30 -> x26, starting transfers between devices: 46.2 us -> 34.5 us  [send(): return lax.ppermute(array, AXES, where)]
    ppermute x30 -> x26, waiting for transfers between devices: 101 us -> 101 us  [send(): return lax.ppermute(array, AXES, where)]
  transfers between devices with their start and end apart: 30 -> 26, of which waited for: 19 -> 20; matrix products, arithmetic and copies ran while one was open for 1% -> 1% of each run, Pallas kernels for 19% -> 20%
where the time goes in v3:
time: 177 us
  waiting for transfers between devices  101 us (57%)
  Pallas kernels  36.7 us (21%)
  starting transfers between devices  34.5 us (19%)
  other arithmetic  3.09 us (2%)
    ppermute x26, waiting for transfers between devices, send(): return lax.ppermute(array, AXES, where)  101 us
    ppermute x26, starting transfers between devices, send(): return lax.ppermute(array, AXES, where)  34.5 us
    pallas_call x2, Pallas kernels, early_products(): kernel_call(early_kernel, shape(2 * half, columns, F32), grid=(columns //...  6.32 us
    pallas_call x1, Pallas kernels, back_to_rows(): kernel_call(back_kernel, shape(rows, 2 * width + SIDE, BF16), grid=(rows...  5.81 us
    pallas_call x3, Pallas kernels, total(): kernel_call(total_kernel, jax.ShapeDtypeStruct(halves, F32), grid=(half /...  5.52 us
    pallas_call x3, Pallas kernels, later_grads(): kernel_call(later_grad_kernel, (shape(half, units, F32),) * 2 + (shape(2...  5.1 us
    pallas_call x3, Pallas kernels, first_grads(): kernel_call(first_grad_kernel, (shape(2 * half, units, BF16),) * 2, grid=...  4.99 us
  transfers between devices with their start and end apart: 26, of which 20 were waited for; matrix products, arithmetic and copies ran while one was open for 1% of the time, Pallas kernels for 20%

profile of v3, /device:TPU:0, one launch (start us, length us, event | category | flops | bytes accessed | tf_op | source)
XLA Modules:
  0.0 176.7 jit_solution(10282078798365768301)
XLA Ops:
  0.7 1.8 %pad_maximum_fusion.own_ref.refs_0_.refs_5_ = bf16[512,2304]{1,0:T(8,128)(2,1)S(1)} fusion(bf16[512,768]{1,0:T(8,128)(2,1)} %bitcast.33, bf16[512,768]{1,0:T(8,128)(2,1)} %bitcast.34, bf16[512,768]{1,0:T(8,128)(2,1)} %bitcast.35), kind=kLoop, calls=%fused_computation | loop fusion | flops 7077888 | bytes 4718592 | tf_op jit(solution)/shard_map/concatenate | solution.py:552
  2.5 3.0 %collective-permute-start.4 = (bf16[512,2304]{1,0:T(8,128)(2,1)S(1)}, bf16[512,2304]{1,0:T(8,128)(2,1)S(1)}, u32[]{:S(2)}, u32[]{:S(2)}) collective-permute-start(bf16[512,2304]{1,0:T(8,128)(2,1)S(1)} %pad_maximum_fusion.own_ref.refs_0_.refs_5_), channel_id=1, source_target_pairs={{0,16},{1,17},{2,18},{3,19},{4,20},{5,21},{6,22},{7,23},{8,24},{9,... | collective-permute-start | bytes 7077896 | tf_op jit(solution)/shard_map/ppermute | solution.py:151
  5.5 1.5 collective-permute-start.3
  7.2 2.6 %collective-permute-start = (bf16[64,4224]{1,0:T(8,128)(2,1)S(1)}, bf16[64,4224]{1,0:T(8,128)(2,1)S(1)}, u32[]{:S(2)}, u32[]{:S(2)}) collective-permute-start(bf16[64,4224]{1,0:T(8,128)(2,1)S(1)} %shard_map.118), channel_id=1, source_target_pairs={{0,4},{1,5},{2,0},{3,1},{4,6},{5,7},{6,2},{7,3},{8,12},{9,13},{10,... | collective-permute-start | bytes 1622024 | tf_op jit(solution)/shard_map/ppermute | solution.py:151
  9.8 11.0 %collective-permute-done = bf16[64,4224]{1,0:T(8,128)(2,1)S(1)} collective-permute-done((bf16[64,4224]{1,0:T(8,128)(2,1)S(1)}, bf16[64,4224]{1,0:T(8,128)(2,1)S(1)}, u32[]{:S(2)}, u32[]{:S(2)}) %collective-permute-start) | collective-permute-done | bytes 540704 | tf_op jit(solution)/shard_map/ppermute | solution.py:151
  20.7 3.4 %collective-permute-start.1 = (bf16[64,4224]{1,0:T(8,128)(2,1)S(1)}, bf16[64,4224]{1,0:T(8,128)(2,1)S(1)}, u32[]{:S(2)}, u32[]{:S(2)}) collective-permute-start(bf16[64,4224]{1,0:T(8,128)(2,1)S(1)} %collective-permute-done), channel_id=1, source_target_pairs={{0,4},{1,5},{2,0},{3,1},{4,6},{5,7},{6,2},{7,3},{8,12},{9,13},{10,... | collective-permute-start | bytes 1622024 | tf_op jit(solution)/shard_map/ppermute | solution.py:151
  24.1 10.0 %collective-permute-done.1 = bf16[64,4224]{1,0:T(8,128)(2,1)S(1)} collective-permute-done((bf16[64,4224]{1,0:T(8,128)(2,1)S(1)}, bf16[64,4224]{1,0:T(8,128)(2,1)S(1)}, u32[]{:S(2)}, u32[]{:S(2)}) %collective-permute-start.1) | collective-permute-done | bytes 540704 | tf_op jit(solution)/shard_map/ppermute | solution.py:151
  34.2 3.4 %collective-permute-start.2 = (bf16[64,4224]{1,0:T(8,128)(2,1)S(1)}, bf16[64,4224]{1,0:T(8,128)(2,1)S(1)}, u32[]{:S(2)}, u32[]{:S(2)}) collective-permute-start(bf16[64,4224]{1,0:T(8,128)(2,1)S(1)} %collective-permute-done.1), channel_id=1, source_target_pairs={{0,4},{1,5},{2,0},{3,1},{4,6},{5,7},{6,2},{7,3},{8,12},{9,13},{10,... | collective-permute-start | bytes 1622024 | tf_op jit(solution)/shard_map/ppermute | solution.py:151
  37.5 9.1 %collective-permute-done.2 = bf16[64,4224]{1,0:T(8,128)(2,1)S(1)} collective-permute-done((bf16[64,4224]{1,0:T(8,128)(2,1)S(1)}, bf16[64,4224]{1,0:T(8,128)(2,1)S(1)}, u32[]{:S(2)}, u32[]{:S(2)}) %collective-permute-start.2) | collective-permute-done | bytes 540704 | tf_op jit(solution)/shard_map/ppermute | solution.py:151
  46.8 9.9 %collective-permute-done.4.y_ref.refs_2_.refs_7_ = bf16[512,2304]{1,0:T(8,128)(2,1)S(1)} collective-permute-done((bf16[512,2304]{1,0:T(8,128)(2,1)S(1)}, bf16[512,2304]{1,0:T(8,128)(2,1)S(1)}, u32[]{:S(2)}, u32[]{:S(2)}) %collective-permute-start.4) | collective-permute-done | bytes 2359328 | tf_op jit(solution)/shard_map/ppermute | solution.py:151
  56.8 1.5 collective-permute-done.3.x_ref.refs_1_.refs_6_
  58.3 1.6 collective-permute-start.7
  61.0 1.7 collective-permute-start.8
  62.7 2.1 %shard_map.120.early_ref = f32[512,768]{1,0:T(8,128)S(1)} custom-call(bf16[256,4224]{1,0:T(8,128)(2,1)S(1)} %pad_maximum_fusion.1.own_rows.own_ref.refs_0_.refs_2_, bf16[256,4224]{1,0:T(8,128)(2,1)S(1)} %collective-permute-done.5.other_rows.other_ref.refs_1_.refs_3_, bf16[512,2304]{1,0:T(8,128)(2,1)S(1)} %pad_maximum_fusion.own_ref.refs_0_.refs_5_, ...), custom_call_target="tpu_custom_call" | custom-call | tf_op jit(solution)/shard_map/pallas_call | solution.py:273
  64.9 4.2 %shard_map.119.refs_4_.refs_5_ = f32[512,1536]{1,0:T(8,128)S(1)} custom-call(bf16[256,4224]{1,0:T(8,128)(2,1)S(1)} %pad_maximum_fusion.1.own_rows.own_ref.refs_0_.refs_2_, bf16[256,4224]{1,0:T(8,128)(2,1)S(1)} %collective-permute-done.5.other_rows.other_ref.refs_1_.refs_3_, bf16[512,2304]{1,0:T(8,128)(2,1)S(1)} %pad_maximum_fusion.own_ref.refs_0_.refs_5_, ...), custom_call_target="tpu_custom_call" | custom-call | tf_op jit(solution)/shard_map/pallas_call | solution.py:273
  69.1 3.2 %shard_map.121.turned_ref = bf16[4096,512]{1,0:T(8,128)(2,1)S(1)} custom-call(bf16[256,4224]{1,0:T(8,128)(2,1)S(1)} %pad_maximum_fusion.1.own_rows.own_ref.refs_0_.refs_2_, bf16[256,4224]{1,0:T(8,128)(2,1)S(1)} %collective-permute-done.5.other_rows.other_ref.refs_1_.refs_3_), custom_call_target="tpu_custom_call" | custom-call | tf_op jit(solution)/shard_map/pallas_call | solution.py:245
  72.3 6.4 %collective-permute-done.7.refs_7_.refs_9_ = bf16[256,1536]{1,0:T(8,128)(2,1)S(1)} collective-permute-done((bf16[256,1536]{1,0:T(8,128)(2,1)S(1)}, bf16[256,1536]{1,0:T(8,128)(2,1)S(1)}, u32[]{:S(2)}, u32[]{:S(2)}) %collective-permute-start.7) | collective-permute-done | bytes 786464 | tf_op jit(solution)/shard_map/ppermute | solution.py:151
  78.7 1.7 collective-permute-done.6.refs_6_.refs_8_
  80.3 2.6 %shard_map.122 = (bf16[512,768]{1,0:T(8,128)(2,1)S(1)}, f32[512,768]{1,0:T(8,128)S(1)}, f32[512,768]{1,0:T(8,128)S(1)}, f32[512,768]{1,0:T(8,128)S(1)}) custom-call(bf16[256,4224]{1,0:T(8,128)(2,1)S(1)} %pad_maximum_fusion.1.own_rows.own_ref.refs_0_.refs_2_, bf16[256,4224]{1,0:T(8,128)(2,1)S(1)} %collective-permute-done.5.other_rows.other_ref.refs_1_.refs_3_, ...), custom_call_target="tpu_custom_call" | custom-call | tf_op jit(solution)/shard_map/pallas_call | solution.py:311
  83.0 1.7 shard_map.123
  84.6 2.1 %collective-permute-done.9.last_ref.refs_4_ = bf16[256,768]{1,0:T(8,128)(2,1)S(1)} collective-permute-done((bf16[256,768]{1,0:T(8,128)(2,1)S(1)}, bf16[256,768]{1,0:T(8,128)(2,1)S(1)}, u32[]{:S(2)}, u32[]{:S(2)}) %collective-permute-start.9) | collective-permute-done | bytes 393248 | tf_op jit(solution)/shard_map/ppermute | solution.py:151
  86.7 1.3 collective-permute-done.8.first_ref.refs_3_
  89.0 1.7 shard_map.124
  90.7 2.2 %shard_map.125 = (bf16[512,768]{1,0:T(8,128)(2,1)S(1)}, bf16[512,768]{1,0:T(8,128)(2,1)S(1)}, bf16[512,128]{1,0:T(8,128)(2,1)S(1)}) custom-call(bf16[256,4224]{1,0:T(8,128)(2,1)S(1)} %pad_maximum_fusion.1.own_rows.own_ref.refs_0_.refs_2_, bf16[256,4224]{1,0:T(8,128)(2,1)S(1)} %collective-permute-done.5.other_rows.other_ref.refs_1_.refs_3_, ...), custom_call_target="tpu_custom_call" | custom-call | tf_op jit(solution)/shard_map/pallas_call | solution.py:352
  92.8 1.7 shard_map.126
  94.5 5.8 %shard_map.127 = bf16[512,4224]{1,0:T(8,128)(2,1)S(1)} custom-call(bf16[512,768]{1,0:T(8,128)(2,1)S(1)} %get-tuple-element.68.term_ref.scaled_ref, bf16[512,768]{1,0:T(8,128)(2,1)S(1)} %get-tuple-element.90.term_ref.d_gate_ref, bf16[512,768]{1,0:T(8,128)(2,1)S(1)} %get-tuple-element.100.d_up_ref.term_ref, bf16[512,128]{1,0:T(8,128)(2,1)S(1)} %get-tuple-element.83.dots_ref, ...), custom_call_target="tpu_custom_call" | custom-call | tf_op jit(solution)/shard_map/pallas_call | solution.py:465
  100.5 6.4 %collective-permute-done.10 = bf16[512,768]{1,0:T(8,128)(2,1)S(1)} collective-permute-done((bf16[512,768]{1,0:T(8,128)(2,1)S(1)}, bf16[512,768]{1,0:T(8,128)(2,1)S(1)}, u32[]{:S(2)}, u32[]{:S(2)}) %collective-permute-start.10) | collective-permute-done | bytes 786464 | tf_op jit(solution)/shard_map/ppermute | solution.py:151
  107.2 1.5 collective-permute-start.16
  109.2 2.3 %collective-permute-done.12 = bf16[256,4224]{1,0:T(8,128)(2,1)S(1)} collective-permute-done((bf16[256,4224]{1,0:T(8,128)(2,1)S(1)}, bf16[256,4224]{1,0:T(8,128)(2,1)S(1)}, u32[]{:S(2)}, u32[]{:S(2)}) %collective-permute-start.12) | collective-permute-done | bytes 2162720 | tf_op jit(solution)/shard_map/ppermute | solution.py:151
  111.6 2.6 %collective-permute-start.13 = (bf16[64,4224]{1,0:T(8,128)(2,1)S(1)}, bf16[64,4224]{1,0:T(8,128)(2,1)S(1)}, u32[]{:S(2)}, u32[]{:S(2)}) collective-permute-start(bf16[64,4224]{1,0:T(8,128)(2,1)S(1)} %add_convert_fusion.3), channel_id=1, source_target_pairs={{0,4},{1,5},{2,0},{3,1},{4,6},{5,7},{6,2},{7,3},{8,12},{9,13},{10,... | collective-permute-start | bytes 1622024 | tf_op jit(solution)/shard_map/ppermute | solution.py:151
  114.2 1.7 shard_map.130
  115.9 1.7 shard_map.129
  117.6 1.6 collective-permute-start.18
  119.7 7.9 %collective-permute-done.16 = bf16[512,768]{1,0:T(8,128)(2,1)S(1)} collective-permute-done((bf16[512,768]{1,0:T(8,128)(2,1)S(1)}, bf16[512,768]{1,0:T(8,128)(2,1)S(1)}, u32[]{:S(2)}, u32[]{:S(2)}) %collective-permute-start.16) | collective-permute-done | bytes 786464 | tf_op jit(solution)/shard_map/ppermute | solution.py:151
  127.5 1.5 collective-permute-done.17
  129.9 2.6 %collective-permute-start.14 = (bf16[64,4224]{1,0:T(8,128)(2,1)S(1)}, bf16[64,4224]{1,0:T(8,128)(2,1)S(1)}, u32[]{:S(2)}, u32[]{:S(2)}) collective-permute-start(bf16[64,4224]{1,0:T(8,128)(2,1)S(1)} %add_convert_fusion.2), channel_id=1, source_target_pairs={{0,4},{1,5},{2,0},{3,1},{4,6},{5,7},{6,2},{7,3},{8,12},{9,13},{10,... | collective-permute-start | bytes 1622024 | tf_op jit(solution)/shard_map/ppermute | solution.py:151
  132.6 0.6 collective-permute-start.22
  133.2 11.2 %collective-permute-done.18 = bf16[512,768]{1,0:T(8,128)(2,1)S(1)} collective-permute-done((bf16[512,768]{1,0:T(8,128)(2,1)S(1)}, bf16[512,768]{1,0:T(8,128)(2,1)S(1)}, u32[]{:S(2)}, u32[]{:S(2)}) %collective-permute-start.18) | collective-permute-done | bytes 786464 | tf_op jit(solution)/shard_map/ppermute | solution.py:151
  144.4 1.5 collective-permute-done.19
  147.4 2.7 %collective-permute-start.15 = (bf16[64,4224]{1,0:T(8,128)(2,1)S(1)}, bf16[64,4224]{1,0:T(8,128)(2,1)S(1)}, u32[]{:S(2)}, u32[]{:S(2)}) collective-permute-start(bf16[64,4224]{1,0:T(8,128)(2,1)S(1)} %add_convert_fusion.1), channel_id=1, source_target_pairs={{0,4},{1,5},{2,0},{3,1},{4,6},{5,7},{6,2},{7,3},{8,12},{9,13},{10,... | collective-permute-start | bytes 1622024 | tf_op jit(solution)/shard_map/ppermute | solution.py:151
  150.1 1.7 shard_map.132
  151.8 2.6 %collective-permute-done.23.late_y = bf16[256,768]{1,0:T(8,128)(2,1)S(1)} collective-permute-done((bf16[256,768]{1,0:T(8,128)(2,1)S(1)}, bf16[256,768]{1,0:T(8,128)(2,1)S(1)}, u32[]{:S(2)}, u32[]{:S(2)}) %collective-permute-start.23) | collective-permute-done | bytes 393248 | tf_op jit(solution)/shard_map/ppermute | solution.py:151
  154.3 1.8 %shard_map.133 = f32[2,256,768]{2,1,0:T(8,128)} custom-call(f32[2,256,768]{2,1,0:T(8,128)S(1)} %bitcast.24, bf16[2,256,768]{2,1,0:T(8,128)(2,1)S(1)} %bitcast.18, bf16[2,256,768]{2,1,0:T(8,128)(2,1)S(1)} %bitcast.19, bf16[256,768]{1,0:T(8,128)(2,1)S(1)} %collective-permute-done.22.late_x, bf16[256,768]{1,0:T(8,128)(2,1)S(1)} %collective-permute-done.23.late_y), custom_call_target="tpu_custom_call" | custom-call | tf_op jit(solution)/shard_map/pallas_call | solution.py:492
  156.2 5.9 %collective-permute-done.21.late_y = bf16[256,768]{1,0:T(8,128)(2,1)S(1)} collective-permute-done((bf16[256,768]{1,0:T(8,128)(2,1)S(1)}, bf16[256,768]{1,0:T(8,128)(2,1)S(1)}, u32[]{:S(2)}, u32[]{:S(2)}) %collective-permute-start.21) | collective-permute-done | bytes 393248 | tf_op jit(solution)/shard_map/ppermute | solution.py:151
  162.1 1.8 %shard_map.131 = f32[2,256,768]{2,1,0:T(8,128)} custom-call(f32[2,256,768]{2,1,0:T(8,128)S(1)} %bitcast.25, bf16[2,256,768]{2,1,0:T(8,128)(2,1)S(1)} %bitcast.22, bf16[2,256,768]{2,1,0:T(8,128)(2,1)S(1)} %bitcast.23, bf16[256,768]{1,0:T(8,128)(2,1)S(1)} %collective-permute-done.20.late_x, bf16[256,768]{1,0:T(8,128)(2,1)S(1)} %collective-permute-done.21.late_y), custom_call_target="tpu_custom_call" | custom-call | tf_op jit(solution)/shard_map/pallas_call | solution.py:492
  165.4 0.8 shard_map.128
  166.2 8.3 %collective-permute-done.25.late_y = bf16[256,768]{1,0:T(8,128)(2,1)S(1)} collective-permute-done((bf16[256,768]{1,0:T(8,128)(2,1)S(1)}, bf16[256,768]{1,0:T(8,128)(2,1)S(1)}, u32[]{:S(2)}, u32[]{:S(2)}) %collective-permute-start.25) | collective-permute-done | bytes 393248 | tf_op jit(solution)/shard_map/ppermute | solution.py:151
  174.8 1.8 %shard_map.134 = f32[2,256,768]{2,1,0:T(8,128)} custom-call(f32[2,256,768]{2,1,0:T(8,128)S(1)} %bitcast.26, bf16[2,256,768]{2,1,0:T(8,128)(2,1)S(1)} %bitcast.20, bf16[2,256,768]{2,1,0:T(8,128)(2,1)S(1)} %bitcast.21, bf16[256,768]{1,0:T(8,128)(2,1)S(1)} %collective-permute-done.24.late_x, bf16[256,768]{1,0:T(8,128)(2,1)S(1)} %collective-permute-done.25.late_y), custom_call_target="tpu_custom_call" | custom-call | tf_op jit(solution)/shard_map/pallas_call | solution.py:492
  (46 shorter events, 8.1 us)
Async XLA Ops:
  0.6 6.4 %copy-start = (bf16[64,2048]{1,0:T(8,128)(2,1)S(1)}, bf16[64,2048]{1,0:T(8,128)(2,1)}, u32[]{:S(2)}) copy-start(bf16[64,2048]{1,0:T(8,128)(2,1)} %tokens_ref.1) | copy-start | bytes 786436
  0.6 6.4 %copy-start.1 = (bf16[64,2048]{1,0:T(8,128)(2,1)S(1)}, bf16[64,2048]{1,0:T(8,128)(2,1)}, u32[]{:S(2)}) copy-start(bf16[64,2048]{1,0:T(8,128)(2,1)} %cot_ref.1) | copy-start | bytes 786436
  0.7 6.4 %copy-start.2 = (s32[64,6]{0,1:T(8,128)S(1)}, s32[64,6]{0,1:T(8,128)}, u32[]{:S(2)}) copy-start(s32[64,6]{0,1:T(8,128)} %param.8) | copy-start | bytes 4612
  0.7 6.4 %copy-start.3 = (f32[64,6]{0,1:T(8,128)S(1)}, f32[64,6]{0,1:T(8,128)}, u32[]{:S(2)}) copy-start(f32[64,6]{0,1:T(8,128)} %param.9) | copy-start | bytes 4612
  2.5 54.3 %collective-permute-start.4 = (bf16[512,2304]{1,0:T(8,128)(2,1)S(1)}, bf16[512,2304]{1,0:T(8,128)(2,1)S(1)}, u32[]{:S(2)}, u32[]{:S(2)}) collective-permute-start(bf16[512,2304]{1,0:T(8,128)(2,1)S(1)} %pad_maximum_fusion.own_ref.refs_0_.refs_5_), channel_id=1, source_target_pairs={{0,16},{1,17},{2,18},{3,19},{4,20},{5,21},{6,22},{7,23},{8,24},{9,... | collective-permute-start | bytes 7077896 | tf_op jit(solution)/shard_map/ppermute | solution.py:151
  5.5 52.7 %collective-permute-start.3 = (bf16[512,2304]{1,0:T(8,128)(2,1)S(1)}, bf16[512,2304]{1,0:T(8,128)(2,1)S(1)}, u32[]{:S(2)}, u32[]{:S(2)}) collective-permute-start(bf16[512,2304]{1,0:T(8,128)(2,1)S(1)} %pad_maximum_fusion.own_ref.refs_0_.refs_5_), channel_id=1, source_target_pairs={{0,8},{1,9},{2,10},{3,11},{4,12},{5,13},{6,14},{7,15},{8,0},{9,1},... | collective-permute-start | bytes 7077896 | tf_op jit(solution)/shard_map/ppermute | solution.py:151
  7.2 13.6 %collective-permute-start = (bf16[64,4224]{1,0:T(8,128)(2,1)S(1)}, bf16[64,4224]{1,0:T(8,128)(2,1)S(1)}, u32[]{:S(2)}, u32[]{:S(2)}) collective-permute-start(bf16[64,4224]{1,0:T(8,128)(2,1)S(1)} %shard_map.118), channel_id=1, source_target_pairs={{0,4},{1,5},{2,0},{3,1},{4,6},{5,7},{6,2},{7,3},{8,12},{9,13},{10,... | collective-permute-start | bytes 1622024 | tf_op jit(solution)/shard_map/ppermute | solution.py:151
  20.7 13.4 %collective-permute-start.1 = (bf16[64,4224]{1,0:T(8,128)(2,1)S(1)}, bf16[64,4224]{1,0:T(8,128)(2,1)S(1)}, u32[]{:S(2)}, u32[]{:S(2)}) collective-permute-start(bf16[64,4224]{1,0:T(8,128)(2,1)S(1)} %collective-permute-done), channel_id=1, source_target_pairs={{0,4},{1,5},{2,0},{3,1},{4,6},{5,7},{6,2},{7,3},{8,12},{9,13},{10,... | collective-permute-start | bytes 1622024 | tf_op jit(solution)/shard_map/ppermute | solution.py:151
  34.2 12.5 %collective-permute-start.2 = (bf16[64,4224]{1,0:T(8,128)(2,1)S(1)}, bf16[64,4224]{1,0:T(8,128)(2,1)S(1)}, u32[]{:S(2)}, u32[]{:S(2)}) collective-permute-start(bf16[64,4224]{1,0:T(8,128)(2,1)S(1)} %collective-permute-done.1), channel_id=1, source_target_pairs={{0,4},{1,5},{2,0},{3,1},{4,6},{5,7},{6,2},{7,3},{8,12},{9,13},{10,... | collective-permute-start | bytes 1622024 | tf_op jit(solution)/shard_map/ppermute | solution.py:151
  58.2 4.5 %collective-permute-start.5 = (bf16[256,4224]{1,0:T(8,128)(2,1)S(1)}, bf16[256,4224]{1,0:T(8,128)(2,1)S(1)}, u32[]{:S(2)}, u32[]{:S(2)}) collective-permute-start(bf16[256,4224]{1,0:T(8,128)(2,1)S(1)} %pad_maximum_fusion.1.own_rows.own_ref.refs_0_.refs_2_), channel_id=1, source_target_pairs={{0,1},{1,0},{2,3},{3,2},{4,5},{5,4},{6,7},{7,6},{8,9},{9,8},{10,11... | collective-permute-start | bytes 6488072 | tf_op jit(solution)/shard_map/ppermute | solution.py:151
  58.3 20.4 %collective-permute-start.7 = (bf16[256,1536]{1,0:T(8,128)(2,1)S(1)}, bf16[256,1536]{1,0:T(8,128)(2,1)S(1)}, u32[]{:S(2)}, u32[]{:S(2)}) collective-permute-start(bf16[256,1536]{1,0:T(8,128)(2,1)S(1)} %slice.77), channel_id=1, source_target_pairs={{0,8},{1,9},{2,10},{3,11},{4,12},{5,13},{6,14},{7,15},{8,0},{9,1},... | collective-permute-start | bytes 2359304 | tf_op jit(solution)/shard_map/ppermute | solution.py:151
  59.9 20.4 %collective-permute-start.6 = (bf16[256,1536]{1,0:T(8,128)(2,1)S(1)}, bf16[256,1536]{1,0:T(8,128)(2,1)S(1)}, u32[]{:S(2)}, u32[]{:S(2)}) collective-permute-start(bf16[256,1536]{1,0:T(8,128)(2,1)S(1)} %slice.76), channel_id=1, source_target_pairs={{0,16},{1,17},{2,18},{3,19},{4,20},{5,21},{6,22},{7,23},{8,24},{9,... | collective-permute-start | bytes 2359304 | tf_op jit(solution)/shard_map/ppermute | solution.py:151
  60.5 26.2 %collective-permute-start.9 = (bf16[256,768]{1,0:T(8,128)(2,1)S(1)}, bf16[256,768]{1,0:T(8,128)(2,1)S(1)}, u32[]{:S(2)}, u32[]{:S(2)}) collective-permute-start(bf16[256,768]{1,0:T(8,128)(2,1)S(1)} %slice.79), channel_id=1, source_target_pairs={{0,8},{1,9},{2,10},{3,11},{4,12},{5,13},{6,14},{7,15},{8,0},{9,1},... | collective-permute-start | bytes 1179656 | tf_op jit(solution)/shard_map/ppermute | solution.py:151
  61.0 27.1 %collective-permute-start.8 = (bf16[256,768]{1,0:T(8,128)(2,1)S(1)}, bf16[256,768]{1,0:T(8,128)(2,1)S(1)}, u32[]{:S(2)}, u32[]{:S(2)}) collective-permute-start(bf16[256,768]{1,0:T(8,128)(2,1)S(1)} %slice.78), channel_id=1, source_target_pairs={{0,16},{1,17},{2,18},{3,19},{4,20},{5,21},{6,22},{7,23},{8,24},{9,... | collective-permute-start | bytes 1179656 | tf_op jit(solution)/shard_map/ppermute | solution.py:151
  88.1 18.9 %collective-permute-start.10 = (bf16[512,768]{1,0:T(8,128)(2,1)S(1)}, bf16[512,768]{1,0:T(8,128)(2,1)S(1)}, u32[]{:S(2)}, u32[]{:S(2)}) collective-permute-start(bf16[512,768]{1,0:T(8,128)(2,1)S(1)} %get-tuple-element.84), channel_id=1, source_target_pairs={{0,8},{1,9},{2,10},{3,11},{4,12},{5,13},{6,14},{7,15},{8,0},{9,1},... | collective-permute-start | bytes 2359304 | tf_op jit(solution)/shard_map/ppermute | solution.py:151
  88.6 18.6 %collective-permute-start.11 = (bf16[512,768]{1,0:T(8,128)(2,1)S(1)}, bf16[512,768]{1,0:T(8,128)(2,1)S(1)}, u32[]{:S(2)}, u32[]{:S(2)}) collective-permute-start(bf16[512,768]{1,0:T(8,128)(2,1)S(1)} %get-tuple-element.85), channel_id=1, source_target_pairs={{0,16},{1,17},{2,18},{3,19},{4,20},{5,21},{6,22},{7,23},{8,24},{9,... | collective-permute-start | bytes 2359304 | tf_op jit(solution)/shard_map/ppermute | solution.py:151
  107.2 4.3 %collective-permute-start.12 = (bf16[256,4224]{1,0:T(8,128)(2,1)S(1)}, bf16[256,4224]{1,0:T(8,128)(2,1)S(1)}, u32[]{:S(2)}, u32[]{:S(2)}) collective-permute-start(bf16[256,4224]{1,0:T(8,128)(2,1)S(1)} %slice.81), channel_id=1, source_target_pairs={{0,1},{1,0},{2,3},{3,2},{4,5},{5,4},{6,7},{7,6},{8,9},{9,8},{10,11... | collective-permute-start | bytes 6488072 | tf_op jit(solution)/shard_map/ppermute | solution.py:151
  107.2 20.3 %collective-permute-start.16 = (bf16[512,768]{1,0:T(8,128)(2,1)S(1)}, bf16[512,768]{1,0:T(8,128)(2,1)S(1)}, u32[]{:S(2)}, u32[]{:S(2)}) collective-permute-start(bf16[512,768]{1,0:T(8,128)(2,1)S(1)} %get-tuple-element.79), channel_id=1, source_target_pairs={{0,8},{1,9},{2,10},{3,11},{4,12},{5,13},{6,14},{7,15},{8,0},{9,1},... | collective-permute-start | bytes 2359304 | tf_op jit(solution)/shard_map/ppermute | solution.py:151
  108.7 20.4 %collective-permute-start.17 = (bf16[512,768]{1,0:T(8,128)(2,1)S(1)}, bf16[512,768]{1,0:T(8,128)(2,1)S(1)}, u32[]{:S(2)}, u32[]{:S(2)}) collective-permute-start(bf16[512,768]{1,0:T(8,128)(2,1)S(1)} %get-tuple-element.80), channel_id=1, source_target_pairs={{0,16},{1,17},{2,18},{3,19},{4,20},{5,21},{6,22},{7,23},{8,24},{9,... | collective-permute-start | bytes 2359304 | tf_op jit(solution)/shard_map/ppermute | solution.py:151
  111.6 18.1 %collective-permute-start.13 = (bf16[64,4224]{1,0:T(8,128)(2,1)S(1)}, bf16[64,4224]{1,0:T(8,128)(2,1)S(1)}, u32[]{:S(2)}, u32[]{:S(2)}) collective-permute-start(bf16[64,4224]{1,0:T(8,128)(2,1)S(1)} %add_convert_fusion.3), channel_id=1, source_target_pairs={{0,4},{1,5},{2,0},{3,1},{4,6},{5,7},{6,2},{7,3},{8,12},{9,13},{10,... | collective-permute-start | bytes 1622024 | tf_op jit(solution)/shard_map/ppermute | solution.py:151
  117.6 26.8 %collective-permute-start.18 = (bf16[512,768]{1,0:T(8,128)(2,1)S(1)}, bf16[512,768]{1,0:T(8,128)(2,1)S(1)}, u32[]{:S(2)}, u32[]{:S(2)}) collective-permute-start(bf16[512,768]{1,0:T(8,128)(2,1)S(1)} %get-tuple-element.96), channel_id=1, source_target_pairs={{0,8},{1,9},{2,10},{3,11},{4,12},{5,13},{6,14},{7,15},{8,0},{9,1},... | collective-permute-start | bytes 2359304 | tf_op jit(solution)/shard_map/ppermute | solution.py:151
  119.1 26.8 %collective-permute-start.19 = (bf16[512,768]{1,0:T(8,128)(2,1)S(1)}, bf16[512,768]{1,0:T(8,128)(2,1)S(1)}, u32[]{:S(2)}, u32[]{:S(2)}) collective-permute-start(bf16[512,768]{1,0:T(8,128)(2,1)S(1)} %get-tuple-element.97), channel_id=1, source_target_pairs={{0,16},{1,17},{2,18},{3,19},{4,20},{5,21},{6,22},{7,23},{8,24},{9,... | collective-permute-start | bytes 2359304 | tf_op jit(solution)/shard_map/ppermute | solution.py:151
  129.1 25.2 %collective-permute-start.23 = (bf16[256,768]{1,0:T(8,128)(2,1)S(1)}, bf16[256,768]{1,0:T(8,128)(2,1)S(1)}, u32[]{:S(2)}, u32[]{:S(2)}) collective-permute-start(bf16[256,768]{1,0:T(8,128)(2,1)S(1)} %add_convert_fusion.6), channel_id=1, source_target_pairs={{0,16},{1,17},{2,18},{3,19},{4,20},{5,21},{6,22},{7,23},{8,24},{9,... | collective-permute-start | bytes 1179656 | tf_op jit(solution)/shard_map/ppermute | solution.py:151
  129.9 17.3 %collective-permute-start.14 = (bf16[64,4224]{1,0:T(8,128)(2,1)S(1)}, bf16[64,4224]{1,0:T(8,128)(2,1)S(1)}, u32[]{:S(2)}, u32[]{:S(2)}) collective-permute-start(bf16[64,4224]{1,0:T(8,128)(2,1)S(1)} %add_convert_fusion.2), channel_id=1, source_target_pairs={{0,4},{1,5},{2,0},{3,1},{4,6},{5,7},{6,2},{7,3},{8,12},{9,13},{10,... | collective-permute-start | bytes 1622024 | tf_op jit(solution)/shard_map/ppermute | solution.py:151
  132.6 21.7 %collective-permute-start.22 = (bf16[256,768]{1,0:T(8,128)(2,1)S(1)}, bf16[256,768]{1,0:T(8,128)(2,1)S(1)}, u32[]{:S(2)}, u32[]{:S(2)}) collective-permute-start(bf16[256,768]{1,0:T(8,128)(2,1)S(1)} %add_convert_fusion.7), channel_id=1, source_target_pairs={{0,8},{1,9},{2,10},{3,11},{4,12},{5,13},{6,14},{7,15},{8,0},{9,1},... | collective-permute-start | bytes 1179656 | tf_op jit(solution)/shard_map/ppermute | solution.py:151
  146.0 16.1 %collective-permute-start.21 = (bf16[256,768]{1,0:T(8,128)(2,1)S(1)}, bf16[256,768]{1,0:T(8,128)(2,1)S(1)}, u32[]{:S(2)}, u32[]{:S(2)}) collective-permute-start(bf16[256,768]{1,0:T(8,128)(2,1)S(1)} %add_convert_fusion.8), channel_id=1, source_target_pairs={{0,16},{1,17},{2,18},{3,19},{4,20},{5,21},{6,22},{7,23},{8,24},{9,... | collective-permute-start | bytes 1179656 | tf_op jit(solution)/shard_map/ppermute | solution.py:151
  146.6 15.4 %collective-permute-start.20 = (bf16[256,768]{1,0:T(8,128)(2,1)S(1)}, bf16[256,768]{1,0:T(8,128)(2,1)S(1)}, u32[]{:S(2)}, u32[]{:S(2)}) collective-permute-start(bf16[256,768]{1,0:T(8,128)(2,1)S(1)} %add_convert_fusion.9), channel_id=1, source_target_pairs={{0,8},{1,9},{2,10},{3,11},{4,12},{5,13},{6,14},{7,15},{8,0},{9,1},... | collective-permute-start | bytes 1179656 | tf_op jit(solution)/shard_map/ppermute | solution.py:151
  147.4 17.8 %collective-permute-start.15 = (bf16[64,4224]{1,0:T(8,128)(2,1)S(1)}, bf16[64,4224]{1,0:T(8,128)(2,1)S(1)}, u32[]{:S(2)}, u32[]{:S(2)}) collective-permute-start(bf16[64,4224]{1,0:T(8,128)(2,1)S(1)} %add_convert_fusion.1), channel_id=1, source_target_pairs={{0,4},{1,5},{2,0},{3,1},{4,6},{5,7},{6,2},{7,3},{8,12},{9,13},{10,... | collective-permute-start | bytes 1622024 | tf_op jit(solution)/shard_map/ppermute | solution.py:151
  164.0 10.5 %collective-permute-start.25 = (bf16[256,768]{1,0:T(8,128)(2,1)S(1)}, bf16[256,768]{1,0:T(8,128)(2,1)S(1)}, u32[]{:S(2)}, u32[]{:S(2)}) collective-permute-start(bf16[256,768]{1,0:T(8,128)(2,1)S(1)} %add_convert_fusion.4), channel_id=1, source_target_pairs={{0,16},{1,17},{2,18},{3,19},{4,20},{5,21},{6,22},{7,23},{8,24},{9,... | collective-permute-start | bytes 1179656 | tf_op jit(solution)/shard_map/ppermute | solution.py:151
  164.6 10.2 %collective-permute-start.24 = (bf16[256,768]{1,0:T(8,128)(2,1)S(1)}, bf16[256,768]{1,0:T(8,128)(2,1)S(1)}, u32[]{:S(2)}, u32[]{:S(2)}) collective-permute-start(bf16[256,768]{1,0:T(8,128)(2,1)S(1)} %add_convert_fusion.5), channel_id=1, source_target_pairs={{0,8},{1,9},{2,10},{3,11},{4,12},{5,13},{6,14},{7,15},{8,0},{9,1},... | collective-permute-start | bytes 1179656 | tf_op jit(solution)/shard_map/ppermute | solution.py:151

commit v4 on v3

--- a/solution.py
+++ b/solution.py
@@ -208,29 +208,58 @@
     )(tokens, cotangent, expert_ids.T, gate_probs.T)
 
 
-def unpack_kernel(sums_ref, ids_ref, mixed_out, back_out, prob_out):
+def weights_and_rows(weights, tokens, blocks):
+    rows, width = tokens.shape
+    dp = lax.axis_index("dp")
+    columns = jnp.split(tokens, 4, axis=1)
+    wanted = jnp.concatenate([lax.select_n(dp ^ r, *columns) for r in blocks], axis=1)
+    wanted = jnp.concatenate([wanted[: rows // 2], wanted[rows // 2 :]], axis=1)
+    weights = jnp.concatenate(weights, axis=1)
+    spare = weights.shape[1] - width
+    return jnp.concatenate([weights, jnp.pad(wanted, ((0, 0), (0, spare)))], axis=0)
+
+
+def side_rows(arrived, depth, width):
+    sides = arrived[depth:]
+    return jnp.concatenate([sides[:, : width // 2], sides[:, width // 2 : width]])
+
+
+def unpack_kernel(own_ref, core_ref, line_ref, ids_ref, mixed_out, back_out, prob_out):
     rows, width = mixed_out.shape
     block = width // 4
+
+    def total(at):
+        return own_ref[:, at].astype(F32) + core_ref[:, at].astype(F32) + line_ref[:, at].astype(F32)
+
     for r in range(4):
         there = block_at(r, block)
-        mixed_out[:, there] = sums_ref[:, r * block : (r + 1) * block]
-        back_out[:, there] = sums_ref[:, width + r * block : width + (r + 1) * block]
+        start = r * block
+        mixed_out[:, there] = total(slice(start, start + block)).astype(BF16)
+        start += width
+        back_out[:, there] = total(slice(start, start + block)).astype(BF16)
     lane = iota(8, SIDE, 1)
     adder = ((lane < 24) & (lane % 8 == iota(8, SIDE, 0))).astype(BF16)
-    by_expert = lax.dot_general(adder, sums_ref[:, 2 * width :], ACROSS, preferred_element_type=F32)
+    parts = total(slice(2 * width, 2 * width + SIDE)).astype(BF16)
+    by_expert = lax.dot_general(adder, parts, ACROSS, preferred_element_type=F32)
     for k in range(ids_ref.shape[0]):
         hit = iota(8, rows, 0) == ids_ref[k : k + 1, :]
         prob_out[k : k + 1, :] = jnp.sum(jnp.where(hit, by_expert, 0.0), axis=0, keepdims=True)
 
 
-def unpack(sums, expert_ids, width):
-    own = shape(sums.shape[0], width, BF16)
+def unpack(shares, arrived, line, expert_ids, width):
+    rows, columns = line.shape
+    own = shape(rows, width, BF16)
+    ids = expert_ids.T
+    first = pl.BlockSpec((rows, columns), lambda i: (0, 0))
+    wide = pl.BlockSpec((rows, width), lambda i: (0, 0))
+    small = pl.BlockSpec(ids.shape, lambda i: (0, 0))
     mixed, back, prob = kernel_call(
         unpack_kernel,
-        (own, own, shape(*expert_ids.T.shape, F32)),
-        in_specs=[VMEM] * 2,
-        out_specs=(VMEM,) * 3,
-    )(sums, expert_ids.T)
+        (own, own, shape(*ids.shape, F32)),
+        grid=(1,),
+        in_specs=[first] * 3 + [small],
+        out_specs=(wide, wide, small),
+    )(shares, arrived, line, ids)
     return mixed, back, prob.T
 
 
@@ -240,15 +269,15 @@
     out_ref[:, rows:] = other_ref[...].T
 
 
-def turn(whole, width):
-    rows = whole[0].shape[0]
+def turn(both, tiles, place_of):
+    rows = both[0].shape[0]
     return kernel_call(
         turn_kernel,
-        shape(width, 2 * rows, BF16),
-        grid=(width // TILE,),
-        in_specs=[pl.BlockSpec((rows, TILE), lambda i: (0, i))] * 2,
+        shape(tiles * TILE, 2 * rows, BF16),
+        grid=(tiles,),
+        in_specs=[pl.BlockSpec((rows, TILE), lambda i: (0, place_of(i)))] * 2,
         out_specs=pl.BlockSpec((TILE, 2 * rows), lambda i: (i, 0)),
-    )(*whole)
+    )(*both)
 
 
 def times_pieces(rows_ref, pieces):
@@ -269,7 +298,7 @@
 
 def early_products(whole, direct, width, which, start, columns):
     half = whole[0].shape[0]
-    piece = pl.BlockSpec((direct[0].shape[0], TILE), lambda j: (0, start // TILE + j))
+    piece = pl.BlockSpec((width // 4, TILE), lambda j: (0, start // TILE + j))
     return kernel_call(
         early_kernel,
         shape(2 * half, columns, F32),
@@ -362,81 +391,99 @@
     )(*whole, early, *corner, for_gate, for_up, hidden)
 
 
-def first_half_blocks(i):
-    return jnp.where(i == 3, 4, 7 - 4 * (i % 2) - i // 2)
-
-
-def later_half_blocks(i):
-    return jnp.where(i < 2, 2 + 3 * i, i - 2)
-
-
-def first_grad_kernel(turned_ref, term_ref, to_x, to_y):
+def corner_grad_kernel(turned_ref, term_ref, to_x, to_y):
     step = pl.program_id(0)
     part = jnp.dot(turned_ref[...], term_ref[...], preferred_element_type=F32).astype(BF16)
 
-    @pl.when(step < 2)
+    @pl.when(step == 0)
     def _():
         to_x[...] = part
 
-    @pl.when(step >= 2)
+    @pl.when(step == 1)
     def _():
         to_y[...] = part
+
+
+def corner_grads(turned, first, term, width):
+    rows, units = term.shape
+    half = width // 8
+    once = pl.BlockSpec((half, units), lambda i: (0, 0))
+    return kernel_call(
+        corner_grad_kernel,
+        (shape(half, units, BF16),) * 2,
+        grid=(2,),
+        in_specs=[
+            pl.BlockSpec((half, rows), lambda i: (first + 7 - i, 0)),
+            pl.BlockSpec((rows, units), lambda i: (0, 0)),
+        ],
+        out_specs=(once, once),
+    )(turned, term)
 
 
 def later_grad_kernel(turned_ref, term_ref, for_x, for_y, own):
     step = pl.program_id(0)
     part = jnp.dot(turned_ref[...], term_ref[...], preferred_element_type=F32)
 
-    @pl.when(step == 0)
+    for place, out in enumerate((for_x, for_y, own)):
+
+        @pl.when(step // 2 == place)
+        def _(out=out):
+            out[...] = part
+
+
+def later_grads(turned, first, term, width):
+    rows, units = term.shape
+    half = width // 8
+
+    def at(start):
+        return pl.BlockSpec((half, units), lambda i: (jnp.clip(i - start, 0, 1), 0))
+
+    return kernel_call(
+        later_grad_kernel,
+        (shape(2 * half, units, F32),) * 3,
+        grid=(6,),
+        in_specs=[
+            pl.BlockSpec((half, rows), lambda i: (first + (i + 2) % 6, 0)),
+            pl.BlockSpec((rows, units), lambda i: (0, 0)),
+        ],
+        out_specs=(at(0), at(2), at(4)),
+    )(turned, term)
+
+
+def pair_grad_kernel(turned_ref, other_turned_ref, term_ref, other_term_ref, away, own):
+    step = pl.program_id(0)
+    part = jnp.dot(turned_ref[...], term_ref[...], preferred_element_type=F32)
+    part += jnp.dot(other_turned_ref[...], other_term_ref[...], preferred_element_type=F32)
+
+    @pl.when(step < 2)
     def _():
-        for_x[...] = part
-
-    @pl.when(step == 1)
-    def _():
-        for_y[...] = part
+        away[...] = part.astype(BF16)
 
     @pl.when(step >= 2)
     def _():
         own[...] = part
 
 
-def first_grads(turned, first, width, term):
+def pair_grads(turned, first, gap, other_turned, other_first, term, other_term, width):
     rows, units = term.shape
     half = width // 8
 
     def at(start):
         return pl.BlockSpec((half, units), lambda i: (jnp.clip(i - start, 0, 1), 0))
 
-    return kernel_call(
-        first_grad_kernel,
-        (shape(2 * half, units, BF16),) * 2,
+    def tile(start, jump):
+        return pl.BlockSpec(
+            (half, rows), lambda i: (start + i % 2 + jnp.where(i < 2, 2 * jump, 0), 0)
+        )
+
+    return kernel_call(
+        pair_grad_kernel,
+        (shape(2 * half, units, BF16), shape(2 * half, units, F32)),
         grid=(4,),
-        in_specs=[
-            pl.BlockSpec((half, rows), lambda i: (first + first_half_blocks(i), 0)),
-            pl.BlockSpec((rows, units), lambda i: (0, 0)),
-        ],
+        in_specs=[tile(first, gap), tile(other_first, 1)]
+        + [pl.BlockSpec((rows, units), lambda i: (0, 0))] * 2,
         out_specs=(at(0), at(2)),
-    )(turned, term)
-
-
-def later_grads(turned, first, width, term):
-    rows, units = term.shape
-    half = width // 8
-    once = pl.BlockSpec((half, units), lambda i: (0, 0))
-    return kernel_call(
-        later_grad_kernel,
-        (shape(half, units, F32),) * 2 + (shape(2 * half, units, F32),),
-        grid=(4,),
-        in_specs=[
-            pl.BlockSpec((half, rows), lambda i: (first + later_half_blocks(i), 0)),
-            pl.BlockSpec((rows, units), lambda i: (0, 0)),
-        ],
-        out_specs=(
-            once,
-            once,
-            pl.BlockSpec((half, units), lambda i: (jnp.clip(i - 2, 0, 1), 0)),
-        ),
-    )(turned, term)
+    )(turned, other_turned, term, other_term)
 
 
 def back_kernel(scaled_ref, d_gate_ref, d_up_ref, dots_ref, *refs):
@@ -459,7 +506,7 @@
 
 def back_to_rows(scaled, d_gate, d_up, dots, direct, down, gate_up, width):
     rows, units = scaled.shape
-    depth = direct[0].shape[0]
+    depth = width // 4
     term = pl.BlockSpec((TILE, units), lambda i: (i, 0))
     corner = [pl.BlockSpec((depth // 2, n * units), lambda i: (0, 0)) for n in (1, 1, 2, 2)]
     return kernel_call(
@@ -476,68 +523,59 @@
     )(scaled, d_gate, d_up, dots, *direct, *down, *direct, *gate_up)
 
 
-def total_kernel(own_ref, from_x, from_y, late_x, late_y, out_ref):
-    out_ref[0] = own_ref[0] + (from_y[0].astype(F32) + late_x[...].astype(F32))
-    out_ref[1] = own_ref[1] + (from_x[0].astype(F32) + late_y[...].astype(F32))
-
-
-def total(own, from_x, from_y, late_x, late_y):
+def total_kernel(own_ref, *refs):
+    others, out_ref = refs[:-1], refs[-1]
+    out_ref[0] = own_ref[...] + sum(other[...].astype(F32) for other in others)
+
+
+def total(own, *others):
     block, units = own.shape
-    half = block // 2
-    step = half // 4
-    both = pl.BlockSpec((2, step, units), lambda i: (0, i, 0))
-    low = pl.BlockSpec((1, step, units), lambda i: (1, i, 0))
-    late = pl.BlockSpec((step, units), lambda i: (i, 0))
-    halves = (2, half, units)
+    step = block // 4
+    rows = pl.BlockSpec((step, units), lambda i: (i, 0))
     return kernel_call(
         total_kernel,
-        jax.ShapeDtypeStruct(halves, F32),
-        grid=(half // step,),
-        in_specs=[both, low, low, late, late],
-        out_specs=both,
-    )(own.reshape(halves), from_x.reshape(halves), from_y.reshape(halves), late_x, late_y).reshape(
-        1, block, units
-    )
-
-
-def send_corner(from_x, from_y, columns):
-    half = from_x.shape[0] // 2
-    return [send(from_x[:half, columns], TO_Y), send(from_y[half:, columns], TO_X)]
-
-
-def send_first(to_x, to_y):
-    return send(to_x, TO_X), send(to_y, TO_Y)
-
-
-def send_later(for_x, for_y, from_x, from_y):
-    half = for_x.shape[0]
-    late_x = send((for_x + from_y[:half].astype(F32)).astype(BF16), TO_X)
-    late_y = send((for_y + from_x[:half].astype(F32)).astype(BF16), TO_Y)
-    return late_x, late_y
-
-
-def gather_rows(own, before):
+        jax.ShapeDtypeStruct((1, block, units), F32),
+        grid=(block // step,),
+        in_specs=[rows] * (1 + len(others)),
+        out_specs=pl.BlockSpec((1, step, units), lambda i: (0, i, 0)),
+    )(own, *others)
+
+
+def send_corner(from_x, from_y, columns, depth):
+    half = depth // 2
+    return [send(from_x[:half, columns], TO_Y), send(from_y[half:depth, columns], TO_X)]
+
+
+def along_line(own, before_second=()):
     slots = [own]
-    for _ in range(3):
-        slots.append(send(slots[-1], ALONG_Z))
+    for step in range(3):
+        moving = after(slots[-1], before_second) if step == 1 else slots[-1]
+        slots.append(send(moving, ALONG_Z))
+    return slots
+
+
+def from_both_cores(slots, before):
     own_core = after(jnp.concatenate(slots), before)
     return own_core, send(own_core, TO_CORE)
+
+
+def send_down(for_x, for_y, from_x, from_y):
+    half = from_x.shape[0]
+    for_x = jnp.concatenate([for_x[:half] + from_y.astype(F32), for_x[half:]])
+    for_y = jnp.concatenate([for_y[:half], for_y[half:] + from_x.astype(F32)])
+    return send(for_x.astype(BF16), TO_X), send(for_y.astype(BF16), TO_Y)
 
 
 def sum_over_experts(rows, before):
     half = rows.shape[0] // 2
     block = half // 4
-    arrived = send(after(rows[half:], before), TO_CORE)
-
-    def both_cores(slot):
+    arrived = send(rows[half:], TO_CORE)
+    moving = 0.0
+    for slot, wait in zip((1, 2, 3), before):
         at = slice(slot * block, (slot + 1) * block)
-        return rows[at].astype(F32) + arrived[at].astype(F32)
-
-    steps = [both_cores(1).astype(BF16)]
-    for slot in (2, 3, 0):
-        moving = send(steps[-1], ALONG_Z)
-        steps.append((both_cores(slot) + moving.astype(F32)).astype(BF16))
-    return steps
+        total = rows[at].astype(F32) + arrived[at].astype(F32) + moving
+        moving = send(after(total.astype(BF16), wait), ALONG_Z).astype(F32)
+    return arrived, moving.astype(BF16)
 
 
 def after(arrays, *others):
@@ -547,51 +585,49 @@
 def dense_plan(tokens, expert_ids, gate_probs, cotangent, gate_proj, up_proj, down_proj):
     width = tokens.shape[1]
     units = gate_proj.shape[2]
-    halves = width // TILE
-
-    shard = jnp.concatenate([gate_proj[0], up_proj[0], down_proj[0]], axis=1)
-    direct = [shard, send(shard, TO_X), send(shard, TO_Y)]
-    whole = gather_rows(pack(tokens, cotangent, expert_ids, gate_probs), direct)
-    gate_up_corner = send_corner(*direct[1:], slice(0, 2 * units))
-    down_corner = send_corner(*direct[1:], slice(2 * units, 3 * units))
+
+    depth = gate_proj.shape[1]
+    weights = (gate_proj[0], up_proj[0], down_proj[0])
+    to_x = weights_and_rows(weights, tokens, (1, 3))
+    to_y = weights_and_rows(weights, tokens, (2, 3))
+    packed = pack(tokens, cotangent, expert_ids, gate_probs)
+    direct = [to_x, send(to_x, TO_X), send(to_y, TO_Y)]
+    whole = from_both_cores(along_line(packed), direct)
+    side = [side_rows(direct[2], depth, width), side_rows(direct[1], depth, width)]
+    gate_up_corner = send_corner(*direct[1:], slice(0, 2 * units), depth)
+    down_corner = send_corner(*direct[1:], slice(2 * units, 3 * units), depth)
     early_gate_up = early_products(whole, direct, width, 0, 0, 2 * units)
-    turned = turn(whole, 2 * width)
     early_down = early_products(whole, direct, width, 1, 2 * units, units)
+    turned = turn(whole, 14, lambda i: jnp.where(i < 6, i, i + 2))
+    extra = along_line(jnp.concatenate(side, axis=1), (early_gate_up, early_down, turned))
     early_gate_up, early_down, turned, gate_up_corner = lax.optimization_barrier(
         (early_gate_up, early_down, turned, gate_up_corner)
     )
 
     scaled, for_gate, for_up, hidden = forward(whole, early_gate_up, gate_up_corner, width, units)
-    down_sent = first_grads(turned, halves, width, scaled)
-    down_first = send_first(*after(down_sent, down_corner))
-    scaled, whole, hidden = after((scaled, whole, hidden), down_sent)
-    *down_later, down_own = later_grads(turned, halves, width, scaled)
-    hidden = after(hidden, down_own)
-    d_gate, d_up, dots = backward(
-        whole, early_down, down_corner, for_gate, for_up, hidden, width
-    )
-    gate_sent = first_grads(turned, 0, width, d_gate)
-    gate_first = send_first(*gate_sent)
-    d_gate, d_up = after((d_gate, d_up), gate_sent)
-    up_sent = first_grads(turned, 0, width, d_up)
+    corner_sent = after(corner_grads(turned, 6, scaled, width), down_corner, extra[2])
+    corner_x, corner_y = send(corner_sent[0], TO_X), send(corner_sent[1], TO_Y)
+    hidden, scaled = after((hidden, scaled), corner_sent)
+    d_gate, d_up, dots = backward(whole, early_down, down_corner, for_gate, for_up, hidden, width)
+    other_gate = send(d_gate, TO_X)
+    other_up = send(d_up, TO_Y)
     shares = back_to_rows(scaled, d_gate, d_up, dots, direct, down_corner, gate_up_corner, width)
-    steps = sum_over_experts(shares, down_first)
-    d_gate, d_up = after((d_gate, d_up), shares)
-    *gate_later, gate_own = later_grads(turned, 0, width, d_gate)
-    *up_later, up_own = later_grads(turned, 0, width, d_up)
-
-    up_first = send_first(*after(up_sent, down_first))
-    down_later = after(down_later, gate_first, steps[0])
-    down_late = send_later(*down_later, *down_first)
-    gate_later = after(gate_later, up_first, steps[1])
-    gate_late = send_later(*gate_later, *gate_first)
-    grad_down = total(down_own, *down_first, *down_late)
-    up_later = after(up_later, grad_down, steps[2])
-    up_late = send_later(*up_later, *up_first)
-    outs = unpack(steps[3], expert_ids, width)
-    grad_gate = total(gate_own, *gate_first, *gate_late)
-    up_late = after(up_late, grad_gate, outs)
-    grad_up = total(up_own, *up_first, *up_late)
+    scaled = after(scaled, shares)
+    for_x, for_y, down_own = later_grads(turned, 6, scaled, width)
+    down_back = send_down(for_x, for_y, corner_x, corner_y)
+    shares = after(shares, corner_x, corner_y, extra[3])
+    other_turned = turn(from_both_cores(extra, corner_x), 8, lambda i: i)
+    gate_away, gate_own = pair_grads(turned, 0, 2, other_turned, 4, d_gate, other_gate, width)
+    gate_back = send(gate_away, TO_Y)
+    up_away, up_own = pair_grads(turned, 0, 1, other_turned, 0, d_up, other_up, width)
+    up_back = send(up_away, TO_X)
+    grad_down = total(down_own, *after(down_back, gate_away, up_away))
+    arrived, line = sum_over_experts(shares, (other_turned, (other_gate, other_up), grad_down))
+    outs = unpack(shares, arrived, line, expert_ids, width)
+    gate_back = after(gate_back, outs)
+    grad_gate = total(gate_own, gate_back)
+    up_back = after(up_back, grad_gate)
+    grad_up = total(up_own, up_back)
     return (*outs, grad_gate, grad_up, grad_down)
 
 

time: 177 us -> 165 us (0.932)
  waiting for transfers between devices: 101 us -> 81.1 us
  starting transfers between devices: 34.5 us -> 40.6 us
  other arithmetic: 3.09 us -> 6.08 us
    ppermute x26, waiting for transfers between devices: 101 us -> 81.1 us  [send(): return lax.ppermute(array, AXES, where)]
    ppermute x26, starting transfers between devices: 34.5 us -> 40.6 us  [send(): return lax.ppermute(array, AXES, where)]
    select_n x0 -> x2, other arithmetic: none -> 2.03 us  [weights_and_rows(): lax.select_n(dp ^ r, *columns)]
    pallas_call x11 -> x10, Pallas kernels: 19.6 us -> 18.7 us  [the longest x3 5.1 us: total(): kernel_call(total_kernel, jax.ShapeDtypeStruct((1, block, units), F32), g...]
  transfers between devices with their start and end apart: 26 -> 26, of which waited for: 20 -> 14; matrix products, arithmetic and copies ran while one was open for 1% -> 1% of each run, Pallas kernels for 20% -> 21%
where the time goes in v4:
time: 165 us
  waiting for transfers between devices  81.1 us (49%)
  starting transfers between devices  40.6 us (25%)
  Pallas kernels  35.7 us (22%)
  other arithmetic  6.08 us (4%)
    ppermute x26, waiting for transfers between devices, send(): return lax.ppermute(array, AXES, where)  81.1 us
    ppermute x26, starting transfers between devices, send(): return lax.ppermute(array, AXES, where)  40.6 us
    pallas_call x2, Pallas kernels, early_products(): kernel_call(early_kernel, shape(2 * half, columns, F32), grid=(columns //...  6.32 us
    pallas_call x1, Pallas kernels, back_to_rows(): kernel_call(back_kernel, shape(rows, 2 * width + SIDE, BF16), grid=(rows...  5.81 us
    pallas_call x3, Pallas kernels, total(): kernel_call(total_kernel, jax.ShapeDtypeStruct((1, block, units), F32), g...  5.1 us
    pallas_call x2, Pallas kernels, pair_grads(): kernel_call(pair_grad_kernel, (shape(2 * half, units, BF16), shape(2 * ha...  4.99 us
    pallas_call x2, Pallas kernels, turn(): kernel_call(turn_kernel, shape(tiles * TILE, 2 * rows, BF16), grid=(tiles...  4.2 us
  transfers between devices with their start and end apart: 26, of which 14 were waited for; matrix products, arithmetic and copies ran while one was open for 1% of the time, Pallas kernels for 21%

profile of v4, /device:TPU:0, one launch (start us, length us, event | category | flops | bytes accessed | tf_op | source)
XLA Modules:
  0.0 164.9 jit_solution(10772979829160689567)
XLA Ops:
  0.7 1.1 select_select_fusion.1
  1.7 1.0 select_select_fusion
  2.8 3.0 %pad_maximum_fusion.2 = (bf16[544,2304]{1,0:T(8,128)(2,1)S(1)}, bf16[544,2304]{1,0:T(8,128)(2,1)S(1)}) fusion(bf16[32,2304]{1,0:T(8,128)(2,1)S(1)} %get-tuple-element.94, bf16[512,768]{1,0:T(8,128)(2,1)S(1)} %bitcast.9, bf16[512,768]{1,0:T(8,128)(2,1)S(1)} %bitcast.10, bf16[512,768]{1,0:T(8,128)(2,1)} %bitcast.11, bf16[32,2304]{1,0:T(8,128)(2,1)S(1)} %get-tuple-element.95), kind=kLoop, calls=%fused_computation.2 | loop fusion | flops 13787136 | bytes 7667712 | tf_op jit(solution)/shard_map/concatenate | solution.py:219
  5.8 3.0 %collective-permute-start.4 = (bf16[544,2304]{1,0:T(8,128)(2,1)S(1)}, bf16[544,2304]{1,0:T(8,128)(2,1)S(1)}, u32[]{:S(2)}, u32[]{:S(2)}) collective-permute-start(bf16[544,2304]{1,0:T(8,128)(2,1)S(1)} %get-tuple-element.90), channel_id=1, source_target_pairs={{0,16},{1,17},{2,18},{3,19},{4,20},{5,21},{6,22},{7,23},{8,24},{9,... | collective-permute-start | bytes 7520264 | tf_op jit(solution)/shard_map/ppermute | solution.py:151
  8.9 1.5 collective-permute-start.3
  10.5 2.6 %collective-permute-start = (bf16[64,4224]{1,0:T(8,128)(2,1)S(1)}, bf16[64,4224]{1,0:T(8,128)(2,1)S(1)}, u32[]{:S(2)}, u32[]{:S(2)}) collective-permute-start(bf16[64,4224]{1,0:T(8,128)(2,1)S(1)} %shard_map.118), channel_id=1, source_target_pairs={{0,4},{1,5},{2,0},{3,1},{4,6},{5,7},{6,2},{7,3},{8,12},{9,13},{10,... | collective-permute-start | bytes 1622024 | tf_op jit(solution)/shard_map/ppermute | solution.py:151
  13.1 11.0 %collective-permute-done = bf16[64,4224]{1,0:T(8,128)(2,1)S(1)} collective-permute-done((bf16[64,4224]{1,0:T(8,128)(2,1)S(1)}, bf16[64,4224]{1,0:T(8,128)(2,1)S(1)}, u32[]{:S(2)}, u32[]{:S(2)}) %collective-permute-start) | collective-permute-done | bytes 540704 | tf_op jit(solution)/shard_map/ppermute | solution.py:151
  24.1 3.4 %collective-permute-start.1 = (bf16[64,4224]{1,0:T(8,128)(2,1)S(1)}, bf16[64,4224]{1,0:T(8,128)(2,1)S(1)}, u32[]{:S(2)}, u32[]{:S(2)}) collective-permute-start(bf16[64,4224]{1,0:T(8,128)(2,1)S(1)} %collective-permute-done), channel_id=1, source_target_pairs={{0,4},{1,5},{2,0},{3,1},{4,6},{5,7},{6,2},{7,3},{8,12},{9,13},{10,... | collective-permute-start | bytes 1622024 | tf_op jit(solution)/shard_map/ppermute | solution.py:151
  27.5 10.0 %collective-permute-done.1 = bf16[64,4224]{1,0:T(8,128)(2,1)S(1)} collective-permute-done((bf16[64,4224]{1,0:T(8,128)(2,1)S(1)}, bf16[64,4224]{1,0:T(8,128)(2,1)S(1)}, u32[]{:S(2)}, u32[]{:S(2)}) %collective-permute-start.1) | collective-permute-done | bytes 540704 | tf_op jit(solution)/shard_map/ppermute | solution.py:151
  37.5 3.4 %collective-permute-start.2 = (bf16[64,4224]{1,0:T(8,128)(2,1)S(1)}, bf16[64,4224]{1,0:T(8,128)(2,1)S(1)}, u32[]{:S(2)}, u32[]{:S(2)}) collective-permute-start(bf16[64,4224]{1,0:T(8,128)(2,1)S(1)} %collective-permute-done.1), channel_id=1, source_target_pairs={{0,4},{1,5},{2,0},{3,1},{4,6},{5,7},{6,2},{7,3},{8,12},{9,13},{10,... | collective-permute-start | bytes 1622024 | tf_op jit(solution)/shard_map/ppermute | solution.py:151
  40.9 9.1 %collective-permute-done.2 = bf16[64,4224]{1,0:T(8,128)(2,1)S(1)} collective-permute-done((bf16[64,4224]{1,0:T(8,128)(2,1)S(1)}, bf16[64,4224]{1,0:T(8,128)(2,1)S(1)}, u32[]{:S(2)}, u32[]{:S(2)}) %collective-permute-start.2) | collective-permute-done | bytes 540704 | tf_op jit(solution)/shard_map/ppermute | solution.py:151
  50.2 13.1 %collective-permute-done.4.y_ref.refs_2_.refs_7_ = bf16[544,2304]{1,0:T(8,128)(2,1)S(1)} collective-permute-done((bf16[544,2304]{1,0:T(8,128)(2,1)S(1)}, bf16[544,2304]{1,0:T(8,128)(2,1)S(1)}, u32[]{:S(2)}, u32[]{:S(2)}) %collective-permute-start.4) | collective-permute-done | bytes 2506784 | tf_op jit(solution)/shard_map/ppermute | solution.py:151
  63.3 1.5 collective-permute-done.3.x_ref.refs_1_.refs_6_
  64.8 1.6 collective-permute-start.7
  67.0 2.6 %collective-permute-start.10 = (bf16[64,2048]{1,0:T(8,128)(2,1)S(1)}, bf16[64,2048]{1,0:T(8,128)(2,1)S(1)}, u32[]{:S(2)}, u32[]{:S(2)}) collective-permute-start(bf16[64,2048]{1,0:T(8,128)(2,1)S(1)} %maximum_maximum_fusion), channel_id=1, source_target_pairs={{0,4},{1,5},{2,0},{3,1},{4,6},{5,7},{6,2},{7,3},{8,12},{9,13},{10,... | collective-permute-start | bytes 786440 | tf_op jit(solution)/shard_map/ppermute | solution.py:151
  70.3 1.6 collective-permute-start.8
  71.9 2.1 %shard_map.120.early_ref = f32[512,768]{1,0:T(8,128)S(1)} custom-call(bf16[256,4224]{1,0:T(8,128)(2,1)S(1)} %pad_maximum_fusion.3.own_rows.own_ref.refs_0_.refs_2_, bf16[256,4224]{1,0:T(8,128)(2,1)S(1)} %collective-permute-done.5.other_rows.other_ref.refs_1_.refs_3_, bf16[544,2304]{1,0:T(8,128)(2,1)S(1)} %get-tuple-element.91.own_ref.refs_0_.refs_5_, ...), custom_call_target="tpu_custom_call" | custom-call | tf_op jit(solution)/shard_map/pallas_call | solution.py:302
  74.1 4.2 %shard_map.119.refs_4_.refs_5_ = f32[512,1536]{1,0:T(8,128)S(1)} custom-call(bf16[256,4224]{1,0:T(8,128)(2,1)S(1)} %pad_maximum_fusion.3.own_rows.own_ref.refs_0_.refs_2_, bf16[256,4224]{1,0:T(8,128)(2,1)S(1)} %collective-permute-done.5.other_rows.other_ref.refs_1_.refs_3_, bf16[544,2304]{1,0:T(8,128)(2,1)S(1)} %get-tuple-element.91.own_ref.refs_0_.refs_5_, ...), custom_call_target="tpu_custom_call" | custom-call | tf_op jit(solution)/shard_map/pallas_call | solution.py:302
  78.3 2.8 %shard_map.121.turned_ref = bf16[3584,512]{1,0:T(8,128)(2,1)S(1)} custom-call(bf16[256,4224]{1,0:T(8,128)(2,1)S(1)} %pad_maximum_fusion.3.own_rows.own_ref.refs_0_.refs_2_, bf16[256,4224]{1,0:T(8,128)(2,1)S(1)} %collective-permute-done.5.other_rows.other_ref.refs_1_.refs_3_), custom_call_target="tpu_custom_call" | custom-call | tf_op jit(solution)/shard_map/pallas_call | solution.py:274
  81.1 1.6 collective-permute-start.11
  82.8 2.4 %collective-permute-done.7.refs_7_.refs_9_ = bf16[256,1536]{1,0:T(8,128)(2,1)S(1)} collective-permute-done((bf16[256,1536]{1,0:T(8,128)(2,1)S(1)}, bf16[256,1536]{1,0:T(8,128)(2,1)S(1)}, u32[]{:S(2)}, u32[]{:S(2)}) %collective-permute-start.7) | collective-permute-done | bytes 786464 | tf_op jit(solution)/shard_map/ppermute | solution.py:151
  85.2 1.7 %collective-permute-done.6.refs_6_.refs_8_ = bf16[256,1536]{1,0:T(8,128)(2,1)S(1)} collective-permute-done((bf16[256,1536]{1,0:T(8,128)(2,1)S(1)}, bf16[256,1536]{1,0:T(8,128)(2,1)S(1)}, u32[]{:S(2)}, u32[]{:S(2)}) %collective-permute-start.6) | collective-permute-done | bytes 786464 | tf_op jit(solution)/shard_map/ppermute | solution.py:151
  86.8 2.6 %shard_map.122 = (bf16[512,768]{1,0:T(8,128)(2,1)S(1)}, f32[512,768]{1,0:T(8,128)S(1)}, f32[512,768]{1,0:T(8,128)S(1)}, f32[512,768]{1,0:T(8,128)S(1)}) custom-call(bf16[256,4224]{1,0:T(8,128)(2,1)S(1)} %pad_maximum_fusion.3.own_rows.own_ref.refs_0_.refs_2_, bf16[256,4224]{1,0:T(8,128)(2,1)S(1)} %collective-permute-done.5.other_rows.other_ref.refs_1_.refs_3_, ...), custom_call_target="tpu_custom_call" | custom-call | tf_op jit(solution)/shard_map/pallas_call | solution.py:340
  90.3 2.9 %collective-permute-done.9.last_ref.refs_4_ = bf16[256,768]{1,0:T(8,128)(2,1)S(1)} collective-permute-done((bf16[256,768]{1,0:T(8,128)(2,1)S(1)}, bf16[256,768]{1,0:T(8,128)(2,1)S(1)}, u32[]{:S(2)}, u32[]{:S(2)}) %collective-permute-start.9) | collective-permute-done | bytes 393248 | tf_op jit(solution)/shard_map/ppermute | solution.py:151
  93.2 1.3 collective-permute-done.8.first_ref.refs_3_
  95.5 2.7 %collective-permute-start.14 = (bf16[64,2048]{1,0:T(8,128)(2,1)S(1)}, bf16[64,2048]{1,0:T(8,128)(2,1)S(1)}, u32[]{:S(2)}, u32[]{:S(2)}) collective-permute-start(bf16[64,2048]{1,0:T(8,128)(2,1)S(1)} %collective-permute-done.11), channel_id=1, source_target_pairs={{0,4},{1,5},{2,0},{3,1},{4,6},{5,7},{6,2},{7,3},{8,12},{9,13},{10,... | collective-permute-start | bytes 786440 | tf_op jit(solution)/shard_map/ppermute | solution.py:151
  98.2 2.1 %shard_map.124 = (bf16[512,768]{1,0:T(8,128)(2,1)S(1)}, bf16[512,768]{1,0:T(8,128)(2,1)S(1)}, bf16[512,128]{1,0:T(8,128)(2,1)S(1)}) custom-call(bf16[256,4224]{1,0:T(8,128)(2,1)S(1)} %pad_maximum_fusion.3.own_rows.own_ref.refs_0_.refs_2_, bf16[256,4224]{1,0:T(8,128)(2,1)S(1)} %collective-permute-done.5.other_rows.other_ref.refs_1_.refs_3_, ...), custom_call_target="tpu_custom_call" | custom-call | tf_op jit(solution)/shard_map/pallas_call | solution.py:381
  100.3 5.8 %shard_map.125.own_ref = bf16[512,4224]{1,0:T(8,128)(2,1)S(1)} custom-call(bf16[512,768]{1,0:T(8,128)(2,1)S(1)} %get-tuple-element.70.term_ref.scaled_ref, bf16[512,768]{1,0:T(8,128)(2,1)S(1)} %get-tuple-element.63.d_gate_ref.term_ref, bf16[512,768]{1,0:T(8,128)(2,1)S(1)} %get-tuple-element.64.d_up_ref.term_ref, ...), custom_call_target="tpu_custom_call" | custom-call | tf_op jit(solution)/shard_map/pallas_call | solution.py:512
  107.1 1.5 collective-permute-start.18
  108.6 1.5 collective-permute-start.19
  110.1 2.5 %shard_map.127 = (f32[512,768]{1,0:T(8,128)S(1)}, f32[512,768]{1,0:T(8,128)S(1)}, f32[512,768]{1,0:T(8,128)S(1)}) custom-call(bf16[3584,512]{1,0:T(8,128)(2,1)S(1)} %shard_map.121.turned_ref, bf16[512,768]{1,0:T(8,128)(2,1)S(1)} %get-tuple-element.70.term_ref.scaled_ref), custom_call_target="tpu_custom_call" | custom-call | tf_op jit(solution)/shard_map/pallas_call | solution.py:441
  112.7 1.4 shard_map.126.other_turned_ref
  114.2 1.6 collective-permute-start.17
  116.0 1.0 collective-permute-start.22
  117.2 1.6 collective-permute-start.21
  118.7 9.3 %collective-permute-done.17 = bf16[64,4224]{1,0:T(8,128)(2,1)S(1)} collective-permute-done((bf16[64,4224]{1,0:T(8,128)(2,1)S(1)}, bf16[64,4224]{1,0:T(8,128)(2,1)S(1)}, u32[]{:S(2)}, u32[]{:S(2)}) %collective-permute-start.17) | collective-permute-done | bytes 540704 | tf_op jit(solution)/shard_map/ppermute | solution.py:151
  129.0 1.9 %collective-permute-start.20 = (bf16[64,4224]{1,0:T(8,128)(2,1)S(1)}, bf16[64,4224]{1,0:T(8,128)(2,1)S(1)}, u32[]{:S(2)}, u32[]{:S(2)}) collective-permute-start(bf16[64,4224]{1,0:T(8,128)(2,1)S(1)} %add_convert_fusion.1), channel_id=1, source_target_pairs={{0,4},{1,5},{2,0},{3,1},{4,6},{5,7},{6,2},{7,3},{8,12},{9,13},{10,... | collective-permute-start | bytes 1622024 | tf_op jit(solution)/shard_map/ppermute | solution.py:151
  130.8 2.5 %shard_map.129 = (bf16[512,768]{1,0:T(8,128)(2,1)S(1)}, f32[512,768]{1,0:T(8,128)S(1)}) custom-call(bf16[3584,512]{1,0:T(8,128)(2,1)S(1)} %shard_map.121.turned_ref, bf16[2048,512]{1,0:T(8,128)(2,1)S(1)} %shard_map.126.other_turned_ref, bf16[512,768]{1,0:T(8,128)(2,1)S(1)} %get-tuple-element.64.d_up_ref.term_ref, ...), custom_call_target="tpu_custom_call" | custom-call | tf_op jit(solution)/shard_map/pallas_call | solution.py:479
  133.4 1.6 collective-permute-start.25
  134.9 2.5 %shard_map.128 = (bf16[512,768]{1,0:T(8,128)(2,1)S(1)}, f32[512,768]{1,0:T(8,128)S(1)}) custom-call(bf16[3584,512]{1,0:T(8,128)(2,1)S(1)} %shard_map.121.turned_ref, bf16[2048,512]{1,0:T(8,128)(2,1)S(1)} %shard_map.126.other_turned_ref, bf16[512,768]{1,0:T(8,128)(2,1)S(1)} %get-tuple-element.63.d_gate_ref.term_ref, ...), custom_call_target="tpu_custom_call" | custom-call | tf_op jit(solution)/shard_map/pallas_call | solution.py:479
  137.4 1.5 collective-permute-start.24
  138.9 6.9 %collective-permute-done.22.refs_1_ = bf16[512,768]{1,0:T(8,128)(2,1)S(1)} collective-permute-done((bf16[512,768]{1,0:T(8,128)(2,1)S(1)}, bf16[512,768]{1,0:T(8,128)(2,1)S(1)}, u32[]{:S(2)}, u32[]{:S(2)}) %collective-permute-start.22) | collective-permute-done | bytes 786464 | tf_op jit(solution)/shard_map/ppermute | solution.py:151
  145.8 1.7 %shard_map.130 = f32[1,512,768]{2,1,0:T(8,128)} custom-call(f32[512,768]{1,0:T(8,128)S(1)} %get-tuple-element.71.own_ref, bf16[512,768]{1,0:T(8,128)(2,1)S(1)} %collective-permute-done.21.refs_0_, bf16[512,768]{1,0:T(8,128)(2,1)S(1)} %collective-permute-done.22.refs_1_), custom_call_target="tpu_custom_call" | custom-call | tf_op jit(solution)/shard_map/pallas_call | solution.py:535
  147.8 1.7 %collective-permute-start.23 = (bf16[64,4224]{1,0:T(8,128)(2,1)S(1)}, bf16[64,4224]{1,0:T(8,128)(2,1)S(1)}, u32[]{:S(2)}, u32[]{:S(2)}) collective-permute-start(bf16[64,4224]{1,0:T(8,128)(2,1)S(1)} %add_convert_fusion), channel_id=1, source_target_pairs={{0,4},{1,5},{2,0},{3,1},{4,6},{5,7},{6,2},{7,3},{8,12},{9,13},{10,... | collective-permute-start | bytes 1622024 | tf_op jit(solution)/shard_map/ppermute | solution.py:151
  149.5 10.3 %collective-permute-done.23.line_ref = bf16[64,4224]{1,0:T(8,128)(2,1)S(1)} collective-permute-done((bf16[64,4224]{1,0:T(8,128)(2,1)S(1)}, bf16[64,4224]{1,0:T(8,128)(2,1)S(1)}, u32[]{:S(2)}, u32[]{:S(2)}) %collective-permute-start.23) | collective-permute-done | bytes 540704 | tf_op jit(solution)/shard_map/ppermute | solution.py:151
  159.7 1.0 shard_map.131
  161.5 1.7 %shard_map.132 = f32[1,512,768]{2,1,0:T(8,128)} custom-call(f32[512,768]{1,0:T(8,128)S(1)} %get-tuple-element.82.own_ref, bf16[512,768]{1,0:T(8,128)(2,1)S(1)} %collective-permute-done.24.refs_0_), custom_call_target="tpu_custom_call" | custom-call | tf_op jit(solution)/shard_map/pallas_call | solution.py:535
  163.2 1.7 %shard_map.133 = f32[1,512,768]{2,1,0:T(8,128)} custom-call(f32[512,768]{1,0:T(8,128)S(1)} %get-tuple-element.84.own_ref, bf16[512,768]{1,0:T(8,128)(2,1)S(1)} %collective-permute-done.25.refs_0_), custom_call_target="tpu_custom_call" | custom-call | tf_op jit(solution)/shard_map/pallas_call | solution.py:535
  (56 shorter events, 6.7 us)
Async XLA Ops:
  0.6 2.1 %copy-start.4 = (bf16[1,512,768]{2,1,0:T(8,128)(2,1)S(1)}, bf16[1,512,768]{2,1,0:T(8,128)(2,1)}, u32[]{:S(2)}) copy-start(bf16[1,512,768]{2,1,0:T(8,128)(2,1)} %param.13) | copy-start | bytes 2359300
  0.6 2.1 %copy-start.5 = (bf16[1,512,768]{2,1,0:T(8,128)(2,1)S(1)}, bf16[1,512,768]{2,1,0:T(8,128)(2,1)}, u32[]{:S(2)}) copy-start(bf16[1,512,768]{2,1,0:T(8,128)(2,1)} %param.12) | copy-start | bytes 2359300
  2.8 7.6 %copy-start = (bf16[64,2048]{1,0:T(8,128)(2,1)S(1)}, bf16[64,2048]{1,0:T(8,128)(2,1)}, u32[]{:S(2)}) copy-start(bf16[64,2048]{1,0:T(8,128)(2,1)} %tokens_ref.1) | copy-start | bytes 786436
  2.8 7.6 %copy-start.1 = (bf16[64,2048]{1,0:T(8,128)(2,1)S(1)}, bf16[64,2048]{1,0:T(8,128)(2,1)}, u32[]{:S(2)}) copy-start(bf16[64,2048]{1,0:T(8,128)(2,1)} %cot_ref.1) | copy-start | bytes 786436
  2.8 7.6 %copy-start.2 = (s32[64,6]{0,1:T(8,128)S(1)}, s32[64,6]{0,1:T(8,128)}, u32[]{:S(2)}) copy-start(s32[64,6]{0,1:T(8,128)} %param.8) | copy-start | bytes 4612
  2.8 7.6 %copy-start.3 = (f32[64,6]{0,1:T(8,128)S(1)}, f32[64,6]{0,1:T(8,128)}, u32[]{:S(2)}) copy-start(f32[64,6]{0,1:T(8,128)} %param.9) | copy-start | bytes 4612
  5.8 57.4 %collective-permute-start.4 = (bf16[544,2304]{1,0:T(8,128)(2,1)S(1)}, bf16[544,2304]{1,0:T(8,128)(2,1)S(1)}, u32[]{:S(2)}, u32[]{:S(2)}) collective-permute-start(bf16[544,2304]{1,0:T(8,128)(2,1)S(1)} %get-tuple-element.90), channel_id=1, source_target_pairs={{0,16},{1,17},{2,18},{3,19},{4,20},{5,21},{6,22},{7,23},{8,24},{9,... | collective-permute-start | bytes 7520264 | tf_op jit(solution)/shard_map/ppermute | solution.py:151
  8.9 55.9 %collective-permute-start.3 = (bf16[544,2304]{1,0:T(8,128)(2,1)S(1)}, bf16[544,2304]{1,0:T(8,128)(2,1)S(1)}, u32[]{:S(2)}, u32[]{:S(2)}) collective-permute-start(bf16[544,2304]{1,0:T(8,128)(2,1)S(1)} %get-tuple-element.91.own_ref.refs_0_.refs_5_), channel_id=1, source_target_pairs={{0,8},{1,9},{2,10},{3,11},{4,12},{5,13},{6,14},{7,15},{8,0},{9,1},... | collective-permute-start | bytes 7520264 | tf_op jit(solution)/shard_map/ppermute | solution.py:151
  10.5 13.6 %collective-permute-start = (bf16[64,4224]{1,0:T(8,128)(2,1)S(1)}, bf16[64,4224]{1,0:T(8,128)(2,1)S(1)}, u32[]{:S(2)}, u32[]{:S(2)}) collective-permute-start(bf16[64,4224]{1,0:T(8,128)(2,1)S(1)} %shard_map.118), channel_id=1, source_target_pairs={{0,4},{1,5},{2,0},{3,1},{4,6},{5,7},{6,2},{7,3},{8,12},{9,13},{10,... | collective-permute-start | bytes 1622024 | tf_op jit(solution)/shard_map/ppermute | solution.py:151
  24.1 13.4 %collective-permute-start.1 = (bf16[64,4224]{1,0:T(8,128)(2,1)S(1)}, bf16[64,4224]{1,0:T(8,128)(2,1)S(1)}, u32[]{:S(2)}, u32[]{:S(2)}) collective-permute-start(bf16[64,4224]{1,0:T(8,128)(2,1)S(1)} %collective-permute-done), channel_id=1, source_target_pairs={{0,4},{1,5},{2,0},{3,1},{4,6},{5,7},{6,2},{7,3},{8,12},{9,13},{10,... | collective-permute-start | bytes 1622024 | tf_op jit(solution)/shard_map/ppermute | solution.py:151
  37.5 12.5 %collective-permute-start.2 = (bf16[64,4224]{1,0:T(8,128)(2,1)S(1)}, bf16[64,4224]{1,0:T(8,128)(2,1)S(1)}, u32[]{:S(2)}, u32[]{:S(2)}) collective-permute-start(bf16[64,4224]{1,0:T(8,128)(2,1)S(1)} %collective-permute-done.1), channel_id=1, source_target_pairs={{0,4},{1,5},{2,0},{3,1},{4,6},{5,7},{6,2},{7,3},{8,12},{9,13},{10,... | collective-permute-start | bytes 1622024 | tf_op jit(solution)/shard_map/ppermute | solution.py:151
  64.7 5.6 %collective-permute-start.5 = (bf16[256,4224]{1,0:T(8,128)(2,1)S(1)}, bf16[256,4224]{1,0:T(8,128)(2,1)S(1)}, u32[]{:S(2)}, u32[]{:S(2)}) collective-permute-start(bf16[256,4224]{1,0:T(8,128)(2,1)S(1)} %pad_maximum_fusion.3.own_rows.own_ref.refs_0_.refs_2_), channel_id=1, source_target_pairs={{0,1},{1,0},{2,3},{3,2},{4,5},{5,4},{6,7},{7,6},{8,9},{9,8},{10,11... | collective-permute-start | bytes 6488072 | tf_op jit(solution)/shard_map/ppermute | solution.py:151
  64.8 20.4 %collective-permute-start.7 = (bf16[256,1536]{1,0:T(8,128)(2,1)S(1)}, bf16[256,1536]{1,0:T(8,128)(2,1)S(1)}, u32[]{:S(2)}, u32[]{:S(2)}) collective-permute-start(bf16[256,1536]{1,0:T(8,128)(2,1)S(1)} %slice.105), channel_id=1, source_target_pairs={{0,8},{1,9},{2,10},{3,11},{4,12},{5,13},{6,14},{7,15},{8,0},{9,1},... | collective-permute-start | bytes 2359304 | tf_op jit(solution)/shard_map/ppermute | solution.py:151
  66.4 20.4 %collective-permute-start.6 = (bf16[256,1536]{1,0:T(8,128)(2,1)S(1)}, bf16[256,1536]{1,0:T(8,128)(2,1)S(1)}, u32[]{:S(2)}, u32[]{:S(2)}) collective-permute-start(bf16[256,1536]{1,0:T(8,128)(2,1)S(1)} %slice.104), channel_id=1, source_target_pairs={{0,16},{1,17},{2,18},{3,19},{4,20},{5,21},{6,22},{7,23},{8,24},{9,... | collective-permute-start | bytes 2359304 | tf_op jit(solution)/shard_map/ppermute | solution.py:151
  67.0 14.1 %collective-permute-start.10 = (bf16[64,2048]{1,0:T(8,128)(2,1)S(1)}, bf16[64,2048]{1,0:T(8,128)(2,1)S(1)}, u32[]{:S(2)}, u32[]{:S(2)}) collective-permute-start(bf16[64,2048]{1,0:T(8,128)(2,1)S(1)} %maximum_maximum_fusion), channel_id=1, source_target_pairs={{0,4},{1,5},{2,0},{3,1},{4,6},{5,7},{6,2},{7,3},{8,12},{9,13},{10,... | collective-permute-start | bytes 786440 | tf_op jit(solution)/shard_map/ppermute | solution.py:151
  69.7 23.5 %collective-permute-start.9 = (bf16[256,768]{1,0:T(8,128)(2,1)S(1)}, bf16[256,768]{1,0:T(8,128)(2,1)S(1)}, u32[]{:S(2)}, u32[]{:S(2)}) collective-permute-start(bf16[256,768]{1,0:T(8,128)(2,1)S(1)} %slice.107), channel_id=1, source_target_pairs={{0,8},{1,9},{2,10},{3,11},{4,12},{5,13},{6,14},{7,15},{8,0},{9,1},... | collective-permute-start | bytes 1179656 | tf_op jit(solution)/shard_map/ppermute | solution.py:151
  70.3 24.2 %collective-permute-start.8 = (bf16[256,768]{1,0:T(8,128)(2,1)S(1)}, bf16[256,768]{1,0:T(8,128)(2,1)S(1)}, u32[]{:S(2)}, u32[]{:S(2)}) collective-permute-start(bf16[256,768]{1,0:T(8,128)(2,1)S(1)} %slice.106), channel_id=1, source_target_pairs={{0,16},{1,17},{2,18},{3,19},{4,20},{5,21},{6,22},{7,23},{8,24},{9,... | collective-permute-start | bytes 1179656 | tf_op jit(solution)/shard_map/ppermute | solution.py:151
  81.1 13.4 %collective-permute-start.11 = (bf16[64,2048]{1,0:T(8,128)(2,1)S(1)}, bf16[64,2048]{1,0:T(8,128)(2,1)S(1)}, u32[]{:S(2)}, u32[]{:S(2)}) collective-permute-start(bf16[64,2048]{1,0:T(8,128)(2,1)S(1)} %collective-permute-done.10), channel_id=1, source_target_pairs={{0,4},{1,5},{2,0},{3,1},{4,6},{5,7},{6,2},{7,3},{8,12},{9,13},{10,... | collective-permute-start | bytes 786440 | tf_op jit(solution)/shard_map/ppermute | solution.py:151
  94.6 11.6 %collective-permute-start.12 = (bf16[256,768]{1,0:T(8,128)(2,1)S(1)}, bf16[256,768]{1,0:T(8,128)(2,1)S(1)}, u32[]{:S(2)}, u32[]{:S(2)}) collective-permute-start(bf16[256,768]{1,0:T(8,128)(2,1)S(1)} %get-tuple-element.56), channel_id=1, source_target_pairs={{0,8},{1,9},{2,10},{3,11},{4,12},{5,13},{6,14},{7,15},{8,0},{9,1},... | collective-permute-start | bytes 1179656 | tf_op jit(solution)/shard_map/ppermute | solution.py:151
  95.1 11.1 %collective-permute-start.13 = (bf16[256,768]{1,0:T(8,128)(2,1)S(1)}, bf16[256,768]{1,0:T(8,128)(2,1)S(1)}, u32[]{:S(2)}, u32[]{:S(2)}) collective-permute-start(bf16[256,768]{1,0:T(8,128)(2,1)S(1)} %get-tuple-element.57), channel_id=1, source_target_pairs={{0,16},{1,17},{2,18},{3,19},{4,20},{5,21},{6,22},{7,23},{8,24},{9,... | collective-permute-start | bytes 1179656 | tf_op jit(solution)/shard_map/ppermute | solution.py:151
  95.5 10.7 %collective-permute-start.14 = (bf16[64,2048]{1,0:T(8,128)(2,1)S(1)}, bf16[64,2048]{1,0:T(8,128)(2,1)S(1)}, u32[]{:S(2)}, u32[]{:S(2)}) collective-permute-start(bf16[64,2048]{1,0:T(8,128)(2,1)S(1)} %collective-permute-done.11), channel_id=1, source_target_pairs={{0,4},{1,5},{2,0},{3,1},{4,6},{5,7},{6,2},{7,3},{8,12},{9,13},{10,... | collective-permute-start | bytes 786440 | tf_op jit(solution)/shard_map/ppermute | solution.py:151
  106.4 7.7 %collective-permute-start.15 = (bf16[256,4224]{1,0:T(8,128)(2,1)S(1)}, bf16[256,4224]{1,0:T(8,128)(2,1)S(1)}, u32[]{:S(2)}, u32[]{:S(2)}) collective-permute-start(bf16[256,4224]{1,0:T(8,128)(2,1)S(1)} %slice.89), channel_id=1, source_target_pairs={{0,1},{1,0},{2,3},{3,2},{4,5},{5,4},{6,7},{7,6},{8,9},{9,8},{10,11... | collective-permute-start | bytes 6488072 | tf_op jit(solution)/shard_map/ppermute | solution.py:151
  106.5 6.2 %collective-permute-start.16 = (bf16[256,2048]{1,0:T(8,128)(2,1)S(1)}, bf16[256,2048]{1,0:T(8,128)(2,1)S(1)}, u32[]{:S(2)}, u32[]{:S(2)}) collective-permute-start(bf16[256,2048]{1,0:T(8,128)(2,1)S(1)} %pad_maximum_fusion.4.own_ref), channel_id=1, source_target_pairs={{0,1},{1,0},{2,3},{3,2},{4,5},{5,4},{6,7},{7,6},{8,9},{9,8},{10,11... | collective-permute-start | bytes 3145736 | tf_op jit(solution)/shard_map/ppermute | solution.py:151
  107.1 21.2 %collective-permute-start.18 = (bf16[512,768]{1,0:T(8,128)(2,1)S(1)}, bf16[512,768]{1,0:T(8,128)(2,1)S(1)}, u32[]{:S(2)}, u32[]{:S(2)}) collective-permute-start(bf16[512,768]{1,0:T(8,128)(2,1)S(1)} %get-tuple-element.63.d_gate_ref.term_ref), channel_id=1, source_target_pairs={{0,8},{1,9},{2,10},{3,11},{4,12},{5,13},{6,14},{7,15},{8,0},{9,1},... | collective-permute-start | bytes 2359304 | tf_op jit(solution)/shard_map/ppermute | solution.py:151
  108.6 20.4 %collective-permute-start.19 = (bf16[512,768]{1,0:T(8,128)(2,1)S(1)}, bf16[512,768]{1,0:T(8,128)(2,1)S(1)}, u32[]{:S(2)}, u32[]{:S(2)}) collective-permute-start(bf16[512,768]{1,0:T(8,128)(2,1)S(1)} %get-tuple-element.64.d_up_ref.term_ref), channel_id=1, source_target_pairs={{0,16},{1,17},{2,18},{3,19},{4,20},{5,21},{6,22},{7,23},{8,24},{9,... | collective-permute-start | bytes 2359304 | tf_op jit(solution)/shard_map/ppermute | solution.py:151
  114.2 13.8 %collective-permute-start.17 = (bf16[64,4224]{1,0:T(8,128)(2,1)S(1)}, bf16[64,4224]{1,0:T(8,128)(2,1)S(1)}, u32[]{:S(2)}, u32[]{:S(2)}) collective-permute-start(bf16[64,4224]{1,0:T(8,128)(2,1)S(1)} %add_convert_fusion.2), channel_id=1, source_target_pairs={{0,4},{1,5},{2,0},{3,1},{4,6},{5,7},{6,2},{7,3},{8,12},{9,13},{10,... | collective-permute-start | bytes 1622024 | tf_op jit(solution)/shard_map/ppermute | solution.py:151
  116.0 29.8 %collective-permute-start.22 = (bf16[512,768]{1,0:T(8,128)(2,1)S(1)}, bf16[512,768]{1,0:T(8,128)(2,1)S(1)}, u32[]{:S(2)}, u32[]{:S(2)}) collective-permute-start(bf16[512,768]{1,0:T(8,128)(2,1)S(1)} %pad_maximum_fusion.6), channel_id=1, source_target_pairs={{0,16},{1,17},{2,18},{3,19},{4,20},{5,21},{6,22},{7,23},{8,24},{9,... | collective-permute-start | bytes 2359304 | tf_op jit(solution)/shard_map/ppermute | solution.py:151
  117.2 28.7 %collective-permute-start.21 = (bf16[512,768]{1,0:T(8,128)(2,1)S(1)}, bf16[512,768]{1,0:T(8,128)(2,1)S(1)}, u32[]{:S(2)}, u32[]{:S(2)}) collective-permute-start(bf16[512,768]{1,0:T(8,128)(2,1)S(1)} %pad_maximum_fusion.5), channel_id=1, source_target_pairs={{0,8},{1,9},{2,10},{3,11},{4,12},{5,13},{6,14},{7,15},{8,0},{9,1},... | collective-permute-start | bytes 2359304 | tf_op jit(solution)/shard_map/ppermute | solution.py:151
  129.0 18.6 %collective-permute-start.20 = (bf16[64,4224]{1,0:T(8,128)(2,1)S(1)}, bf16[64,4224]{1,0:T(8,128)(2,1)S(1)}, u32[]{:S(2)}, u32[]{:S(2)}) collective-permute-start(bf16[64,4224]{1,0:T(8,128)(2,1)S(1)} %add_convert_fusion.1), channel_id=1, source_target_pairs={{0,4},{1,5},{2,0},{3,1},{4,6},{5,7},{6,2},{7,3},{8,12},{9,13},{10,... | collective-permute-start | bytes 1622024 | tf_op jit(solution)/shard_map/ppermute | solution.py:151
  133.4 29.8 %collective-permute-start.25 = (bf16[512,768]{1,0:T(8,128)(2,1)S(1)}, bf16[512,768]{1,0:T(8,128)(2,1)S(1)}, u32[]{:S(2)}, u32[]{:S(2)}) collective-permute-start(bf16[512,768]{1,0:T(8,128)(2,1)S(1)} %get-tuple-element.75), channel_id=1, source_target_pairs={{0,8},{1,9},{2,10},{3,11},{4,12},{5,13},{6,14},{7,15},{8,0},{9,1},... | collective-permute-start | bytes 2359304 | tf_op jit(solution)/shard_map/ppermute | solution.py:151
  137.4 24.1 %collective-permute-start.24 = (bf16[512,768]{1,0:T(8,128)(2,1)S(1)}, bf16[512,768]{1,0:T(8,128)(2,1)S(1)}, u32[]{:S(2)}, u32[]{:S(2)}) collective-permute-start(bf16[512,768]{1,0:T(8,128)(2,1)S(1)} %get-tuple-element.74), channel_id=1, source_target_pairs={{0,16},{1,17},{2,18},{3,19},{4,20},{5,21},{6,22},{7,23},{8,24},{9,... | collective-permute-start | bytes 2359304 | tf_op jit(solution)/shard_map/ppermute | solution.py:151
  147.8 12.0 %collective-permute-start.23 = (bf16[64,4224]{1,0:T(8,128)(2,1)S(1)}, bf16[64,4224]{1,0:T(8,128)(2,1)S(1)}, u32[]{:S(2)}, u32[]{:S(2)}) collective-permute-start(bf16[64,4224]{1,0:T(8,128)(2,1)S(1)} %add_convert_fusion), channel_id=1, source_target_pairs={{0,4},{1,5},{2,0},{3,1},{4,6},{5,7},{6,2},{7,3},{8,12},{9,13},{10,... | collective-permute-start | bytes 1622024 | tf_op jit(solution)/shard_map/ppermute | solution.py:151

commit v5 on v4

--- a/solution.py
+++ b/solution.py
@@ -208,19 +208,26 @@
     )(tokens, cotangent, expert_ids.T, gate_probs.T)
 
 
-def weights_and_rows(weights, tokens, blocks):
+def weights_and_rows(weights, tokens):
     rows, width = tokens.shape
     dp = lax.axis_index("dp")
+    weights = jnp.concatenate(weights, axis=1)
+    weights, tokens = lax.optimization_barrier((weights, tokens))
     columns = jnp.split(tokens, 4, axis=1)
-    wanted = jnp.concatenate([lax.select_n(dp ^ r, *columns) for r in blocks], axis=1)
-    wanted = jnp.concatenate([wanted[: rows // 2], wanted[rows // 2 :]], axis=1)
-    weights = jnp.concatenate(weights, axis=1)
     spare = weights.shape[1] - width
-    return jnp.concatenate([weights, jnp.pad(wanted, ((0, 0), (0, spare)))], axis=0)
-
-
-def side_rows(arrived, depth, width):
-    sides = arrived[depth:]
+
+    def wanted(blocks):
+        two = jnp.concatenate([lax.select_n(dp ^ r, *columns) for r in blocks], axis=1)
+        two = jnp.concatenate([two[: rows // 2], two[rows // 2 :]], axis=1)
+        return jnp.pad(two, ((0, 0), (0, spare)))
+
+    return (
+        jnp.concatenate([weights, wanted((1, 3))]),
+        jnp.concatenate([weights, wanted((2, 3))]),
+    )
+
+
+def side_rows(sides, width):
     return jnp.concatenate([sides[:, : width // 2], sides[:, width // 2 : width]])
 
 
@@ -504,41 +511,49 @@
     out_ref[:, 2 * width :] = dots_ref[...]
 
 
-def back_to_rows(scaled, d_gate, d_up, dots, direct, down, gate_up, width):
-    rows, units = scaled.shape
+def back_to_rows(half, scaled, d_gate, d_up, dots, direct, down, gate_up, width):
+    units = scaled.shape[1]
+    rows = scaled.shape[0] // 2
     depth = width // 4
-    term = pl.BlockSpec((TILE, units), lambda i: (i, 0))
+    term = pl.BlockSpec((rows, units), lambda i: (half, 0))
     corner = [pl.BlockSpec((depth // 2, n * units), lambda i: (0, 0)) for n in (1, 1, 2, 2)]
     return kernel_call(
         back_kernel,
         shape(rows, 2 * width + SIDE, BF16),
-        grid=(rows // TILE,),
+        grid=(1,),
         in_specs=[term] * 3
-        + [pl.BlockSpec((TILE, SIDE), lambda i: (i, 0))]
+        + [pl.BlockSpec((rows, SIDE), lambda i: (half, 0))]
         + [pl.BlockSpec((depth, units), lambda i: (0, 2))] * 3
         + corner[:2]
         + [pl.BlockSpec((depth, 2 * units), lambda i: (0, 0))] * 3
         + corner[2:],
-        out_specs=pl.BlockSpec((TILE, 2 * width + SIDE), lambda i: (i, 0)),
+        out_specs=pl.BlockSpec((rows, 2 * width + SIDE), lambda i: (0, 0)),
     )(scaled, d_gate, d_up, dots, *direct, *down, *direct, *gate_up)
 
 
-def total_kernel(own_ref, *refs):
-    others, out_ref = refs[:-1], refs[-1]
-    out_ref[0] = own_ref[...] + sum(other[...].astype(F32) for other in others)
-
-
-def total(own, *others):
-    block, units = own.shape
+def total_kernel(counts, *refs):
+    outs = refs[-len(counts) :]
+    for count, out_ref in zip(counts, outs):
+        terms, refs = refs[:count], refs[count:]
+        out_ref[0] = terms[0][...] + sum(term[...].astype(F32) for term in terms[1:])
+
+
+def totals(*groups):
+    block, units = groups[0][0].shape
     step = block // 4
     rows = pl.BlockSpec((step, units), lambda i: (i, 0))
-    return kernel_call(
-        total_kernel,
-        jax.ShapeDtypeStruct((1, block, units), F32),
+    counts = [len(group) for group in groups]
+
+    def body(*refs):
+        total_kernel(counts, *refs)
+
+    return kernel_call(
+        body,
+        (jax.ShapeDtypeStruct((1, block, units), F32),) * len(groups),
         grid=(block // step,),
-        in_specs=[rows] * (1 + len(others)),
-        out_specs=pl.BlockSpec((1, step, units), lambda i: (0, i, 0)),
-    )(own, *others)
+        in_specs=[rows] * sum(counts),
+        out_specs=(pl.BlockSpec((1, step, units), lambda i: (0, i, 0)),) * len(groups),
+    )(*[term for group in groups for term in group])
 
 
 def send_corner(from_x, from_y, columns, depth):
@@ -546,17 +561,15 @@
     return [send(from_x[:half, columns], TO_Y), send(from_y[half:depth, columns], TO_X)]
 
 
-def along_line(own, before_second=()):
+def along_line(own, before=((), (), ())):
     slots = [own]
-    for step in range(3):
-        moving = after(slots[-1], before_second) if step == 1 else slots[-1]
-        slots.append(send(moving, ALONG_Z))
+    for wait in before:
+        slots.append(send(after(slots[-1], *wait), ALONG_Z))
     return slots
 
 
-def from_both_cores(slots, before):
-    own_core = after(jnp.concatenate(slots), before)
-    return own_core, send(own_core, TO_CORE)
+def from_both_cores(own_core, before):
+    return own_core, send(after(own_core, before), TO_CORE)
 
 
 def send_down(for_x, for_y, from_x, from_y):
@@ -566,14 +579,13 @@
     return send(for_x.astype(BF16), TO_X), send(for_y.astype(BF16), TO_Y)
 
 
-def sum_over_experts(rows, before):
-    half = rows.shape[0] // 2
-    block = half // 4
-    arrived = send(rows[half:], TO_CORE)
+def sum_over_experts(own, other, before):
+    block = own.shape[0] // 4
+    arrived = send(other, TO_CORE)
     moving = 0.0
     for slot, wait in zip((1, 2, 3), before):
         at = slice(slot * block, (slot + 1) * block)
-        total = rows[at].astype(F32) + arrived[at].astype(F32) + moving
+        total = own[at].astype(F32) + arrived[at].astype(F32) + moving
         moving = send(after(total.astype(BF16), wait), ALONG_Z).astype(F32)
     return arrived, moving.astype(BF16)
 
@@ -588,46 +600,50 @@
 
     depth = gate_proj.shape[1]
     weights = (gate_proj[0], up_proj[0], down_proj[0])
-    to_x = weights_and_rows(weights, tokens, (1, 3))
-    to_y = weights_and_rows(weights, tokens, (2, 3))
+    to_x, to_y = weights_and_rows(weights, tokens)
     packed = pack(tokens, cotangent, expert_ids, gate_probs)
-    direct = [to_x, send(to_x, TO_X), send(to_y, TO_Y)]
-    whole = from_both_cores(along_line(packed), direct)
-    side = [side_rows(direct[2], depth, width), side_rows(direct[1], depth, width)]
+    from_x, from_y = send(to_x, TO_X), send(to_y, TO_Y)
+    direct = [to_x, from_x, from_y]
+    whole = from_both_cores(jnp.concatenate(along_line(packed)), (from_x, from_y))
+    side = [side_rows(from_y[depth:], width), side_rows(from_x[depth:], width)]
     gate_up_corner = send_corner(*direct[1:], slice(0, 2 * units), depth)
     down_corner = send_corner(*direct[1:], slice(2 * units, 3 * units), depth)
     early_gate_up = early_products(whole, direct, width, 0, 0, 2 * units)
     early_down = early_products(whole, direct, width, 1, 2 * units, units)
     turned = turn(whole, 14, lambda i: jnp.where(i < 6, i, i + 2))
-    extra = along_line(jnp.concatenate(side, axis=1), (early_gate_up, early_down, turned))
+    extra = along_line(
+        jnp.concatenate(side, axis=1), ((), (early_gate_up,), (early_down, turned))
+    )
     early_gate_up, early_down, turned, gate_up_corner = lax.optimization_barrier(
         (early_gate_up, early_down, turned, gate_up_corner)
     )
 
     scaled, for_gate, for_up, hidden = forward(whole, early_gate_up, gate_up_corner, width, units)
-    corner_sent = after(corner_grads(turned, 6, scaled, width), down_corner, extra[2])
+    corner_sent = corner_grads(turned, 6, scaled, width)
     corner_x, corner_y = send(corner_sent[0], TO_X), send(corner_sent[1], TO_Y)
     hidden, scaled = after((hidden, scaled), corner_sent)
     d_gate, d_up, dots = backward(whole, early_down, down_corner, for_gate, for_up, hidden, width)
     other_gate = send(d_gate, TO_X)
     other_up = send(d_up, TO_Y)
-    shares = back_to_rows(scaled, d_gate, d_up, dots, direct, down_corner, gate_up_corner, width)
-    scaled = after(scaled, shares)
+    back_terms = (scaled, d_gate, d_up, dots, direct, down_corner, gate_up_corner, width)
+    other_shares = back_to_rows(1, *back_terms)
+    own_shares = back_to_rows(0, *after(back_terms[:4], other_shares), *back_terms[4:])
+    scaled = after(scaled, other_shares)
     for_x, for_y, down_own = later_grads(turned, 6, scaled, width)
     down_back = send_down(for_x, for_y, corner_x, corner_y)
-    shares = after(shares, corner_x, corner_y, extra[3])
+    extra = jnp.concatenate(extra[:3] + [after(extra[3], down_corner)])
+    other_shares = after(other_shares, corner_x, corner_y, extra)
     other_turned = turn(from_both_cores(extra, corner_x), 8, lambda i: i)
     gate_away, gate_own = pair_grads(turned, 0, 2, other_turned, 4, d_gate, other_gate, width)
     gate_back = send(gate_away, TO_Y)
     up_away, up_own = pair_grads(turned, 0, 1, other_turned, 0, d_up, other_up, width)
     up_back = send(up_away, TO_X)
-    grad_down = total(down_own, *after(down_back, gate_away, up_away))
-    arrived, line = sum_over_experts(shares, (other_turned, (other_gate, other_up), grad_down))
-    outs = unpack(shares, arrived, line, expert_ids, width)
-    gate_back = after(gate_back, outs)
-    grad_gate = total(gate_own, gate_back)
-    up_back = after(up_back, grad_gate)
-    grad_up = total(up_own, up_back)
+    down_back = after(down_back, gate_away, up_away)
+    arrived, line = sum_over_experts(own_shares, other_shares, (other_turned, (other_gate, other_up), down_back))
+    (grad_down,) = totals((down_own, *down_back))
+    outs = unpack(own_shares, arrived, line, expert_ids, width)
+    gate_back, up_back = after((gate_back, up_back), outs, grad_down)
+    grad_gate, grad_up = totals((gate_own, gate_back), (up_own, up_back))
     return (*outs, grad_gate, grad_up, grad_down)
 
 

time: 165 us -> 156 us (0.945)
  waiting for transfers between devices: 81.1 us -> 73.9 us
  starting transfers between devices: 40.6 us -> 43.8 us
  other arithmetic: 6.08 us -> 3.22 us
  Pallas kernels: 35.7 us -> 33.9 us
    ppermute x26, waiting for transfers between devices: 81.1 us -> 73.9 us  [send(): return lax.ppermute(array, AXES, where)]
    ppermute x26, starting transfers between devices: 40.6 us -> 43.8 us  [send(): return lax.ppermute(array, AXES, where)]
    select_n x2, other arithmetic: 2.03 us -> 0.04 us  [wanted(): lax.select_n(dp ^ r, *columns)]
    pallas_call x4, Pallas kernels: 10.9 us -> 9.2 us  [the longest x2 5.29 us: back_to_rows(): kernel_call(back_kernel, shape(rows, 2 * width + SIDE, BF16), grid=(1,),...]
  transfers between devices with their start and end apart: 26 -> 26, of which waited for: 14 -> 15; matrix products, arithmetic and copies ran while one was open for 1% -> 1% of each run, Pallas kernels for 21% -> 20%
where the time goes in v5:
time: 156 us
  waiting for transfers between devices  73.9 us (47%)
  starting transfers between devices  43.8 us (28%)
  Pallas kernels  33.9 us (22%)
  other arithmetic  3.22 us (2%)
    ppermute x26, waiting for transfers between devices, send(): return lax.ppermute(array, AXES, where)  73.9 us
    ppermute x26, starting transfers between devices, send(): return lax.ppermute(array, AXES, where)  43.8 us
    pallas_call x2, Pallas kernels, early_products(): kernel_call(early_kernel, shape(2 * half, columns, F32), grid=(columns //...  6.3 us
    pallas_call x2, Pallas kernels, back_to_rows(): kernel_call(back_kernel, shape(rows, 2 * width + SIDE, BF16), grid=(1,),...  5.29 us
    pallas_call x2, Pallas kernels, pair_grads(): kernel_call(pair_grad_kernel, (shape(2 * half, units, BF16), shape(2 * ha...  4.99 us
    pallas_call x2, Pallas kernels, turn(): kernel_call(turn_kernel, shape(tiles * TILE, 2 * rows, BF16), grid=(tiles...  4.2 us
    pallas_call x2, Pallas kernels, totals(): kernel_call(body, (jax.ShapeDtypeStruct((1, block, units), F32),) * len(g...  3.9 us
  transfers between devices with their start and end apart: 26, of which 15 were waited for; matrix products, arithmetic and copies ran while one was open for 1% of the time, Pallas kernels for 20%

profile of v5, /device:TPU:0, one launch (start us, length us, event | category | flops | bytes accessed | tf_op | source)
XLA Modules:
  0.0 156.2 jit_solution(454477301001812684)
XLA Ops:
  0.7 1.8 %pad_maximum_fusion.2 = bf16[512,2304]{1,0:T(8,128)(2,1)S(1)} fusion(bf16[512,768]{1,0:T(8,128)(2,1)} %bitcast.9, bf16[512,768]{1,0:T(8,128)(2,1)} %bitcast.10, bf16[512,768]{1,0:T(8,128)(2,1)} %bitcast.11), kind=kLoop, calls=%fused_computation.2 | loop fusion | flops 7077888 | bytes 4718592 | tf_op jit(solution)/shard_map/concatenate | solution.py:214
  3.0 3.0 %collective-permute-start.4 = (bf16[544,2304]{1,0:T(8,128)(2,1)S(1)}, bf16[544,2304]{1,0:T(8,128)(2,1)S(1)}, u32[]{:S(2)}, u32[]{:S(2)}) collective-permute-start(bf16[544,2304]{1,0:T(8,128)(2,1)S(1)} %get-tuple-element.106), channel_id=1, source_target_pairs={{0,16},{1,17},{2,18},{3,19},{4,20},{5,21},{6,22},{7,23},{8,24},{9,... | collective-permute-start | bytes 7520264 | tf_op jit(solution)/shard_map/ppermute | solution.py:151
  6.0 1.5 collective-permute-start.3
  7.6 2.6 %collective-permute-start = (bf16[64,4224]{1,0:T(8,128)(2,1)S(1)}, bf16[64,4224]{1,0:T(8,128)(2,1)S(1)}, u32[]{:S(2)}, u32[]{:S(2)}) collective-permute-start(bf16[64,4224]{1,0:T(8,128)(2,1)S(1)} %shard_map.118), channel_id=1, source_target_pairs={{0,4},{1,5},{2,0},{3,1},{4,6},{5,7},{6,2},{7,3},{8,12},{9,13},{10,... | collective-permute-start | bytes 1622024 | tf_op jit(solution)/shard_map/ppermute | solution.py:151
  10.2 11.0 %collective-permute-done = bf16[64,4224]{1,0:T(8,128)(2,1)S(1)} collective-permute-done((bf16[64,4224]{1,0:T(8,128)(2,1)S(1)}, bf16[64,4224]{1,0:T(8,128)(2,1)S(1)}, u32[]{:S(2)}, u32[]{:S(2)}) %collective-permute-start) | collective-permute-done | bytes 540704 | tf_op jit(solution)/shard_map/ppermute | solution.py:151
  21.2 3.4 %collective-permute-start.1 = (bf16[64,4224]{1,0:T(8,128)(2,1)S(1)}, bf16[64,4224]{1,0:T(8,128)(2,1)S(1)}, u32[]{:S(2)}, u32[]{:S(2)}) collective-permute-start(bf16[64,4224]{1,0:T(8,128)(2,1)S(1)} %collective-permute-done), channel_id=1, source_target_pairs={{0,4},{1,5},{2,0},{3,1},{4,6},{5,7},{6,2},{7,3},{8,12},{9,13},{10,... | collective-permute-start | bytes 1622024 | tf_op jit(solution)/shard_map/ppermute | solution.py:151
  24.6 10.0 %collective-permute-done.1 = bf16[64,4224]{1,0:T(8,128)(2,1)S(1)} collective-permute-done((bf16[64,4224]{1,0:T(8,128)(2,1)S(1)}, bf16[64,4224]{1,0:T(8,128)(2,1)S(1)}, u32[]{:S(2)}, u32[]{:S(2)}) %collective-permute-start.1) | collective-permute-done | bytes 540704 | tf_op jit(solution)/shard_map/ppermute | solution.py:151
  34.6 3.4 %collective-permute-start.2 = (bf16[64,4224]{1,0:T(8,128)(2,1)S(1)}, bf16[64,4224]{1,0:T(8,128)(2,1)S(1)}, u32[]{:S(2)}, u32[]{:S(2)}) collective-permute-start(bf16[64,4224]{1,0:T(8,128)(2,1)S(1)} %collective-permute-done.1), channel_id=1, source_target_pairs={{0,4},{1,5},{2,0},{3,1},{4,6},{5,7},{6,2},{7,3},{8,12},{9,13},{10,... | collective-permute-start | bytes 1622024 | tf_op jit(solution)/shard_map/ppermute | solution.py:151
  38.0 9.1 %collective-permute-done.2 = bf16[64,4224]{1,0:T(8,128)(2,1)S(1)} collective-permute-done((bf16[64,4224]{1,0:T(8,128)(2,1)S(1)}, bf16[64,4224]{1,0:T(8,128)(2,1)S(1)}, u32[]{:S(2)}, u32[]{:S(2)}) %collective-permute-start.2) | collective-permute-done | bytes 540704 | tf_op jit(solution)/shard_map/ppermute | solution.py:151
  47.3 13.1 %collective-permute-done.4.y_ref.refs_2_.refs_7_ = bf16[544,2304]{1,0:T(8,128)(2,1)S(1)} collective-permute-done((bf16[544,2304]{1,0:T(8,128)(2,1)S(1)}, bf16[544,2304]{1,0:T(8,128)(2,1)S(1)}, u32[]{:S(2)}, u32[]{:S(2)}) %collective-permute-start.4) | collective-permute-done | bytes 2506784 | tf_op jit(solution)/shard_map/ppermute | solution.py:151
  60.4 1.5 collective-permute-done.3.x_ref.refs_1_.refs_6_
  61.9 1.6 collective-permute-start.7
  64.2 2.6 %collective-permute-start.12 = (bf16[64,2048]{1,0:T(8,128)(2,1)S(1)}, bf16[64,2048]{1,0:T(8,128)(2,1)S(1)}, u32[]{:S(2)}, u32[]{:S(2)}) collective-permute-start(bf16[64,2048]{1,0:T(8,128)(2,1)S(1)} %maximum_maximum_fusion), channel_id=1, source_target_pairs={{0,4},{1,5},{2,0},{3,1},{4,6},{5,7},{6,2},{7,3},{8,12},{9,13},{10,... | collective-permute-start | bytes 786440 | tf_op jit(solution)/shard_map/ppermute | solution.py:151
  66.8 4.2 %shard_map.119.refs_4_.refs_5_ = f32[512,1536]{1,0:T(8,128)S(1)} custom-call(bf16[256,4224]{1,0:T(8,128)(2,1)S(1)} %pad_maximum_fusion.3.own_rows.own_ref.refs_0_.refs_2_, bf16[256,4224]{1,0:T(8,128)(2,1)S(1)} %collective-permute-done.5.other_rows.other_ref.refs_1_.refs_3_, bf16[544,2304]{1,0:T(8,128)(2,1)S(1)} %get-tuple-element.107.own_ref.refs_0_.refs_5_, ...), custom_call_target="tpu_custom_call" | custom-call | tf_op jit(solution)/shard_map/pallas_call | solution.py:309
  71.0 1.5 collective-permute-done.12
  72.5 3.4 %collective-permute-start.13 = (bf16[64,2048]{1,0:T(8,128)(2,1)S(1)}, bf16[64,2048]{1,0:T(8,128)(2,1)S(1)}, u32[]{:S(2)}, u32[]{:S(2)}) collective-permute-start(bf16[64,2048]{1,0:T(8,128)(2,1)S(1)} %collective-permute-done.12), channel_id=1, source_target_pairs={{0,4},{1,5},{2,0},{3,1},{4,6},{5,7},{6,2},{7,3},{8,12},{9,13},{10,... | collective-permute-start | bytes 786440 | tf_op jit(solution)/shard_map/ppermute | solution.py:151
  76.5 1.6 %collective-permute-start.8 = (bf16[256,768]{1,0:T(8,128)(2,1)S(1)}, bf16[256,768]{1,0:T(8,128)(2,1)S(1)}, u32[]{:S(2)}, u32[]{:S(2)}) collective-permute-start(bf16[256,768]{1,0:T(8,128)(2,1)S(1)} %slice.102), channel_id=1, source_target_pairs={{0,16},{1,17},{2,18},{3,19},{4,20},{5,21},{6,22},{7,23},{8,24},{9,... | collective-permute-start | bytes 1179656 | tf_op jit(solution)/shard_map/ppermute | solution.py:151
  78.1 2.1 %shard_map.120.early_ref = f32[512,768]{1,0:T(8,128)S(1)} custom-call(bf16[256,4224]{1,0:T(8,128)(2,1)S(1)} %pad_maximum_fusion.3.own_rows.own_ref.refs_0_.refs_2_, bf16[256,4224]{1,0:T(8,128)(2,1)S(1)} %collective-permute-done.5.other_rows.other_ref.refs_1_.refs_3_, bf16[544,2304]{1,0:T(8,128)(2,1)S(1)} %get-tuple-element.107.own_ref.refs_0_.refs_5_, ...), custom_call_target="tpu_custom_call" | custom-call | tf_op jit(solution)/shard_map/pallas_call | solution.py:309
  80.3 2.8 %shard_map.121.turned_ref = bf16[3584,512]{1,0:T(8,128)(2,1)S(1)} custom-call(bf16[256,4224]{1,0:T(8,128)(2,1)S(1)} %pad_maximum_fusion.3.own_rows.own_ref.refs_0_.refs_2_, bf16[256,4224]{1,0:T(8,128)(2,1)S(1)} %collective-permute-done.5.other_rows.other_ref.refs_1_.refs_3_), custom_call_target="tpu_custom_call" | custom-call | tf_op jit(solution)/shard_map/pallas_call | solution.py:281
  83.1 0.9 collective-permute-start.14
  84.1 2.6 %shard_map.122 = (bf16[512,768]{1,0:T(8,128)(2,1)S(1)}, f32[512,768]{1,0:T(8,128)S(1)}, f32[512,768]{1,0:T(8,128)S(1)}, f32[512,768]{1,0:T(8,128)S(1)}) custom-call(bf16[256,4224]{1,0:T(8,128)(2,1)S(1)} %pad_maximum_fusion.3.own_rows.own_ref.refs_0_.refs_2_, bf16[256,4224]{1,0:T(8,128)(2,1)S(1)} %collective-permute-done.5.other_rows.other_ref.refs_1_.refs_3_, ...), custom_call_target="tpu_custom_call" | custom-call | tf_op jit(solution)/shard_map/pallas_call | solution.py:347
  86.7 0.8 shard_map.123
  87.5 1.4 collective-permute-start.10
  89.7 1.1 collective-permute-done.9.last_ref.refs_4_
  90.7 1.7 %collective-permute-done.8.first_ref.refs_3_ = bf16[256,768]{1,0:T(8,128)(2,1)S(1)} collective-permute-done((bf16[256,768]{1,0:T(8,128)(2,1)S(1)}, bf16[256,768]{1,0:T(8,128)(2,1)S(1)}, u32[]{:S(2)}, u32[]{:S(2)}) %collective-permute-start.8) | collective-permute-done | bytes 393248 | tf_op jit(solution)/shard_map/ppermute | solution.py:151
  92.4 2.1 %shard_map.124 = (bf16[512,768]{1,0:T(8,128)(2,1)S(1)}, bf16[512,768]{1,0:T(8,128)(2,1)S(1)}, bf16[512,128]{1,0:T(8,128)(2,1)S(1)}) custom-call(bf16[256,4224]{1,0:T(8,128)(2,1)S(1)} %pad_maximum_fusion.3.own_rows.own_ref.refs_0_.refs_2_, bf16[256,4224]{1,0:T(8,128)(2,1)S(1)} %collective-permute-done.5.other_rows.other_ref.refs_1_.refs_3_, ...), custom_call_target="tpu_custom_call" | custom-call | tf_op jit(solution)/shard_map/pallas_call | solution.py:388
  94.5 2.6 %shard_map.125 = bf16[256,4224]{1,0:T(8,128)(2,1)S(1)} custom-call(bf16[512,768]{1,0:T(8,128)(2,1)S(1)} %get-tuple-element.84.term_ref.scaled_ref, bf16[512,768]{1,0:T(8,128)(2,1)S(1)} %get-tuple-element.74.d_gate_ref.term_ref, bf16[512,768]{1,0:T(8,128)(2,1)S(1)} %get-tuple-element.75.d_up_ref.term_ref, bf16[512,128]{1,0:T(8,128)(2,1)S(1)} %get-tuple-element.76.dots_ref, ...), custom_call_target="tpu_custom_call" | custom-call | tf_op jit(solution)/shard_map/pallas_call | solution.py:520
  97.3 1.5 collective-permute-done.10
  98.8 1.3 collective-permute-done.11
  101.5 2.5 %shard_map.128 = (f32[512,768]{1,0:T(8,128)S(1)}, f32[512,768]{1,0:T(8,128)S(1)}, f32[512,768]{1,0:T(8,128)S(1)}) custom-call(bf16[3584,512]{1,0:T(8,128)(2,1)S(1)} %shard_map.121.turned_ref, bf16[512,768]{1,0:T(8,128)(2,1)S(1)} %get-tuple-element.84.term_ref.scaled_ref), custom_call_target="tpu_custom_call" | custom-call | tf_op jit(solution)/shard_map/pallas_call | solution.py:448
  104.2 2.6 %shard_map.126.own_ref = bf16[256,4224]{1,0:T(8,128)(2,1)S(1)} custom-call(bf16[512,768]{1,0:T(8,128)(2,1)S(1)} %get-tuple-element.84.term_ref.scaled_ref, bf16[512,768]{1,0:T(8,128)(2,1)S(1)} %get-tuple-element.74.d_gate_ref.term_ref, bf16[512,768]{1,0:T(8,128)(2,1)S(1)} %get-tuple-element.75.d_up_ref.term_ref, ...), custom_call_target="tpu_custom_call" | custom-call | tf_op jit(solution)/shard_map/pallas_call | solution.py:520
  106.8 1.4 shard_map.127.other_turned_ref
  108.3 2.8 %collective-permute-start.17 = (bf16[64,4224]{1,0:T(8,128)(2,1)S(1)}, bf16[64,4224]{1,0:T(8,128)(2,1)S(1)}, u32[]{:S(2)}, u32[]{:S(2)}) collective-permute-start(bf16[64,4224]{1,0:T(8,128)(2,1)S(1)} %add_convert_fusion.2), channel_id=1, source_target_pairs={{0,4},{1,5},{2,0},{3,1},{4,6},{5,7},{6,2},{7,3},{8,12},{9,13},{10,... | collective-permute-start | bytes 1622024 | tf_op jit(solution)/shard_map/ppermute | solution.py:151
  111.3 1.6 %collective-permute-start.22 = (bf16[512,768]{1,0:T(8,128)(2,1)S(1)}, bf16[512,768]{1,0:T(8,128)(2,1)S(1)}, u32[]{:S(2)}, u32[]{:S(2)}) collective-permute-start(bf16[512,768]{1,0:T(8,128)(2,1)S(1)} %pad_maximum_fusion.6), channel_id=1, source_target_pairs={{0,16},{1,17},{2,18},{3,19},{4,20},{5,21},{6,22},{7,23},{8,24},{9,... | collective-permute-start | bytes 2359304 | tf_op jit(solution)/shard_map/ppermute | solution.py:151
  113.0 1.6 collective-permute-start.21
  114.5 7.7 %collective-permute-done.17 = bf16[64,4224]{1,0:T(8,128)(2,1)S(1)} collective-permute-done((bf16[64,4224]{1,0:T(8,128)(2,1)S(1)}, bf16[64,4224]{1,0:T(8,128)(2,1)S(1)}, u32[]{:S(2)}, u32[]{:S(2)}) %collective-permute-start.17) | collective-permute-done | bytes 540704 | tf_op jit(solution)/shard_map/ppermute | solution.py:151
  122.5 3.4 %collective-permute-start.20 = (bf16[64,4224]{1,0:T(8,128)(2,1)S(1)}, bf16[64,4224]{1,0:T(8,128)(2,1)S(1)}, u32[]{:S(2)}, u32[]{:S(2)}) collective-permute-start(bf16[64,4224]{1,0:T(8,128)(2,1)S(1)} %add_convert_fusion.1), channel_id=1, source_target_pairs={{0,4},{1,5},{2,0},{3,1},{4,6},{5,7},{6,2},{7,3},{8,12},{9,13},{10,... | collective-permute-start | bytes 1622024 | tf_op jit(solution)/shard_map/ppermute | solution.py:151
  125.9 2.5 %shard_map.130 = (bf16[512,768]{1,0:T(8,128)(2,1)S(1)}, f32[512,768]{1,0:T(8,128)S(1)}) custom-call(bf16[3584,512]{1,0:T(8,128)(2,1)S(1)} %shard_map.121.turned_ref, bf16[2048,512]{1,0:T(8,128)(2,1)S(1)} %shard_map.127.other_turned_ref, bf16[512,768]{1,0:T(8,128)(2,1)S(1)} %get-tuple-element.75.d_up_ref.term_ref, ...), custom_call_target="tpu_custom_call" | custom-call | tf_op jit(solution)/shard_map/pallas_call | solution.py:486
  128.4 1.6 collective-permute-start.25
  130.0 2.5 %shard_map.129 = (bf16[512,768]{1,0:T(8,128)(2,1)S(1)}, f32[512,768]{1,0:T(8,128)S(1)}) custom-call(bf16[3584,512]{1,0:T(8,128)(2,1)S(1)} %shard_map.121.turned_ref, bf16[2048,512]{1,0:T(8,128)(2,1)S(1)} %shard_map.127.other_turned_ref, bf16[512,768]{1,0:T(8,128)(2,1)S(1)} %get-tuple-element.74.d_gate_ref.term_ref, ...), custom_call_target="tpu_custom_call" | custom-call | tf_op jit(solution)/shard_map/pallas_call | solution.py:486
  132.5 1.6 %collective-permute-start.24 = (bf16[512,768]{1,0:T(8,128)(2,1)S(1)}, bf16[512,768]{1,0:T(8,128)(2,1)S(1)}, u32[]{:S(2)}, u32[]{:S(2)}) collective-permute-start(bf16[512,768]{1,0:T(8,128)(2,1)S(1)} %get-tuple-element.87), channel_id=1, source_target_pairs={{0,16},{1,17},{2,18},{3,19},{4,20},{5,21},{6,22},{7,23},{8,24},{9,... | collective-permute-start | bytes 2359304 | tf_op jit(solution)/shard_map/ppermute | solution.py:151
  134.1 4.4 %collective-permute-done.22.refs_2_ = bf16[512,768]{1,0:T(8,128)(2,1)S(1)} collective-permute-done((bf16[512,768]{1,0:T(8,128)(2,1)S(1)}, bf16[512,768]{1,0:T(8,128)(2,1)S(1)}, u32[]{:S(2)}, u32[]{:S(2)}) %collective-permute-start.22) | collective-permute-done | bytes 786464 | tf_op jit(solution)/shard_map/ppermute | solution.py:151
  138.7 2.6 %collective-permute-start.23 = (bf16[64,4224]{1,0:T(8,128)(2,1)S(1)}, bf16[64,4224]{1,0:T(8,128)(2,1)S(1)}, u32[]{:S(2)}, u32[]{:S(2)}) collective-permute-start(bf16[64,4224]{1,0:T(8,128)(2,1)S(1)} %add_convert_fusion), channel_id=1, source_target_pairs={{0,4},{1,5},{2,0},{3,1},{4,6},{5,7},{6,2},{7,3},{8,12},{9,13},{10,... | collective-permute-start | bytes 1622024 | tf_op jit(solution)/shard_map/ppermute | solution.py:151
  141.3 1.8 %shard_map.132 = f32[1,512,768]{2,1,0:T(8,128)} custom-call(f32[512,768]{1,0:T(8,128)S(1)} %get-tuple-element.96.refs_0_, bf16[512,768]{1,0:T(8,128)(2,1)S(1)} %collective-permute-done.21.refs_1_, bf16[512,768]{1,0:T(8,128)(2,1)S(1)} %collective-permute-done.22.refs_2_), custom_call_target="tpu_custom_call" | custom-call | tf_op jit(solution)/shard_map/pallas_call | solution.py:550
  143.1 7.6 %collective-permute-done.23.line_ref = bf16[64,4224]{1,0:T(8,128)(2,1)S(1)} collective-permute-done((bf16[64,4224]{1,0:T(8,128)(2,1)S(1)}, bf16[64,4224]{1,0:T(8,128)(2,1)S(1)}, u32[]{:S(2)}, u32[]{:S(2)}) %collective-permute-start.23) | collective-permute-done | bytes 540704 | tf_op jit(solution)/shard_map/ppermute | solution.py:151
  150.6 1.0 shard_map.131
  151.6 2.2 %collective-permute-done.25.refs_3_ = bf16[512,768]{1,0:T(8,128)(2,1)S(1)} collective-permute-done((bf16[512,768]{1,0:T(8,128)(2,1)S(1)}, bf16[512,768]{1,0:T(8,128)(2,1)S(1)}, u32[]{:S(2)}, u32[]{:S(2)}) %collective-permute-start.25) | collective-permute-done | bytes 786464 | tf_op jit(solution)/shard_map/ppermute | solution.py:151
  154.0 2.2 %shard_map.133 = (f32[1,512,768]{2,1,0:T(8,128)}, f32[1,512,768]{2,1,0:T(8,128)}) custom-call(f32[512,768]{1,0:T(8,128)S(1)} %get-tuple-element.95.refs_0_, bf16[512,768]{1,0:T(8,128)(2,1)S(1)} %collective-permute-done.24.refs_1_, f32[512,768]{1,0:T(8,128)S(1)} %get-tuple-element.98.refs_2_, bf16[512,768]{1,0:T(8,128)(2,1)S(1)} %collective-permute-done.25.refs_3_), custom_call_target="tpu_custom_call" | custom-call | tf_op jit(solution)/shard_map/pallas_call | solution.py:550
  (52 shorter events, 5.5 us)
Async XLA Ops:
  0.7 1.8 %copy-start = (bf16[64,2048]{1,0:T(8,128)(2,1)S(1)}, bf16[64,2048]{1,0:T(8,128)(2,1)}, u32[]{:S(2)}) copy-start(bf16[64,2048]{1,0:T(8,128)(2,1)} %tokens_ref.1) | copy-start | bytes 786436
  2.6 4.9 %copy-start.1 = (bf16[64,2048]{1,0:T(8,128)(2,1)S(1)}, bf16[64,2048]{1,0:T(8,128)(2,1)}, u32[]{:S(2)}) copy-start(bf16[64,2048]{1,0:T(8,128)(2,1)} %cot_ref.1) | copy-start | bytes 786436
  2.6 4.9 %copy-start.2 = (s32[64,6]{0,1:T(8,128)S(1)}, s32[64,6]{0,1:T(8,128)}, u32[]{:S(2)}) copy-start(s32[64,6]{0,1:T(8,128)} %param.8) | copy-start | bytes 4612
  2.6 4.9 %copy-start.3 = (f32[64,6]{0,1:T(8,128)S(1)}, f32[64,6]{0,1:T(8,128)}, u32[]{:S(2)}) copy-start(f32[64,6]{0,1:T(8,128)} %param.9) | copy-start | bytes 4612
  3.0 57.4 %collective-permute-start.4 = (bf16[544,2304]{1,0:T(8,128)(2,1)S(1)}, bf16[544,2304]{1,0:T(8,128)(2,1)S(1)}, u32[]{:S(2)}, u32[]{:S(2)}) collective-permute-start(bf16[544,2304]{1,0:T(8,128)(2,1)S(1)} %get-tuple-element.106), channel_id=1, source_target_pairs={{0,16},{1,17},{2,18},{3,19},{4,20},{5,21},{6,22},{7,23},{8,24},{9,... | collective-permute-start | bytes 7520264 | tf_op jit(solution)/shard_map/ppermute | solution.py:151
  6.0 55.9 %collective-permute-start.3 = (bf16[544,2304]{1,0:T(8,128)(2,1)S(1)}, bf16[544,2304]{1,0:T(8,128)(2,1)S(1)}, u32[]{:S(2)}, u32[]{:S(2)}) collective-permute-start(bf16[544,2304]{1,0:T(8,128)(2,1)S(1)} %get-tuple-element.107.own_ref.refs_0_.refs_5_), channel_id=1, source_target_pairs={{0,8},{1,9},{2,10},{3,11},{4,12},{5,13},{6,14},{7,15},{8,0},{9,1},... | collective-permute-start | bytes 7520264 | tf_op jit(solution)/shard_map/ppermute | solution.py:151
  7.6 13.6 %collective-permute-start = (bf16[64,4224]{1,0:T(8,128)(2,1)S(1)}, bf16[64,4224]{1,0:T(8,128)(2,1)S(1)}, u32[]{:S(2)}, u32[]{:S(2)}) collective-permute-start(bf16[64,4224]{1,0:T(8,128)(2,1)S(1)} %shard_map.118), channel_id=1, source_target_pairs={{0,4},{1,5},{2,0},{3,1},{4,6},{5,7},{6,2},{7,3},{8,12},{9,13},{10,... | collective-permute-start | bytes 1622024 | tf_op jit(solution)/shard_map/ppermute | solution.py:151
  21.2 13.4 %collective-permute-start.1 = (bf16[64,4224]{1,0:T(8,128)(2,1)S(1)}, bf16[64,4224]{1,0:T(8,128)(2,1)S(1)}, u32[]{:S(2)}, u32[]{:S(2)}) collective-permute-start(bf16[64,4224]{1,0:T(8,128)(2,1)S(1)} %collective-permute-done), channel_id=1, source_target_pairs={{0,4},{1,5},{2,0},{3,1},{4,6},{5,7},{6,2},{7,3},{8,12},{9,13},{10,... | collective-permute-start | bytes 1622024 | tf_op jit(solution)/shard_map/ppermute | solution.py:151
  34.6 12.5 %collective-permute-start.2 = (bf16[64,4224]{1,0:T(8,128)(2,1)S(1)}, bf16[64,4224]{1,0:T(8,128)(2,1)S(1)}, u32[]{:S(2)}, u32[]{:S(2)}) collective-permute-start(bf16[64,4224]{1,0:T(8,128)(2,1)S(1)} %collective-permute-done.1), channel_id=1, source_target_pairs={{0,4},{1,5},{2,0},{3,1},{4,6},{5,7},{6,2},{7,3},{8,12},{9,13},{10,... | collective-permute-start | bytes 1622024 | tf_op jit(solution)/shard_map/ppermute | solution.py:151
  61.9 5.0 %collective-permute-start.5 = (bf16[256,4224]{1,0:T(8,128)(2,1)S(1)}, bf16[256,4224]{1,0:T(8,128)(2,1)S(1)}, u32[]{:S(2)}, u32[]{:S(2)}) collective-permute-start(bf16[256,4224]{1,0:T(8,128)(2,1)S(1)} %pad_maximum_fusion.3.own_rows.own_ref.refs_0_.refs_2_), channel_id=1, source_target_pairs={{0,1},{1,0},{2,3},{3,2},{4,5},{5,4},{6,7},{7,6},{8,9},{9,8},{10,11... | collective-permute-start | bytes 6488072 | tf_op jit(solution)/shard_map/ppermute | solution.py:151
  61.9 22.1 %collective-permute-start.7 = (bf16[256,1536]{1,0:T(8,128)(2,1)S(1)}, bf16[256,1536]{1,0:T(8,128)(2,1)S(1)}, u32[]{:S(2)}, u32[]{:S(2)}) collective-permute-start(bf16[256,1536]{1,0:T(8,128)(2,1)S(1)} %slice.101), channel_id=1, source_target_pairs={{0,8},{1,9},{2,10},{3,11},{4,12},{5,13},{6,14},{7,15},{8,0},{9,1},... | collective-permute-start | bytes 2359304 | tf_op jit(solution)/shard_map/ppermute | solution.py:151
  63.5 20.5 %collective-permute-start.6 = (bf16[256,1536]{1,0:T(8,128)(2,1)S(1)}, bf16[256,1536]{1,0:T(8,128)(2,1)S(1)}, u32[]{:S(2)}, u32[]{:S(2)}) collective-permute-start(bf16[256,1536]{1,0:T(8,128)(2,1)S(1)} %slice.100), channel_id=1, source_target_pairs={{0,16},{1,17},{2,18},{3,19},{4,20},{5,21},{6,22},{7,23},{8,24},{9,... | collective-permute-start | bytes 2359304 | tf_op jit(solution)/shard_map/ppermute | solution.py:151
  64.2 8.3 %collective-permute-start.12 = (bf16[64,2048]{1,0:T(8,128)(2,1)S(1)}, bf16[64,2048]{1,0:T(8,128)(2,1)S(1)}, u32[]{:S(2)}, u32[]{:S(2)}) collective-permute-start(bf16[64,2048]{1,0:T(8,128)(2,1)S(1)} %maximum_maximum_fusion), channel_id=1, source_target_pairs={{0,4},{1,5},{2,0},{3,1},{4,6},{5,7},{6,2},{7,3},{8,12},{9,13},{10,... | collective-permute-start | bytes 786440 | tf_op jit(solution)/shard_map/ppermute | solution.py:151
  72.5 10.6 %collective-permute-start.13 = (bf16[64,2048]{1,0:T(8,128)(2,1)S(1)}, bf16[64,2048]{1,0:T(8,128)(2,1)S(1)}, u32[]{:S(2)}, u32[]{:S(2)}) collective-permute-start(bf16[64,2048]{1,0:T(8,128)(2,1)S(1)} %collective-permute-done.12), channel_id=1, source_target_pairs={{0,4},{1,5},{2,0},{3,1},{4,6},{5,7},{6,2},{7,3},{8,12},{9,13},{10,... | collective-permute-start | bytes 786440 | tf_op jit(solution)/shard_map/ppermute | solution.py:151
  75.9 14.9 %collective-permute-start.9 = (bf16[256,768]{1,0:T(8,128)(2,1)S(1)}, bf16[256,768]{1,0:T(8,128)(2,1)S(1)}, u32[]{:S(2)}, u32[]{:S(2)}) collective-permute-start(bf16[256,768]{1,0:T(8,128)(2,1)S(1)} %slice.103), channel_id=1, source_target_pairs={{0,8},{1,9},{2,10},{3,11},{4,12},{5,13},{6,14},{7,15},{8,0},{9,1},... | collective-permute-start | bytes 1179656 | tf_op jit(solution)/shard_map/ppermute | solution.py:151
  76.5 15.9 %collective-permute-start.8 = (bf16[256,768]{1,0:T(8,128)(2,1)S(1)}, bf16[256,768]{1,0:T(8,128)(2,1)S(1)}, u32[]{:S(2)}, u32[]{:S(2)}) collective-permute-start(bf16[256,768]{1,0:T(8,128)(2,1)S(1)} %slice.102), channel_id=1, source_target_pairs={{0,16},{1,17},{2,18},{3,19},{4,20},{5,21},{6,22},{7,23},{8,24},{9,... | collective-permute-start | bytes 1179656 | tf_op jit(solution)/shard_map/ppermute | solution.py:151
  83.1 14.1 %collective-permute-start.14 = (bf16[64,2048]{1,0:T(8,128)(2,1)S(1)}, bf16[64,2048]{1,0:T(8,128)(2,1)S(1)}, u32[]{:S(2)}, u32[]{:S(2)}) collective-permute-start(bf16[64,2048]{1,0:T(8,128)(2,1)S(1)} %collective-permute-done.13), channel_id=1, source_target_pairs={{0,4},{1,5},{2,0},{3,1},{4,6},{5,7},{6,2},{7,3},{8,12},{9,13},{10,... | collective-permute-start | bytes 786440 | tf_op jit(solution)/shard_map/ppermute | solution.py:151
  87.5 11.3 %collective-permute-start.10 = (bf16[256,768]{1,0:T(8,128)(2,1)S(1)}, bf16[256,768]{1,0:T(8,128)(2,1)S(1)}, u32[]{:S(2)}, u32[]{:S(2)}) collective-permute-start(bf16[256,768]{1,0:T(8,128)(2,1)S(1)} %get-tuple-element.63), channel_id=1, source_target_pairs={{0,8},{1,9},{2,10},{3,11},{4,12},{5,13},{6,14},{7,15},{8,0},{9,1},... | collective-permute-start | bytes 1179656 | tf_op jit(solution)/shard_map/ppermute | solution.py:151
  88.9 11.2 %collective-permute-start.11 = (bf16[256,768]{1,0:T(8,128)(2,1)S(1)}, bf16[256,768]{1,0:T(8,128)(2,1)S(1)}, u32[]{:S(2)}, u32[]{:S(2)}) collective-permute-start(bf16[256,768]{1,0:T(8,128)(2,1)S(1)} %get-tuple-element.64), channel_id=1, source_target_pairs={{0,16},{1,17},{2,18},{3,19},{4,20},{5,21},{6,22},{7,23},{8,24},{9,... | collective-permute-start | bytes 1179656 | tf_op jit(solution)/shard_map/ppermute | solution.py:151
  100.1 8.1 %collective-permute-start.15 = (bf16[256,4224]{1,0:T(8,128)(2,1)S(1)}, bf16[256,4224]{1,0:T(8,128)(2,1)S(1)}, u32[]{:S(2)}, u32[]{:S(2)}) collective-permute-start(bf16[256,4224]{1,0:T(8,128)(2,1)S(1)} %shard_map.125), channel_id=1, source_target_pairs={{0,1},{1,0},{2,3},{3,2},{4,5},{5,4},{6,7},{7,6},{8,9},{9,8},{10,11... | collective-permute-start | bytes 6488072 | tf_op jit(solution)/shard_map/ppermute | solution.py:151
  100.1 6.7 %collective-permute-start.16 = (bf16[256,2048]{1,0:T(8,128)(2,1)S(1)}, bf16[256,2048]{1,0:T(8,128)(2,1)S(1)}, u32[]{:S(2)}, u32[]{:S(2)}) collective-permute-start(bf16[256,2048]{1,0:T(8,128)(2,1)S(1)} %pad_maximum_fusion.4.own_ref), channel_id=1, source_target_pairs={{0,1},{1,0},{2,3},{3,2},{4,5},{5,4},{6,7},{7,6},{8,9},{9,8},{10,11... | collective-permute-start | bytes 3145736 | tf_op jit(solution)/shard_map/ppermute | solution.py:151
  100.6 21.8 %collective-permute-start.18 = (bf16[512,768]{1,0:T(8,128)(2,1)S(1)}, bf16[512,768]{1,0:T(8,128)(2,1)S(1)}, u32[]{:S(2)}, u32[]{:S(2)}) collective-permute-start(bf16[512,768]{1,0:T(8,128)(2,1)S(1)} %get-tuple-element.74.d_gate_ref.term_ref), channel_id=1, source_target_pairs={{0,8},{1,9},{2,10},{3,11},{4,12},{5,13},{6,14},{7,15},{8,0},{9,1},... | collective-permute-start | bytes 2359304 | tf_op jit(solution)/shard_map/ppermute | solution.py:151
  101.2 21.3 %collective-permute-start.19 = (bf16[512,768]{1,0:T(8,128)(2,1)S(1)}, bf16[512,768]{1,0:T(8,128)(2,1)S(1)}, u32[]{:S(2)}, u32[]{:S(2)}) collective-permute-start(bf16[512,768]{1,0:T(8,128)(2,1)S(1)} %get-tuple-element.75.d_up_ref.term_ref), channel_id=1, source_target_pairs={{0,16},{1,17},{2,18},{3,19},{4,20},{5,21},{6,22},{7,23},{8,24},{9,... | collective-permute-start | bytes 2359304 | tf_op jit(solution)/shard_map/ppermute | solution.py:151
  108.3 13.9 %collective-permute-start.17 = (bf16[64,4224]{1,0:T(8,128)(2,1)S(1)}, bf16[64,4224]{1,0:T(8,128)(2,1)S(1)}, u32[]{:S(2)}, u32[]{:S(2)}) collective-permute-start(bf16[64,4224]{1,0:T(8,128)(2,1)S(1)} %add_convert_fusion.2), channel_id=1, source_target_pairs={{0,4},{1,5},{2,0},{3,1},{4,6},{5,7},{6,2},{7,3},{8,12},{9,13},{10,... | collective-permute-start | bytes 1622024 | tf_op jit(solution)/shard_map/ppermute | solution.py:151
  111.3 27.2 %collective-permute-start.22 = (bf16[512,768]{1,0:T(8,128)(2,1)S(1)}, bf16[512,768]{1,0:T(8,128)(2,1)S(1)}, u32[]{:S(2)}, u32[]{:S(2)}) collective-permute-start(bf16[512,768]{1,0:T(8,128)(2,1)S(1)} %pad_maximum_fusion.6), channel_id=1, source_target_pairs={{0,16},{1,17},{2,18},{3,19},{4,20},{5,21},{6,22},{7,23},{8,24},{9,... | collective-permute-start | bytes 2359304 | tf_op jit(solution)/shard_map/ppermute | solution.py:151
  113.0 25.5 %collective-permute-start.21 = (bf16[512,768]{1,0:T(8,128)(2,1)S(1)}, bf16[512,768]{1,0:T(8,128)(2,1)S(1)}, u32[]{:S(2)}, u32[]{:S(2)}) collective-permute-start(bf16[512,768]{1,0:T(8,128)(2,1)S(1)} %pad_maximum_fusion.5), channel_id=1, source_target_pairs={{0,8},{1,9},{2,10},{3,11},{4,12},{5,13},{6,14},{7,15},{8,0},{9,1},... | collective-permute-start | bytes 2359304 | tf_op jit(solution)/shard_map/ppermute | solution.py:151
  122.5 16.0 %collective-permute-start.20 = (bf16[64,4224]{1,0:T(8,128)(2,1)S(1)}, bf16[64,4224]{1,0:T(8,128)(2,1)S(1)}, u32[]{:S(2)}, u32[]{:S(2)}) collective-permute-start(bf16[64,4224]{1,0:T(8,128)(2,1)S(1)} %add_convert_fusion.1), channel_id=1, source_target_pairs={{0,4},{1,5},{2,0},{3,1},{4,6},{5,7},{6,2},{7,3},{8,12},{9,13},{10,... | collective-permute-start | bytes 1622024 | tf_op jit(solution)/shard_map/ppermute | solution.py:151
  128.4 25.4 %collective-permute-start.25 = (bf16[512,768]{1,0:T(8,128)(2,1)S(1)}, bf16[512,768]{1,0:T(8,128)(2,1)S(1)}, u32[]{:S(2)}, u32[]{:S(2)}) collective-permute-start(bf16[512,768]{1,0:T(8,128)(2,1)S(1)} %get-tuple-element.88), channel_id=1, source_target_pairs={{0,8},{1,9},{2,10},{3,11},{4,12},{5,13},{6,14},{7,15},{8,0},{9,1},... | collective-permute-start | bytes 2359304 | tf_op jit(solution)/shard_map/ppermute | solution.py:151
  132.5 21.6 %collective-permute-start.24 = (bf16[512,768]{1,0:T(8,128)(2,1)S(1)}, bf16[512,768]{1,0:T(8,128)(2,1)S(1)}, u32[]{:S(2)}, u32[]{:S(2)}) collective-permute-start(bf16[512,768]{1,0:T(8,128)(2,1)S(1)} %get-tuple-element.87), channel_id=1, source_target_pairs={{0,16},{1,17},{2,18},{3,19},{4,20},{5,21},{6,22},{7,23},{8,24},{9,... | collective-permute-start | bytes 2359304 | tf_op jit(solution)/shard_map/ppermute | solution.py:151
  138.7 12.0 %collective-permute-start.23 = (bf16[64,4224]{1,0:T(8,128)(2,1)S(1)}, bf16[64,4224]{1,0:T(8,128)(2,1)S(1)}, u32[]{:S(2)}, u32[]{:S(2)}) collective-permute-start(bf16[64,4224]{1,0:T(8,128)(2,1)S(1)} %add_convert_fusion), channel_id=1, source_target_pairs={{0,4},{1,5},{2,0},{3,1},{4,6},{5,7},{6,2},{7,3},{8,12},{9,13},{10,... | collective-permute-start | bytes 1622024 | tf_op jit(solution)/shard_map/ppermute | solution.py:151

commit v6 on v5

--- a/solution.py
+++ b/solution.py
@@ -540,7 +540,7 @@
 
 def totals(*groups):
     block, units = groups[0][0].shape
-    step = block // 4
+    step = block // 2
     rows = pl.BlockSpec((step, units), lambda i: (i, 0))
     counts = [len(group) for group in groups]
 
@@ -579,15 +579,25 @@
     return send(for_x.astype(BF16), TO_X), send(for_y.astype(BF16), TO_Y)
 
 
-def sum_over_experts(own, other, before):
+def swap_cores(own, other, before):
     block = own.shape[0] // 4
-    arrived = send(other, TO_CORE)
-    moving = 0.0
-    for slot, wait in zip((1, 2, 3), before):
-        at = slice(slot * block, (slot + 1) * block)
-        total = own[at].astype(F32) + arrived[at].astype(F32) + moving
-        moving = send(after(total.astype(BF16), wait), ALONG_Z).astype(F32)
-    return arrived, moving.astype(BF16)
+    second = send(after(other[block : 2 * block], before), TO_CORE)
+    third = send(other[2 * block : 3 * block], TO_CORE)
+    rest = send(jnp.concatenate([other[3 * block :], other[:block]]), TO_CORE)
+    first = (own[block : 2 * block].astype(F32) + second.astype(F32)).astype(BF16)
+    return first, third, rest
+
+
+def sum_along_line(own, swapped, before):
+    block = own.shape[0] // 4
+    moving, third, rest = swapped
+    for slot, wait in zip((2, 3, 0), before):
+        moving = send(after(moving, wait), ALONG_Z)
+        if slot:
+            piece = third if slot == 2 else rest[:block]
+            total = own[slot * block : (slot + 1) * block].astype(F32) + piece.astype(F32)
+            moving = (total + moving.astype(F32)).astype(BF16)
+    return rest[block:], moving
 
 
 def after(arrays, *others):
@@ -625,21 +635,23 @@
     d_gate, d_up, dots = backward(whole, early_down, down_corner, for_gate, for_up, hidden, width)
     other_gate = send(d_gate, TO_X)
     other_up = send(d_up, TO_Y)
+    extra = jnp.concatenate(extra[:3] + [after(extra[3], down_corner)])
     back_terms = (scaled, d_gate, d_up, dots, direct, down_corner, gate_up_corner, width)
-    other_shares = back_to_rows(1, *back_terms)
+    other_shares = back_to_rows(1, *after(back_terms[:4], extra), *back_terms[4:])
     own_shares = back_to_rows(0, *after(back_terms[:4], other_shares), *back_terms[4:])
-    scaled = after(scaled, other_shares)
+    swapped = swap_cores(own_shares, other_shares, (corner_x, corner_y))
+    scaled = after(scaled, swapped[0], swapped[2])
     for_x, for_y, down_own = later_grads(turned, 6, scaled, width)
     down_back = send_down(for_x, for_y, corner_x, corner_y)
-    extra = jnp.concatenate(extra[:3] + [after(extra[3], down_corner)])
-    other_shares = after(other_shares, corner_x, corner_y, extra)
     other_turned = turn(from_both_cores(extra, corner_x), 8, lambda i: i)
     gate_away, gate_own = pair_grads(turned, 0, 2, other_turned, 4, d_gate, other_gate, width)
     gate_back = send(gate_away, TO_Y)
     up_away, up_own = pair_grads(turned, 0, 1, other_turned, 0, d_up, other_up, width)
     up_back = send(up_away, TO_X)
     down_back = after(down_back, gate_away, up_away)
-    arrived, line = sum_over_experts(own_shares, other_shares, (other_turned, (other_gate, other_up), down_back))
+    arrived, line = sum_along_line(
+        own_shares, swapped, (other_turned, (other_gate, other_up), down_back)
+    )
     (grad_down,) = totals((down_own, *down_back))
     outs = unpack(own_shares, arrived, line, expert_ids, width)
     gate_back, up_back = after((gate_back, up_back), outs, grad_down)

time: 156 us -> 153 us (0.981)
  starting transfers between devices: 43.8 us -> 41.2 us
    ppermute x26 -> x28, starting transfers between devices: 43.8 us -> 41.2 us  [send(): return lax.ppermute(array, AXES, where)]
    ppermute x26 -> x28, waiting for transfers between devices: 73.9 us -> 73.6 us  [send(): return lax.ppermute(array, AXES, where)]
  transfers between devices with their start and end apart: 26 -> 28, of which waited for: 15 -> 14; matrix products, arithmetic and copies ran while one was open for 1% -> 1% of each run, Pallas kernels for 20% -> 20%
where the time goes in v6:
time: 153 us
  waiting for transfers between devices  73.6 us (48%)
  starting transfers between devices  41.2 us (27%)
  Pallas kernels  33.1 us (22%)
  other arithmetic  3.29 us (2%)
    ppermute x28, waiting for transfers between devices, send(): return lax.ppermute(array, AXES, where)  73.6 us
    ppermute x28, starting transfers between devices, send(): return lax.ppermute(array, AXES, where)  41.2 us
    pallas_call x2, Pallas kernels, early_products(): kernel_call(early_kernel, shape(2 * half, columns, F32), grid=(columns //...  6.3 us
    pallas_call x2, Pallas kernels, back_to_rows(): kernel_call(back_kernel, shape(rows, 2 * width + SIDE, BF16), grid=(1,),...  5.28 us
    pallas_call x2, Pallas kernels, pair_grads(): kernel_call(pair_grad_kernel, (shape(2 * half, units, BF16), shape(2 * ha...  4.99 us
    pallas_call x2, Pallas kernels, turn(): kernel_call(turn_kernel, shape(tiles * TILE, 2 * rows, BF16), grid=(tiles...  4.2 us
    pallas_call x2, Pallas kernels, totals(): kernel_call(body, (jax.ShapeDtypeStruct((1, block, units), F32),) * len(g...  3.08 us
  transfers between devices with their start and end apart: 28, of which 14 were waited for; matrix products, arithmetic and copies ran while one was open for 1% of the time, Pallas kernels for 20%

profile of v6, /device:TPU:0, one launch (start us, length us, event | category | flops | bytes accessed | tf_op | source)
XLA Modules:
  0.0 152.7 jit_solution(14671157378044437221)
XLA Ops:
  0.7 1.8 %pad_maximum_fusion.2 = bf16[512,2304]{1,0:T(8,128)(2,1)S(1)} fusion(bf16[512,768]{1,0:T(8,128)(2,1)} %bitcast.9, bf16[512,768]{1,0:T(8,128)(2,1)} %bitcast.10, bf16[512,768]{1,0:T(8,128)(2,1)} %bitcast.11), kind=kLoop, calls=%fused_computation.2 | loop fusion | flops 7077888 | bytes 4718592 | tf_op jit(solution)/shard_map/concatenate | solution.py:214
  3.0 3.0 %collective-permute-start.4 = (bf16[544,2304]{1,0:T(8,128)(2,1)S(1)}, bf16[544,2304]{1,0:T(8,128)(2,1)S(1)}, u32[]{:S(2)}, u32[]{:S(2)}) collective-permute-start(bf16[544,2304]{1,0:T(8,128)(2,1)S(1)} %get-tuple-element.114), channel_id=1, source_target_pairs={{0,16},{1,17},{2,18},{3,19},{4,20},{5,21},{6,22},{7,23},{8,24},{9,... | collective-permute-start | bytes 7520264 | tf_op jit(solution)/shard_map/ppermute | solution.py:151
  6.0 1.5 collective-permute-start.3
  7.6 2.6 %collective-permute-start = (bf16[64,4224]{1,0:T(8,128)(2,1)S(1)}, bf16[64,4224]{1,0:T(8,128)(2,1)S(1)}, u32[]{:S(2)}, u32[]{:S(2)}) collective-permute-start(bf16[64,4224]{1,0:T(8,128)(2,1)S(1)} %shard_map.118), channel_id=1, source_target_pairs={{0,4},{1,5},{2,0},{3,1},{4,6},{5,7},{6,2},{7,3},{8,12},{9,13},{10,... | collective-permute-start | bytes 1622024 | tf_op jit(solution)/shard_map/ppermute | solution.py:151
  10.2 11.0 %collective-permute-done = bf16[64,4224]{1,0:T(8,128)(2,1)S(1)} collective-permute-done((bf16[64,4224]{1,0:T(8,128)(2,1)S(1)}, bf16[64,4224]{1,0:T(8,128)(2,1)S(1)}, u32[]{:S(2)}, u32[]{:S(2)}) %collective-permute-start) | collective-permute-done | bytes 540704 | tf_op jit(solution)/shard_map/ppermute | solution.py:151
  21.2 3.4 %collective-permute-start.1 = (bf16[64,4224]{1,0:T(8,128)(2,1)S(1)}, bf16[64,4224]{1,0:T(8,128)(2,1)S(1)}, u32[]{:S(2)}, u32[]{:S(2)}) collective-permute-start(bf16[64,4224]{1,0:T(8,128)(2,1)S(1)} %collective-permute-done), channel_id=1, source_target_pairs={{0,4},{1,5},{2,0},{3,1},{4,6},{5,7},{6,2},{7,3},{8,12},{9,13},{10,... | collective-permute-start | bytes 1622024 | tf_op jit(solution)/shard_map/ppermute | solution.py:151
  24.6 10.0 %collective-permute-done.1 = bf16[64,4224]{1,0:T(8,128)(2,1)S(1)} collective-permute-done((bf16[64,4224]{1,0:T(8,128)(2,1)S(1)}, bf16[64,4224]{1,0:T(8,128)(2,1)S(1)}, u32[]{:S(2)}, u32[]{:S(2)}) %collective-permute-start.1) | collective-permute-done | bytes 540704 | tf_op jit(solution)/shard_map/ppermute | solution.py:151
  34.6 3.4 %collective-permute-start.2 = (bf16[64,4224]{1,0:T(8,128)(2,1)S(1)}, bf16[64,4224]{1,0:T(8,128)(2,1)S(1)}, u32[]{:S(2)}, u32[]{:S(2)}) collective-permute-start(bf16[64,4224]{1,0:T(8,128)(2,1)S(1)} %collective-permute-done.1), channel_id=1, source_target_pairs={{0,4},{1,5},{2,0},{3,1},{4,6},{5,7},{6,2},{7,3},{8,12},{9,13},{10,... | collective-permute-start | bytes 1622024 | tf_op jit(solution)/shard_map/ppermute | solution.py:151
  38.0 9.1 %collective-permute-done.2 = bf16[64,4224]{1,0:T(8,128)(2,1)S(1)} collective-permute-done((bf16[64,4224]{1,0:T(8,128)(2,1)S(1)}, bf16[64,4224]{1,0:T(8,128)(2,1)S(1)}, u32[]{:S(2)}, u32[]{:S(2)}) %collective-permute-start.2) | collective-permute-done | bytes 540704 | tf_op jit(solution)/shard_map/ppermute | solution.py:151
  47.3 13.1 %collective-permute-done.4.y_ref.refs_2_.refs_7_ = bf16[544,2304]{1,0:T(8,128)(2,1)S(1)} collective-permute-done((bf16[544,2304]{1,0:T(8,128)(2,1)S(1)}, bf16[544,2304]{1,0:T(8,128)(2,1)S(1)}, u32[]{:S(2)}, u32[]{:S(2)}) %collective-permute-start.4) | collective-permute-done | bytes 2506784 | tf_op jit(solution)/shard_map/ppermute | solution.py:151
  60.4 1.5 collective-permute-done.3.x_ref.refs_1_.refs_6_
  61.9 1.6 %collective-permute-start.7 = (bf16[256,1536]{1,0:T(8,128)(2,1)S(1)}, bf16[256,1536]{1,0:T(8,128)(2,1)S(1)}, u32[]{:S(2)}, u32[]{:S(2)}) collective-permute-start(bf16[256,1536]{1,0:T(8,128)(2,1)S(1)} %slice.113), channel_id=1, source_target_pairs={{0,8},{1,9},{2,10},{3,11},{4,12},{5,13},{6,14},{7,15},{8,0},{9,1},... | collective-permute-start | bytes 2359304 | tf_op jit(solution)/shard_map/ppermute | solution.py:151
  64.2 2.6 %collective-permute-start.10 = (bf16[64,2048]{1,0:T(8,128)(2,1)S(1)}, bf16[64,2048]{1,0:T(8,128)(2,1)S(1)}, u32[]{:S(2)}, u32[]{:S(2)}) collective-permute-start(bf16[64,2048]{1,0:T(8,128)(2,1)S(1)} %maximum_maximum_fusion), channel_id=1, source_target_pairs={{0,4},{1,5},{2,0},{3,1},{4,6},{5,7},{6,2},{7,3},{8,12},{9,13},{10,... | collective-permute-start | bytes 786440 | tf_op jit(solution)/shard_map/ppermute | solution.py:151
  66.8 4.2 %shard_map.119.refs_4_.refs_5_ = f32[512,1536]{1,0:T(8,128)S(1)} custom-call(bf16[256,4224]{1,0:T(8,128)(2,1)S(1)} %pad_maximum_fusion.3.own_rows.own_ref.refs_0_.refs_2_, bf16[256,4224]{1,0:T(8,128)(2,1)S(1)} %collective-permute-done.5.other_rows.other_ref.refs_1_.refs_3_, bf16[544,2304]{1,0:T(8,128)(2,1)S(1)} %get-tuple-element.115.own_ref.refs_0_.refs_5_, ...), custom_call_target="tpu_custom_call" | custom-call | tf_op jit(solution)/shard_map/pallas_call | solution.py:309
  71.0 1.5 collective-permute-done.10
  72.5 3.4 %collective-permute-start.11 = (bf16[64,2048]{1,0:T(8,128)(2,1)S(1)}, bf16[64,2048]{1,0:T(8,128)(2,1)S(1)}, u32[]{:S(2)}, u32[]{:S(2)}) collective-permute-start(bf16[64,2048]{1,0:T(8,128)(2,1)S(1)} %collective-permute-done.10), channel_id=1, source_target_pairs={{0,4},{1,5},{2,0},{3,1},{4,6},{5,7},{6,2},{7,3},{8,12},{9,13},{10,... | collective-permute-start | bytes 786440 | tf_op jit(solution)/shard_map/ppermute | solution.py:151
  76.5 1.6 %collective-permute-start.8 = (bf16[256,768]{1,0:T(8,128)(2,1)S(1)}, bf16[256,768]{1,0:T(8,128)(2,1)S(1)}, u32[]{:S(2)}, u32[]{:S(2)}) collective-permute-start(bf16[256,768]{1,0:T(8,128)(2,1)S(1)} %slice.114), channel_id=1, source_target_pairs={{0,16},{1,17},{2,18},{3,19},{4,20},{5,21},{6,22},{7,23},{8,24},{9,... | collective-permute-start | bytes 1179656 | tf_op jit(solution)/shard_map/ppermute | solution.py:151
  78.1 2.1 %shard_map.120.early_ref = f32[512,768]{1,0:T(8,128)S(1)} custom-call(bf16[256,4224]{1,0:T(8,128)(2,1)S(1)} %pad_maximum_fusion.3.own_rows.own_ref.refs_0_.refs_2_, bf16[256,4224]{1,0:T(8,128)(2,1)S(1)} %collective-permute-done.5.other_rows.other_ref.refs_1_.refs_3_, bf16[544,2304]{1,0:T(8,128)(2,1)S(1)} %get-tuple-element.115.own_ref.refs_0_.refs_5_, ...), custom_call_target="tpu_custom_call" | custom-call | tf_op jit(solution)/shard_map/pallas_call | solution.py:309
  80.3 2.8 %shard_map.121.turned_ref = bf16[3584,512]{1,0:T(8,128)(2,1)S(1)} custom-call(bf16[256,4224]{1,0:T(8,128)(2,1)S(1)} %pad_maximum_fusion.3.own_rows.own_ref.refs_0_.refs_2_, bf16[256,4224]{1,0:T(8,128)(2,1)S(1)} %collective-permute-done.5.other_rows.other_ref.refs_1_.refs_3_), custom_call_target="tpu_custom_call" | custom-call | tf_op jit(solution)/shard_map/pallas_call | solution.py:281
  83.1 0.9 collective-permute-start.12
  84.1 2.6 %shard_map.122 = (bf16[512,768]{1,0:T(8,128)(2,1)S(1)}, f32[512,768]{1,0:T(8,128)S(1)}, f32[512,768]{1,0:T(8,128)S(1)}, f32[512,768]{1,0:T(8,128)S(1)}) custom-call(bf16[256,4224]{1,0:T(8,128)(2,1)S(1)} %pad_maximum_fusion.3.own_rows.own_ref.refs_0_.refs_2_, bf16[256,4224]{1,0:T(8,128)(2,1)S(1)} %collective-permute-done.5.other_rows.other_ref.refs_1_.refs_3_, ...), custom_call_target="tpu_custom_call" | custom-call | tf_op jit(solution)/shard_map/pallas_call | solution.py:347
  86.7 0.8 shard_map.123
  87.5 1.4 collective-permute-start.15
  88.9 0.8 collective-permute-start.16
  89.6 1.1 collective-permute-done.9.last_ref.refs_4_
  90.7 1.7 %collective-permute-done.8.first_ref.refs_3_ = bf16[256,768]{1,0:T(8,128)(2,1)S(1)} collective-permute-done((bf16[256,768]{1,0:T(8,128)(2,1)S(1)}, bf16[256,768]{1,0:T(8,128)(2,1)S(1)}, u32[]{:S(2)}, u32[]{:S(2)}) %collective-permute-start.8) | collective-permute-done | bytes 393248 | tf_op jit(solution)/shard_map/ppermute | solution.py:151
  92.4 2.1 %shard_map.124 = (bf16[512,768]{1,0:T(8,128)(2,1)S(1)}, bf16[512,768]{1,0:T(8,128)(2,1)S(1)}, bf16[512,128]{1,0:T(8,128)(2,1)S(1)}) custom-call(bf16[256,4224]{1,0:T(8,128)(2,1)S(1)} %pad_maximum_fusion.3.own_rows.own_ref.refs_0_.refs_2_, bf16[256,4224]{1,0:T(8,128)(2,1)S(1)} %collective-permute-done.5.other_rows.other_ref.refs_1_.refs_3_, ...), custom_call_target="tpu_custom_call" | custom-call | tf_op jit(solution)/shard_map/pallas_call | solution.py:388
  94.5 0.6 collective-permute-start.20
  95.6 2.6 %shard_map.125 = bf16[256,4224]{1,0:T(8,128)(2,1)S(1)} custom-call(bf16[512,768]{1,0:T(8,128)(2,1)S(1)} %get-tuple-element.92.term_ref.scaled_ref, bf16[512,768]{1,0:T(8,128)(2,1)S(1)} %get-tuple-element.85.d_gate_ref.term_ref, bf16[512,768]{1,0:T(8,128)(2,1)S(1)} %get-tuple-element.86.d_up_ref.term_ref, bf16[512,128]{1,0:T(8,128)(2,1)S(1)} %get-tuple-element.87.dots_ref, ...), custom_call_target="tpu_custom_call" | custom-call | tf_op jit(solution)/shard_map/pallas_call | solution.py:520
  98.4 1.3 collective-permute-done.15
  99.6 1.3 collective-permute-done.16
  101.5 2.6 %shard_map.126.own_ref = bf16[256,4224]{1,0:T(8,128)(2,1)S(1)} custom-call(bf16[512,768]{1,0:T(8,128)(2,1)S(1)} %get-tuple-element.92.term_ref.scaled_ref, bf16[512,768]{1,0:T(8,128)(2,1)S(1)} %get-tuple-element.85.d_gate_ref.term_ref, bf16[512,768]{1,0:T(8,128)(2,1)S(1)} %get-tuple-element.86.d_up_ref.term_ref, ...), custom_call_target="tpu_custom_call" | custom-call | tf_op jit(solution)/shard_map/pallas_call | solution.py:520
  104.4 1.4 shard_map.127.other_turned_ref
  105.8 2.7 %collective-permute-start.19 = (bf16[64,4224]{1,0:T(8,128)(2,1)S(1)}, bf16[64,4224]{1,0:T(8,128)(2,1)S(1)}, u32[]{:S(2)}, u32[]{:S(2)}) collective-permute-start(bf16[64,4224]{1,0:T(8,128)(2,1)S(1)} %add_convert_fusion.2), channel_id=1, source_target_pairs={{0,4},{1,5},{2,0},{3,1},{4,6},{5,7},{6,2},{7,3},{8,12},{9,13},{10,... | collective-permute-start | bytes 1622024 | tf_op jit(solution)/shard_map/ppermute | solution.py:151
  108.5 2.5 %shard_map.128 = (f32[512,768]{1,0:T(8,128)S(1)}, f32[512,768]{1,0:T(8,128)S(1)}, f32[512,768]{1,0:T(8,128)S(1)}) custom-call(bf16[3584,512]{1,0:T(8,128)(2,1)S(1)} %shard_map.121.turned_ref, bf16[512,768]{1,0:T(8,128)(2,1)S(1)} %get-tuple-element.92.term_ref.scaled_ref), custom_call_target="tpu_custom_call" | custom-call | tf_op jit(solution)/shard_map/pallas_call | solution.py:448
  112.0 0.8 collective-permute-start.23
  112.8 7.8 %collective-permute-done.19 = bf16[64,4224]{1,0:T(8,128)(2,1)S(1)} collective-permute-done((bf16[64,4224]{1,0:T(8,128)(2,1)S(1)}, bf16[64,4224]{1,0:T(8,128)(2,1)S(1)}, u32[]{:S(2)}, u32[]{:S(2)}) %collective-permute-start.19) | collective-permute-done | bytes 540704 | tf_op jit(solution)/shard_map/ppermute | solution.py:151
  120.9 3.4 %collective-permute-start.22 = (bf16[64,4224]{1,0:T(8,128)(2,1)S(1)}, bf16[64,4224]{1,0:T(8,128)(2,1)S(1)}, u32[]{:S(2)}, u32[]{:S(2)}) collective-permute-start(bf16[64,4224]{1,0:T(8,128)(2,1)S(1)} %add_convert_fusion.1), channel_id=1, source_target_pairs={{0,4},{1,5},{2,0},{3,1},{4,6},{5,7},{6,2},{7,3},{8,12},{9,13},{10,... | collective-permute-start | bytes 1622024 | tf_op jit(solution)/shard_map/ppermute | solution.py:151
  124.3 2.5 %shard_map.130 = (bf16[512,768]{1,0:T(8,128)(2,1)S(1)}, f32[512,768]{1,0:T(8,128)S(1)}) custom-call(bf16[3584,512]{1,0:T(8,128)(2,1)S(1)} %shard_map.121.turned_ref, bf16[2048,512]{1,0:T(8,128)(2,1)S(1)} %shard_map.127.other_turned_ref, bf16[512,768]{1,0:T(8,128)(2,1)S(1)} %get-tuple-element.86.d_up_ref.term_ref, ...), custom_call_target="tpu_custom_call" | custom-call | tf_op jit(solution)/shard_map/pallas_call | solution.py:486
  126.8 0.8 collective-permute-start.27
  127.6 2.5 %shard_map.129 = (bf16[512,768]{1,0:T(8,128)(2,1)S(1)}, f32[512,768]{1,0:T(8,128)S(1)}) custom-call(bf16[3584,512]{1,0:T(8,128)(2,1)S(1)} %shard_map.121.turned_ref, bf16[2048,512]{1,0:T(8,128)(2,1)S(1)} %shard_map.127.other_turned_ref, bf16[512,768]{1,0:T(8,128)(2,1)S(1)} %get-tuple-element.85.d_gate_ref.term_ref, ...), custom_call_target="tpu_custom_call" | custom-call | tf_op jit(solution)/shard_map/pallas_call | solution.py:486
  130.7 3.9 %collective-permute-done.24.refs_2_ = bf16[512,768]{1,0:T(8,128)(2,1)S(1)} collective-permute-done((bf16[512,768]{1,0:T(8,128)(2,1)S(1)}, bf16[512,768]{1,0:T(8,128)(2,1)S(1)}, u32[]{:S(2)}, u32[]{:S(2)}) %collective-permute-start.24) | collective-permute-done | bytes 786464 | tf_op jit(solution)/shard_map/ppermute | solution.py:151
  134.6 1.1 collective-permute-done.22
  135.9 3.4 %collective-permute-start.25 = (bf16[64,4224]{1,0:T(8,128)(2,1)S(1)}, bf16[64,4224]{1,0:T(8,128)(2,1)S(1)}, u32[]{:S(2)}, u32[]{:S(2)}) collective-permute-start(bf16[64,4224]{1,0:T(8,128)(2,1)S(1)} %add_convert_fusion), channel_id=1, source_target_pairs={{0,4},{1,5},{2,0},{3,1},{4,6},{5,7},{6,2},{7,3},{8,12},{9,13},{10,... | collective-permute-start | bytes 1622024 | tf_op jit(solution)/shard_map/ppermute | solution.py:151
  139.4 1.3 shard_map.132
  140.7 9.2 %collective-permute-done.25.line_ref = bf16[64,4224]{1,0:T(8,128)(2,1)S(1)} collective-permute-done((bf16[64,4224]{1,0:T(8,128)(2,1)S(1)}, bf16[64,4224]{1,0:T(8,128)(2,1)S(1)}, u32[]{:S(2)}, u32[]{:S(2)}) %collective-permute-start.25) | collective-permute-done | bytes 540704 | tf_op jit(solution)/shard_map/ppermute | solution.py:151
  149.9 1.0 shard_map.131
  150.9 1.8 %shard_map.133 = (f32[1,512,768]{2,1,0:T(8,128)}, f32[1,512,768]{2,1,0:T(8,128)}) custom-call(f32[512,768]{1,0:T(8,128)S(1)} %get-tuple-element.103.refs_0_, bf16[512,768]{1,0:T(8,128)(2,1)S(1)} %collective-permute-done.26.refs_1_, f32[512,768]{1,0:T(8,128)S(1)} %get-tuple-element.106.refs_2_, bf16[512,768]{1,0:T(8,128)(2,1)S(1)} %collective-permute-done.27.refs_3_), custom_call_target="tpu_custom_call" | custom-call | tf_op jit(solution)/shard_map/pallas_call | solution.py:550
  (59 shorter events, 5.4 us)
Async XLA Ops:
  0.7 1.8 %copy-start = (bf16[64,2048]{1,0:T(8,128)(2,1)S(1)}, bf16[64,2048]{1,0:T(8,128)(2,1)}, u32[]{:S(2)}) copy-start(bf16[64,2048]{1,0:T(8,128)(2,1)} %tokens_ref.1) | copy-start | bytes 786436
  2.6 4.9 %copy-start.1 = (bf16[64,2048]{1,0:T(8,128)(2,1)S(1)}, bf16[64,2048]{1,0:T(8,128)(2,1)}, u32[]{:S(2)}) copy-start(bf16[64,2048]{1,0:T(8,128)(2,1)} %cot_ref.1) | copy-start | bytes 786436
  2.6 4.9 %copy-start.2 = (s32[64,6]{0,1:T(8,128)S(1)}, s32[64,6]{0,1:T(8,128)}, u32[]{:S(2)}) copy-start(s32[64,6]{0,1:T(8,128)} %param.8) | copy-start | bytes 4612
  2.6 4.9 %copy-start.3 = (f32[64,6]{0,1:T(8,128)S(1)}, f32[64,6]{0,1:T(8,128)}, u32[]{:S(2)}) copy-start(f32[64,6]{0,1:T(8,128)} %param.9) | copy-start | bytes 4612
  3.0 57.4 %collective-permute-start.4 = (bf16[544,2304]{1,0:T(8,128)(2,1)S(1)}, bf16[544,2304]{1,0:T(8,128)(2,1)S(1)}, u32[]{:S(2)}, u32[]{:S(2)}) collective-permute-start(bf16[544,2304]{1,0:T(8,128)(2,1)S(1)} %get-tuple-element.114), channel_id=1, source_target_pairs={{0,16},{1,17},{2,18},{3,19},{4,20},{5,21},{6,22},{7,23},{8,24},{9,... | collective-permute-start | bytes 7520264 | tf_op jit(solution)/shard_map/ppermute | solution.py:151
  6.0 55.9 %collective-permute-start.3 = (bf16[544,2304]{1,0:T(8,128)(2,1)S(1)}, bf16[544,2304]{1,0:T(8,128)(2,1)S(1)}, u32[]{:S(2)}, u32[]{:S(2)}) collective-permute-start(bf16[544,2304]{1,0:T(8,128)(2,1)S(1)} %get-tuple-element.115.own_ref.refs_0_.refs_5_), channel_id=1, source_target_pairs={{0,8},{1,9},{2,10},{3,11},{4,12},{5,13},{6,14},{7,15},{8,0},{9,1},... | collective-permute-start | bytes 7520264 | tf_op jit(solution)/shard_map/ppermute | solution.py:151
  7.6 13.6 %collective-permute-start = (bf16[64,4224]{1,0:T(8,128)(2,1)S(1)}, bf16[64,4224]{1,0:T(8,128)(2,1)S(1)}, u32[]{:S(2)}, u32[]{:S(2)}) collective-permute-start(bf16[64,4224]{1,0:T(8,128)(2,1)S(1)} %shard_map.118), channel_id=1, source_target_pairs={{0,4},{1,5},{2,0},{3,1},{4,6},{5,7},{6,2},{7,3},{8,12},{9,13},{10,... | collective-permute-start | bytes 1622024 | tf_op jit(solution)/shard_map/ppermute | solution.py:151
  21.2 13.4 %collective-permute-start.1 = (bf16[64,4224]{1,0:T(8,128)(2,1)S(1)}, bf16[64,4224]{1,0:T(8,128)(2,1)S(1)}, u32[]{:S(2)}, u32[]{:S(2)}) collective-permute-start(bf16[64,4224]{1,0:T(8,128)(2,1)S(1)} %collective-permute-done), channel_id=1, source_target_pairs={{0,4},{1,5},{2,0},{3,1},{4,6},{5,7},{6,2},{7,3},{8,12},{9,13},{10,... | collective-permute-start | bytes 1622024 | tf_op jit(solution)/shard_map/ppermute | solution.py:151
  34.6 12.5 %collective-permute-start.2 = (bf16[64,4224]{1,0:T(8,128)(2,1)S(1)}, bf16[64,4224]{1,0:T(8,128)(2,1)S(1)}, u32[]{:S(2)}, u32[]{:S(2)}) collective-permute-start(bf16[64,4224]{1,0:T(8,128)(2,1)S(1)} %collective-permute-done.1), channel_id=1, source_target_pairs={{0,4},{1,5},{2,0},{3,1},{4,6},{5,7},{6,2},{7,3},{8,12},{9,13},{10,... | collective-permute-start | bytes 1622024 | tf_op jit(solution)/shard_map/ppermute | solution.py:151
  61.9 5.0 %collective-permute-start.5 = (bf16[256,4224]{1,0:T(8,128)(2,1)S(1)}, bf16[256,4224]{1,0:T(8,128)(2,1)S(1)}, u32[]{:S(2)}, u32[]{:S(2)}) collective-permute-start(bf16[256,4224]{1,0:T(8,128)(2,1)S(1)} %pad_maximum_fusion.3.own_rows.own_ref.refs_0_.refs_2_), channel_id=1, source_target_pairs={{0,1},{1,0},{2,3},{3,2},{4,5},{5,4},{6,7},{7,6},{8,9},{9,8},{10,11... | collective-permute-start | bytes 6488072 | tf_op jit(solution)/shard_map/ppermute | solution.py:151
  61.9 22.1 %collective-permute-start.7 = (bf16[256,1536]{1,0:T(8,128)(2,1)S(1)}, bf16[256,1536]{1,0:T(8,128)(2,1)S(1)}, u32[]{:S(2)}, u32[]{:S(2)}) collective-permute-start(bf16[256,1536]{1,0:T(8,128)(2,1)S(1)} %slice.113), channel_id=1, source_target_pairs={{0,8},{1,9},{2,10},{3,11},{4,12},{5,13},{6,14},{7,15},{8,0},{9,1},... | collective-permute-start | bytes 2359304 | tf_op jit(solution)/shard_map/ppermute | solution.py:151
  63.5 20.5 %collective-permute-start.6 = (bf16[256,1536]{1,0:T(8,128)(2,1)S(1)}, bf16[256,1536]{1,0:T(8,128)(2,1)S(1)}, u32[]{:S(2)}, u32[]{:S(2)}) collective-permute-start(bf16[256,1536]{1,0:T(8,128)(2,1)S(1)} %slice.112), channel_id=1, source_target_pairs={{0,16},{1,17},{2,18},{3,19},{4,20},{5,21},{6,22},{7,23},{8,24},{9,... | collective-permute-start | bytes 2359304 | tf_op jit(solution)/shard_map/ppermute | solution.py:151
  64.2 8.3 %collective-permute-start.10 = (bf16[64,2048]{1,0:T(8,128)(2,1)S(1)}, bf16[64,2048]{1,0:T(8,128)(2,1)S(1)}, u32[]{:S(2)}, u32[]{:S(2)}) collective-permute-start(bf16[64,2048]{1,0:T(8,128)(2,1)S(1)} %maximum_maximum_fusion), channel_id=1, source_target_pairs={{0,4},{1,5},{2,0},{3,1},{4,6},{5,7},{6,2},{7,3},{8,12},{9,13},{10,... | collective-permute-start | bytes 786440 | tf_op jit(solution)/shard_map/ppermute | solution.py:151
  72.5 10.6 %collective-permute-start.11 = (bf16[64,2048]{1,0:T(8,128)(2,1)S(1)}, bf16[64,2048]{1,0:T(8,128)(2,1)S(1)}, u32[]{:S(2)}, u32[]{:S(2)}) collective-permute-start(bf16[64,2048]{1,0:T(8,128)(2,1)S(1)} %collective-permute-done.10), channel_id=1, source_target_pairs={{0,4},{1,5},{2,0},{3,1},{4,6},{5,7},{6,2},{7,3},{8,12},{9,13},{10,... | collective-permute-start | bytes 786440 | tf_op jit(solution)/shard_map/ppermute | solution.py:151
  75.9 14.9 %collective-permute-start.9 = (bf16[256,768]{1,0:T(8,128)(2,1)S(1)}, bf16[256,768]{1,0:T(8,128)(2,1)S(1)}, u32[]{:S(2)}, u32[]{:S(2)}) collective-permute-start(bf16[256,768]{1,0:T(8,128)(2,1)S(1)} %slice.115), channel_id=1, source_target_pairs={{0,8},{1,9},{2,10},{3,11},{4,12},{5,13},{6,14},{7,15},{8,0},{9,1},... | collective-permute-start | bytes 1179656 | tf_op jit(solution)/shard_map/ppermute | solution.py:151
  76.5 15.9 %collective-permute-start.8 = (bf16[256,768]{1,0:T(8,128)(2,1)S(1)}, bf16[256,768]{1,0:T(8,128)(2,1)S(1)}, u32[]{:S(2)}, u32[]{:S(2)}) collective-permute-start(bf16[256,768]{1,0:T(8,128)(2,1)S(1)} %slice.114), channel_id=1, source_target_pairs={{0,16},{1,17},{2,18},{3,19},{4,20},{5,21},{6,22},{7,23},{8,24},{9,... | collective-permute-start | bytes 1179656 | tf_op jit(solution)/shard_map/ppermute | solution.py:151
  83.1 12.4 %collective-permute-start.12 = (bf16[64,2048]{1,0:T(8,128)(2,1)S(1)}, bf16[64,2048]{1,0:T(8,128)(2,1)S(1)}, u32[]{:S(2)}, u32[]{:S(2)}) collective-permute-start(bf16[64,2048]{1,0:T(8,128)(2,1)S(1)} %collective-permute-done.11), channel_id=1, source_target_pairs={{0,4},{1,5},{2,0},{3,1},{4,6},{5,7},{6,2},{7,3},{8,12},{9,13},{10,... | collective-permute-start | bytes 786440 | tf_op jit(solution)/shard_map/ppermute | solution.py:151
  87.5 12.1 %collective-permute-start.15 = (bf16[256,768]{1,0:T(8,128)(2,1)S(1)}, bf16[256,768]{1,0:T(8,128)(2,1)S(1)}, u32[]{:S(2)}, u32[]{:S(2)}) collective-permute-start(bf16[256,768]{1,0:T(8,128)(2,1)S(1)} %get-tuple-element.67), channel_id=1, source_target_pairs={{0,8},{1,9},{2,10},{3,11},{4,12},{5,13},{6,14},{7,15},{8,0},{9,1},... | collective-permute-start | bytes 1179656 | tf_op jit(solution)/shard_map/ppermute | solution.py:151
  88.9 12.1 %collective-permute-start.16 = (bf16[256,768]{1,0:T(8,128)(2,1)S(1)}, bf16[256,768]{1,0:T(8,128)(2,1)S(1)}, u32[]{:S(2)}, u32[]{:S(2)}) collective-permute-start(bf16[256,768]{1,0:T(8,128)(2,1)S(1)} %get-tuple-element.68), channel_id=1, source_target_pairs={{0,16},{1,17},{2,18},{3,19},{4,20},{5,21},{6,22},{7,23},{8,24},{9,... | collective-permute-start | bytes 1179656 | tf_op jit(solution)/shard_map/ppermute | solution.py:151
  94.5 26.3 %collective-permute-start.20 = (bf16[512,768]{1,0:T(8,128)(2,1)S(1)}, bf16[512,768]{1,0:T(8,128)(2,1)S(1)}, u32[]{:S(2)}, u32[]{:S(2)}) collective-permute-start(bf16[512,768]{1,0:T(8,128)(2,1)S(1)} %get-tuple-element.85.d_gate_ref.term_ref), channel_id=1, source_target_pairs={{0,8},{1,9},{2,10},{3,11},{4,12},{5,13},{6,14},{7,15},{8,0},{9,1},... | collective-permute-start | bytes 2359304 | tf_op jit(solution)/shard_map/ppermute | solution.py:151
  95.1 25.7 %collective-permute-start.21 = (bf16[512,768]{1,0:T(8,128)(2,1)S(1)}, bf16[512,768]{1,0:T(8,128)(2,1)S(1)}, u32[]{:S(2)}, u32[]{:S(2)}) collective-permute-start(bf16[512,768]{1,0:T(8,128)(2,1)S(1)} %get-tuple-element.86.d_up_ref.term_ref), channel_id=1, source_target_pairs={{0,16},{1,17},{2,18},{3,19},{4,20},{5,21},{6,22},{7,23},{8,24},{9,... | collective-permute-start | bytes 2359304 | tf_op jit(solution)/shard_map/ppermute | solution.py:151
  99.6 4.8 %collective-permute-start.18 = (bf16[256,2048]{1,0:T(8,128)(2,1)S(1)}, bf16[256,2048]{1,0:T(8,128)(2,1)S(1)}, u32[]{:S(2)}, u32[]{:S(2)}) collective-permute-start(bf16[256,2048]{1,0:T(8,128)(2,1)S(1)} %pad_maximum_fusion.5.own_ref), channel_id=1, source_target_pairs={{0,1},{1,0},{2,3},{3,2},{4,5},{5,4},{6,7},{7,6},{8,9},{9,8},{10,11... | collective-permute-start | bytes 3145736 | tf_op jit(solution)/shard_map/ppermute | solution.py:151
  100.9 3.2 %collective-permute-start.17 = (bf16[64,4224]{1,0:T(8,128)(2,1)S(1)}, bf16[64,4224]{1,0:T(8,128)(2,1)S(1)}, u32[]{:S(2)}, u32[]{:S(2)}) collective-permute-start(bf16[64,4224]{1,0:T(8,128)(2,1)S(1)} %get-tuple-element.88), channel_id=1, source_target_pairs={{0,1},{1,0},{2,3},{3,2},{4,5},{5,4},{6,7},{7,6},{8,9},{9,8},{10,11... | collective-permute-start | bytes 1622024 | tf_op jit(solution)/shard_map/ppermute | solution.py:151
  100.9 11.0 %collective-permute-start.14 = (bf16[64,4224]{1,0:T(8,128)(2,1)S(1)}, bf16[64,4224]{1,0:T(8,128)(2,1)S(1)}, u32[]{:S(2)}, u32[]{:S(2)}) collective-permute-start(bf16[64,4224]{1,0:T(8,128)(2,1)S(1)} %get-tuple-element.116), channel_id=1, source_target_pairs={{0,1},{1,0},{2,3},{3,2},{4,5},{5,4},{6,7},{7,6},{8,9},{9,8},{10,11... | collective-permute-start | bytes 1622024 | tf_op jit(solution)/shard_map/ppermute | solution.py:151
  104.2 4.3 %collective-permute-start.13 = (bf16[128,4224]{1,0:T(8,128)(2,1)S(1)}, bf16[128,4224]{1,0:T(8,128)(2,1)S(1)}, u32[]{:S(2)}, u32[]{:S(2)}) collective-permute-start(bf16[128,4224]{1,0:T(8,128)(2,1)S(1)} %pad_maximum_fusion.4), channel_id=1, source_target_pairs={{0,1},{1,0},{2,3},{3,2},{4,5},{5,4},{6,7},{7,6},{8,9},{9,8},{10,11... | collective-permute-start | bytes 3244040 | tf_op jit(solution)/shard_map/ppermute | solution.py:151
  105.8 14.9 %collective-permute-start.19 = (bf16[64,4224]{1,0:T(8,128)(2,1)S(1)}, bf16[64,4224]{1,0:T(8,128)(2,1)S(1)}, u32[]{:S(2)}, u32[]{:S(2)}) collective-permute-start(bf16[64,4224]{1,0:T(8,128)(2,1)S(1)} %add_convert_fusion.2), channel_id=1, source_target_pairs={{0,4},{1,5},{2,0},{3,1},{4,6},{5,7},{6,2},{7,3},{8,12},{9,13},{10,... | collective-permute-start | bytes 1622024 | tf_op jit(solution)/shard_map/ppermute | solution.py:151
  111.3 23.4 %collective-permute-start.24 = (bf16[512,768]{1,0:T(8,128)(2,1)S(1)}, bf16[512,768]{1,0:T(8,128)(2,1)S(1)}, u32[]{:S(2)}, u32[]{:S(2)}) collective-permute-start(bf16[512,768]{1,0:T(8,128)(2,1)S(1)} %pad_maximum_fusion.7), channel_id=1, source_target_pairs={{0,16},{1,17},{2,18},{3,19},{4,20},{5,21},{6,22},{7,23},{8,24},{9,... | collective-permute-start | bytes 2359304 | tf_op jit(solution)/shard_map/ppermute | solution.py:151
  112.0 22.7 %collective-permute-start.23 = (bf16[512,768]{1,0:T(8,128)(2,1)S(1)}, bf16[512,768]{1,0:T(8,128)(2,1)S(1)}, u32[]{:S(2)}, u32[]{:S(2)}) collective-permute-start(bf16[512,768]{1,0:T(8,128)(2,1)S(1)} %pad_maximum_fusion.6), channel_id=1, source_target_pairs={{0,8},{1,9},{2,10},{3,11},{4,12},{5,13},{6,14},{7,15},{8,0},{9,1},... | collective-permute-start | bytes 2359304 | tf_op jit(solution)/shard_map/ppermute | solution.py:151
  120.9 14.8 %collective-permute-start.22 = (bf16[64,4224]{1,0:T(8,128)(2,1)S(1)}, bf16[64,4224]{1,0:T(8,128)(2,1)S(1)}, u32[]{:S(2)}, u32[]{:S(2)}) collective-permute-start(bf16[64,4224]{1,0:T(8,128)(2,1)S(1)} %add_convert_fusion.1), channel_id=1, source_target_pairs={{0,4},{1,5},{2,0},{3,1},{4,6},{5,7},{6,2},{7,3},{8,12},{9,13},{10,... | collective-permute-start | bytes 1622024 | tf_op jit(solution)/shard_map/ppermute | solution.py:151
  126.8 24.1 %collective-permute-start.27 = (bf16[512,768]{1,0:T(8,128)(2,1)S(1)}, bf16[512,768]{1,0:T(8,128)(2,1)S(1)}, u32[]{:S(2)}, u32[]{:S(2)}) collective-permute-start(bf16[512,768]{1,0:T(8,128)(2,1)S(1)} %get-tuple-element.96), channel_id=1, source_target_pairs={{0,8},{1,9},{2,10},{3,11},{4,12},{5,13},{6,14},{7,15},{8,0},{9,1},... | collective-permute-start | bytes 2359304 | tf_op jit(solution)/shard_map/ppermute | solution.py:151
  130.1 20.8 %collective-permute-start.26 = (bf16[512,768]{1,0:T(8,128)(2,1)S(1)}, bf16[512,768]{1,0:T(8,128)(2,1)S(1)}, u32[]{:S(2)}, u32[]{:S(2)}) collective-permute-start(bf16[512,768]{1,0:T(8,128)(2,1)S(1)} %get-tuple-element.95), channel_id=1, source_target_pairs={{0,16},{1,17},{2,18},{3,19},{4,20},{5,21},{6,22},{7,23},{8,24},{9,... | collective-permute-start | bytes 2359304 | tf_op jit(solution)/shard_map/ppermute | solution.py:151
  135.9 14.0 %collective-permute-start.25 = (bf16[64,4224]{1,0:T(8,128)(2,1)S(1)}, bf16[64,4224]{1,0:T(8,128)(2,1)S(1)}, u32[]{:S(2)}, u32[]{:S(2)}) collective-permute-start(bf16[64,4224]{1,0:T(8,128)(2,1)S(1)} %add_convert_fusion), channel_id=1, source_target_pairs={{0,4},{1,5},{2,0},{3,1},{4,6},{5,7},{6,2},{7,3},{8,12},{9,13},{10,... | collective-permute-start | bytes 1622024 | tf_op jit(solution)/shard_map/ppermute | solution.py:151

commit v7 on v6

--- a/solution.py
+++ b/solution.py
@@ -182,7 +182,7 @@
     return pl.ds(pl.multiple_of((lax.axis_index("dp") ^ relative) * block, block), block)
 
 
-def pack_kernel(tokens_ref, cot_ref, ids_ref, probs_ref, out_ref):
+def pack_kernel(tokens_ref, cot_ref, ids_ref, probs_ref, out_ref, for_x_ref, for_y_ref):
     rows, width = tokens_ref.shape
     block = width // 4
     for r in range(4):
@@ -196,39 +196,39 @@
     same = (iota(rows, rows, 0) == iota(rows, rows, 1)).astype(BF16)
     turned = lax.dot_general(same, exact_parts(prob, place), ACROSS, preferred_element_type=F32)
     out_ref[:, 2 * width :] = turned.astype(BF16)
-
-
-def pack(tokens, cotangent, expert_ids, gate_probs):
+    band = rows // 4
+    across = for_x_ref.shape[1] // block
+    for out, blocks in ((for_x_ref, (1, 3)), (for_y_ref, (2, 3))):
+        out[...] = jnp.zeros_like(out)
+        for index in range(8):
+            down, right = index // across * band, index % across * block
+            q = index // 2 * band
+            out[down : down + band, right : right + block] = tokens_ref[
+                q : q + band, block_at(blocks[index % 2], block)
+            ]
+
+
+def pack(tokens, cotangent, expert_ids, gate_probs, columns):
     rows, width = tokens.shape
+    across = columns // (width // 4)
+    side = shape(-(-8 // across) * (rows // 4), columns, BF16)
     return kernel_call(
         pack_kernel,
-        shape(rows, 2 * width + SIDE, BF16),
+        (shape(rows, 2 * width + SIDE, BF16), side, side),
         in_specs=[VMEM] * 4,
-        out_specs=VMEM,
+        out_specs=(VMEM,) * 3,
     )(tokens, cotangent, expert_ids.T, gate_probs.T)
 
 
-def weights_and_rows(weights, tokens):
-    rows, width = tokens.shape
-    dp = lax.axis_index("dp")
-    weights = jnp.concatenate(weights, axis=1)
-    weights, tokens = lax.optimization_barrier((weights, tokens))
-    columns = jnp.split(tokens, 4, axis=1)
-    spare = weights.shape[1] - width
-
-    def wanted(blocks):
-        two = jnp.concatenate([lax.select_n(dp ^ r, *columns) for r in blocks], axis=1)
-        two = jnp.concatenate([two[: rows // 2], two[rows // 2 :]], axis=1)
-        return jnp.pad(two, ((0, 0), (0, spare)))
-
-    return (
-        jnp.concatenate([weights, wanted((1, 3))]),
-        jnp.concatenate([weights, wanted((2, 3))]),
-    )
-
-
-def side_rows(sides, width):
-    return jnp.concatenate([sides[:, : width // 2], sides[:, width // 2 : width]])
+def side_rows(sides, rows, width):
+    band, block = rows // 4, width // 4
+    across = sides.shape[1] // block
+
+    def at(index):
+        down, right = index // across * band, index % across * block
+        return sides[down : down + band, right : right + block]
+
+    return jnp.concatenate([jnp.concatenate([at(2 * q), at(2 * q + 1)], axis=1) for q in range(4)])
 
 
 def unpack_kernel(own_ref, core_ref, line_ref, ids_ref, mixed_out, back_out, prob_out):
@@ -303,9 +303,9 @@
     out_ref[half:] = times_pieces(other_rows, (own_ref, x_ref, y_ref))
 
 
-def early_products(whole, direct, width, which, start, columns):
+def early_products(whole, direct, width, which, columns):
     half = whole[0].shape[0]
-    piece = pl.BlockSpec((width // 4, TILE), lambda j: (0, start // TILE + j))
+    piece = pl.BlockSpec((width // 4, TILE), lambda j: (0, j))
     return kernel_call(
         early_kernel,
         shape(2 * half, columns, F32),
@@ -511,24 +511,28 @@
     out_ref[:, 2 * width :] = dots_ref[...]
 
 
-def back_to_rows(half, scaled, d_gate, d_up, dots, direct, down, gate_up, width):
+def back_to_rows(half, scaled, d_gate, d_up, dots, downs, gate_ups, width):
     units = scaled.shape[1]
     rows = scaled.shape[0] // 2
     depth = width // 4
     term = pl.BlockSpec((rows, units), lambda i: (half, 0))
-    corner = [pl.BlockSpec((depth // 2, n * units), lambda i: (0, 0)) for n in (1, 1, 2, 2)]
+
+    def pieces(columns):
+        return [
+            pl.BlockSpec((part, columns), lambda i: (0, 0))
+            for part in (depth, depth, depth, depth // 2, depth // 2)
+        ]
+
     return kernel_call(
         back_kernel,
         shape(rows, 2 * width + SIDE, BF16),
         grid=(1,),
         in_specs=[term] * 3
         + [pl.BlockSpec((rows, SIDE), lambda i: (half, 0))]
-        + [pl.BlockSpec((depth, units), lambda i: (0, 2))] * 3
-        + corner[:2]
-        + [pl.BlockSpec((depth, 2 * units), lambda i: (0, 0))] * 3
-        + corner[2:],
+        + pieces(units)
+        + pieces(2 * units),
         out_specs=pl.BlockSpec((rows, 2 * width + SIDE), lambda i: (0, 0)),
-    )(scaled, d_gate, d_up, dots, *direct, *down, *direct, *gate_up)
+    )(scaled, d_gate, d_up, dots, *downs, *gate_ups)
 
 
 def total_kernel(counts, *refs):
@@ -556,9 +560,9 @@
     )(*[term for group in groups for term in group])
 
 
-def send_corner(from_x, from_y, columns, depth):
+def send_corner(from_x, from_y, depth):
     half = depth // 2
-    return [send(from_x[:half, columns], TO_Y), send(from_y[half:depth, columns], TO_X)]
+    return [send(from_x[:half], TO_Y), send(from_y[half:depth], TO_X)]
 
 
 def along_line(own, before=((), (), ())):
@@ -609,17 +613,21 @@
     units = gate_proj.shape[2]
 
     depth = gate_proj.shape[1]
-    weights = (gate_proj[0], up_proj[0], down_proj[0])
-    to_x, to_y = weights_and_rows(weights, tokens)
-    packed = pack(tokens, cotangent, expert_ids, gate_probs)
+    rows = tokens.shape[0]
+    down = [down_proj[0], send(down_proj[0], TO_X), send(down_proj[0], TO_Y)]
+    packed, for_x, for_y = pack(tokens, cotangent, expert_ids, gate_probs, 2 * units)
+    gate_up = jnp.concatenate([gate_proj[0], up_proj[0]], axis=1)
+    gate_up = lax.optimization_barrier(gate_up)
+    to_x, to_y = jnp.concatenate([gate_up, for_x]), jnp.concatenate([gate_up, for_y])
     from_x, from_y = send(to_x, TO_X), send(to_y, TO_Y)
     direct = [to_x, from_x, from_y]
-    whole = from_both_cores(jnp.concatenate(along_line(packed)), (from_x, from_y))
-    side = [side_rows(from_y[depth:], width), side_rows(from_x[depth:], width)]
-    gate_up_corner = send_corner(*direct[1:], slice(0, 2 * units), depth)
-    down_corner = send_corner(*direct[1:], slice(2 * units, 3 * units), depth)
-    early_gate_up = early_products(whole, direct, width, 0, 0, 2 * units)
-    early_down = early_products(whole, direct, width, 1, 2 * units, units)
+    line = along_line(packed, ((), (down,), ()))
+    whole = from_both_cores(jnp.concatenate(line), (from_x, from_y))
+    side = [side_rows(from_y[depth:], rows, width), side_rows(from_x[depth:], rows, width)]
+    gate_up_corner = send_corner(from_x, from_y, depth)
+    down_corner = send_corner(*down[1:], depth)
+    early_gate_up = early_products(whole, direct, width, 0, 2 * units)
+    early_down = early_products(whole, down, width, 1, units)
     turned = turn(whole, 14, lambda i: jnp.where(i < 6, i, i + 2))
     extra = along_line(
         jnp.concatenate(side, axis=1), ((), (early_gate_up,), (early_down, turned))
@@ -636,7 +644,8 @@
     other_gate = send(d_gate, TO_X)
     other_up = send(d_up, TO_Y)
     extra = jnp.concatenate(extra[:3] + [after(extra[3], down_corner)])
-    back_terms = (scaled, d_gate, d_up, dots, direct, down_corner, gate_up_corner, width)
+    pieces = (down + down_corner, direct + gate_up_corner)
+    back_terms = (scaled, d_gate, d_up, dots, *pieces, width)
     other_shares = back_to_rows(1, *after(back_terms[:4], extra), *back_terms[4:])
     own_shares = back_to_rows(0, *after(back_terms[:4], other_shares), *back_terms[4:])
     swapped = swap_cores(own_shares, other_shares, (corner_x, corner_y))

time: 153 us -> 151 us (0.987)
  waiting for transfers between devices: 73.6 us -> 67.1 us
  local copies, waits for them, and re-layouts: 0.47 us -> 3.93 us
    ppermute x28 -> x30, waiting for transfers between devices: 73.6 us -> 67.1 us  [send(): return lax.ppermute(array, AXES, where)]
    unnamed x8 -> x15, local copies, waits for them, and re-layouts: 0.02 us -> 3.42 us
    ppermute x28 -> x30, starting transfers between devices: 41.2 us -> 42.3 us  [send(): return lax.ppermute(array, AXES, where)]
  transfers between devices with their start and end apart: 28 -> 30, of which waited for: 14 -> 16; matrix products, arithmetic and copies ran while one was open for 1% -> 3% of each run, Pallas kernels for 20% -> 21%
where the time goes in v7:
time: 151 us
  waiting for transfers between devices  67.1 us (44%)
  starting transfers between devices  42.3 us (28%)
  Pallas kernels  33.1 us (22%)
  local copies, waits for them, and re-layouts  3.93 us (3%)
  other arithmetic  3.21 us (2%)
    ppermute x30, waiting for transfers between devices, send(): return lax.ppermute(array, AXES, where)  67.1 us
    ppermute x30, starting transfers between devices, send(): return lax.ppermute(array, AXES, where)  42.3 us
    pallas_call x2, Pallas kernels, early_products(): kernel_call(early_kernel, shape(2 * half, columns, F32), grid=(columns //...  6.3 us
    pallas_call x2, Pallas kernels, back_to_rows(): kernel_call(back_kernel, shape(rows, 2 * width + SIDE, BF16), grid=(1,),...  5.28 us
    pallas_call x2, Pallas kernels, pair_grads(): kernel_call(pair_grad_kernel, (shape(2 * half, units, BF16), shape(2 * ha...  4.99 us
    pallas_call x2, Pallas kernels, turn(): kernel_call(turn_kernel, shape(tiles * TILE, 2 * rows, BF16), grid=(tiles...  4.2 us
    unnamed x15, local copies, waits for them, and re-layouts  3.42 us
    pallas_call x2, Pallas kernels, totals(): kernel_call(body, (jax.ShapeDtypeStruct((1, block, units), F32),) * len(g...  3.08 us
  transfers between devices with their start and end apart: 30, of which 16 were waited for; matrix products, arithmetic and copies ran while one was open for 3% of the time, Pallas kernels for 21%

profile of v7, /device:TPU:0, one launch (start us, length us, event | category | flops | bytes accessed | tf_op | source)
XLA Modules:
  0.0 150.6 jit_solution(8443195597965751504)
XLA Ops:
  0.6 3.0 %collective-permute-start.2 = (bf16[512,768]{1,0:T(8,128)(2,1)}, bf16[512,768]{1,0:T(8,128)(2,1)S(1)}, u32[]{:S(2)}, u32[]{:S(2)}) collective-permute-start(bf16[512,768]{1,0:T(8,128)(2,1)} %bitcast.6), channel_id=1, source_target_pairs={{0,16},{1,17},{2,18},{3,19},{4,20},{5,21},{6,22},{7,23},{8,24},{9,... | collective-permute-start | bytes 2359304 | tf_op jit(solution)/shard_map/ppermute | solution.py:151
  3.7 1.5 collective-permute-start.1
  5.2 0.9 copy-done.1
  6.1 0.9 copy-done.2
  8.6 2.6 %collective-permute-start = (bf16[64,4224]{1,0:T(8,128)(2,1)S(1)}, bf16[64,4224]{1,0:T(8,128)(2,1)S(1)}, u32[]{:S(2)}, u32[]{:S(2)}) collective-permute-start(bf16[64,4224]{1,0:T(8,128)(2,1)S(1)} %get-tuple-element.60), channel_id=1, source_target_pairs={{0,4},{1,5},{2,0},{3,1},{4,6},{5,7},{6,2},{7,3},{8,12},{9,13},{10,... | collective-permute-start | bytes 1622024 | tf_op jit(solution)/shard_map/ppermute | solution.py:151
  11.2 1.5 pad_maximum_fusion.2
  14.0 8.1 %collective-permute-done = bf16[64,4224]{1,0:T(8,128)(2,1)S(1)} collective-permute-done((bf16[64,4224]{1,0:T(8,128)(2,1)S(1)}, bf16[64,4224]{1,0:T(8,128)(2,1)S(1)}, u32[]{:S(2)}, u32[]{:S(2)}) %collective-permute-start) | collective-permute-done | bytes 540704 | tf_op jit(solution)/shard_map/ppermute | solution.py:151
  22.2 2.1 %collective-permute-done.1.x_ref.refs_1_ = bf16[512,768]{1,0:T(8,128)(2,1)S(1)} collective-permute-done((bf16[512,768]{1,0:T(8,128)(2,1)}, bf16[512,768]{1,0:T(8,128)(2,1)S(1)}, u32[]{:S(2)}, u32[]{:S(2)}) %collective-permute-start.1) | collective-permute-done | bytes 786464 | tf_op jit(solution)/shard_map/ppermute | solution.py:151
  24.3 2.6 %collective-permute-start.3 = (bf16[64,4224]{1,0:T(8,128)(2,1)S(1)}, bf16[64,4224]{1,0:T(8,128)(2,1)S(1)}, u32[]{:S(2)}, u32[]{:S(2)}) collective-permute-start(bf16[64,4224]{1,0:T(8,128)(2,1)S(1)} %collective-permute-done), channel_id=1, source_target_pairs={{0,4},{1,5},{2,0},{3,1},{4,6},{5,7},{6,2},{7,3},{8,12},{9,13},{10,... | collective-permute-start | bytes 1622024 | tf_op jit(solution)/shard_map/ppermute | solution.py:151
  27.0 9.1 %collective-permute-done.3 = bf16[64,4224]{1,0:T(8,128)(2,1)S(1)} collective-permute-done((bf16[64,4224]{1,0:T(8,128)(2,1)S(1)}, bf16[64,4224]{1,0:T(8,128)(2,1)S(1)}, u32[]{:S(2)}, u32[]{:S(2)}) %collective-permute-start.3) | collective-permute-done | bytes 540704 | tf_op jit(solution)/shard_map/ppermute | solution.py:151
  36.0 3.3 %collective-permute-start.4 = (bf16[64,4224]{1,0:T(8,128)(2,1)S(1)}, bf16[64,4224]{1,0:T(8,128)(2,1)S(1)}, u32[]{:S(2)}, u32[]{:S(2)}) collective-permute-start(bf16[64,4224]{1,0:T(8,128)(2,1)S(1)} %collective-permute-done.3), channel_id=1, source_target_pairs={{0,4},{1,5},{2,0},{3,1},{4,6},{5,7},{6,2},{7,3},{8,12},{9,13},{10,... | collective-permute-start | bytes 1622024 | tf_op jit(solution)/shard_map/ppermute | solution.py:151
  39.4 8.0 %collective-permute-done.4 = bf16[64,4224]{1,0:T(8,128)(2,1)S(1)} collective-permute-done((bf16[64,4224]{1,0:T(8,128)(2,1)S(1)}, bf16[64,4224]{1,0:T(8,128)(2,1)S(1)}, u32[]{:S(2)}, u32[]{:S(2)}) %collective-permute-start.4) | collective-permute-done | bytes 540704 | tf_op jit(solution)/shard_map/ppermute | solution.py:151
  47.4 10.8 %collective-permute-done.6.y_ref.refs_7_ = bf16[560,1536]{1,0:T(8,128)(2,1)S(1)} collective-permute-done((bf16[560,1536]{1,0:T(8,128)(2,1)S(1)}, bf16[560,1536]{1,0:T(8,128)(2,1)S(1)}, u32[]{:S(2)}, u32[]{:S(2)}) %collective-permute-start.6) | collective-permute-done | bytes 1720352 | tf_op jit(solution)/shard_map/ppermute | solution.py:151
  58.3 1.5 collective-permute-done.5.x_ref.refs_6_
  59.8 1.6 %collective-permute-start.9 = (bf16[256,1536]{1,0:T(8,128)(2,1)S(1)}, bf16[256,1536]{1,0:T(8,128)(2,1)S(1)}, u32[]{:S(2)}, u32[]{:S(2)}) collective-permute-start(bf16[256,1536]{1,0:T(8,128)(2,1)S(1)} %slice.123), channel_id=1, source_target_pairs={{0,8},{1,9},{2,10},{3,11},{4,12},{5,13},{6,14},{7,15},{8,0},{9,1},... | collective-permute-start | bytes 2359304 | tf_op jit(solution)/shard_map/ppermute | solution.py:151
  62.0 2.6 %collective-permute-start.12 = (bf16[64,2048]{1,0:T(8,128)(2,1)S(1)}, bf16[64,2048]{1,0:T(8,128)(2,1)S(1)}, u32[]{:S(2)}, u32[]{:S(2)}) collective-permute-start(bf16[64,2048]{1,0:T(8,128)(2,1)S(1)} %maximum_maximum_fusion), channel_id=1, source_target_pairs={{0,4},{1,5},{2,0},{3,1},{4,6},{5,7},{6,2},{7,3},{8,12},{9,13},{10,... | collective-permute-start | bytes 786440 | tf_op jit(solution)/shard_map/ppermute | solution.py:151
  64.7 4.2 %shard_map.119.refs_4_.refs_5_ = f32[512,1536]{1,0:T(8,128)S(1)} custom-call(bf16[256,4224]{1,0:T(8,128)(2,1)S(1)} %constant_dynamic-update-slice_fusion.own_rows.own_ref.refs_0_.refs_2_, bf16[256,4224]{1,0:T(8,128)(2,1)S(1)} %collective-permute-done.7.other_rows.other_ref.refs_1_.refs_3_, bf16[560,1536]{1,0:T(8,128)(2,1)S(1)} %get-tuple-element.129.own_ref.refs_5_, ...), custom_call_target="tpu_custom_call" | custom-call | tf_op jit(solution)/shard_map/pallas_call | solution.py:309
  68.9 1.5 collective-permute-done.12
  70.4 3.4 %collective-permute-start.13 = (bf16[64,2048]{1,0:T(8,128)(2,1)S(1)}, bf16[64,2048]{1,0:T(8,128)(2,1)S(1)}, u32[]{:S(2)}, u32[]{:S(2)}) collective-permute-start(bf16[64,2048]{1,0:T(8,128)(2,1)S(1)} %collective-permute-done.12), channel_id=1, source_target_pairs={{0,4},{1,5},{2,0},{3,1},{4,6},{5,7},{6,2},{7,3},{8,12},{9,13},{10,... | collective-permute-start | bytes 786440 | tf_op jit(solution)/shard_map/ppermute | solution.py:151
  74.4 1.6 %collective-permute-start.10 = (bf16[256,768]{1,0:T(8,128)(2,1)S(1)}, bf16[256,768]{1,0:T(8,128)(2,1)S(1)}, u32[]{:S(2)}, u32[]{:S(2)}) collective-permute-start(bf16[256,768]{1,0:T(8,128)(2,1)S(1)} %slice.124), channel_id=1, source_target_pairs={{0,16},{1,17},{2,18},{3,19},{4,20},{5,21},{6,22},{7,23},{8,24},{9,... | collective-permute-start | bytes 1179656 | tf_op jit(solution)/shard_map/ppermute | solution.py:151
  76.0 2.1 %shard_map.120.early_ref = f32[512,768]{1,0:T(8,128)S(1)} custom-call(bf16[256,4224]{1,0:T(8,128)(2,1)S(1)} %constant_dynamic-update-slice_fusion.own_rows.own_ref.refs_0_.refs_2_, bf16[256,4224]{1,0:T(8,128)(2,1)S(1)} %collective-permute-done.7.other_rows.other_ref.refs_1_.refs_3_, bf16[512,768]{1,0:T(8,128)(2,1)S(1)} %bitcast.8, ...), custom_call_target="tpu_custom_call" | custom-call | tf_op jit(solution)/shard_map/pallas_call | solution.py:309
  78.1 2.8 %shard_map.121.turned_ref = bf16[3584,512]{1,0:T(8,128)(2,1)S(1)} custom-call(bf16[256,4224]{1,0:T(8,128)(2,1)S(1)} %constant_dynamic-update-slice_fusion.own_rows.own_ref.refs_0_.refs_2_, bf16[256,4224]{1,0:T(8,128)(2,1)S(1)} %collective-permute-done.7.other_rows.other_ref.refs_1_.refs_3_), custom_call_target="tpu_custom_call" | custom-call | tf_op jit(solution)/shard_map/pallas_call | solution.py:281
  81.0 0.9 collective-permute-start.14
  82.0 2.6 %shard_map.122 = (bf16[512,768]{1,0:T(8,128)(2,1)S(1)}, f32[512,768]{1,0:T(8,128)S(1)}, f32[512,768]{1,0:T(8,128)S(1)}, f32[512,768]{1,0:T(8,128)S(1)}) custom-call(bf16[256,4224]{1,0:T(8,128)(2,1)S(1)} %constant_dynamic-update-slice_fusion.own_rows.own_ref.refs_0_.refs_2_, bf16[256,4224]{1,0:T(8,128)(2,1)S(1)} %collective-permute-done.7.other_rows.other_ref.refs_1_.refs_3_, ...), custom_call_target="tpu_custom_call" | custom-call | tf_op jit(solution)/shard_map/pallas_call | solution.py:347
  84.6 0.8 shard_map.123
  85.4 1.3 collective-permute-start.17
  87.5 1.1 collective-permute-done.11.last_ref.refs_4_
  88.6 1.6 %collective-permute-done.10.first_ref.refs_3_ = bf16[256,768]{1,0:T(8,128)(2,1)S(1)} collective-permute-done((bf16[256,768]{1,0:T(8,128)(2,1)S(1)}, bf16[256,768]{1,0:T(8,128)(2,1)S(1)}, u32[]{:S(2)}, u32[]{:S(2)}) %collective-permute-start.10) | collective-permute-done | bytes 393248 | tf_op jit(solution)/shard_map/ppermute | solution.py:151
  90.3 2.1 %shard_map.124 = (bf16[512,768]{1,0:T(8,128)(2,1)S(1)}, bf16[512,768]{1,0:T(8,128)(2,1)S(1)}, bf16[512,128]{1,0:T(8,128)(2,1)S(1)}) custom-call(bf16[256,4224]{1,0:T(8,128)(2,1)S(1)} %constant_dynamic-update-slice_fusion.own_rows.own_ref.refs_0_.refs_2_, bf16[256,4224]{1,0:T(8,128)(2,1)S(1)} %collective-permute-done.7.other_rows.other_ref.refs_1_.refs_3_, ...), custom_call_target="tpu_custom_call" | custom-call | tf_op jit(solution)/shard_map/pallas_call | solution.py:388
  94.0 2.6 %shard_map.125 = bf16[256,4224]{1,0:T(8,128)(2,1)S(1)} custom-call(bf16[512,768]{1,0:T(8,128)(2,1)S(1)} %get-tuple-element.96.term_ref.scaled_ref, bf16[512,768]{1,0:T(8,128)(2,1)S(1)} %get-tuple-element.89.d_gate_ref.term_ref, bf16[512,768]{1,0:T(8,128)(2,1)S(1)} %get-tuple-element.90.d_up_ref.term_ref, bf16[512,128]{1,0:T(8,128)(2,1)S(1)} %get-tuple-element.91.dots_ref, ...), custom_call_target="tpu_custom_call" | custom-call | tf_op jit(solution)/shard_map/pallas_call | solution.py:526
  97.5 1.3 collective-permute-done.18
  99.3 2.6 %shard_map.126.own_ref = bf16[256,4224]{1,0:T(8,128)(2,1)S(1)} custom-call(bf16[512,768]{1,0:T(8,128)(2,1)S(1)} %get-tuple-element.96.term_ref.scaled_ref, bf16[512,768]{1,0:T(8,128)(2,1)S(1)} %get-tuple-element.89.d_gate_ref.term_ref, bf16[512,768]{1,0:T(8,128)(2,1)S(1)} %get-tuple-element.90.d_up_ref.term_ref, ...), custom_call_target="tpu_custom_call" | custom-call | tf_op jit(solution)/shard_map/pallas_call | solution.py:526
  102.3 1.4 shard_map.127.other_turned_ref
  103.7 2.7 %collective-permute-start.21 = (bf16[64,4224]{1,0:T(8,128)(2,1)S(1)}, bf16[64,4224]{1,0:T(8,128)(2,1)S(1)}, u32[]{:S(2)}, u32[]{:S(2)}) collective-permute-start(bf16[64,4224]{1,0:T(8,128)(2,1)S(1)} %add_convert_fusion.2), channel_id=1, source_target_pairs={{0,4},{1,5},{2,0},{3,1},{4,6},{5,7},{6,2},{7,3},{8,12},{9,13},{10,... | collective-permute-start | bytes 1622024 | tf_op jit(solution)/shard_map/ppermute | solution.py:151
  106.4 2.5 %shard_map.128 = (f32[512,768]{1,0:T(8,128)S(1)}, f32[512,768]{1,0:T(8,128)S(1)}, f32[512,768]{1,0:T(8,128)S(1)}) custom-call(bf16[3584,512]{1,0:T(8,128)(2,1)S(1)} %shard_map.121.turned_ref, bf16[512,768]{1,0:T(8,128)(2,1)S(1)} %get-tuple-element.96.term_ref.scaled_ref), custom_call_target="tpu_custom_call" | custom-call | tf_op jit(solution)/shard_map/pallas_call | solution.py:448
  109.9 1.4 collective-permute-start.25
  111.3 7.3 %collective-permute-done.21 = bf16[64,4224]{1,0:T(8,128)(2,1)S(1)} collective-permute-done((bf16[64,4224]{1,0:T(8,128)(2,1)S(1)}, bf16[64,4224]{1,0:T(8,128)(2,1)S(1)}, u32[]{:S(2)}, u32[]{:S(2)}) %collective-permute-start.21) | collective-permute-done | bytes 540704 | tf_op jit(solution)/shard_map/ppermute | solution.py:151
  118.8 3.4 %collective-permute-start.24 = (bf16[64,4224]{1,0:T(8,128)(2,1)S(1)}, bf16[64,4224]{1,0:T(8,128)(2,1)S(1)}, u32[]{:S(2)}, u32[]{:S(2)}) collective-permute-start(bf16[64,4224]{1,0:T(8,128)(2,1)S(1)} %add_convert_fusion.1), channel_id=1, source_target_pairs={{0,4},{1,5},{2,0},{3,1},{4,6},{5,7},{6,2},{7,3},{8,12},{9,13},{10,... | collective-permute-start | bytes 1622024 | tf_op jit(solution)/shard_map/ppermute | solution.py:151
  122.2 2.5 %shard_map.130 = (bf16[512,768]{1,0:T(8,128)(2,1)S(1)}, f32[512,768]{1,0:T(8,128)S(1)}) custom-call(bf16[3584,512]{1,0:T(8,128)(2,1)S(1)} %shard_map.121.turned_ref, bf16[2048,512]{1,0:T(8,128)(2,1)S(1)} %shard_map.127.other_turned_ref, bf16[512,768]{1,0:T(8,128)(2,1)S(1)} %get-tuple-element.90.d_up_ref.term_ref, ...), custom_call_target="tpu_custom_call" | custom-call | tf_op jit(solution)/shard_map/pallas_call | solution.py:486
  124.7 0.8 collective-permute-start.29
  125.5 2.5 %shard_map.129 = (bf16[512,768]{1,0:T(8,128)(2,1)S(1)}, f32[512,768]{1,0:T(8,128)S(1)}) custom-call(bf16[3584,512]{1,0:T(8,128)(2,1)S(1)} %shard_map.121.turned_ref, bf16[2048,512]{1,0:T(8,128)(2,1)S(1)} %shard_map.127.other_turned_ref, bf16[512,768]{1,0:T(8,128)(2,1)S(1)} %get-tuple-element.89.d_gate_ref.term_ref, ...), custom_call_target="tpu_custom_call" | custom-call | tf_op jit(solution)/shard_map/pallas_call | solution.py:486
  128.8 3.7 %collective-permute-done.26.refs_2_ = bf16[512,768]{1,0:T(8,128)(2,1)S(1)} collective-permute-done((bf16[512,768]{1,0:T(8,128)(2,1)S(1)}, bf16[512,768]{1,0:T(8,128)(2,1)S(1)}, u32[]{:S(2)}, u32[]{:S(2)}) %collective-permute-start.26) | collective-permute-done | bytes 786464 | tf_op jit(solution)/shard_map/ppermute | solution.py:151
  132.5 1.1 collective-permute-done.24
  133.8 3.4 %collective-permute-start.27 = (bf16[64,4224]{1,0:T(8,128)(2,1)S(1)}, bf16[64,4224]{1,0:T(8,128)(2,1)S(1)}, u32[]{:S(2)}, u32[]{:S(2)}) collective-permute-start(bf16[64,4224]{1,0:T(8,128)(2,1)S(1)} %add_convert_fusion), channel_id=1, source_target_pairs={{0,4},{1,5},{2,0},{3,1},{4,6},{5,7},{6,2},{7,3},{8,12},{9,13},{10,... | collective-permute-start | bytes 1622024 | tf_op jit(solution)/shard_map/ppermute | solution.py:151
  137.3 1.3 shard_map.132
  138.6 9.2 %collective-permute-done.27.line_ref = bf16[64,4224]{1,0:T(8,128)(2,1)S(1)} collective-permute-done((bf16[64,4224]{1,0:T(8,128)(2,1)S(1)}, bf16[64,4224]{1,0:T(8,128)(2,1)S(1)}, u32[]{:S(2)}, u32[]{:S(2)}) %collective-permute-start.27) | collective-permute-done | bytes 540704 | tf_op jit(solution)/shard_map/ppermute | solution.py:151
  147.8 1.0 shard_map.131
  148.8 1.8 %shard_map.133 = (f32[1,512,768]{2,1,0:T(8,128)}, f32[1,512,768]{2,1,0:T(8,128)}) custom-call(f32[512,768]{1,0:T(8,128)S(1)} %get-tuple-element.107.refs_0_, bf16[512,768]{1,0:T(8,128)(2,1)S(1)} %collective-permute-done.28.refs_1_, f32[512,768]{1,0:T(8,128)S(1)} %get-tuple-element.110.refs_2_, bf16[512,768]{1,0:T(8,128)(2,1)S(1)} %collective-permute-done.29.refs_3_), custom_call_target="tpu_custom_call" | custom-call | tf_op jit(solution)/shard_map/pallas_call | solution.py:554
  (68 shorter events, 10.7 us)
Async XLA Ops:
  0.6 21.6 %collective-permute-start.2 = (bf16[512,768]{1,0:T(8,128)(2,1)}, bf16[512,768]{1,0:T(8,128)(2,1)S(1)}, u32[]{:S(2)}, u32[]{:S(2)}) collective-permute-start(bf16[512,768]{1,0:T(8,128)(2,1)} %bitcast.6), channel_id=1, source_target_pairs={{0,16},{1,17},{2,18},{3,19},{4,20},{5,21},{6,22},{7,23},{8,24},{9,... | collective-permute-start | bytes 2359304 | tf_op jit(solution)/shard_map/ppermute | solution.py:151
  3.7 20.7 %collective-permute-start.1 = (bf16[512,768]{1,0:T(8,128)(2,1)}, bf16[512,768]{1,0:T(8,128)(2,1)S(1)}, u32[]{:S(2)}, u32[]{:S(2)}) collective-permute-start(bf16[512,768]{1,0:T(8,128)(2,1)} %bitcast.7), channel_id=1, source_target_pairs={{0,8},{1,9},{2,10},{3,11},{4,12},{5,13},{6,14},{7,15},{8,0},{9,1},... | collective-permute-start | bytes 2359304 | tf_op jit(solution)/shard_map/ppermute | solution.py:151
  5.2 0.9 copy-start.1
  6.1 0.9 copy-start.2
  7.1 0.7 copy-start.3
  7.7 0.7 copy-start.5
  8.6 13.6 %collective-permute-start = (bf16[64,4224]{1,0:T(8,128)(2,1)S(1)}, bf16[64,4224]{1,0:T(8,128)(2,1)S(1)}, u32[]{:S(2)}, u32[]{:S(2)}) collective-permute-start(bf16[64,4224]{1,0:T(8,128)(2,1)S(1)} %get-tuple-element.60), channel_id=1, source_target_pairs={{0,4},{1,5},{2,0},{3,1},{4,6},{5,7},{6,2},{7,3},{8,12},{9,13},{10,... | collective-permute-start | bytes 1622024 | tf_op jit(solution)/shard_map/ppermute | solution.py:151
  12.9 45.4 %collective-permute-start.6 = (bf16[560,1536]{1,0:T(8,128)(2,1)S(1)}, bf16[560,1536]{1,0:T(8,128)(2,1)S(1)}, u32[]{:S(2)}, u32[]{:S(2)}) collective-permute-start(bf16[560,1536]{1,0:T(8,128)(2,1)S(1)} %get-tuple-element.128), channel_id=1, source_target_pairs={{0,16},{1,17},{2,18},{3,19},{4,20},{5,21},{6,22},{7,23},{8,24},{9,... | collective-permute-start | bytes 5160968 | tf_op jit(solution)/shard_map/ppermute | solution.py:151
  13.5 46.3 %collective-permute-start.5 = (bf16[560,1536]{1,0:T(8,128)(2,1)S(1)}, bf16[560,1536]{1,0:T(8,128)(2,1)S(1)}, u32[]{:S(2)}, u32[]{:S(2)}) collective-permute-start(bf16[560,1536]{1,0:T(8,128)(2,1)S(1)} %get-tuple-element.129.own_ref.refs_5_), channel_id=1, source_target_pairs={{0,8},{1,9},{2,10},{3,11},{4,12},{5,13},{6,14},{7,15},{8,0},{9,1},... | collective-permute-start | bytes 5160968 | tf_op jit(solution)/shard_map/ppermute | solution.py:151
  24.3 11.7 %collective-permute-start.3 = (bf16[64,4224]{1,0:T(8,128)(2,1)S(1)}, bf16[64,4224]{1,0:T(8,128)(2,1)S(1)}, u32[]{:S(2)}, u32[]{:S(2)}) collective-permute-start(bf16[64,4224]{1,0:T(8,128)(2,1)S(1)} %collective-permute-done), channel_id=1, source_target_pairs={{0,4},{1,5},{2,0},{3,1},{4,6},{5,7},{6,2},{7,3},{8,12},{9,13},{10,... | collective-permute-start | bytes 1622024 | tf_op jit(solution)/shard_map/ppermute | solution.py:151
  36.0 11.3 %collective-permute-start.4 = (bf16[64,4224]{1,0:T(8,128)(2,1)S(1)}, bf16[64,4224]{1,0:T(8,128)(2,1)S(1)}, u32[]{:S(2)}, u32[]{:S(2)}) collective-permute-start(bf16[64,4224]{1,0:T(8,128)(2,1)S(1)} %collective-permute-done.3), channel_id=1, source_target_pairs={{0,4},{1,5},{2,0},{3,1},{4,6},{5,7},{6,2},{7,3},{8,12},{9,13},{10,... | collective-permute-start | bytes 1622024 | tf_op jit(solution)/shard_map/ppermute | solution.py:151
  59.7 5.0 %collective-permute-start.7 = (bf16[256,4224]{1,0:T(8,128)(2,1)S(1)}, bf16[256,4224]{1,0:T(8,128)(2,1)S(1)}, u32[]{:S(2)}, u32[]{:S(2)}) collective-permute-start(bf16[256,4224]{1,0:T(8,128)(2,1)S(1)} %constant_dynamic-update-slice_fusion.own_rows.own_ref.refs_0_.refs_2_), channel_id=1, source_target_pairs={{0,1},{1,0},{2,3},{3,2},{4,5},{5,4},{6,7},{7,6},{8,9},{9,8},{10,11... | collective-permute-start | bytes 6488072 | tf_op jit(solution)/shard_map/ppermute | solution.py:151
  59.8 22.1 %collective-permute-start.9 = (bf16[256,1536]{1,0:T(8,128)(2,1)S(1)}, bf16[256,1536]{1,0:T(8,128)(2,1)S(1)}, u32[]{:S(2)}, u32[]{:S(2)}) collective-permute-start(bf16[256,1536]{1,0:T(8,128)(2,1)S(1)} %slice.123), channel_id=1, source_target_pairs={{0,8},{1,9},{2,10},{3,11},{4,12},{5,13},{6,14},{7,15},{8,0},{9,1},... | collective-permute-start | bytes 2359304 | tf_op jit(solution)/shard_map/ppermute | solution.py:151
  61.4 20.5 %collective-permute-start.8 = (bf16[256,1536]{1,0:T(8,128)(2,1)S(1)}, bf16[256,1536]{1,0:T(8,128)(2,1)S(1)}, u32[]{:S(2)}, u32[]{:S(2)}) collective-permute-start(bf16[256,1536]{1,0:T(8,128)(2,1)S(1)} %slice.122), channel_id=1, source_target_pairs={{0,16},{1,17},{2,18},{3,19},{4,20},{5,21},{6,22},{7,23},{8,24},{9,... | collective-permute-start | bytes 2359304 | tf_op jit(solution)/shard_map/ppermute | solution.py:151
  62.0 8.3 %collective-permute-start.12 = (bf16[64,2048]{1,0:T(8,128)(2,1)S(1)}, bf16[64,2048]{1,0:T(8,128)(2,1)S(1)}, u32[]{:S(2)}, u32[]{:S(2)}) collective-permute-start(bf16[64,2048]{1,0:T(8,128)(2,1)S(1)} %maximum_maximum_fusion), channel_id=1, source_target_pairs={{0,4},{1,5},{2,0},{3,1},{4,6},{5,7},{6,2},{7,3},{8,12},{9,13},{10,... | collective-permute-start | bytes 786440 | tf_op jit(solution)/shard_map/ppermute | solution.py:151
  68.9 7.1 %copy-start = (bf16[1,512,768]{2,1,0:T(8,128)(2,1)S(1)}, bf16[1,512,768]{2,1,0:T(8,128)(2,1)}, u32[]{:S(2)}) copy-start(bf16[1,512,768]{2,1,0:T(8,128)(2,1)} %param.13) | copy-start | bytes 2359300
  70.4 10.6 %collective-permute-start.13 = (bf16[64,2048]{1,0:T(8,128)(2,1)S(1)}, bf16[64,2048]{1,0:T(8,128)(2,1)S(1)}, u32[]{:S(2)}, u32[]{:S(2)}) collective-permute-start(bf16[64,2048]{1,0:T(8,128)(2,1)S(1)} %collective-permute-done.12), channel_id=1, source_target_pairs={{0,4},{1,5},{2,0},{3,1},{4,6},{5,7},{6,2},{7,3},{8,12},{9,13},{10,... | collective-permute-start | bytes 786440 | tf_op jit(solution)/shard_map/ppermute | solution.py:151
  73.8 14.9 %collective-permute-start.11 = (bf16[256,768]{1,0:T(8,128)(2,1)S(1)}, bf16[256,768]{1,0:T(8,128)(2,1)S(1)}, u32[]{:S(2)}, u32[]{:S(2)}) collective-permute-start(bf16[256,768]{1,0:T(8,128)(2,1)S(1)} %slice.125), channel_id=1, source_target_pairs={{0,8},{1,9},{2,10},{3,11},{4,12},{5,13},{6,14},{7,15},{8,0},{9,1},... | collective-permute-start | bytes 1179656 | tf_op jit(solution)/shard_map/ppermute | solution.py:151
  74.4 15.9 %collective-permute-start.10 = (bf16[256,768]{1,0:T(8,128)(2,1)S(1)}, bf16[256,768]{1,0:T(8,128)(2,1)S(1)}, u32[]{:S(2)}, u32[]{:S(2)}) collective-permute-start(bf16[256,768]{1,0:T(8,128)(2,1)S(1)} %slice.124), channel_id=1, source_target_pairs={{0,16},{1,17},{2,18},{3,19},{4,20},{5,21},{6,22},{7,23},{8,24},{9,... | collective-permute-start | bytes 1179656 | tf_op jit(solution)/shard_map/ppermute | solution.py:151
  81.0 12.4 %collective-permute-start.14 = (bf16[64,2048]{1,0:T(8,128)(2,1)S(1)}, bf16[64,2048]{1,0:T(8,128)(2,1)S(1)}, u32[]{:S(2)}, u32[]{:S(2)}) collective-permute-start(bf16[64,2048]{1,0:T(8,128)(2,1)S(1)} %collective-permute-done.13), channel_id=1, source_target_pairs={{0,4},{1,5},{2,0},{3,1},{4,6},{5,7},{6,2},{7,3},{8,12},{9,13},{10,... | collective-permute-start | bytes 786440 | tf_op jit(solution)/shard_map/ppermute | solution.py:151
  85.4 12.1 %collective-permute-start.17 = (bf16[256,768]{1,0:T(8,128)(2,1)S(1)}, bf16[256,768]{1,0:T(8,128)(2,1)S(1)}, u32[]{:S(2)}, u32[]{:S(2)}) collective-permute-start(bf16[256,768]{1,0:T(8,128)(2,1)S(1)} %get-tuple-element.71), channel_id=1, source_target_pairs={{0,8},{1,9},{2,10},{3,11},{4,12},{5,13},{6,14},{7,15},{8,0},{9,1},... | collective-permute-start | bytes 1179656 | tf_op jit(solution)/shard_map/ppermute | solution.py:151
  86.8 12.1 %collective-permute-start.18 = (bf16[256,768]{1,0:T(8,128)(2,1)S(1)}, bf16[256,768]{1,0:T(8,128)(2,1)S(1)}, u32[]{:S(2)}, u32[]{:S(2)}) collective-permute-start(bf16[256,768]{1,0:T(8,128)(2,1)S(1)} %get-tuple-element.72), channel_id=1, source_target_pairs={{0,16},{1,17},{2,18},{3,19},{4,20},{5,21},{6,22},{7,23},{8,24},{9,... | collective-permute-start | bytes 1179656 | tf_op jit(solution)/shard_map/ppermute | solution.py:151
  92.4 26.3 %collective-permute-start.22 = (bf16[512,768]{1,0:T(8,128)(2,1)S(1)}, bf16[512,768]{1,0:T(8,128)(2,1)S(1)}, u32[]{:S(2)}, u32[]{:S(2)}) collective-permute-start(bf16[512,768]{1,0:T(8,128)(2,1)S(1)} %get-tuple-element.89.d_gate_ref.term_ref), channel_id=1, source_target_pairs={{0,8},{1,9},{2,10},{3,11},{4,12},{5,13},{6,14},{7,15},{8,0},{9,1},... | collective-permute-start | bytes 2359304 | tf_op jit(solution)/shard_map/ppermute | solution.py:151
  93.0 25.7 %collective-permute-start.23 = (bf16[512,768]{1,0:T(8,128)(2,1)S(1)}, bf16[512,768]{1,0:T(8,128)(2,1)S(1)}, u32[]{:S(2)}, u32[]{:S(2)}) collective-permute-start(bf16[512,768]{1,0:T(8,128)(2,1)S(1)} %get-tuple-element.90.d_up_ref.term_ref), channel_id=1, source_target_pairs={{0,16},{1,17},{2,18},{3,19},{4,20},{5,21},{6,22},{7,23},{8,24},{9,... | collective-permute-start | bytes 2359304 | tf_op jit(solution)/shard_map/ppermute | solution.py:151
  97.5 4.7 %collective-permute-start.20 = (bf16[256,2048]{1,0:T(8,128)(2,1)S(1)}, bf16[256,2048]{1,0:T(8,128)(2,1)S(1)}, u32[]{:S(2)}, u32[]{:S(2)}) collective-permute-start(bf16[256,2048]{1,0:T(8,128)(2,1)S(1)} %pad_maximum_fusion.4.own_ref), channel_id=1, source_target_pairs={{0,1},{1,0},{2,3},{3,2},{4,5},{5,4},{6,7},{7,6},{8,9},{9,8},{10,11... | collective-permute-start | bytes 3145736 | tf_op jit(solution)/shard_map/ppermute | solution.py:151
  98.8 3.2 %collective-permute-start.19 = (bf16[64,4224]{1,0:T(8,128)(2,1)S(1)}, bf16[64,4224]{1,0:T(8,128)(2,1)S(1)}, u32[]{:S(2)}, u32[]{:S(2)}) collective-permute-start(bf16[64,4224]{1,0:T(8,128)(2,1)S(1)} %get-tuple-element.92), channel_id=1, source_target_pairs={{0,1},{1,0},{2,3},{3,2},{4,5},{5,4},{6,7},{7,6},{8,9},{9,8},{10,11... | collective-permute-start | bytes 1622024 | tf_op jit(solution)/shard_map/ppermute | solution.py:151
  98.8 11.0 %collective-permute-start.16 = (bf16[64,4224]{1,0:T(8,128)(2,1)S(1)}, bf16[64,4224]{1,0:T(8,128)(2,1)S(1)}, u32[]{:S(2)}, u32[]{:S(2)}) collective-permute-start(bf16[64,4224]{1,0:T(8,128)(2,1)S(1)} %get-tuple-element.114), channel_id=1, source_target_pairs={{0,1},{1,0},{2,3},{3,2},{4,5},{5,4},{6,7},{7,6},{8,9},{9,8},{10,11... | collective-permute-start | bytes 1622024 | tf_op jit(solution)/shard_map/ppermute | solution.py:151
  102.1 4.3 %collective-permute-start.15 = (bf16[128,4224]{1,0:T(8,128)(2,1)S(1)}, bf16[128,4224]{1,0:T(8,128)(2,1)S(1)}, u32[]{:S(2)}, u32[]{:S(2)}) collective-permute-start(bf16[128,4224]{1,0:T(8,128)(2,1)S(1)} %pad_maximum_fusion.3), channel_id=1, source_target_pairs={{0,1},{1,0},{2,3},{3,2},{4,5},{5,4},{6,7},{7,6},{8,9},{9,8},{10,11... | collective-permute-start | bytes 3244040 | tf_op jit(solution)/shard_map/ppermute | solution.py:151
  103.7 14.9 %collective-permute-start.21 = (bf16[64,4224]{1,0:T(8,128)(2,1)S(1)}, bf16[64,4224]{1,0:T(8,128)(2,1)S(1)}, u32[]{:S(2)}, u32[]{:S(2)}) collective-permute-start(bf16[64,4224]{1,0:T(8,128)(2,1)S(1)} %add_convert_fusion.2), channel_id=1, source_target_pairs={{0,4},{1,5},{2,0},{3,1},{4,6},{5,7},{6,2},{7,3},{8,12},{9,13},{10,... | collective-permute-start | bytes 1622024 | tf_op jit(solution)/shard_map/ppermute | solution.py:151
  109.1 23.4 %collective-permute-start.26 = (bf16[512,768]{1,0:T(8,128)(2,1)S(1)}, bf16[512,768]{1,0:T(8,128)(2,1)S(1)}, u32[]{:S(2)}, u32[]{:S(2)}) collective-permute-start(bf16[512,768]{1,0:T(8,128)(2,1)S(1)} %pad_maximum_fusion.6), channel_id=1, source_target_pairs={{0,16},{1,17},{2,18},{3,19},{4,20},{5,21},{6,22},{7,23},{8,24},{9,... | collective-permute-start | bytes 2359304 | tf_op jit(solution)/shard_map/ppermute | solution.py:151
  109.9 22.7 %collective-permute-start.25 = (bf16[512,768]{1,0:T(8,128)(2,1)S(1)}, bf16[512,768]{1,0:T(8,128)(2,1)S(1)}, u32[]{:S(2)}, u32[]{:S(2)}) collective-permute-start(bf16[512,768]{1,0:T(8,128)(2,1)S(1)} %pad_maximum_fusion.5), channel_id=1, source_target_pairs={{0,8},{1,9},{2,10},{3,11},{4,12},{5,13},{6,14},{7,15},{8,0},{9,1},... | collective-permute-start | bytes 2359304 | tf_op jit(solution)/shard_map/ppermute | solution.py:151
  118.8 14.8 %collective-permute-start.24 = (bf16[64,4224]{1,0:T(8,128)(2,1)S(1)}, bf16[64,4224]{1,0:T(8,128)(2,1)S(1)}, u32[]{:S(2)}, u32[]{:S(2)}) collective-permute-start(bf16[64,4224]{1,0:T(8,128)(2,1)S(1)} %add_convert_fusion.1), channel_id=1, source_target_pairs={{0,4},{1,5},{2,0},{3,1},{4,6},{5,7},{6,2},{7,3},{8,12},{9,13},{10,... | collective-permute-start | bytes 1622024 | tf_op jit(solution)/shard_map/ppermute | solution.py:151
  124.7 24.1 %collective-permute-start.29 = (bf16[512,768]{1,0:T(8,128)(2,1)S(1)}, bf16[512,768]{1,0:T(8,128)(2,1)S(1)}, u32[]{:S(2)}, u32[]{:S(2)}) collective-permute-start(bf16[512,768]{1,0:T(8,128)(2,1)S(1)} %get-tuple-element.100), channel_id=1, source_target_pairs={{0,8},{1,9},{2,10},{3,11},{4,12},{5,13},{6,14},{7,15},{8,0},{9,1},... | collective-permute-start | bytes 2359304 | tf_op jit(solution)/shard_map/ppermute | solution.py:151
  128.0 20.7 %collective-permute-start.28 = (bf16[512,768]{1,0:T(8,128)(2,1)S(1)}, bf16[512,768]{1,0:T(8,128)(2,1)S(1)}, u32[]{:S(2)}, u32[]{:S(2)}) collective-permute-start(bf16[512,768]{1,0:T(8,128)(2,1)S(1)} %get-tuple-element.99), channel_id=1, source_target_pairs={{0,16},{1,17},{2,18},{3,19},{4,20},{5,21},{6,22},{7,23},{8,24},{9,... | collective-permute-start | bytes 2359304 | tf_op jit(solution)/shard_map/ppermute | solution.py:151
  133.8 14.0 %collective-permute-start.27 = (bf16[64,4224]{1,0:T(8,128)(2,1)S(1)}, bf16[64,4224]{1,0:T(8,128)(2,1)S(1)}, u32[]{:S(2)}, u32[]{:S(2)}) collective-permute-start(bf16[64,4224]{1,0:T(8,128)(2,1)S(1)} %add_convert_fusion), channel_id=1, source_target_pairs={{0,4},{1,5},{2,0},{3,1},{4,6},{5,7},{6,2},{7,3},{8,12},{9,13},{10,... | collective-permute-start | bytes 1622024 | tf_op jit(solution)/shard_map/ppermute | solution.py:151
  137.3 10.5 %copy-start.4 = (s32[64,6]{0,1:T(8,128)S(1)}, s32[64,6]{0,1:T(8,128)}, u32[]{:S(2)}) copy-start(s32[64,6]{0,1:T(8,128)} %param.8) | copy-start | bytes 4612

commit v8 on v7

--- a/solution.py
+++ b/solution.py
@@ -622,7 +622,7 @@
     from_x, from_y = send(to_x, TO_X), send(to_y, TO_Y)
     direct = [to_x, from_x, from_y]
     line = along_line(packed, ((), (down,), ()))
-    whole = from_both_cores(jnp.concatenate(line), (from_x, from_y))
+    whole = from_both_cores(jnp.concatenate(line), from_y)
     side = [side_rows(from_y[depth:], rows, width), side_rows(from_x[depth:], rows, width)]
     gate_up_corner = send_corner(from_x, from_y, depth)
     down_corner = send_corner(*down[1:], depth)

time: 151 us -> 150 us (level)
  waiting for transfers between devices: 67.1 us -> 63.1 us
  starting transfers between devices: 42.3 us -> 45 us
    ppermute x30, waiting for transfers between devices: 67.1 us -> 63.1 us  [send(): return lax.ppermute(array, AXES, where)]
    ppermute x30, starting transfers between devices: 42.3 us -> 45 us  [send(): return lax.ppermute(array, AXES, where)]
  transfers between devices with their start and end apart: 30 -> 30, of which waited for: 16 -> 15; matrix products, arithmetic and copies ran while one was open for 3% -> 3% of each run, Pallas kernels for 21% -> 21%
where the time goes in v8:
time: 150 us; the launch traced here: 149 us
  waiting for transfers between devices  63.1 us (42%)
  starting transfers between devices  45 us (30%)
  Pallas kernels  33.1 us (22%)
  local copies, waits for them, and re-layouts  3.93 us (3%)
  other arithmetic  3.21 us (2%)
    ppermute x30, waiting for transfers between devices, send(): return lax.ppermute(array, AXES, where)  63.1 us
    ppermute x30, starting transfers between devices, send(): return lax.ppermute(array, AXES, where)  45 us
    pallas_call x2, Pallas kernels, early_products(): kernel_call(early_kernel, shape(2 * half, columns, F32), grid=(columns //...  6.29 us
    pallas_call x2, Pallas kernels, back_to_rows(): kernel_call(back_kernel, shape(rows, 2 * width + SIDE, BF16), grid=(1,),...  5.28 us
    pallas_call x2, Pallas kernels, pair_grads(): kernel_call(pair_grad_kernel, (shape(2 * half, units, BF16), shape(2 * ha...  4.99 us
    pallas_call x2, Pallas kernels, turn(): kernel_call(turn_kernel, shape(tiles * TILE, 2 * rows, BF16), grid=(tiles...  4.2 us
    unnamed x15, local copies, waits for them, and re-layouts  3.42 us
    pallas_call x2, Pallas kernels, totals(): kernel_call(body, (jax.ShapeDtypeStruct((1, block, units), F32),) * len(g...  3.08 us
  transfers between devices with their start and end apart: 30, of which 15 were waited for; matrix products, arithmetic and copies ran while one was open for 3% of the time, Pallas kernels for 21%

profile of v8, /device:TPU:0, one launch (start us, length us, event | category | flops | bytes accessed | tf_op | source)
XLA Modules:
  0.0 149.4 jit_solution(8040124626399004259)
XLA Ops:
  0.6 3.0 %collective-permute-start.2 = (bf16[512,768]{1,0:T(8,128)(2,1)}, bf16[512,768]{1,0:T(8,128)(2,1)S(1)}, u32[]{:S(2)}, u32[]{:S(2)}) collective-permute-start(bf16[512,768]{1,0:T(8,128)(2,1)} %bitcast.6), channel_id=1, source_target_pairs={{0,16},{1,17},{2,18},{3,19},{4,20},{5,21},{6,22},{7,23},{8,24},{9,... | collective-permute-start | bytes 2359304 | tf_op jit(solution)/shard_map/ppermute | solution.py:151
  3.7 1.5 collective-permute-start.1
  5.2 0.9 copy-done.1
  6.1 0.9 copy-done.2
  8.6 2.6 %collective-permute-start = (bf16[64,4224]{1,0:T(8,128)(2,1)S(1)}, bf16[64,4224]{1,0:T(8,128)(2,1)S(1)}, u32[]{:S(2)}, u32[]{:S(2)}) collective-permute-start(bf16[64,4224]{1,0:T(8,128)(2,1)S(1)} %get-tuple-element.60), channel_id=1, source_target_pairs={{0,4},{1,5},{2,0},{3,1},{4,6},{5,7},{6,2},{7,3},{8,12},{9,13},{10,... | collective-permute-start | bytes 1622024 | tf_op jit(solution)/shard_map/ppermute | solution.py:151
  11.2 1.5 pad_maximum_fusion.2
  14.0 8.1 %collective-permute-done = bf16[64,4224]{1,0:T(8,128)(2,1)S(1)} collective-permute-done((bf16[64,4224]{1,0:T(8,128)(2,1)S(1)}, bf16[64,4224]{1,0:T(8,128)(2,1)S(1)}, u32[]{:S(2)}, u32[]{:S(2)}) %collective-permute-start) | collective-permute-done | bytes 540704 | tf_op jit(solution)/shard_map/ppermute | solution.py:151
  22.2 2.1 %collective-permute-done.1.x_ref.refs_1_ = bf16[512,768]{1,0:T(8,128)(2,1)S(1)} collective-permute-done((bf16[512,768]{1,0:T(8,128)(2,1)}, bf16[512,768]{1,0:T(8,128)(2,1)S(1)}, u32[]{:S(2)}, u32[]{:S(2)}) %collective-permute-start.1) | collective-permute-done | bytes 786464 | tf_op jit(solution)/shard_map/ppermute | solution.py:151
  24.3 2.6 %collective-permute-start.3 = (bf16[64,4224]{1,0:T(8,128)(2,1)S(1)}, bf16[64,4224]{1,0:T(8,128)(2,1)S(1)}, u32[]{:S(2)}, u32[]{:S(2)}) collective-permute-start(bf16[64,4224]{1,0:T(8,128)(2,1)S(1)} %collective-permute-done), channel_id=1, source_target_pairs={{0,4},{1,5},{2,0},{3,1},{4,6},{5,7},{6,2},{7,3},{8,12},{9,13},{10,... | collective-permute-start | bytes 1622024 | tf_op jit(solution)/shard_map/ppermute | solution.py:151
  27.0 9.1 %collective-permute-done.3 = bf16[64,4224]{1,0:T(8,128)(2,1)S(1)} collective-permute-done((bf16[64,4224]{1,0:T(8,128)(2,1)S(1)}, bf16[64,4224]{1,0:T(8,128)(2,1)S(1)}, u32[]{:S(2)}, u32[]{:S(2)}) %collective-permute-start.3) | collective-permute-done | bytes 540704 | tf_op jit(solution)/shard_map/ppermute | solution.py:151
  36.0 3.3 %collective-permute-start.4 = (bf16[64,4224]{1,0:T(8,128)(2,1)S(1)}, bf16[64,4224]{1,0:T(8,128)(2,1)S(1)}, u32[]{:S(2)}, u32[]{:S(2)}) collective-permute-start(bf16[64,4224]{1,0:T(8,128)(2,1)S(1)} %collective-permute-done.3), channel_id=1, source_target_pairs={{0,4},{1,5},{2,0},{3,1},{4,6},{5,7},{6,2},{7,3},{8,12},{9,13},{10,... | collective-permute-start | bytes 1622024 | tf_op jit(solution)/shard_map/ppermute | solution.py:151
  39.4 8.0 %collective-permute-done.4 = bf16[64,4224]{1,0:T(8,128)(2,1)S(1)} collective-permute-done((bf16[64,4224]{1,0:T(8,128)(2,1)S(1)}, bf16[64,4224]{1,0:T(8,128)(2,1)S(1)}, u32[]{:S(2)}, u32[]{:S(2)}) %collective-permute-start.4) | collective-permute-done | bytes 540704 | tf_op jit(solution)/shard_map/ppermute | solution.py:151
  47.4 10.8 %collective-permute-done.5.y_ref.refs_7_ = bf16[560,1536]{1,0:T(8,128)(2,1)S(1)} collective-permute-done((bf16[560,1536]{1,0:T(8,128)(2,1)S(1)}, bf16[560,1536]{1,0:T(8,128)(2,1)S(1)}, u32[]{:S(2)}, u32[]{:S(2)}) %collective-permute-start.5) | collective-permute-done | bytes 1720352 | tf_op jit(solution)/shard_map/ppermute | solution.py:151
  58.3 1.8 %collective-permute-start.9 = (bf16[256,1536]{1,0:T(8,128)(2,1)S(1)}, bf16[256,1536]{1,0:T(8,128)(2,1)S(1)}, u32[]{:S(2)}, u32[]{:S(2)}) collective-permute-start(bf16[256,1536]{1,0:T(8,128)(2,1)S(1)} %slice.123), channel_id=1, source_target_pairs={{0,8},{1,9},{2,10},{3,11},{4,12},{5,13},{6,14},{7,15},{8,0},{9,1},... | collective-permute-start | bytes 2359304 | tf_op jit(solution)/shard_map/ppermute | solution.py:151
  60.2 1.6 %collective-permute-start.8 = (bf16[256,1536]{1,0:T(8,128)(2,1)S(1)}, bf16[256,1536]{1,0:T(8,128)(2,1)S(1)}, u32[]{:S(2)}, u32[]{:S(2)}) collective-permute-start(bf16[256,1536]{1,0:T(8,128)(2,1)S(1)} %slice.122), channel_id=1, source_target_pairs={{0,16},{1,17},{2,18},{3,19},{4,20},{5,21},{6,22},{7,23},{8,24},{9,... | collective-permute-start | bytes 2359304 | tf_op jit(solution)/shard_map/ppermute | solution.py:151
  61.8 2.6 %collective-permute-start.12 = (bf16[64,2048]{1,0:T(8,128)(2,1)S(1)}, bf16[64,2048]{1,0:T(8,128)(2,1)S(1)}, u32[]{:S(2)}, u32[]{:S(2)}) collective-permute-start(bf16[64,2048]{1,0:T(8,128)(2,1)S(1)} %maximum_maximum_fusion), channel_id=1, source_target_pairs={{0,4},{1,5},{2,0},{3,1},{4,6},{5,7},{6,2},{7,3},{8,12},{9,13},{10,... | collective-permute-start | bytes 786440 | tf_op jit(solution)/shard_map/ppermute | solution.py:151
  64.5 4.2 %shard_map.119.refs_4_.refs_5_ = f32[512,1536]{1,0:T(8,128)S(1)} custom-call(bf16[256,4224]{1,0:T(8,128)(2,1)S(1)} %constant_dynamic-update-slice_fusion.own_rows.own_ref.refs_0_.refs_2_, bf16[256,4224]{1,0:T(8,128)(2,1)S(1)} %collective-permute-done.6.other_rows.other_ref.refs_1_.refs_3_, bf16[560,1536]{1,0:T(8,128)(2,1)S(1)} %get-tuple-element.128.own_ref.refs_5_, ...), custom_call_target="tpu_custom_call" | custom-call | tf_op jit(solution)/shard_map/pallas_call | solution.py:309
  68.6 1.5 %collective-permute-done.12 = bf16[64,2048]{1,0:T(8,128)(2,1)S(1)} collective-permute-done((bf16[64,2048]{1,0:T(8,128)(2,1)S(1)}, bf16[64,2048]{1,0:T(8,128)(2,1)S(1)}, u32[]{:S(2)}, u32[]{:S(2)}) %collective-permute-start.12) | collective-permute-done | bytes 262176 | tf_op jit(solution)/shard_map/ppermute | solution.py:151
  70.1 3.4 %collective-permute-start.13 = (bf16[64,2048]{1,0:T(8,128)(2,1)S(1)}, bf16[64,2048]{1,0:T(8,128)(2,1)S(1)}, u32[]{:S(2)}, u32[]{:S(2)}) collective-permute-start(bf16[64,2048]{1,0:T(8,128)(2,1)S(1)} %collective-permute-done.12), channel_id=1, source_target_pairs={{0,4},{1,5},{2,0},{3,1},{4,6},{5,7},{6,2},{7,3},{8,12},{9,13},{10,... | collective-permute-start | bytes 786440 | tf_op jit(solution)/shard_map/ppermute | solution.py:151
  74.8 2.1 %shard_map.120.early_ref = f32[512,768]{1,0:T(8,128)S(1)} custom-call(bf16[256,4224]{1,0:T(8,128)(2,1)S(1)} %constant_dynamic-update-slice_fusion.own_rows.own_ref.refs_0_.refs_2_, bf16[256,4224]{1,0:T(8,128)(2,1)S(1)} %collective-permute-done.6.other_rows.other_ref.refs_1_.refs_3_, bf16[512,768]{1,0:T(8,128)(2,1)S(1)} %bitcast.8, ...), custom_call_target="tpu_custom_call" | custom-call | tf_op jit(solution)/shard_map/pallas_call | solution.py:309
  76.9 2.8 %shard_map.121.turned_ref = bf16[3584,512]{1,0:T(8,128)(2,1)S(1)} custom-call(bf16[256,4224]{1,0:T(8,128)(2,1)S(1)} %constant_dynamic-update-slice_fusion.own_rows.own_ref.refs_0_.refs_2_, bf16[256,4224]{1,0:T(8,128)(2,1)S(1)} %collective-permute-done.6.other_rows.other_ref.refs_1_.refs_3_), custom_call_target="tpu_custom_call" | custom-call | tf_op jit(solution)/shard_map/pallas_call | solution.py:281
  79.8 2.0 %collective-permute-start.14 = (bf16[64,2048]{1,0:T(8,128)(2,1)S(1)}, bf16[64,2048]{1,0:T(8,128)(2,1)S(1)}, u32[]{:S(2)}, u32[]{:S(2)}) collective-permute-start(bf16[64,2048]{1,0:T(8,128)(2,1)S(1)} %collective-permute-done.13), channel_id=1, source_target_pairs={{0,4},{1,5},{2,0},{3,1},{4,6},{5,7},{6,2},{7,3},{8,12},{9,13},{10,... | collective-permute-start | bytes 786440 | tf_op jit(solution)/shard_map/ppermute | solution.py:151
  81.7 2.6 %shard_map.122 = (bf16[512,768]{1,0:T(8,128)(2,1)S(1)}, f32[512,768]{1,0:T(8,128)S(1)}, f32[512,768]{1,0:T(8,128)S(1)}, f32[512,768]{1,0:T(8,128)S(1)}) custom-call(bf16[256,4224]{1,0:T(8,128)(2,1)S(1)} %constant_dynamic-update-slice_fusion.own_rows.own_ref.refs_0_.refs_2_, bf16[256,4224]{1,0:T(8,128)(2,1)S(1)} %collective-permute-done.6.other_rows.other_ref.refs_1_.refs_3_, ...), custom_call_target="tpu_custom_call" | custom-call | tf_op jit(solution)/shard_map/pallas_call | solution.py:347
  84.3 0.8 shard_map.123
  85.8 1.3 collective-permute-start.18
  87.2 1.9 %collective-permute-done.10.first_ref.refs_3_ = bf16[256,768]{1,0:T(8,128)(2,1)S(1)} collective-permute-done((bf16[256,768]{1,0:T(8,128)(2,1)S(1)}, bf16[256,768]{1,0:T(8,128)(2,1)S(1)}, u32[]{:S(2)}, u32[]{:S(2)}) %collective-permute-start.10) | collective-permute-done | bytes 393248 | tf_op jit(solution)/shard_map/ppermute | solution.py:151
  89.0 2.1 %shard_map.124 = (bf16[512,768]{1,0:T(8,128)(2,1)S(1)}, bf16[512,768]{1,0:T(8,128)(2,1)S(1)}, bf16[512,128]{1,0:T(8,128)(2,1)S(1)}) custom-call(bf16[256,4224]{1,0:T(8,128)(2,1)S(1)} %constant_dynamic-update-slice_fusion.own_rows.own_ref.refs_0_.refs_2_, bf16[256,4224]{1,0:T(8,128)(2,1)S(1)} %collective-permute-done.6.other_rows.other_ref.refs_1_.refs_3_, ...), custom_call_target="tpu_custom_call" | custom-call | tf_op jit(solution)/shard_map/pallas_call | solution.py:388
  92.0 1.3 collective-permute-start.23
  94.0 2.6 %shard_map.125 = bf16[256,4224]{1,0:T(8,128)(2,1)S(1)} custom-call(bf16[512,768]{1,0:T(8,128)(2,1)S(1)} %get-tuple-element.96.term_ref.scaled_ref, bf16[512,768]{1,0:T(8,128)(2,1)S(1)} %get-tuple-element.89.d_gate_ref.term_ref, bf16[512,768]{1,0:T(8,128)(2,1)S(1)} %get-tuple-element.90.d_up_ref.term_ref, bf16[512,128]{1,0:T(8,128)(2,1)S(1)} %get-tuple-element.91.dots_ref, ...), custom_call_target="tpu_custom_call" | custom-call | tf_op jit(solution)/shard_map/pallas_call | solution.py:526
  98.4 2.6 %shard_map.126.own_ref = bf16[256,4224]{1,0:T(8,128)(2,1)S(1)} custom-call(bf16[512,768]{1,0:T(8,128)(2,1)S(1)} %get-tuple-element.96.term_ref.scaled_ref, bf16[512,768]{1,0:T(8,128)(2,1)S(1)} %get-tuple-element.89.d_gate_ref.term_ref, bf16[512,768]{1,0:T(8,128)(2,1)S(1)} %get-tuple-element.90.d_up_ref.term_ref, ...), custom_call_target="tpu_custom_call" | custom-call | tf_op jit(solution)/shard_map/pallas_call | solution.py:526
  101.3 1.4 shard_map.127.other_turned_ref
  102.7 2.4 %collective-permute-start.21 = (bf16[64,4224]{1,0:T(8,128)(2,1)S(1)}, bf16[64,4224]{1,0:T(8,128)(2,1)S(1)}, u32[]{:S(2)}, u32[]{:S(2)}) collective-permute-start(bf16[64,4224]{1,0:T(8,128)(2,1)S(1)} %add_convert_fusion.2), channel_id=1, source_target_pairs={{0,4},{1,5},{2,0},{3,1},{4,6},{5,7},{6,2},{7,3},{8,12},{9,13},{10,... | collective-permute-start | bytes 1622024 | tf_op jit(solution)/shard_map/ppermute | solution.py:151
  105.1 2.5 %shard_map.128 = (f32[512,768]{1,0:T(8,128)S(1)}, f32[512,768]{1,0:T(8,128)S(1)}, f32[512,768]{1,0:T(8,128)S(1)}) custom-call(bf16[3584,512]{1,0:T(8,128)(2,1)S(1)} %shard_map.121.turned_ref, bf16[512,768]{1,0:T(8,128)(2,1)S(1)} %get-tuple-element.96.term_ref.scaled_ref), custom_call_target="tpu_custom_call" | custom-call | tf_op jit(solution)/shard_map/pallas_call | solution.py:448
  107.9 1.6 %collective-permute-start.26 = (bf16[512,768]{1,0:T(8,128)(2,1)S(1)}, bf16[512,768]{1,0:T(8,128)(2,1)S(1)}, u32[]{:S(2)}, u32[]{:S(2)}) collective-permute-start(bf16[512,768]{1,0:T(8,128)(2,1)S(1)} %pad_maximum_fusion.6), channel_id=1, source_target_pairs={{0,16},{1,17},{2,18},{3,19},{4,20},{5,21},{6,22},{7,23},{8,24},{9,... | collective-permute-start | bytes 2359304 | tf_op jit(solution)/shard_map/ppermute | solution.py:151
  109.6 0.8 collective-permute-start.25
  110.5 7.1 %collective-permute-done.21 = bf16[64,4224]{1,0:T(8,128)(2,1)S(1)} collective-permute-done((bf16[64,4224]{1,0:T(8,128)(2,1)S(1)}, bf16[64,4224]{1,0:T(8,128)(2,1)S(1)}, u32[]{:S(2)}, u32[]{:S(2)}) %collective-permute-start.21) | collective-permute-done | bytes 540704 | tf_op jit(solution)/shard_map/ppermute | solution.py:151
  117.8 3.2 %collective-permute-start.24 = (bf16[64,4224]{1,0:T(8,128)(2,1)S(1)}, bf16[64,4224]{1,0:T(8,128)(2,1)S(1)}, u32[]{:S(2)}, u32[]{:S(2)}) collective-permute-start(bf16[64,4224]{1,0:T(8,128)(2,1)S(1)} %add_convert_fusion.1), channel_id=1, source_target_pairs={{0,4},{1,5},{2,0},{3,1},{4,6},{5,7},{6,2},{7,3},{8,12},{9,13},{10,... | collective-permute-start | bytes 1622024 | tf_op jit(solution)/shard_map/ppermute | solution.py:151
  121.0 2.5 %shard_map.130 = (bf16[512,768]{1,0:T(8,128)(2,1)S(1)}, f32[512,768]{1,0:T(8,128)S(1)}) custom-call(bf16[3584,512]{1,0:T(8,128)(2,1)S(1)} %shard_map.121.turned_ref, bf16[2048,512]{1,0:T(8,128)(2,1)S(1)} %shard_map.127.other_turned_ref, bf16[512,768]{1,0:T(8,128)(2,1)S(1)} %get-tuple-element.90.d_up_ref.term_ref, ...), custom_call_target="tpu_custom_call" | custom-call | tf_op jit(solution)/shard_map/pallas_call | solution.py:486
  123.5 1.3 collective-permute-start.29
  124.7 2.5 %shard_map.129 = (bf16[512,768]{1,0:T(8,128)(2,1)S(1)}, f32[512,768]{1,0:T(8,128)S(1)}) custom-call(bf16[3584,512]{1,0:T(8,128)(2,1)S(1)} %shard_map.121.turned_ref, bf16[2048,512]{1,0:T(8,128)(2,1)S(1)} %shard_map.127.other_turned_ref, bf16[512,768]{1,0:T(8,128)(2,1)S(1)} %get-tuple-element.89.d_gate_ref.term_ref, ...), custom_call_target="tpu_custom_call" | custom-call | tf_op jit(solution)/shard_map/pallas_call | solution.py:486
  127.2 1.1 collective-permute-start.28
  128.4 3.2 %collective-permute-done.26.refs_2_ = bf16[512,768]{1,0:T(8,128)(2,1)S(1)} collective-permute-done((bf16[512,768]{1,0:T(8,128)(2,1)S(1)}, bf16[512,768]{1,0:T(8,128)(2,1)S(1)}, u32[]{:S(2)}, u32[]{:S(2)}) %collective-permute-start.26) | collective-permute-done | bytes 786464 | tf_op jit(solution)/shard_map/ppermute | solution.py:151
  131.6 0.8 collective-permute-done.24
  132.6 3.4 %collective-permute-start.27 = (bf16[64,4224]{1,0:T(8,128)(2,1)S(1)}, bf16[64,4224]{1,0:T(8,128)(2,1)S(1)}, u32[]{:S(2)}, u32[]{:S(2)}) collective-permute-start(bf16[64,4224]{1,0:T(8,128)(2,1)S(1)} %add_convert_fusion), channel_id=1, source_target_pairs={{0,4},{1,5},{2,0},{3,1},{4,6},{5,7},{6,2},{7,3},{8,12},{9,13},{10,... | collective-permute-start | bytes 1622024 | tf_op jit(solution)/shard_map/ppermute | solution.py:151
  136.1 1.3 shard_map.132
  137.3 9.2 %collective-permute-done.27.line_ref = bf16[64,4224]{1,0:T(8,128)(2,1)S(1)} collective-permute-done((bf16[64,4224]{1,0:T(8,128)(2,1)S(1)}, bf16[64,4224]{1,0:T(8,128)(2,1)S(1)}, u32[]{:S(2)}, u32[]{:S(2)}) %collective-permute-start.27) | collective-permute-done | bytes 540704 | tf_op jit(solution)/shard_map/ppermute | solution.py:151
  146.5 1.0 shard_map.131
  147.5 1.8 %shard_map.133 = (f32[1,512,768]{2,1,0:T(8,128)}, f32[1,512,768]{2,1,0:T(8,128)}) custom-call(f32[512,768]{1,0:T(8,128)S(1)} %get-tuple-element.107.refs_0_, bf16[512,768]{1,0:T(8,128)(2,1)S(1)} %collective-permute-done.28.refs_1_, f32[512,768]{1,0:T(8,128)S(1)} %get-tuple-element.110.refs_2_, bf16[512,768]{1,0:T(8,128)(2,1)S(1)} %collective-permute-done.29.refs_3_), custom_call_target="tpu_custom_call" | custom-call | tf_op jit(solution)/shard_map/pallas_call | solution.py:554
  (68 shorter events, 9.5 us)
Async XLA Ops:
  0.6 21.6 %collective-permute-start.2 = (bf16[512,768]{1,0:T(8,128)(2,1)}, bf16[512,768]{1,0:T(8,128)(2,1)S(1)}, u32[]{:S(2)}, u32[]{:S(2)}) collective-permute-start(bf16[512,768]{1,0:T(8,128)(2,1)} %bitcast.6), channel_id=1, source_target_pairs={{0,16},{1,17},{2,18},{3,19},{4,20},{5,21},{6,22},{7,23},{8,24},{9,... | collective-permute-start | bytes 2359304 | tf_op jit(solution)/shard_map/ppermute | solution.py:151
  3.7 20.7 %collective-permute-start.1 = (bf16[512,768]{1,0:T(8,128)(2,1)}, bf16[512,768]{1,0:T(8,128)(2,1)S(1)}, u32[]{:S(2)}, u32[]{:S(2)}) collective-permute-start(bf16[512,768]{1,0:T(8,128)(2,1)} %bitcast.7), channel_id=1, source_target_pairs={{0,8},{1,9},{2,10},{3,11},{4,12},{5,13},{6,14},{7,15},{8,0},{9,1},... | collective-permute-start | bytes 2359304 | tf_op jit(solution)/shard_map/ppermute | solution.py:151
  5.2 0.9 copy-start.1
  6.1 0.9 copy-start.2
  7.1 0.7 copy-start.3
  7.7 0.7 copy-start.5
  8.6 13.6 %collective-permute-start = (bf16[64,4224]{1,0:T(8,128)(2,1)S(1)}, bf16[64,4224]{1,0:T(8,128)(2,1)S(1)}, u32[]{:S(2)}, u32[]{:S(2)}) collective-permute-start(bf16[64,4224]{1,0:T(8,128)(2,1)S(1)} %get-tuple-element.60), channel_id=1, source_target_pairs={{0,4},{1,5},{2,0},{3,1},{4,6},{5,7},{6,2},{7,3},{8,12},{9,13},{10,... | collective-permute-start | bytes 1622024 | tf_op jit(solution)/shard_map/ppermute | solution.py:151
  12.9 45.4 %collective-permute-start.5 = (bf16[560,1536]{1,0:T(8,128)(2,1)S(1)}, bf16[560,1536]{1,0:T(8,128)(2,1)S(1)}, u32[]{:S(2)}, u32[]{:S(2)}) collective-permute-start(bf16[560,1536]{1,0:T(8,128)(2,1)S(1)} %get-tuple-element.129), channel_id=1, source_target_pairs={{0,16},{1,17},{2,18},{3,19},{4,20},{5,21},{6,22},{7,23},{8,24},{9,... | collective-permute-start | bytes 5160968 | tf_op jit(solution)/shard_map/ppermute | solution.py:151
  13.5 46.7 %collective-permute-start.7 = (bf16[560,1536]{1,0:T(8,128)(2,1)S(1)}, bf16[560,1536]{1,0:T(8,128)(2,1)S(1)}, u32[]{:S(2)}, u32[]{:S(2)}) collective-permute-start(bf16[560,1536]{1,0:T(8,128)(2,1)S(1)} %get-tuple-element.128.own_ref.refs_5_), channel_id=1, source_target_pairs={{0,8},{1,9},{2,10},{3,11},{4,12},{5,13},{6,14},{7,15},{8,0},{9,1},... | collective-permute-start | bytes 5160968 | tf_op jit(solution)/shard_map/ppermute | solution.py:151
  24.3 11.7 %collective-permute-start.3 = (bf16[64,4224]{1,0:T(8,128)(2,1)S(1)}, bf16[64,4224]{1,0:T(8,128)(2,1)S(1)}, u32[]{:S(2)}, u32[]{:S(2)}) collective-permute-start(bf16[64,4224]{1,0:T(8,128)(2,1)S(1)} %collective-permute-done), channel_id=1, source_target_pairs={{0,4},{1,5},{2,0},{3,1},{4,6},{5,7},{6,2},{7,3},{8,12},{9,13},{10,... | collective-permute-start | bytes 1622024 | tf_op jit(solution)/shard_map/ppermute | solution.py:151
  36.0 11.3 %collective-permute-start.4 = (bf16[64,4224]{1,0:T(8,128)(2,1)S(1)}, bf16[64,4224]{1,0:T(8,128)(2,1)S(1)}, u32[]{:S(2)}, u32[]{:S(2)}) collective-permute-start(bf16[64,4224]{1,0:T(8,128)(2,1)S(1)} %collective-permute-done.3), channel_id=1, source_target_pairs={{0,4},{1,5},{2,0},{3,1},{4,6},{5,7},{6,2},{7,3},{8,12},{9,13},{10,... | collective-permute-start | bytes 1622024 | tf_op jit(solution)/shard_map/ppermute | solution.py:151
  58.3 6.2 %collective-permute-start.6 = (bf16[256,4224]{1,0:T(8,128)(2,1)S(1)}, bf16[256,4224]{1,0:T(8,128)(2,1)S(1)}, u32[]{:S(2)}, u32[]{:S(2)}) collective-permute-start(bf16[256,4224]{1,0:T(8,128)(2,1)S(1)} %constant_dynamic-update-slice_fusion.own_rows.own_ref.refs_0_.refs_2_), channel_id=1, source_target_pairs={{0,1},{1,0},{2,3},{3,2},{4,5},{5,4},{6,7},{7,6},{8,9},{9,8},{10,11... | collective-permute-start | bytes 6488072 | tf_op jit(solution)/shard_map/ppermute | solution.py:151
  58.3 23.4 %collective-permute-start.9 = (bf16[256,1536]{1,0:T(8,128)(2,1)S(1)}, bf16[256,1536]{1,0:T(8,128)(2,1)S(1)}, u32[]{:S(2)}, u32[]{:S(2)}) collective-permute-start(bf16[256,1536]{1,0:T(8,128)(2,1)S(1)} %slice.123), channel_id=1, source_target_pairs={{0,8},{1,9},{2,10},{3,11},{4,12},{5,13},{6,14},{7,15},{8,0},{9,1},... | collective-permute-start | bytes 2359304 | tf_op jit(solution)/shard_map/ppermute | solution.py:151
  60.2 21.6 %collective-permute-start.8 = (bf16[256,1536]{1,0:T(8,128)(2,1)S(1)}, bf16[256,1536]{1,0:T(8,128)(2,1)S(1)}, u32[]{:S(2)}, u32[]{:S(2)}) collective-permute-start(bf16[256,1536]{1,0:T(8,128)(2,1)S(1)} %slice.122), channel_id=1, source_target_pairs={{0,16},{1,17},{2,18},{3,19},{4,20},{5,21},{6,22},{7,23},{8,24},{9,... | collective-permute-start | bytes 2359304 | tf_op jit(solution)/shard_map/ppermute | solution.py:151
  61.8 8.3 %collective-permute-start.12 = (bf16[64,2048]{1,0:T(8,128)(2,1)S(1)}, bf16[64,2048]{1,0:T(8,128)(2,1)S(1)}, u32[]{:S(2)}, u32[]{:S(2)}) collective-permute-start(bf16[64,2048]{1,0:T(8,128)(2,1)S(1)} %maximum_maximum_fusion), channel_id=1, source_target_pairs={{0,4},{1,5},{2,0},{3,1},{4,6},{5,7},{6,2},{7,3},{8,12},{9,13},{10,... | collective-permute-start | bytes 786440 | tf_op jit(solution)/shard_map/ppermute | solution.py:151
  68.6 6.1 %copy-start = (bf16[1,512,768]{2,1,0:T(8,128)(2,1)S(1)}, bf16[1,512,768]{2,1,0:T(8,128)(2,1)}, u32[]{:S(2)}) copy-start(bf16[1,512,768]{2,1,0:T(8,128)(2,1)} %param.13) | copy-start | bytes 2359300
  70.1 9.6 %collective-permute-start.13 = (bf16[64,2048]{1,0:T(8,128)(2,1)S(1)}, bf16[64,2048]{1,0:T(8,128)(2,1)S(1)}, u32[]{:S(2)}, u32[]{:S(2)}) collective-permute-start(bf16[64,2048]{1,0:T(8,128)(2,1)S(1)} %collective-permute-done.12), channel_id=1, source_target_pairs={{0,4},{1,5},{2,0},{3,1},{4,6},{5,7},{6,2},{7,3},{8,12},{9,13},{10,... | collective-permute-start | bytes 786440 | tf_op jit(solution)/shard_map/ppermute | solution.py:151
  73.6 13.6 %collective-permute-start.11 = (bf16[256,768]{1,0:T(8,128)(2,1)S(1)}, bf16[256,768]{1,0:T(8,128)(2,1)S(1)}, u32[]{:S(2)}, u32[]{:S(2)}) collective-permute-start(bf16[256,768]{1,0:T(8,128)(2,1)S(1)} %slice.125), channel_id=1, source_target_pairs={{0,8},{1,9},{2,10},{3,11},{4,12},{5,13},{6,14},{7,15},{8,0},{9,1},... | collective-permute-start | bytes 1179656 | tf_op jit(solution)/shard_map/ppermute | solution.py:151
  74.2 14.9 %collective-permute-start.10 = (bf16[256,768]{1,0:T(8,128)(2,1)S(1)}, bf16[256,768]{1,0:T(8,128)(2,1)S(1)}, u32[]{:S(2)}, u32[]{:S(2)}) collective-permute-start(bf16[256,768]{1,0:T(8,128)(2,1)S(1)} %slice.124), channel_id=1, source_target_pairs={{0,16},{1,17},{2,18},{3,19},{4,20},{5,21},{6,22},{7,23},{8,24},{9,... | collective-permute-start | bytes 1179656 | tf_op jit(solution)/shard_map/ppermute | solution.py:151
  79.8 13.5 %collective-permute-start.14 = (bf16[64,2048]{1,0:T(8,128)(2,1)S(1)}, bf16[64,2048]{1,0:T(8,128)(2,1)S(1)}, u32[]{:S(2)}, u32[]{:S(2)}) collective-permute-start(bf16[64,2048]{1,0:T(8,128)(2,1)S(1)} %collective-permute-done.13), channel_id=1, source_target_pairs={{0,4},{1,5},{2,0},{3,1},{4,6},{5,7},{6,2},{7,3},{8,12},{9,13},{10,... | collective-permute-start | bytes 786440 | tf_op jit(solution)/shard_map/ppermute | solution.py:151
  85.2 12.1 %collective-permute-start.17 = (bf16[256,768]{1,0:T(8,128)(2,1)S(1)}, bf16[256,768]{1,0:T(8,128)(2,1)S(1)}, u32[]{:S(2)}, u32[]{:S(2)}) collective-permute-start(bf16[256,768]{1,0:T(8,128)(2,1)S(1)} %get-tuple-element.71), channel_id=1, source_target_pairs={{0,8},{1,9},{2,10},{3,11},{4,12},{5,13},{6,14},{7,15},{8,0},{9,1},... | collective-permute-start | bytes 1179656 | tf_op jit(solution)/shard_map/ppermute | solution.py:151
  85.8 12.1 %collective-permute-start.18 = (bf16[256,768]{1,0:T(8,128)(2,1)S(1)}, bf16[256,768]{1,0:T(8,128)(2,1)S(1)}, u32[]{:S(2)}, u32[]{:S(2)}) collective-permute-start(bf16[256,768]{1,0:T(8,128)(2,1)S(1)} %get-tuple-element.72), channel_id=1, source_target_pairs={{0,16},{1,17},{2,18},{3,19},{4,20},{5,21},{6,22},{7,23},{8,24},{9,... | collective-permute-start | bytes 1179656 | tf_op jit(solution)/shard_map/ppermute | solution.py:151
  91.2 26.6 %collective-permute-start.22 = (bf16[512,768]{1,0:T(8,128)(2,1)S(1)}, bf16[512,768]{1,0:T(8,128)(2,1)S(1)}, u32[]{:S(2)}, u32[]{:S(2)}) collective-permute-start(bf16[512,768]{1,0:T(8,128)(2,1)S(1)} %get-tuple-element.89.d_gate_ref.term_ref), channel_id=1, source_target_pairs={{0,8},{1,9},{2,10},{3,11},{4,12},{5,13},{6,14},{7,15},{8,0},{9,1},... | collective-permute-start | bytes 2359304 | tf_op jit(solution)/shard_map/ppermute | solution.py:151
  92.0 25.8 %collective-permute-start.23 = (bf16[512,768]{1,0:T(8,128)(2,1)S(1)}, bf16[512,768]{1,0:T(8,128)(2,1)S(1)}, u32[]{:S(2)}, u32[]{:S(2)}) collective-permute-start(bf16[512,768]{1,0:T(8,128)(2,1)S(1)} %get-tuple-element.90.d_up_ref.term_ref), channel_id=1, source_target_pairs={{0,16},{1,17},{2,18},{3,19},{4,20},{5,21},{6,22},{7,23},{8,24},{9,... | collective-permute-start | bytes 2359304 | tf_op jit(solution)/shard_map/ppermute | solution.py:151
  97.3 4.0 %collective-permute-start.20 = (bf16[256,2048]{1,0:T(8,128)(2,1)S(1)}, bf16[256,2048]{1,0:T(8,128)(2,1)S(1)}, u32[]{:S(2)}, u32[]{:S(2)}) collective-permute-start(bf16[256,2048]{1,0:T(8,128)(2,1)S(1)} %pad_maximum_fusion.4.own_ref), channel_id=1, source_target_pairs={{0,1},{1,0},{2,3},{3,2},{4,5},{5,4},{6,7},{7,6},{8,9},{9,8},{10,11... | collective-permute-start | bytes 3145736 | tf_op jit(solution)/shard_map/ppermute | solution.py:151
  97.8 3.2 %collective-permute-start.19 = (bf16[64,4224]{1,0:T(8,128)(2,1)S(1)}, bf16[64,4224]{1,0:T(8,128)(2,1)S(1)}, u32[]{:S(2)}, u32[]{:S(2)}) collective-permute-start(bf16[64,4224]{1,0:T(8,128)(2,1)S(1)} %get-tuple-element.92), channel_id=1, source_target_pairs={{0,1},{1,0},{2,3},{3,2},{4,5},{5,4},{6,7},{7,6},{8,9},{9,8},{10,11... | collective-permute-start | bytes 1622024 | tf_op jit(solution)/shard_map/ppermute | solution.py:151
  97.9 11.8 %collective-permute-start.16 = (bf16[64,4224]{1,0:T(8,128)(2,1)S(1)}, bf16[64,4224]{1,0:T(8,128)(2,1)S(1)}, u32[]{:S(2)}, u32[]{:S(2)}) collective-permute-start(bf16[64,4224]{1,0:T(8,128)(2,1)S(1)} %get-tuple-element.114), channel_id=1, source_target_pairs={{0,1},{1,0},{2,3},{3,2},{4,5},{5,4},{6,7},{7,6},{8,9},{9,8},{10,11... | collective-permute-start | bytes 1622024 | tf_op jit(solution)/shard_map/ppermute | solution.py:151
  101.1 4.0 %collective-permute-start.15 = (bf16[128,4224]{1,0:T(8,128)(2,1)S(1)}, bf16[128,4224]{1,0:T(8,128)(2,1)S(1)}, u32[]{:S(2)}, u32[]{:S(2)}) collective-permute-start(bf16[128,4224]{1,0:T(8,128)(2,1)S(1)} %pad_maximum_fusion.3), channel_id=1, source_target_pairs={{0,1},{1,0},{2,3},{3,2},{4,5},{5,4},{6,7},{7,6},{8,9},{9,8},{10,11... | collective-permute-start | bytes 3244040 | tf_op jit(solution)/shard_map/ppermute | solution.py:151
  102.7 14.9 %collective-permute-start.21 = (bf16[64,4224]{1,0:T(8,128)(2,1)S(1)}, bf16[64,4224]{1,0:T(8,128)(2,1)S(1)}, u32[]{:S(2)}, u32[]{:S(2)}) collective-permute-start(bf16[64,4224]{1,0:T(8,128)(2,1)S(1)} %add_convert_fusion.2), channel_id=1, source_target_pairs={{0,4},{1,5},{2,0},{3,1},{4,6},{5,7},{6,2},{7,3},{8,12},{9,13},{10,... | collective-permute-start | bytes 1622024 | tf_op jit(solution)/shard_map/ppermute | solution.py:151
  107.9 23.6 %collective-permute-start.26 = (bf16[512,768]{1,0:T(8,128)(2,1)S(1)}, bf16[512,768]{1,0:T(8,128)(2,1)S(1)}, u32[]{:S(2)}, u32[]{:S(2)}) collective-permute-start(bf16[512,768]{1,0:T(8,128)(2,1)S(1)} %pad_maximum_fusion.6), channel_id=1, source_target_pairs={{0,16},{1,17},{2,18},{3,19},{4,20},{5,21},{6,22},{7,23},{8,24},{9,... | collective-permute-start | bytes 2359304 | tf_op jit(solution)/shard_map/ppermute | solution.py:151
  109.6 21.9 %collective-permute-start.25 = (bf16[512,768]{1,0:T(8,128)(2,1)S(1)}, bf16[512,768]{1,0:T(8,128)(2,1)S(1)}, u32[]{:S(2)}, u32[]{:S(2)}) collective-permute-start(bf16[512,768]{1,0:T(8,128)(2,1)S(1)} %pad_maximum_fusion.5), channel_id=1, source_target_pairs={{0,8},{1,9},{2,10},{3,11},{4,12},{5,13},{6,14},{7,15},{8,0},{9,1},... | collective-permute-start | bytes 2359304 | tf_op jit(solution)/shard_map/ppermute | solution.py:151
  117.8 14.6 %collective-permute-start.24 = (bf16[64,4224]{1,0:T(8,128)(2,1)S(1)}, bf16[64,4224]{1,0:T(8,128)(2,1)S(1)}, u32[]{:S(2)}, u32[]{:S(2)}) collective-permute-start(bf16[64,4224]{1,0:T(8,128)(2,1)S(1)} %add_convert_fusion.1), channel_id=1, source_target_pairs={{0,4},{1,5},{2,0},{3,1},{4,6},{5,7},{6,2},{7,3},{8,12},{9,13},{10,... | collective-permute-start | bytes 1622024 | tf_op jit(solution)/shard_map/ppermute | solution.py:151
  123.5 24.1 %collective-permute-start.29 = (bf16[512,768]{1,0:T(8,128)(2,1)S(1)}, bf16[512,768]{1,0:T(8,128)(2,1)S(1)}, u32[]{:S(2)}, u32[]{:S(2)}) collective-permute-start(bf16[512,768]{1,0:T(8,128)(2,1)S(1)} %get-tuple-element.100), channel_id=1, source_target_pairs={{0,8},{1,9},{2,10},{3,11},{4,12},{5,13},{6,14},{7,15},{8,0},{9,1},... | collective-permute-start | bytes 2359304 | tf_op jit(solution)/shard_map/ppermute | solution.py:151
  127.2 20.3 %collective-permute-start.28 = (bf16[512,768]{1,0:T(8,128)(2,1)S(1)}, bf16[512,768]{1,0:T(8,128)(2,1)S(1)}, u32[]{:S(2)}, u32[]{:S(2)}) collective-permute-start(bf16[512,768]{1,0:T(8,128)(2,1)S(1)} %get-tuple-element.99), channel_id=1, source_target_pairs={{0,16},{1,17},{2,18},{3,19},{4,20},{5,21},{6,22},{7,23},{8,24},{9,... | collective-permute-start | bytes 2359304 | tf_op jit(solution)/shard_map/ppermute | solution.py:151
  132.6 14.0 %collective-permute-start.27 = (bf16[64,4224]{1,0:T(8,128)(2,1)S(1)}, bf16[64,4224]{1,0:T(8,128)(2,1)S(1)}, u32[]{:S(2)}, u32[]{:S(2)}) collective-permute-start(bf16[64,4224]{1,0:T(8,128)(2,1)S(1)} %add_convert_fusion), channel_id=1, source_target_pairs={{0,4},{1,5},{2,0},{3,1},{4,6},{5,7},{6,2},{7,3},{8,12},{9,13},{10,... | collective-permute-start | bytes 1622024 | tf_op jit(solution)/shard_map/ppermute | solution.py:151
  136.1 10.5 %copy-start.4 = (s32[64,6]{0,1:T(8,128)S(1)}, s32[64,6]{0,1:T(8,128)}, u32[]{:S(2)}) copy-start(s32[64,6]{0,1:T(8,128)} %param.8) | copy-start | bytes 4612
